TPU v7x, 512 devices: a whole 4x8x8 slice. The times are simulated.
512 devices in a mesh: row: 16 (over y, core), col: 32 (over z, x).
Axes of the slice: x: 4, y: 8, z: 8, core: 2. Of those that a mesh axis runs over, the one named last changes fastest.
Arguments:
- inverse_top: bfloat16 [12288, 12288], P('row', 'col'), may hold values from -0.0546875 to 0.0546875
- inverse_mid: bfloat16 [2, 8192, 8192], P(None, 'row', 'col'), may hold values from -0.0625 to 0.0625
- inverse_low: bfloat16 [4, 8192, 8192], P(None, 'row', 'col'), may hold values from -0.0625 to 0.0625
- coupling_mid: bfloat16 [2, 4096, 8192], P(None, 'col', 'row'), may hold values from -0.0625 to 0.0625
- coupling_low: bfloat16 [4, 4096, 8192], P(None, 'col', 'row'), may hold values from -0.0625 to 0.0625
- source_top: float32 [12288, 16], P('col'), may hold values from -6 to 6
- source_mid: float32 [2, 8192, 16], P(None, 'col'), may hold values from -6 to 6
- source_low: float32 [4, 8192, 16], P(None, 'col'), may hold values from -6 to 6
- pivots_top: float32 [12288], P('row'), may hold values from -1.5 to 1.5
- pivots_mid: float32 [2, 8192], P(None, 'row'), may hold values from -1.5 to 1.5
- pivots_low: float32 [4, 8192], P(None, 'row'), may hold values from -1.5 to 1.5
- sizes_mid: int32 [2], replicated, may hold values from 4096 to 8192, as said below
- sizes_low: int32 [4], replicated, may hold values from 4096 to 8192, as said below
- blocks_mid: int32 [2, 32], replicated, may hold values from 0 to 95, as said below
- blocks_low: int32 [4, 32], replicated, may hold values from 0 to 63, as said below
Outputs:
- solution_top: float32 [12288, 16], P('col')
- solution_mid: float32 [2, 8192, 16], P(None, 'col')
- solution_low: float32 [4, 8192, 16], P(None, 'col')
Inputs may be any that keep to these rules, and one draw needn't show every extreme that they name: `sizes_mid`: one front of the level has used order exactly 8192, the other at least half of it. `sizes_low`: one front of the level has used order exactly 8192, the others at least half of it. `blocks_mid`: each list names distinct blocks in no particular order, the parent's last block among them. `blocks_low`: each list names distinct blocks in no particular order, the parent's last block among them.
All inputs are finite; a program needn't handle non-finite values.
Results may differ from a plain program's by a relative error of at most 0.015.
Values may be sent and summed in bfloat16 or wider, within the bound.
No kernel may reach another device: no remote copies, remote signals or barrier semaphores. Data moves between devices by JAX's collectives and lax.ppermute only.
A program may use at most 64 MiB of HBM per device.

v0:
```python
import jax
import jax.numpy as jnp
from jax import lax
from jax.sharding import PartitionSpec as P

BLOCK = 128


def level_mask(sizes, count, start):
    index = start + jnp.arange(count, dtype=jnp.int32)
    return (index[None, :] < sizes[:, None]).astype(jnp.float32)[:, :, None]


def diag_forward(inverse, residual, mask_in, mask_out):
    operand = (residual * mask_in).astype(jnp.bfloat16)
    partial_value = jnp.einsum("fij,fjc->fic", inverse, operand, preferred_element_type=jnp.float32)
    return lax.psum(partial_value, "col") * mask_out


def diag_backward(inverse, residual, mask_in, mask_out):
    operand = (residual * mask_in).astype(jnp.bfloat16)
    partial_value = jnp.einsum("fij,fic->fjc", inverse, operand, preferred_element_type=jnp.float32)
    return lax.psum(partial_value, "row") * mask_out


def child_update(coupling, solved):
    partial_value = jnp.einsum(
        "fuk,fkc->fuc", coupling, solved.astype(jnp.bfloat16), preferred_element_type=jnp.float32
    )
    return lax.psum(partial_value, "row")


def place_updates(update, blocks, parent_local):
    whole = lax.all_gather(update, "col", axis=1, tiled=True)
    fronts, urows, width = whole.shape
    tiles = whole.reshape(fronts, urows // BLOCK, BLOCK, width)
    local_blocks = parent_local // BLOCK
    targets = lax.axis_index("col") * local_blocks + jnp.arange(local_blocks, dtype=jnp.int32)
    select = (blocks[:, :, None] == targets[None, None, :]).astype(jnp.float32)
    placed = jnp.einsum(
        "fkb,fkrc->fbrc",
        select,
        tiles,
        preferred_element_type=jnp.float32,
        precision=lax.Precision.HIGHEST,
    )
    placed = placed.reshape(fronts // 2, 2, parent_local, width)
    return placed[:, 0] + placed[:, 1]


def child_rows(solved, blocks):
    parents, plocal, width = solved.shape
    children, listed = blocks.shape
    whole = lax.all_gather(solved, "col", axis=1, tiled=True)
    total_blocks = whole.shape[1] // BLOCK
    tiles = whole.reshape(parents, total_blocks, BLOCK, width)
    mine = listed // lax.axis_size("col")
    chosen = lax.dynamic_slice_in_dim(blocks, lax.axis_index("col") * mine, mine, 1)
    targets = jnp.arange(total_blocks, dtype=jnp.int32)
    select = (chosen[:, :, None] == targets[None, None, :]).astype(jnp.bfloat16)
    select = select.reshape(parents, 2, mine, total_blocks)
    picked = jnp.einsum("pskq,pqrc->pskrc", select, tiles, preferred_element_type=jnp.float32)
    return picked.astype(jnp.bfloat16).reshape(children, mine * BLOCK, width)


def parent_coupling(coupling, picked):
    partial_value = jnp.einsum("fuk,fuc->fkc", coupling, picked, preferred_element_type=jnp.float32)
    return lax.psum(partial_value, "col")


def sweep(inverses, couplings, sources, pivots, sizes, lists):
    depth = len(inverses)
    row_at = lax.axis_index("row")
    col_at = lax.axis_index("col")
    row_masks = []
    col_masks = []
    for level in range(depth):
        fronts, rows_here, cols_here = inverses[level].shape
        row_masks.append(level_mask(sizes[level], rows_here, row_at * rows_here))
        col_masks.append(level_mask(sizes[level], cols_here, col_at * cols_here))
    scaled = [None] * depth
    residual = sources[depth - 1]
    for level in range(depth - 1, -1, -1):
        solved = diag_forward(inverses[level], residual, col_masks[level], row_masks[level])
        scaled[level] = solved * pivots[level][:, :, None]
        if level > 0:
            update = child_update(couplings[level], solved)
            residual = sources[level - 1] - place_updates(
                update, lists[level], sources[level - 1].shape[1]
            )
    outputs = [None] * depth
    carried = None
    for level in range(depth):
        residual = scaled[level] if level == 0 else scaled[level] - carried
        solved = diag_backward(inverses[level], residual, row_masks[level], col_masks[level])
        outputs[level] = solved
        if level + 1 < depth:
            picked = child_rows(solved.astype(jnp.bfloat16), lists[level + 1])
            carried = parent_coupling(couplings[level + 1], picked)
    return outputs


def local(
    inverse_top,
    inverse_mid,
    inverse_low,
    coupling_mid,
    coupling_low,
    source_top,
    source_mid,
    source_low,
    pivots_top,
    pivots_mid,
    pivots_low,
    sizes_mid,
    sizes_low,
    blocks_mid,
    blocks_low,
):
    inverses = [inverse_top[None], inverse_mid, inverse_low]
    couplings = [None, coupling_mid, coupling_low]
    pivots = [pivots_top[None], pivots_mid, pivots_low]
    root_order = inverse_top.shape[0] * lax.axis_size("row")
    sizes = [jnp.full((1,), root_order, jnp.int32), sizes_mid, sizes_low]
    lists = [None, blocks_mid, blocks_low]
    sources = [source_top[None], source_mid, source_low]
    outputs = sweep(inverses, couplings, sources, pivots, sizes, lists)
    return (outputs[0][0], outputs[1], outputs[2])


def solution(mesh):
    placed = (
        P("row", "col"),
        P(None, "row", "col"),
        P(None, "row", "col"),
        P(None, "col", "row"),
        P(None, "col", "row"),
        P("col", None),
        P(None, "col", None),
        P(None, "col", None),
        P("row"),
        P(None, "row"),
        P(None, "row"),
        P(),
        P(),
        P(),
        P(),
    )
    return jax.shard_map(
        local,
        mesh=mesh,
        in_specs=placed,
        out_specs=(P("col", None), P(None, "col", None), P(None, "col", None)),
        check_vma=False,
    )
```

profile of v0, /device:TPU:1, one launch (start us, length us, event | category | flops | bytes accessed | tf_op | source)
XLA Modules:
  0.0 1273.8 jit_solution(6785822471916945202)
XLA Ops:
  7.2 0.0 all-reduce.6.cloned.1.call-start
  7.3 0.7 copy-done.15
  8.0 0.1 compare_convert_fusion.3
  8.0 0.4 copy-done
  8.4 1.9 convolution_bitcast_fusion.1
  10.3 0.0 all-reduce.6.cloned.1.call-update
  10.4 0.0 all-gather.2.cloned.1.call-start
  10.4 0.1 compare_convert_fusion.1
  10.5 154.5 %all-reduce.6.cloned.1.call-done = f32[4,512,16]{1,2,0:T(8,128)} async-done(((f32[4,512,16]{1,2,0:T(8,128)}), f32[4,512,16]{1,2,0:T(8,128)}) %all-reduce.6.cloned.1.call-update) | async-done | bytes 131088 | tf_op jit(solution)/shard_map/psum | solution.py:17
  165.0 1.1 convolution_bitcast_fusion.7
  166.1 46.9 %psum.71 = f32[4,128,16]{1,2,0:T(8,128)} all-reduce(f32[4,128,16]{1,2,0:T(8,128)S(1)} %convolution_bitcast_fusion.7), channel_id=1, replica_groups=mesh['row'=16,'col'=32] {'row'}, use_global_device_ids=true, to_apply=%region_1.0 | all-reduce | flops 8192 | bytes 65536 | tf_op jit(solution)/shard_map/psum | solution.py:30
  213.1 0.0 all-gather.2.cloned.1.call-update
  213.1 0.0 all-reduce.8.cloned.1.call-start
  213.1 0.7 copy-done.13
  213.8 0.2 dynamic-slice_reduce_fusion.1
  214.0 0.6 copy-done.14
  214.7 0.1 compare_convert_fusion.2
  214.7 0.1 compare_convert_fusion
  214.8 72.9 %all-gather.2.cloned.1.call-done = f32[4,4096,16]{1,2,0:T(8,128)} async-done(((f32[4,128,16]{1,2,0:T(8,128)}), f32[4,4096,16]{1,2,0:T(8,128)}) %all-gather.2.cloned.1.call-update) | async-done | bytes 1048592 | tf_op jit(solution)/shard_map/all_gather | solution.py:34
  287.7 1.4 copy.29
  289.2 0.5 fusion.25
  289.7 0.1 reshape.285
  289.7 0.5 copy-done.2
  290.2 0.2 copy-done.7
  290.4 0.9 convolution_bitcast_fusion.4
  291.3 0.0 all-reduce.8.cloned.1.call-update
  291.4 0.0 all-reduce.10.cloned.1.call-start
  291.4 150.3 %all-reduce.8.cloned.1.call-done = f32[2,512,16]{1,2,0:T(8,128)} async-done(((f32[2,512,16]{1,2,0:T(8,128)}), f32[2,512,16]{1,2,0:T(8,128)}) %all-reduce.8.cloned.1.call-update) | async-done | bytes 65552 | tf_op jit(solution)/shard_map/psum | solution.py:17
  441.7 1.0 convolution_bitcast_fusion.9
  442.7 46.9 %psum.73 = f32[2,128,16]{1,2,0:T(8,128)S(1)} all-reduce(f32[2,128,16]{1,2,0:T(8,128)S(1)} %convolution_bitcast_fusion.9), channel_id=1, replica_groups=mesh['row'=16,'col'=32] {'row'}, use_global_device_ids=true, to_apply=%region_3.0 | all-reduce | flops 4096 | bytes 32768 | tf_op jit(solution)/shard_map/psum | solution.py:30
  489.6 34.2 %all_gather.13 = f32[2,4096,16]{1,2,0:T(8,128)S(1)} all-gather(f32[2,128,16]{1,2,0:T(8,128)S(1)} %psum.73), channel_id=1, replica_groups=mesh['row'=16,'col'=32] {'col'}, dimensions={1}, use_global_device_ids=true | all-gather | bytes 540672 | tf_op jit(solution)/shard_map/all_gather | solution.py:34
  523.8 0.1 copy.30
  523.9 0.3 fusion.30
  524.2 0.7 copy-done.1
  524.9 0.0 copy-done.8
  525.0 0.3 convolution_bitcast_fusion.5
  525.2 112.4 %psum.74 = f32[1,768,16]{1,2,0:T(8,128)S(1)} all-reduce(f32[1,768,16]{1,2,0:T(8,128)S(1)} %convolution_bitcast_fusion.5), channel_id=1, replica_groups=mesh['row'=16,'col'=32] {'col'}, use_global_device_ids=true, to_apply=%region_4.0 | all-reduce | flops 12288 | bytes 98304 | tf_op jit(solution)/shard_map/psum | solution.py:17
  637.6 0.2 convolution_bitcast_fusion.8
  637.8 82.7 %psum.75 = f32[1,384,16]{1,2,0:T(8,128)S(1)} all-reduce(f32[1,384,16]{1,2,0:T(8,128)S(1)} %convolution_bitcast_fusion.8), channel_id=1, replica_groups=mesh['row'=16,'col'=32] {'row'}, use_global_device_ids=true, to_apply=%region_5.0 | all-reduce | flops 6144 | bytes 49152 | tf_op jit(solution)/shard_map/psum | solution.py:23
  720.5 0.6 multiply_convert_fusion.11
  721.1 32.1 %all_gather.14 = bf16[1,12288,16]{1,2,0:T(8,128)(2,1)S(1)} all-gather(bf16[1,384,16]{1,2,0:T(8,128)(2,1)S(1)} %get-tuple-element.5), channel_id=1, replica_groups=mesh['row'=16,'col'=32] {'col'}, dimensions={1}, use_global_device_ids=true | all-gather | bytes 405504 | tf_op jit(solution)/shard_map/all_gather | solution.py:54
  753.2 0.1 copy.31
  753.3 0.2 fusion.39
  753.5 0.1 copy.25
  753.7 0.8 convolution_bitcast_fusion.3
  754.5 0.0 all-reduce.10.cloned.1.call-update
  754.5 0.0 all-reduce.12.cloned.1.call-start
  754.6 0.2 dynamic-slice_reduce_fusion
  754.8 0.1 eq.87
  754.9 160.0 %all-reduce.10.cloned.1.call-done = f32[2,512,16]{1,2,0:T(8,128)} async-done(((f32[2,512,16]{1,2,0:T(8,128)}), f32[2,512,16]{1,2,0:T(8,128)}) %all-reduce.10.cloned.1.call-update) | async-done | bytes 65552 | tf_op jit(solution)/shard_map/psum | solution.py:68
  914.9 1.0 convolution_bitcast_fusion.6
  915.9 46.9 %psum.77 = f32[2,256,16]{1,2,0:T(8,128)S(1)} all-reduce(f32[2,256,16]{1,2,0:T(8,128)S(1)} %convolution_bitcast_fusion.6), channel_id=1, replica_groups=mesh['row'=16,'col'=32] {'row'}, use_global_device_ids=true, to_apply=%region_7.0 | all-reduce | flops 8192 | bytes 65536 | tf_op jit(solution)/shard_map/psum | solution.py:23
  962.8 0.6 fusion.46
  963.4 34.2 %all_gather.15 = bf16[2,8192,16]{1,2,0:T(8,128)(2,1)S(1)} all-gather(bf16[2,256,16]{1,2,0:T(8,128)(2,1)S(1)} %get-tuple-element.3), channel_id=1, replica_groups=mesh['row'=16,'col'=32] {'col'}, dimensions={1}, use_global_device_ids=true | all-gather | bytes 540672 | tf_op jit(solution)/shard_map/all_gather | solution.py:54
  997.6 0.1 copy.32
  997.7 0.2 convolution_convert_fusion
  998.0 0.8 convolution_bitcast_fusion
  998.8 0.0 all-reduce.12.cloned.1.call-update
  998.9 0.0 all-reduce.14.cloned.1.call-start
  998.9 156.9 %all-reduce.12.cloned.1.call-done = f32[4,512,16]{1,2,0:T(8,128)} async-done(((f32[4,512,16]{1,2,0:T(8,128)}), f32[4,512,16]{1,2,0:T(8,128)}) %all-reduce.12.cloned.1.call-update) | async-done | bytes 131088 | tf_op jit(solution)/shard_map/psum | solution.py:68
  1155.8 1.8 convolution_bitcast_fusion.2
  1157.6 0.0 all-reduce.14.cloned.1.call-update
  1157.6 107.8 %all-reduce.14.cloned.1.call-done = f32[4,256,16]{1,2,0:T(8,128)} async-done(((f32[4,256,16]{1,2,0:T(8,128)}), f32[4,256,16]{1,2,0:T(8,128)}) %all-reduce.14.cloned.1.call-update) | async-done | bytes 65552 | tf_op jit(solution)/shard_map/psum | solution.py:23
  1265.4 1.5 broadcast_multiply_fusion
  (32 shorter events, 0.1 us)
Async XLA Ops:
  7.2 1.2 copy-start
  7.2 157.8 %all-reduce.6.cloned.1.call-start = ((), (), s32[]{:S(2)}) async-start(), calls=%async_computation | async-start | bytes 262144 | tf_op jit(solution)/shard_map/psum | solution.py:17
  7.2 0.7 copy-start.15
  8.4 156.6 %copy-start.3 = (bf16[4,128,512]{2,1,0:T(8,128)(2,1)S(1)}, bf16[4,128,512]{2,1,0:T(8,128)(2,1)}, u32[]{:S(2)}) copy-start(bf16[4,128,512]{2,1,0:T(8,128)(2,1)} %param.19) | copy-start | bytes 1572868
  10.4 277.3 %all-gather.2.cloned.1.call-start = ((), (), s32[]{:S(2)}) async-start(), calls=%async_computation.1 | async-start | bytes 1081344 | tf_op jit(solution)/shard_map/all_gather | solution.py:34
  213.1 228.6 %all-reduce.8.cloned.1.call-start = ((), (), s32[]{:S(2)}) async-start(), calls=%async_computation.2 | async-start | bytes 131072 | tf_op jit(solution)/shard_map/psum | solution.py:17
  213.1 0.7 copy-start.13
  214.0 0.7 copy-start.14
  287.7 1.4 copy-start.10
  289.2 1.0 copy-start.2
  289.6 0.8 copy-start.7
  290.4 151.2 %copy-start.4 = (bf16[2,128,512]{2,1,0:T(8,128)(2,1)S(1)}, bf16[2,128,512]{2,1,0:T(8,128)(2,1)}, u32[]{:S(2)}) copy-start(bf16[2,128,512]{2,1,0:T(8,128)(2,1)} %param.18) | copy-start | bytes 786436
  291.4 623.5 %all-reduce.10.cloned.1.call-start = ((), (), s32[]{:S(2)}) async-start(), calls=%async_computation.3 | async-start | bytes 131072 | tf_op jit(solution)/shard_map/psum | solution.py:68
  523.9 1.1 copy-start.1
  524.2 0.8 copy-start.8
  525.2 112.4 %copy-start.11 = (f32[768]{0:T(1024)S(1)}, f32[768]{0:T(1024)}, u32[]{:S(2)}) copy-start(f32[768]{0:T(1024)} %param.23) | copy-start | bytes 9220
  754.5 160.4 %copy-start.6 = (f32[2,512,16]{1,2,0:T(8,128)S(1)}, f32[2,512,16]{1,2,0:T(8,128)}, u32[]{:S(2)}) copy-start(f32[2,512,16]{1,2,0:T(8,128)} %all-reduce.8.cloned.1.call-done) | copy-start | bytes 196612
  754.5 160.3 %copy-start.12 = (f32[2,512]{1,0:T(2,128)S(1)}, f32[2,512]{1,0:T(2,128)}, u32[]{:S(2)}) copy-start(f32[2,512]{1,0:T(2,128)} %param.24) | copy-start | bytes 12292
  754.5 401.2 %all-reduce.12.cloned.1.call-start = ((), (), s32[]{:S(2)}) async-start(), calls=%async_computation.4 | async-start | bytes 262144 | tf_op jit(solution)/shard_map/psum | solution.py:68
  998.0 157.8 %copy-start.9 = (f32[4,512]{1,0:T(4,128)S(1)}, f32[4,512]{1,0:T(4,128)}, u32[]{:S(2)}) copy-start(f32[4,512]{1,0:T(4,128)} %param.25) | copy-start | bytes 24580
  998.8 157.0 %copy-start.5 = (f32[4,512,16]{1,2,0:T(8,128)S(1)}, f32[4,512,16]{1,2,0:T(8,128)}, u32[]{:S(2)}) copy-start(f32[4,512,16]{1,2,0:T(8,128)} %all-reduce.6.cloned.1.call-done) | copy-start | bytes 393220
  998.9 266.6 %all-reduce.14.cloned.1.call-start = ((), (), s32[]{:S(2)}) async-start(), calls=%async_computation.5 | async-start | bytes 131072 | tf_op jit(solution)/shard_map/psum | solution.py:23
Sparse Core Ops, SparseCore 0:
  11.5 153.4 all-reduce.5
  213.2 74.4 all-gather.1
  292.1 149.4 all-reduce.7
  754.6 160.1 all-reduce.9
  999.0 156.7 all-reduce.11
  1158.5 106.8 all-reduce.13
where the time goes:
time: 1270 us
  waiting for transfers between devices  802 us (63%)
  blocking collectives  436 us (34%)
  between operations  14.3 us (1%)
    psum x2, waiting for transfers between devices, parent_coupling(): return lax.psum(partial_value, 'col')  317 us
    psum x2, waiting for transfers between devices, diag_forward(): return lax.psum(partial_value, 'col') * mask_out  305 us
    psum x2, blocking collectives, diag_backward(): return lax.psum(partial_value, 'row') * mask_out  130 us
    psum x1, blocking collectives, diag_forward(): return lax.psum(partial_value, 'col') * mask_out  112 us
    psum x1, waiting for transfers between devices, diag_backward(): return lax.psum(partial_value, 'row') * mask_out  108 us
    psum x2, blocking collectives, child_update(): return lax.psum(partial_value, 'row')  93.8 us
    all_gather x1, waiting for transfers between devices, place_updates(): whole = lax.all_gather(update, 'col', axis=1, tiled=True)  72.9 us
    all_gather x2, blocking collectives, child_rows(): whole = lax.all_gather(solved, 'col', axis=1, tiled=True)  66.3 us
  transfers between devices with their start and end apart: 6, of which 6 were waited for; matrix products, arithmetic and copies ran while one was open for 0% of the time, Pallas kernels for 0%

commit v1 on v0

v1 whole, which is shorter than its diff:
```python
import jax
import jax.numpy as jnp
from jax import lax
from jax.sharding import PartitionSpec as P

BLOCK = 128
BF16 = jnp.bfloat16
F32 = jnp.float32


def level_mask(sizes, count, start):
    index = start + jnp.arange(count, dtype=jnp.int32)
    return (index[None, :] < sizes[:, None]).astype(F32)[:, None, :]


def exchange(value, axis, masks):
    size = lax.axis_size(axis)
    return [lax.ppermute(value, axis, [(i, i ^ m) for i in range(size)]) for m in masks]


def sum_stage(partial, axis, masks):
    own = partial.astype(BF16)
    parts = [own] + exchange(own, axis, masks)
    parts = [part.astype(F32) for part in parts]
    while len(parts) > 1:
        parts = [parts[i] + parts[i + 1] for i in range(0, len(parts), 2)]
    return parts[0]


def sum_over_col(partial):
    size = lax.axis_size("col")
    step = 1
    while step < size:
        if step * 4 <= size:
            masks = (step, 2 * step, 3 * step)
            partial = sum_stage(partial, "col", masks)
            step *= 4
        else:
            partial = sum_stage(partial, "col", (step,))
            step *= 2
    return partial


def spread(value, axis):
    size = lax.axis_size(axis)
    copies = jnp.broadcast_to(value.astype(BF16)[None], (size,) + value.shape)
    return lax.all_to_all(copies, axis, 0, 0, tiled=True)


def sum_over_row(partial):
    return jnp.sum(spread(partial, "row").astype(F32), axis=0)


def times_rows(matrix, vector):
    return jnp.einsum("fij,fcj->fci", matrix, vector.astype(BF16), preferred_element_type=F32)


def times_columns(matrix, vector):
    return jnp.einsum("fij,fci->fcj", matrix, vector.astype(BF16), preferred_element_type=F32)


def place_updates(update, blocks, parent_local):
    whole = spread(update, "col")
    count, fronts, width, _ = whole.shape
    local_blocks = parent_local // BLOCK
    targets = lax.axis_index("col") * local_blocks + jnp.arange(local_blocks, dtype=jnp.int32)
    select = (blocks.T[:, :, None] == targets[None, None, :]).astype(F32)
    placed = []
    for b in range(local_blocks):
        terms = select[:, :, b][:, :, None, None] * whole.astype(F32)
        summed = jnp.sum(terms.reshape(count, fronts // 2, 2, width, BLOCK), axis=(0, 2))
        placed.append(summed)
    return jnp.concatenate(placed, axis=-1)


def child_rows(solved, blocks):
    whole = spread(solved, "col")
    _, parents, width, plocal = whole.shape
    local_blocks = plocal // BLOCK
    children = blocks.shape[0]
    mine = lax.dynamic_slice_in_dim(blocks, lax.axis_index("col"), 1, 1)[:, 0]
    picked = []
    for c in range(children):
        at = (mine[c] // local_blocks, c // 2, 0, (mine[c] % local_blocks) * BLOCK)
        picked.append(lax.dynamic_slice(whole, at, (1, 1, width, BLOCK))[0])
    return jnp.concatenate(picked, axis=0)


def sweep(inverses, couplings, sources, pivots, sizes, lists):
    depth = len(inverses)
    row_at = lax.axis_index("row")
    col_at = lax.axis_index("col")
    row_masks = []
    col_masks = []
    for level in range(depth):
        fronts, rows_here, cols_here = inverses[level].shape
        row_masks.append(level_mask(sizes[level], rows_here, row_at * rows_here))
        col_masks.append(level_mask(sizes[level], cols_here, col_at * cols_here))
    scaled = [None] * depth
    residual = sources[depth - 1]
    for level in range(depth - 1, -1, -1):
        solved = sum_over_col(times_rows(inverses[level], residual * col_masks[level]))
        solved = solved * row_masks[level]
        scaled[level] = solved * pivots[level][:, None, :]
        if level > 0:
            update = sum_over_row(times_rows(couplings[level], solved))
            residual = sources[level - 1] - place_updates(
                update, lists[level], sources[level - 1].shape[-1]
            )
    outputs = [None] * depth
    carried = None
    for level in range(depth):
        residual = scaled[level] if level == 0 else scaled[level] - carried
        solved = sum_over_row(times_columns(inverses[level], residual * row_masks[level]))
        solved = solved * col_masks[level]
        outputs[level] = solved
        if level + 1 < depth:
            picked = child_rows(solved, lists[level + 1])
            carried = sum_over_col(times_columns(couplings[level + 1], picked))
    return outputs


def local(
    inverse_top,
    inverse_mid,
    inverse_low,
    coupling_mid,
    coupling_low,
    source_top,
    source_mid,
    source_low,
    pivots_top,
    pivots_mid,
    pivots_low,
    sizes_mid,
    sizes_low,
    blocks_mid,
    blocks_low,
):
    inverses = [inverse_top[None], inverse_mid, inverse_low]
    couplings = [None, coupling_mid, coupling_low]
    pivots = [pivots_top[None], pivots_mid, pivots_low]
    root_order = inverse_top.shape[0] * lax.axis_size("row")
    sizes = [jnp.full((1,), root_order, jnp.int32), sizes_mid, sizes_low]
    lists = [None, blocks_mid, blocks_low]
    sources = [source_top[None], source_mid, source_low]
    sources = [jnp.swapaxes(source, 1, 2) for source in sources]
    outputs = sweep(inverses, couplings, sources, pivots, sizes, lists)
    outputs = [jnp.swapaxes(output, 1, 2) for output in outputs]
    return (outputs[0][0], outputs[1], outputs[2])


def solution(mesh):
    placed = (
        P("row", "col"),
        P(None, "row", "col"),
        P(None, "row", "col"),
        P(None, "col", "row"),
        P(None, "col", "row"),
        P("col", None),
        P(None, "col", None),
        P(None, "col", None),
        P("row"),
        P(None, "row"),
        P(None, "row"),
        P(),
        P(),
        P(),
        P(),
    )
    return jax.shard_map(
        local,
        mesh=mesh,
        in_specs=placed,
        out_specs=(P("col", None), P(None, "col", None), P(None, "col", None)),
        check_vma=False,
    )
```

time: 1270 us -> 369 us (0.29)
  waiting for transfers between devices: 802 us -> 116 us
  blocking collectives: 436 us -> 60.9 us
  starting transfers between devices: 0.25 us -> 158 us
    psum x5 -> x0, waiting for transfers between devices: 729 us -> none  [the longest x2 317 us: parent_coupling(): return lax.psum(partial_value, 'col')]
    psum x5 -> x0, blocking collectives: 336 us -> none  [the longest x2 130 us: diag_backward(): return lax.psum(partial_value, 'row') * mask_out]
    ppermute x0 -> x35, starting transfers between devices: none -> 116 us  [exchange(): lax.ppermute(value, axis, [(i, i ^ m) for i in range(size)])]
    all_gather x3 -> x0, blocking collectives: 100 us -> none  [the longest x2 66.3 us: child_rows(): whole = lax.all_gather(solved, 'col', axis=1, tiled=True)]
    all_gather x1 -> x0, waiting for transfers between devices: 72.9 us -> none  [place_updates(): whole = lax.all_gather(update, 'col', axis=1, tiled=True)]
    all_to_all x0 -> x6, waiting for transfers between devices: none -> 70.8 us  [spread(): return lax.all_to_all(copies, axis, 0, 0, tiled=True)]
    all_to_all x0 -> x3, blocking collectives: none -> 60.9 us  [spread(): return lax.all_to_all(copies, axis, 0, 0, tiled=True)]
    ppermute x0 -> x35, waiting for transfers between devices: none -> 45.3 us  [exchange(): lax.ppermute(value, axis, [(i, i ^ m) for i in range(size)])]
  transfers between devices with their start and end apart: 6 -> 41, of which waited for: 6 -> 30; matrix products, arithmetic and copies ran while one was open for 0% -> 1% of each run, Pallas kernels for 0% -> 0%
where the time goes in v1:
time: 369 us; the launch traced here: 367 us
  starting transfers between devices  158 us (43%)
  waiting for transfers between devices  116 us (31%)
  blocking collectives  60.9 us (17%)
  between operations  15.5 us (4%)
  local copies, waits for them, and re-layouts  9.68 us (3%)
    ppermute x35, starting transfers between devices, exchange(): lax.ppermute(value, axis, [(i, i ^ m) for i in range(size)])  116 us
    all_to_all x6, waiting for transfers between devices, spread(): return lax.all_to_all(copies, axis, 0, 0, tiled=True)  70.8 us
    all_to_all x3, blocking collectives, spread(): return lax.all_to_all(copies, axis, 0, 0, tiled=True)  60.9 us
    ppermute x35, waiting for transfers between devices, exchange(): lax.ppermute(value, axis, [(i, i ^ m) for i in range(size)])  45.3 us
    all_to_all x6, starting transfers between devices, spread(): return lax.all_to_all(copies, axis, 0, 0, tiled=True)  42.1 us
  transfers between devices with their start and end apart: 41, of which 30 were waited for; matrix products, arithmetic and copies ran while one was open for 1% of the time, Pallas kernels for 0%

profile of v1, /device:TPU:1, one launch (start us, length us, event | category | flops | bytes accessed | tf_op | source)
XLA Modules:
  0.0 366.6 jit_solution(16967179547239642628)
XLA Ops:
  1.9 1.2 convolution_convert_fusion.1
  3.1 5.4 %collective-permute-start.2 = (bf16[4,16,512]{2,1,0:T(8,128)(2,1)S(1)}, bf16[4,16,512]{2,1,0:T(8,128)(2,1)S(1)}, u32[]{:S(2)}, u32[]{:S(2)}) collective-permute-start(bf16[4,16,512]{2,1,0:T(8,128)(2,1)S(1)} %convolution_convert_fusion.1), channel_id=1, source_target_pairs={{0,3},{1,2},{2,1},{3,0},{4,7},{5,6},{6,5},{7,4},{8,11},{9,10},{10,... | collective-permute-start | bytes 196616 | tf_op jit(solution)/shard_map/ppermute | solution.py:18
  8.5 2.4 collective-permute-start.1
  10.9 2.0 collective-permute-start
  12.9 2.1 collective-permute-done.1
  15.9 7.9 %collective-permute-start.5 = (bf16[4,16,512]{2,1,0:T(8,128)(2,1)S(1)}, bf16[4,16,512]{2,1,0:T(8,128)(2,1)S(1)}, u32[]{:S(2)}, u32[]{:S(2)}) collective-permute-start(bf16[4,16,512]{2,1,0:T(8,128)(2,1)S(1)} %add_convert_fusion.3), channel_id=1, source_target_pairs={{0,12},{1,13},{2,14},{3,15},{4,8},{5,9},{6,10},{7,11},{8,4},{9,5},... | collective-permute-start | bytes 196616 | tf_op jit(solution)/shard_map/ppermute | solution.py:18
  23.9 1.9 collective-permute-start.4
  25.8 2.2 collective-permute-start.3
  28.0 2.2 collective-permute-done.4
  30.9 7.8 %collective-permute-start.6 = (bf16[4,16,512]{2,1,0:T(8,128)(2,1)S(1)}, bf16[4,16,512]{2,1,0:T(8,128)(2,1)S(1)}, u32[]{:S(2)}, u32[]{:S(2)}) collective-permute-start(bf16[4,16,512]{2,1,0:T(8,128)(2,1)S(1)} %add_convert_fusion.2), channel_id=1, source_target_pairs={{0,16},{1,17},{2,18},{3,19},{4,20},{5,21},{6,22},{7,23},{8,24},{9,... | collective-permute-start | bytes 196616 | tf_op jit(solution)/shard_map/ppermute | solution.py:18
  38.9 1.6 collective-permute-done.6
  40.8 23.2 %all_to_all.45 = bf16[16,4,16,128]{3,2,1,0:T(8,128)(2,1)S(1)} all-to-all(bf16[16,4,16,128]{3,2,1,0:T(8,128)(2,1)S(1)} %broadcast_in_dim.21), channel_id=1, replica_groups=mesh['row'=16,'col'=32] {'row'}, dimensions={0} | all-to-all | bytes 524288 | tf_op jit(solution)/shard_map/all_to_all | solution.py:47
  65.0 10.3 %all-to-all-start.1 = ((bf16[32,4,16,128]{3,2,1,0:T(8,128)(2,1)}), bf16[32,4,16,128]{3,2,1,0:T(8,128)(2,1)S(1)}, u32[]{:S(2)}, u32[]{:S(2)}) async-start(bf16[32,4,16,128]{3,2,1,0:T(8,128)(2,1)} %broadcast_in_dim.22), calls=%async_computation.1 | async-start | bytes 1048576 | tf_op jit(solution)/shard_map/all_to_all | solution.py:47
  75.7 17.0 %all-to-all-done.1 = bf16[32,4,16,128]{3,2,1,0:T(8,128)(2,1)S(1)} async-done(((bf16[32,4,16,128]{3,2,1,0:T(8,128)(2,1)}), bf16[32,4,16,128]{3,2,1,0:T(8,128)(2,1)S(1)}, u32[]{:S(2)}, u32[]{:S(2)}) %all-to-all-start.1) | async-done | bytes 524320 | tf_op jit(solution)/shard_map/all_to_all | solution.py:47
  94.0 4.5 %collective-permute-start.9 = (bf16[2,16,512]{2,1,0:T(8,128)(2,1)S(1)}, bf16[2,16,512]{2,1,0:T(8,128)(2,1)S(1)}, u32[]{:S(2)}, u32[]{:S(2)}) collective-permute-start(bf16[2,16,512]{2,1,0:T(8,128)(2,1)S(1)} %convolution_convert_fusion.4), channel_id=1, source_target_pairs={{0,3},{1,2},{2,1},{3,0},{4,7},{5,6},{6,5},{7,4},{8,11},{9,10},{10,... | collective-permute-start | bytes 98312 | tf_op jit(solution)/shard_map/ppermute | solution.py:18
  98.5 2.3 collective-permute-start.8
  100.8 2.3 collective-permute-start.7
  103.2 1.5 collective-permute-done.8
  105.8 2.8 collective-permute-start.12
  108.7 2.3 collective-permute-start.11
  111.0 4.1 %collective-permute-start.10 = (bf16[2,16,512]{2,1,0:T(8,128)(2,1)S(1)}, bf16[2,16,512]{2,1,0:T(8,128)(2,1)S(1)}, u32[]{:S(2)}, u32[]{:S(2)}) collective-permute-start(bf16[2,16,512]{2,1,0:T(8,128)(2,1)S(1)} %add_convert_fusion.7), channel_id=1, source_target_pairs={{0,4},{1,5},{2,6},{3,7},{4,0},{5,1},{6,2},{7,3},{8,12},{9,13},{10,... | collective-permute-start | bytes 98312 | tf_op jit(solution)/shard_map/ppermute | solution.py:18
  115.1 1.3 collective-permute-done.10
  116.4 3.0 collective-permute-start.13
  119.5 5.7 %collective-permute-done.13 = bf16[2,16,512]{2,1,0:T(8,128)(2,1)S(1)} collective-permute-done((bf16[2,16,512]{2,1,0:T(8,128)(2,1)S(1)}, bf16[2,16,512]{2,1,0:T(8,128)(2,1)S(1)}, u32[]{:S(2)}, u32[]{:S(2)}) %collective-permute-start.13) | collective-permute-done | bytes 32800 | tf_op jit(solution)/shard_map/ppermute | solution.py:18
  126.1 8.3 %all-to-all-start.2 = ((bf16[16,2,16,128]{3,2,1,0:T(8,128)(2,1)}), bf16[16,2,16,128]{3,2,1,0:T(8,128)(2,1)S(1)}, u32[]{:S(2)}, u32[]{:S(2)}) async-start(bf16[16,2,16,128]{3,2,1,0:T(8,128)(2,1)} %broadcast_in_dim.23), calls=%async_computation.2 | async-start | bytes 262144 | tf_op jit(solution)/shard_map/all_to_all | solution.py:47
  134.4 9.2 %all-to-all-done.2 = bf16[16,2,16,128]{3,2,1,0:T(8,128)(2,1)S(1)} async-done(((bf16[16,2,16,128]{3,2,1,0:T(8,128)(2,1)}), bf16[16,2,16,128]{3,2,1,0:T(8,128)(2,1)S(1)}, u32[]{:S(2)}, u32[]{:S(2)}) %all-to-all-start.2) | async-done | bytes 131104 | tf_op jit(solution)/shard_map/all_to_all | solution.py:47
  144.3 5.2 %all-to-all-start.3 = ((bf16[32,2,16,128]{3,2,1,0:T(8,128)(2,1)}), bf16[32,2,16,128]{3,2,1,0:T(8,128)(2,1)S(1)}, u32[]{:S(2)}, u32[]{:S(2)}) async-start(bf16[32,2,16,128]{3,2,1,0:T(8,128)(2,1)} %broadcast_in_dim.24), calls=%async_computation.3 | async-start | bytes 524288 | tf_op jit(solution)/shard_map/all_to_all | solution.py:47
  150.6 11.2 %all-to-all-done.3 = bf16[32,2,16,128]{3,2,1,0:T(8,128)(2,1)S(1)} async-done(((bf16[32,2,16,128]{3,2,1,0:T(8,128)(2,1)}), bf16[32,2,16,128]{3,2,1,0:T(8,128)(2,1)S(1)}, u32[]{:S(2)}, u32[]{:S(2)}) %all-to-all-start.3) | async-done | bytes 262176 | tf_op jit(solution)/shard_map/all_to_all | solution.py:47
  162.8 3.7 %collective-permute-start.16 = (bf16[1,16,768]{2,1,0:T(8,128)(2,1)S(1)}, bf16[1,16,768]{2,1,0:T(8,128)(2,1)S(1)}, u32[]{:S(2)}, u32[]{:S(2)}) collective-permute-start(bf16[1,16,768]{2,1,0:T(8,128)(2,1)S(1)} %fusion), channel_id=1, source_target_pairs={{0,3},{1,2},{2,1},{3,0},{4,7},{5,6},{6,5},{7,4},{8,11},{9,10},{10,... | collective-permute-start | bytes 73736 | tf_op jit(solution)/shard_map/ppermute | solution.py:18
  166.5 2.1 collective-permute-start.15
  168.7 3.2 collective-permute-start.14
  173.6 3.4 collective-permute-start.19
  177.0 2.4 collective-permute-start.18
  179.4 3.4 collective-permute-start.17
  184.1 3.5 collective-permute-start.20
  187.6 5.0 %collective-permute-done.20 = bf16[1,16,768]{2,1,0:T(8,128)(2,1)S(1)} collective-permute-done((bf16[1,16,768]{2,1,0:T(8,128)(2,1)S(1)}, bf16[1,16,768]{2,1,0:T(8,128)(2,1)S(1)}, u32[]{:S(2)}, u32[]{:S(2)}) %collective-permute-start.20) | collective-permute-done | bytes 24608 | tf_op jit(solution)/shard_map/ppermute | solution.py:18
  192.8 18.2 %all_to_all.46 = bf16[16,1,16,384]{3,2,1,0:T(8,128)(2,1)S(1)} all-to-all(bf16[16,1,16,384]{3,2,1,0:T(8,128)(2,1)S(1)} %broadcast_in_dim.25), channel_id=1, replica_groups=mesh['row'=16,'col'=32] {'row'}, dimensions={0} | all-to-all | bytes 393216 | tf_op jit(solution)/shard_map/all_to_all | solution.py:47
  211.8 5.3 %all-to-all-start.5 = ((bf16[32,1,16,384]{3,2,1,0:T(8,128)(2,1)}), bf16[32,1,16,384]{3,2,1,0:T(8,128)(2,1)S(1)}, u32[]{:S(2)}, u32[]{:S(2)}) async-start(bf16[32,1,16,384]{3,2,1,0:T(8,128)(2,1)} %broadcast_in_dim.26), calls=%async_computation.5 | async-start | bytes 786432 | tf_op jit(solution)/shard_map/all_to_all | solution.py:47
  221.7 10.2 %all-to-all-done.5 = bf16[32,1,16,384]{3,2,1,0:T(8,128)(2,1)S(1)} async-done(((bf16[32,1,16,384]{3,2,1,0:T(8,128)(2,1)}), bf16[32,1,16,384]{3,2,1,0:T(8,128)(2,1)S(1)}, u32[]{:S(2)}, u32[]{:S(2)}) %all-to-all-start.5) | async-done | bytes 393248 | tf_op jit(solution)/shard_map/all_to_all | solution.py:47
  232.1 3.8 %collective-permute-start.23 = (bf16[2,16,512]{2,1,0:T(8,128)(2,1)S(1)}, bf16[2,16,512]{2,1,0:T(8,128)(2,1)S(1)}, u32[]{:S(2)}, u32[]{:S(2)}) collective-permute-start(bf16[2,16,512]{2,1,0:T(8,128)(2,1)S(1)} %convolution_convert_fusion.3), channel_id=1, source_target_pairs={{0,3},{1,2},{2,1},{3,0},{4,7},{5,6},{6,5},{7,4},{8,11},{9,10},{10,... | collective-permute-start | bytes 98312 | tf_op jit(solution)/shard_map/ppermute | solution.py:18
  235.9 2.3 collective-permute-start.22
  238.1 3.0 collective-permute-start.21
  242.8 3.8 %collective-permute-start.26 = (bf16[2,16,512]{2,1,0:T(8,128)(2,1)S(1)}, bf16[2,16,512]{2,1,0:T(8,128)(2,1)S(1)}, u32[]{:S(2)}, u32[]{:S(2)}) collective-permute-start(bf16[2,16,512]{2,1,0:T(8,128)(2,1)S(1)} %add_convert_fusion.5), channel_id=1, source_target_pairs={{0,12},{1,13},{2,14},{3,15},{4,8},{5,9},{6,10},{7,11},{8,4},{9,5},... | collective-permute-start | bytes 98312 | tf_op jit(solution)/shard_map/ppermute | solution.py:18
  246.6 2.5 collective-permute-start.25
  249.1 3.0 collective-permute-start.24
  252.6 1.1 collective-permute-done.24
  253.8 3.4 collective-permute-start.27
  257.2 5.2 %collective-permute-done.27 = bf16[2,16,512]{2,1,0:T(8,128)(2,1)S(1)} collective-permute-done((bf16[2,16,512]{2,1,0:T(8,128)(2,1)S(1)}, bf16[2,16,512]{2,1,0:T(8,128)(2,1)S(1)}, u32[]{:S(2)}, u32[]{:S(2)}) %collective-permute-start.27) | collective-permute-done | bytes 32800 | tf_op jit(solution)/shard_map/ppermute | solution.py:18
  262.6 19.5 %all_to_all.47 = bf16[16,2,16,256]{3,2,1,0:T(8,128)(2,1)S(1)} all-to-all(bf16[16,2,16,256]{3,2,1,0:T(8,128)(2,1)S(1)} %broadcast_in_dim.27), channel_id=1, replica_groups=mesh['row'=16,'col'=32] {'row'}, dimensions={0} | all-to-all | bytes 524288 | tf_op jit(solution)/shard_map/all_to_all | solution.py:47
  283.6 5.7 %all-to-all-start.7 = ((bf16[32,2,16,256]{3,2,1,0:T(8,128)(2,1)}), bf16[32,2,16,256]{3,2,1,0:T(8,128)(2,1)S(1)}, u32[]{:S(2)}, u32[]{:S(2)}) async-start(bf16[32,2,16,256]{3,2,1,0:T(8,128)(2,1)} %broadcast_in_dim.28), calls=%async_computation.7 | async-start | bytes 1048576 | tf_op jit(solution)/shard_map/all_to_all | solution.py:47
  300.3 6.4 %all-to-all-done.7 = bf16[32,2,16,256]{3,2,1,0:T(8,128)(2,1)S(1)} async-done(((bf16[32,2,16,256]{3,2,1,0:T(8,128)(2,1)}), bf16[32,2,16,256]{3,2,1,0:T(8,128)(2,1)S(1)}, u32[]{:S(2)}, u32[]{:S(2)}) %all-to-all-start.7) | async-done | bytes 524320 | tf_op jit(solution)/shard_map/all_to_all | solution.py:47
  306.8 4.3 %collective-permute-start.30 = (bf16[4,16,512]{2,1,0:T(8,128)(2,1)S(1)}, bf16[4,16,512]{2,1,0:T(8,128)(2,1)S(1)}, u32[]{:S(2)}, u32[]{:S(2)}) collective-permute-start(bf16[4,16,512]{2,1,0:T(8,128)(2,1)S(1)} %convolution_convert_fusion), channel_id=1, source_target_pairs={{0,3},{1,2},{2,1},{3,0},{4,7},{5,6},{6,5},{7,4},{8,11},{9,10},{10,... | collective-permute-start | bytes 196616 | tf_op jit(solution)/shard_map/ppermute | solution.py:18
  311.2 2.5 collective-permute-start.29
  313.7 2.2 collective-permute-start.28
  315.9 1.8 collective-permute-done.29
  317.7 1.3 collective-permute-done.28
  319.0 2.7 collective-permute-start.33
  321.7 2.9 collective-permute-start.32
  324.6 3.7 %collective-permute-start.31 = (bf16[4,16,512]{2,1,0:T(8,128)(2,1)S(1)}, bf16[4,16,512]{2,1,0:T(8,128)(2,1)S(1)}, u32[]{:S(2)}, u32[]{:S(2)}) collective-permute-start(bf16[4,16,512]{2,1,0:T(8,128)(2,1)S(1)} %add_convert_fusion.1), channel_id=1, source_target_pairs={{0,4},{1,5},{2,6},{3,7},{4,0},{5,1},{6,2},{7,3},{8,12},{9,13},{10,... | collective-permute-start | bytes 196616 | tf_op jit(solution)/shard_map/ppermute | solution.py:18
  329.0 1.6 collective-permute-done.31
  330.7 3.0 collective-permute-start.34
  333.7 6.4 %collective-permute-done.34 = bf16[4,16,512]{2,1,0:T(8,128)(2,1)S(1)} collective-permute-done((bf16[4,16,512]{2,1,0:T(8,128)(2,1)S(1)}, bf16[4,16,512]{2,1,0:T(8,128)(2,1)S(1)}, u32[]{:S(2)}, u32[]{:S(2)}) %collective-permute-start.34) | collective-permute-done | bytes 65568 | tf_op jit(solution)/shard_map/ppermute | solution.py:18
  341.2 7.3 %all-to-all-start.8 = ((bf16[16,4,16,256]{3,2,1,0:T(8,128)(2,1)}), bf16[16,4,16,256]{3,2,1,0:T(8,128)(2,1)S(1)}, u32[]{:S(2)}, u32[]{:S(2)}) async-start(bf16[16,4,16,256]{3,2,1,0:T(8,128)(2,1)} %broadcast_in_dim.29), calls=%async_computation.8 | async-start | bytes 1048576 | tf_op jit(solution)/shard_map/all_to_all | solution.py:47
  349.1 16.7 %all-to-all-done.8 = bf16[16,4,16,256]{3,2,1,0:T(8,128)(2,1)S(1)} async-done(((bf16[16,4,16,256]{3,2,1,0:T(8,128)(2,1)}), bf16[16,4,16,256]{3,2,1,0:T(8,128)(2,1)S(1)}, u32[]{:S(2)}, u32[]{:S(2)}) %all-to-all-start.8) | async-done | bytes 524320 | tf_op jit(solution)/shard_map/all_to_all | solution.py:47
  (115 shorter events, 23.5 us)
Async XLA Ops:
  0.6 1.2 copy-start
  0.7 0.7 copy-start.13
  3.1 37.4 %copy-start.3 = (bf16[4,128,512]{2,1,0:T(8,128)(2,1)S(1)}, bf16[4,128,512]{2,1,0:T(8,128)(2,1)}, u32[]{:S(2)}) copy-start(bf16[4,128,512]{2,1,0:T(8,128)(2,1)} %param.19) | copy-start | bytes 1572868
  3.1 9.8 %collective-permute-start.2 = (bf16[4,16,512]{2,1,0:T(8,128)(2,1)S(1)}, bf16[4,16,512]{2,1,0:T(8,128)(2,1)S(1)}, u32[]{:S(2)}, u32[]{:S(2)}) collective-permute-start(bf16[4,16,512]{2,1,0:T(8,128)(2,1)S(1)} %convolution_convert_fusion.1), channel_id=1, source_target_pairs={{0,3},{1,2},{2,1},{3,0},{4,7},{5,6},{6,5},{7,4},{8,11},{9,10},{10,... | collective-permute-start | bytes 196616 | tf_op jit(solution)/shard_map/ppermute | solution.py:18
  8.5 6.5 %collective-permute-start.1 = (bf16[4,16,512]{2,1,0:T(8,128)(2,1)S(1)}, bf16[4,16,512]{2,1,0:T(8,128)(2,1)S(1)}, u32[]{:S(2)}, u32[]{:S(2)}) collective-permute-start(bf16[4,16,512]{2,1,0:T(8,128)(2,1)S(1)} %convolution_convert_fusion.1), channel_id=1, source_target_pairs={{0,2},{1,3},{2,0},{3,1},{4,6},{5,7},{6,4},{7,5},{8,10},{9,11},{10,... | collective-permute-start | bytes 196616 | tf_op jit(solution)/shard_map/ppermute | solution.py:18
  10.9 5.0 %collective-permute-start = (bf16[4,16,512]{2,1,0:T(8,128)(2,1)S(1)}, bf16[4,16,512]{2,1,0:T(8,128)(2,1)S(1)}, u32[]{:S(2)}, u32[]{:S(2)}) collective-permute-start(bf16[4,16,512]{2,1,0:T(8,128)(2,1)S(1)} %convolution_convert_fusion.1), channel_id=1, source_target_pairs={{0,1},{1,0},{2,3},{3,2},{4,5},{5,4},{6,7},{7,6},{8,9},{9,8},{10,11... | collective-permute-start | bytes 196616 | tf_op jit(solution)/shard_map/ppermute | solution.py:18
  15.9 12.1 %collective-permute-start.5 = (bf16[4,16,512]{2,1,0:T(8,128)(2,1)S(1)}, bf16[4,16,512]{2,1,0:T(8,128)(2,1)S(1)}, u32[]{:S(2)}, u32[]{:S(2)}) collective-permute-start(bf16[4,16,512]{2,1,0:T(8,128)(2,1)S(1)} %add_convert_fusion.3), channel_id=1, source_target_pairs={{0,12},{1,13},{2,14},{3,15},{4,8},{5,9},{6,10},{7,11},{8,4},{9,5},... | collective-permute-start | bytes 196616 | tf_op jit(solution)/shard_map/ppermute | solution.py:18
  23.9 6.3 %collective-permute-start.4 = (bf16[4,16,512]{2,1,0:T(8,128)(2,1)S(1)}, bf16[4,16,512]{2,1,0:T(8,128)(2,1)S(1)}, u32[]{:S(2)}, u32[]{:S(2)}) collective-permute-start(bf16[4,16,512]{2,1,0:T(8,128)(2,1)S(1)} %add_convert_fusion.3), channel_id=1, source_target_pairs={{0,8},{1,9},{2,10},{3,11},{4,12},{5,13},{6,14},{7,15},{8,0},{9,1},... | collective-permute-start | bytes 196616 | tf_op jit(solution)/shard_map/ppermute | solution.py:18
  25.8 5.1 %collective-permute-start.3 = (bf16[4,16,512]{2,1,0:T(8,128)(2,1)S(1)}, bf16[4,16,512]{2,1,0:T(8,128)(2,1)S(1)}, u32[]{:S(2)}, u32[]{:S(2)}) collective-permute-start(bf16[4,16,512]{2,1,0:T(8,128)(2,1)S(1)} %add_convert_fusion.3), channel_id=1, source_target_pairs={{0,4},{1,5},{2,6},{3,7},{4,0},{5,1},{6,2},{7,3},{8,12},{9,13},{10,... | collective-permute-start | bytes 196616 | tf_op jit(solution)/shard_map/ppermute | solution.py:18
  30.9 9.5 %collective-permute-start.6 = (bf16[4,16,512]{2,1,0:T(8,128)(2,1)S(1)}, bf16[4,16,512]{2,1,0:T(8,128)(2,1)S(1)}, u32[]{:S(2)}, u32[]{:S(2)}) collective-permute-start(bf16[4,16,512]{2,1,0:T(8,128)(2,1)S(1)} %add_convert_fusion.2), channel_id=1, source_target_pairs={{0,16},{1,17},{2,18},{3,19},{4,20},{5,21},{6,22},{7,23},{8,24},{9,... | collective-permute-start | bytes 196616 | tf_op jit(solution)/shard_map/ppermute | solution.py:18
  65.0 10.4 %copy-start.8 = (s32[4,32]{1,0:T(4,128)S(1)}, s32[4,32]{1,0:T(4,128)}, u32[]{:S(2)}) copy-start(s32[4,32]{1,0:T(4,128)} %param.29) | copy-start | bytes 1540
  65.0 10.6 %copy-start.12 = (s32[2]{0:T(128)S(1)}, s32[2]{0:T(128)}, u32[]{:S(2)}) copy-start(s32[2]{0:T(128)} %param.26) | copy-start | bytes 28
  65.0 27.7 %all-to-all-start.1 = ((bf16[32,4,16,128]{3,2,1,0:T(8,128)(2,1)}), bf16[32,4,16,128]{3,2,1,0:T(8,128)(2,1)S(1)}, u32[]{:S(2)}, u32[]{:S(2)}) async-start(bf16[32,4,16,128]{3,2,1,0:T(8,128)(2,1)} %broadcast_in_dim.22), calls=%async_computation.1 | async-start | bytes 1048576 | tf_op jit(solution)/shard_map/all_to_all | solution.py:47
  75.3 17.7 %copy-start.2 = (bf16[2,512,256]{2,1,0:T(8,128)(2,1)S(1)}, bf16[2,512,256]{2,1,0:T(8,128)(2,1)}, u32[]{:S(2)}) copy-start(bf16[2,512,256]{2,1,0:T(8,128)(2,1)} %param.16) | copy-start | bytes 1572868
  93.0 0.8 copy-start.5
  94.0 31.2 %copy-start.4 = (bf16[2,128,512]{2,1,0:T(8,128)(2,1)S(1)}, bf16[2,128,512]{2,1,0:T(8,128)(2,1)}, u32[]{:S(2)}) copy-start(bf16[2,128,512]{2,1,0:T(8,128)(2,1)} %param.18) | copy-start | bytes 786436
  94.0 9.1 %collective-permute-start.9 = (bf16[2,16,512]{2,1,0:T(8,128)(2,1)S(1)}, bf16[2,16,512]{2,1,0:T(8,128)(2,1)S(1)}, u32[]{:S(2)}, u32[]{:S(2)}) collective-permute-start(bf16[2,16,512]{2,1,0:T(8,128)(2,1)S(1)} %convolution_convert_fusion.4), channel_id=1, source_target_pairs={{0,3},{1,2},{2,1},{3,0},{4,7},{5,6},{6,5},{7,4},{8,11},{9,10},{10,... | collective-permute-start | bytes 98312 | tf_op jit(solution)/shard_map/ppermute | solution.py:18
  98.5 6.2 %collective-permute-start.8 = (bf16[2,16,512]{2,1,0:T(8,128)(2,1)S(1)}, bf16[2,16,512]{2,1,0:T(8,128)(2,1)S(1)}, u32[]{:S(2)}, u32[]{:S(2)}) collective-permute-start(bf16[2,16,512]{2,1,0:T(8,128)(2,1)S(1)} %convolution_convert_fusion.4), channel_id=1, source_target_pairs={{0,2},{1,3},{2,0},{3,1},{4,6},{5,7},{6,4},{7,5},{8,10},{9,11},{10,... | collective-permute-start | bytes 98312 | tf_op jit(solution)/shard_map/ppermute | solution.py:18
  100.8 5.0 %collective-permute-start.7 = (bf16[2,16,512]{2,1,0:T(8,128)(2,1)S(1)}, bf16[2,16,512]{2,1,0:T(8,128)(2,1)S(1)}, u32[]{:S(2)}, u32[]{:S(2)}) collective-permute-start(bf16[2,16,512]{2,1,0:T(8,128)(2,1)S(1)} %convolution_convert_fusion.4), channel_id=1, source_target_pairs={{0,1},{1,0},{2,3},{3,2},{4,5},{5,4},{6,7},{7,6},{8,9},{9,8},{10,11... | collective-permute-start | bytes 98312 | tf_op jit(solution)/shard_map/ppermute | solution.py:18
  105.8 9.3 %collective-permute-start.12 = (bf16[2,16,512]{2,1,0:T(8,128)(2,1)S(1)}, bf16[2,16,512]{2,1,0:T(8,128)(2,1)S(1)}, u32[]{:S(2)}, u32[]{:S(2)}) collective-permute-start(bf16[2,16,512]{2,1,0:T(8,128)(2,1)S(1)} %add_convert_fusion.7), channel_id=1, source_target_pairs={{0,12},{1,13},{2,14},{3,15},{4,8},{5,9},{6,10},{7,11},{8,4},{9,5},... | collective-permute-start | bytes 98312 | tf_op jit(solution)/shard_map/ppermute | solution.py:18
  108.7 6.5 %collective-permute-start.11 = (bf16[2,16,512]{2,1,0:T(8,128)(2,1)S(1)}, bf16[2,16,512]{2,1,0:T(8,128)(2,1)S(1)}, u32[]{:S(2)}, u32[]{:S(2)}) collective-permute-start(bf16[2,16,512]{2,1,0:T(8,128)(2,1)S(1)} %add_convert_fusion.7), channel_id=1, source_target_pairs={{0,8},{1,9},{2,10},{3,11},{4,12},{5,13},{6,14},{7,15},{8,0},{9,1},... | collective-permute-start | bytes 98312 | tf_op jit(solution)/shard_map/ppermute | solution.py:18
  111.0 5.4 %collective-permute-start.10 = (bf16[2,16,512]{2,1,0:T(8,128)(2,1)S(1)}, bf16[2,16,512]{2,1,0:T(8,128)(2,1)S(1)}, u32[]{:S(2)}, u32[]{:S(2)}) collective-permute-start(bf16[2,16,512]{2,1,0:T(8,128)(2,1)S(1)} %add_convert_fusion.7), channel_id=1, source_target_pairs={{0,4},{1,5},{2,6},{3,7},{4,0},{5,1},{6,2},{7,3},{8,12},{9,13},{10,... | collective-permute-start | bytes 98312 | tf_op jit(solution)/shard_map/ppermute | solution.py:18
  116.4 8.8 %collective-permute-start.13 = (bf16[2,16,512]{2,1,0:T(8,128)(2,1)S(1)}, bf16[2,16,512]{2,1,0:T(8,128)(2,1)S(1)}, u32[]{:S(2)}, u32[]{:S(2)}) collective-permute-start(bf16[2,16,512]{2,1,0:T(8,128)(2,1)S(1)} %add_convert_fusion.6), channel_id=1, source_target_pairs={{0,16},{1,17},{2,18},{3,19},{4,20},{5,21},{6,22},{7,23},{8,24},{9,... | collective-permute-start | bytes 98312 | tf_op jit(solution)/shard_map/ppermute | solution.py:18
  126.1 17.5 %all-to-all-start.2 = ((bf16[16,2,16,128]{3,2,1,0:T(8,128)(2,1)}), bf16[16,2,16,128]{3,2,1,0:T(8,128)(2,1)S(1)}, u32[]{:S(2)}, u32[]{:S(2)}) async-start(bf16[16,2,16,128]{3,2,1,0:T(8,128)(2,1)} %broadcast_in_dim.23), calls=%async_computation.2 | async-start | bytes 262144 | tf_op jit(solution)/shard_map/all_to_all | solution.py:47
  143.6 18.5 %copy-start.1 = (bf16[768,384]{1,0:T(8,128)(2,1)S(1)}, bf16[768,384]{1,0:T(8,128)(2,1)}, u32[]{:S(2)}) copy-start(bf16[768,384]{1,0:T(8,128)(2,1)} %param.15) | copy-start | bytes 1769476
  144.3 17.5 %all-to-all-start.3 = ((bf16[32,2,16,128]{3,2,1,0:T(8,128)(2,1)}), bf16[32,2,16,128]{3,2,1,0:T(8,128)(2,1)S(1)}, u32[]{:S(2)}, u32[]{:S(2)}) async-start(bf16[32,2,16,128]{3,2,1,0:T(8,128)(2,1)} %broadcast_in_dim.24), calls=%async_computation.3 | async-start | bytes 524288 | tf_op jit(solution)/shard_map/all_to_all | solution.py:47
  149.6 0.7 copy-start.11
  161.8 0.7 copy-start.6
  162.8 9.0 %collective-permute-start.16 = (bf16[1,16,768]{2,1,0:T(8,128)(2,1)S(1)}, bf16[1,16,768]{2,1,0:T(8,128)(2,1)S(1)}, u32[]{:S(2)}, u32[]{:S(2)}) collective-permute-start(bf16[1,16,768]{2,1,0:T(8,128)(2,1)S(1)} %fusion), channel_id=1, source_target_pairs={{0,3},{1,2},{2,1},{3,0},{4,7},{5,6},{6,5},{7,4},{8,11},{9,10},{10,... | collective-permute-start | bytes 73736 | tf_op jit(solution)/shard_map/ppermute | solution.py:18
  166.5 6.1 %collective-permute-start.15 = (bf16[1,16,768]{2,1,0:T(8,128)(2,1)S(1)}, bf16[1,16,768]{2,1,0:T(8,128)(2,1)S(1)}, u32[]{:S(2)}, u32[]{:S(2)}) collective-permute-start(bf16[1,16,768]{2,1,0:T(8,128)(2,1)S(1)} %fusion), channel_id=1, source_target_pairs={{0,2},{1,3},{2,0},{3,1},{4,6},{5,7},{6,4},{7,5},{8,10},{9,11},{10,... | collective-permute-start | bytes 73736 | tf_op jit(solution)/shard_map/ppermute | solution.py:18
  168.7 4.9 %collective-permute-start.14 = (bf16[1,16,768]{2,1,0:T(8,128)(2,1)S(1)}, bf16[1,16,768]{2,1,0:T(8,128)(2,1)S(1)}, u32[]{:S(2)}, u32[]{:S(2)}) collective-permute-start(bf16[1,16,768]{2,1,0:T(8,128)(2,1)S(1)} %fusion), channel_id=1, source_target_pairs={{0,1},{1,0},{2,3},{3,2},{4,5},{5,4},{6,7},{7,6},{8,9},{9,8},{10,11... | collective-permute-start | bytes 73736 | tf_op jit(solution)/shard_map/ppermute | solution.py:18
  173.6 9.3 %collective-permute-start.19 = (bf16[1,16,768]{2,1,0:T(8,128)(2,1)S(1)}, bf16[1,16,768]{2,1,0:T(8,128)(2,1)S(1)}, u32[]{:S(2)}, u32[]{:S(2)}) collective-permute-start(bf16[1,16,768]{2,1,0:T(8,128)(2,1)S(1)} %add_convert_fusion.9), channel_id=1, source_target_pairs={{0,12},{1,13},{2,14},{3,15},{4,8},{5,9},{6,10},{7,11},{8,4},{9,5},... | collective-permute-start | bytes 73736 | tf_op jit(solution)/shard_map/ppermute | solution.py:18
  177.0 6.0 %collective-permute-start.18 = (bf16[1,16,768]{2,1,0:T(8,128)(2,1)S(1)}, bf16[1,16,768]{2,1,0:T(8,128)(2,1)S(1)}, u32[]{:S(2)}, u32[]{:S(2)}) collective-permute-start(bf16[1,16,768]{2,1,0:T(8,128)(2,1)S(1)} %add_convert_fusion.9), channel_id=1, source_target_pairs={{0,8},{1,9},{2,10},{3,11},{4,12},{5,13},{6,14},{7,15},{8,0},{9,1},... | collective-permute-start | bytes 73736 | tf_op jit(solution)/shard_map/ppermute | solution.py:18
  179.4 4.6 %collective-permute-start.17 = (bf16[1,16,768]{2,1,0:T(8,128)(2,1)S(1)}, bf16[1,16,768]{2,1,0:T(8,128)(2,1)S(1)}, u32[]{:S(2)}, u32[]{:S(2)}) collective-permute-start(bf16[1,16,768]{2,1,0:T(8,128)(2,1)S(1)} %add_convert_fusion.9), channel_id=1, source_target_pairs={{0,4},{1,5},{2,6},{3,7},{4,0},{5,1},{6,2},{7,3},{8,12},{9,13},{10,... | collective-permute-start | bytes 73736 | tf_op jit(solution)/shard_map/ppermute | solution.py:18
  184.1 8.5 %copy-start.9 = (f32[768]{0:T(1024)S(1)}, f32[768]{0:T(1024)}, u32[]{:S(2)}) copy-start(f32[768]{0:T(1024)} %param.23) | copy-start | bytes 9220
  184.1 8.5 %collective-permute-start.20 = (bf16[1,16,768]{2,1,0:T(8,128)(2,1)S(1)}, bf16[1,16,768]{2,1,0:T(8,128)(2,1)S(1)}, u32[]{:S(2)}, u32[]{:S(2)}) collective-permute-start(bf16[1,16,768]{2,1,0:T(8,128)(2,1)S(1)} %add_convert_fusion.8), channel_id=1, source_target_pairs={{0,16},{1,17},{2,18},{3,19},{4,20},{5,21},{6,22},{7,23},{8,24},{9,... | collective-permute-start | bytes 73736 | tf_op jit(solution)/shard_map/ppermute | solution.py:18
  211.8 20.1 %all-to-all-start.5 = ((bf16[32,1,16,384]{3,2,1,0:T(8,128)(2,1)}), bf16[32,1,16,384]{3,2,1,0:T(8,128)(2,1)S(1)}, u32[]{:S(2)}, u32[]{:S(2)}) async-start(bf16[32,1,16,384]{3,2,1,0:T(8,128)(2,1)} %broadcast_in_dim.26), calls=%async_computation.5 | async-start | bytes 786432 | tf_op jit(solution)/shard_map/all_to_all | solution.py:47
  232.1 9.0 %collective-permute-start.23 = (bf16[2,16,512]{2,1,0:T(8,128)(2,1)S(1)}, bf16[2,16,512]{2,1,0:T(8,128)(2,1)S(1)}, u32[]{:S(2)}, u32[]{:S(2)}) collective-permute-start(bf16[2,16,512]{2,1,0:T(8,128)(2,1)S(1)} %convolution_convert_fusion.3), channel_id=1, source_target_pairs={{0,3},{1,2},{2,1},{3,0},{4,7},{5,6},{6,5},{7,4},{8,11},{9,10},{10,... | collective-permute-start | bytes 98312 | tf_op jit(solution)/shard_map/ppermute | solution.py:18
  235.9 6.2 %collective-permute-start.22 = (bf16[2,16,512]{2,1,0:T(8,128)(2,1)S(1)}, bf16[2,16,512]{2,1,0:T(8,128)(2,1)S(1)}, u32[]{:S(2)}, u32[]{:S(2)}) collective-permute-start(bf16[2,16,512]{2,1,0:T(8,128)(2,1)S(1)} %convolution_convert_fusion.3), channel_id=1, source_target_pairs={{0,2},{1,3},{2,0},{3,1},{4,6},{5,7},{6,4},{7,5},{8,10},{9,11},{10,... | collective-permute-start | bytes 98312 | tf_op jit(solution)/shard_map/ppermute | solution.py:18
  238.1 4.7 %collective-permute-start.21 = (bf16[2,16,512]{2,1,0:T(8,128)(2,1)S(1)}, bf16[2,16,512]{2,1,0:T(8,128)(2,1)S(1)}, u32[]{:S(2)}, u32[]{:S(2)}) collective-permute-start(bf16[2,16,512]{2,1,0:T(8,128)(2,1)S(1)} %convolution_convert_fusion.3), channel_id=1, source_target_pairs={{0,1},{1,0},{2,3},{3,2},{4,5},{5,4},{6,7},{7,6},{8,9},{9,8},{10,11... | collective-permute-start | bytes 98312 | tf_op jit(solution)/shard_map/ppermute | solution.py:18
  242.8 19.6 %copy-start.10 = (f32[2,512]{1,0:T(2,128)S(1)}, f32[2,512]{1,0:T(2,128)}, u32[]{:S(2)}) copy-start(f32[2,512]{1,0:T(2,128)} %param.24) | copy-start | bytes 12292
  242.8 9.3 %collective-permute-start.26 = (bf16[2,16,512]{2,1,0:T(8,128)(2,1)S(1)}, bf16[2,16,512]{2,1,0:T(8,128)(2,1)S(1)}, u32[]{:S(2)}, u32[]{:S(2)}) collective-permute-start(bf16[2,16,512]{2,1,0:T(8,128)(2,1)S(1)} %add_convert_fusion.5), channel_id=1, source_target_pairs={{0,12},{1,13},{2,14},{3,15},{4,8},{5,9},{6,10},{7,11},{8,4},{9,5},... | collective-permute-start | bytes 98312 | tf_op jit(solution)/shard_map/ppermute | solution.py:18
  246.6 6.0 %collective-permute-start.25 = (bf16[2,16,512]{2,1,0:T(8,128)(2,1)S(1)}, bf16[2,16,512]{2,1,0:T(8,128)(2,1)S(1)}, u32[]{:S(2)}, u32[]{:S(2)}) collective-permute-start(bf16[2,16,512]{2,1,0:T(8,128)(2,1)S(1)} %add_convert_fusion.5), channel_id=1, source_target_pairs={{0,8},{1,9},{2,10},{3,11},{4,12},{5,13},{6,14},{7,15},{8,0},{9,1},... | collective-permute-start | bytes 98312 | tf_op jit(solution)/shard_map/ppermute | solution.py:18
  249.1 4.7 %collective-permute-start.24 = (bf16[2,16,512]{2,1,0:T(8,128)(2,1)S(1)}, bf16[2,16,512]{2,1,0:T(8,128)(2,1)S(1)}, u32[]{:S(2)}, u32[]{:S(2)}) collective-permute-start(bf16[2,16,512]{2,1,0:T(8,128)(2,1)S(1)} %add_convert_fusion.5), channel_id=1, source_target_pairs={{0,4},{1,5},{2,6},{3,7},{4,0},{5,1},{6,2},{7,3},{8,12},{9,13},{10,... | collective-permute-start | bytes 98312 | tf_op jit(solution)/shard_map/ppermute | solution.py:18
  253.8 8.6 %collective-permute-start.27 = (bf16[2,16,512]{2,1,0:T(8,128)(2,1)S(1)}, bf16[2,16,512]{2,1,0:T(8,128)(2,1)S(1)}, u32[]{:S(2)}, u32[]{:S(2)}) collective-permute-start(bf16[2,16,512]{2,1,0:T(8,128)(2,1)S(1)} %add_convert_fusion.4), channel_id=1, source_target_pairs={{0,16},{1,17},{2,18},{3,19},{4,20},{5,21},{6,22},{7,23},{8,24},{9,... | collective-permute-start | bytes 98312 | tf_op jit(solution)/shard_map/ppermute | solution.py:18
  283.6 23.0 %all-to-all-start.7 = ((bf16[32,2,16,256]{3,2,1,0:T(8,128)(2,1)}), bf16[32,2,16,256]{3,2,1,0:T(8,128)(2,1)S(1)}, u32[]{:S(2)}, u32[]{:S(2)}) async-start(bf16[32,2,16,256]{3,2,1,0:T(8,128)(2,1)} %broadcast_in_dim.28), calls=%async_computation.7 | async-start | bytes 1048576 | tf_op jit(solution)/shard_map/all_to_all | solution.py:47
  306.8 9.0 %collective-permute-start.30 = (bf16[4,16,512]{2,1,0:T(8,128)(2,1)S(1)}, bf16[4,16,512]{2,1,0:T(8,128)(2,1)S(1)}, u32[]{:S(2)}, u32[]{:S(2)}) collective-permute-start(bf16[4,16,512]{2,1,0:T(8,128)(2,1)S(1)} %convolution_convert_fusion), channel_id=1, source_target_pairs={{0,3},{1,2},{2,1},{3,0},{4,7},{5,6},{6,5},{7,4},{8,11},{9,10},{10,... | collective-permute-start | bytes 196616 | tf_op jit(solution)/shard_map/ppermute | solution.py:18
  311.2 6.5 %collective-permute-start.29 = (bf16[4,16,512]{2,1,0:T(8,128)(2,1)S(1)}, bf16[4,16,512]{2,1,0:T(8,128)(2,1)S(1)}, u32[]{:S(2)}, u32[]{:S(2)}) collective-permute-start(bf16[4,16,512]{2,1,0:T(8,128)(2,1)S(1)} %convolution_convert_fusion), channel_id=1, source_target_pairs={{0,2},{1,3},{2,0},{3,1},{4,6},{5,7},{6,4},{7,5},{8,10},{9,11},{10,... | collective-permute-start | bytes 196616 | tf_op jit(solution)/shard_map/ppermute | solution.py:18
  313.7 5.3 %collective-permute-start.28 = (bf16[4,16,512]{2,1,0:T(8,128)(2,1)S(1)}, bf16[4,16,512]{2,1,0:T(8,128)(2,1)S(1)}, u32[]{:S(2)}, u32[]{:S(2)}) collective-permute-start(bf16[4,16,512]{2,1,0:T(8,128)(2,1)S(1)} %convolution_convert_fusion), channel_id=1, source_target_pairs={{0,1},{1,0},{2,3},{3,2},{4,5},{5,4},{6,7},{7,6},{8,9},{9,8},{10,11... | collective-permute-start | bytes 196616 | tf_op jit(solution)/shard_map/ppermute | solution.py:18
  319.0 21.1 %copy-start.7 = (f32[4,512]{1,0:T(4,128)S(1)}, f32[4,512]{1,0:T(4,128)}, u32[]{:S(2)}) copy-start(f32[4,512]{1,0:T(4,128)} %param.25) | copy-start | bytes 24580
  319.0 9.3 %collective-permute-start.33 = (bf16[4,16,512]{2,1,0:T(8,128)(2,1)S(1)}, bf16[4,16,512]{2,1,0:T(8,128)(2,1)S(1)}, u32[]{:S(2)}, u32[]{:S(2)}) collective-permute-start(bf16[4,16,512]{2,1,0:T(8,128)(2,1)S(1)} %add_convert_fusion.1), channel_id=1, source_target_pairs={{0,12},{1,13},{2,14},{3,15},{4,8},{5,9},{6,10},{7,11},{8,4},{9,5},... | collective-permute-start | bytes 196616 | tf_op jit(solution)/shard_map/ppermute | solution.py:18
  321.7 7.3 %collective-permute-start.32 = (bf16[4,16,512]{2,1,0:T(8,128)(2,1)S(1)}, bf16[4,16,512]{2,1,0:T(8,128)(2,1)S(1)}, u32[]{:S(2)}, u32[]{:S(2)}) collective-permute-start(bf16[4,16,512]{2,1,0:T(8,128)(2,1)S(1)} %add_convert_fusion.1), channel_id=1, source_target_pairs={{0,8},{1,9},{2,10},{3,11},{4,12},{5,13},{6,14},{7,15},{8,0},{9,1},... | collective-permute-start | bytes 196616 | tf_op jit(solution)/shard_map/ppermute | solution.py:18
  324.6 6.1 %collective-permute-start.31 = (bf16[4,16,512]{2,1,0:T(8,128)(2,1)S(1)}, bf16[4,16,512]{2,1,0:T(8,128)(2,1)S(1)}, u32[]{:S(2)}, u32[]{:S(2)}) collective-permute-start(bf16[4,16,512]{2,1,0:T(8,128)(2,1)S(1)} %add_convert_fusion.1), channel_id=1, source_target_pairs={{0,4},{1,5},{2,6},{3,7},{4,0},{5,1},{6,2},{7,3},{8,12},{9,13},{10,... | collective-permute-start | bytes 196616 | tf_op jit(solution)/shard_map/ppermute | solution.py:18
  330.7 9.4 %collective-permute-start.34 = (bf16[4,16,512]{2,1,0:T(8,128)(2,1)S(1)}, bf16[4,16,512]{2,1,0:T(8,128)(2,1)S(1)}, u32[]{:S(2)}, u32[]{:S(2)}) collective-permute-start(bf16[4,16,512]{2,1,0:T(8,128)(2,1)S(1)} %add_convert_fusion), channel_id=1, source_target_pairs={{0,16},{1,17},{2,18},{3,19},{4,20},{5,21},{6,22},{7,23},{8,24},{9,... | collective-permute-start | bytes 196616 | tf_op jit(solution)/shard_map/ppermute | solution.py:18
  341.2 24.6 %all-to-all-start.8 = ((bf16[16,4,16,256]{3,2,1,0:T(8,128)(2,1)}), bf16[16,4,16,256]{3,2,1,0:T(8,128)(2,1)S(1)}, u32[]{:S(2)}, u32[]{:S(2)}) async-start(bf16[16,4,16,256]{3,2,1,0:T(8,128)(2,1)} %broadcast_in_dim.29), calls=%async_computation.8 | async-start | bytes 1048576 | tf_op jit(solution)/shard_map/all_to_all | solution.py:47

commit v2 on v1

--- a/solution.py
+++ b/solution.py
@@ -27,18 +27,38 @@
     return parts[0]
 
 
-def sum_over_col(partial):
+def near_groups():
     size = lax.axis_size("col")
-    step = 1
-    while step < size:
-        if step * 4 <= size:
-            masks = (step, 2 * step, 3 * step)
-            partial = sum_stage(partial, "col", masks)
-            step *= 4
-        else:
-            partial = sum_stage(partial, "col", (step,))
-            step *= 2
-    return partial
+    return [[z * 4 + x for x in range(4)] for z in range(size // 4)]
+
+
+def far_groups():
+    size = lax.axis_size("col")
+    return [[z * 4 + x for z in range(size // 4)] for x in range(4)]
+
+
+def sum_groups(partial, groups):
+    size = len(groups[0])
+    copies = jnp.broadcast_to(partial.astype(BF16)[None], (size,) + partial.shape)
+    parts = lax.all_to_all(copies, "col", 0, 0, axis_index_groups=groups, tiled=True)
+    return jnp.sum(parts.astype(F32), axis=0)
+
+
+def sum_near_far(partial):
+    return sum_groups(sum_groups(partial, near_groups()), far_groups())
+
+
+def sum_permutes_far(partial):
+    return sum_groups(sum_stage(partial, "col", (1, 2, 3)), far_groups())
+
+
+def sum_scattered(partial):
+    size = lax.axis_size("col")
+    fronts, width, count = partial.shape
+    pieces = partial.astype(BF16).reshape(size, 1, fronts * width * count // size)
+    pieces = lax.all_to_all(pieces, "col", 0, 0, tiled=True)
+    mine = jnp.sum(pieces.astype(F32), axis=0)
+    return spread(mine, "col").astype(F32).reshape(fronts, width, count)
 
 
 def spread(value, axis):
@@ -98,8 +118,10 @@
         col_masks.append(level_mask(sizes[level], cols_here, col_at * cols_here))
     scaled = [None] * depth
     residual = sources[depth - 1]
+    forward = [sum_scattered, sum_near_far, sum_near_far]
+    backward = [sum_permutes_far, sum_scattered]
     for level in range(depth - 1, -1, -1):
-        solved = sum_over_col(times_rows(inverses[level], residual * col_masks[level]))
+        solved = forward[level](times_rows(inverses[level], residual * col_masks[level]))
         solved = solved * row_masks[level]
         scaled[level] = solved * pivots[level][:, None, :]
         if level > 0:
@@ -116,7 +138,7 @@
         outputs[level] = solved
         if level + 1 < depth:
             picked = child_rows(solved, lists[level + 1])
-            carried = sum_over_col(times_columns(couplings[level + 1], picked))
+            carried = backward[level](times_columns(couplings[level + 1], picked))
     return outputs
 
 

time: 369 us -> 331 us (0.90)
  starting transfers between devices: 158 us -> 58.9 us
  blocking collectives: 60.9 us -> 112 us
  local copies, waits for them, and re-layouts: 9.68 us -> 15.8 us
  other arithmetic: 3.43 us -> 7.66 us
    ppermute x35 -> x3, starting transfers between devices: 116 us -> 8.98 us  [exchange(): lax.ppermute(value, axis, [(i, i ^ m) for i in range(size)])]
    all_to_all x0 -> x4, blocking collectives: none -> 44 us  [the longest x3 30.4 us: sum_groups(): lax.all_to_all(copies, 'col', 0, 0, axis_index_groups=groups, tiled=True)]
    ppermute x35 -> x3, waiting for transfers between devices: 45.3 us -> 2.53 us  [exchange(): lax.ppermute(value, axis, [(i, i ^ m) for i in range(size)])]
    all_to_all x0 -> x3, waiting for transfers between devices: none -> 32.8 us  [the longest x2 24.2 us: sum_groups(): lax.all_to_all(copies, 'col', 0, 0, axis_index_groups=groups, tiled=True)]
    all_to_all x0 -> x3, starting transfers between devices: none -> 17.3 us  [the longest x2 13.5 us: sum_groups(): lax.all_to_all(copies, 'col', 0, 0, axis_index_groups=groups, tiled=True)]
    all_to_all x6 -> x7, waiting for transfers between devices: 70.8 us -> 80.9 us  [spread(): return lax.all_to_all(copies, axis, 0, 0, tiled=True)]
    all_to_all x6 -> x7, starting transfers between devices: 42.1 us -> 32.6 us  [spread(): return lax.all_to_all(copies, axis, 0, 0, tiled=True)]
    all_to_all x3 -> x4, blocking collectives: 60.9 us -> 68 us  [spread(): return lax.all_to_all(copies, axis, 0, 0, tiled=True)]
  transfers between devices with their start and end apart: 41 -> 13, of which waited for: 30 -> 12; matrix products, arithmetic and copies ran while one was open for 1% -> 1% of each run, Pallas kernels for 0% -> 0%
where the time goes in v2:
time: 331 us; the launch traced here: 329 us
  waiting for transfers between devices  116 us (35%)
  blocking collectives  112 us (34%)
  starting transfers between devices  58.9 us (18%)
  local copies, waits for them, and re-layouts  15.8 us (5%)
  between operations  15.4 us (5%)
  other arithmetic  7.66 us (2%)
    all_to_all x7, waiting for transfers between devices, spread(): return lax.all_to_all(copies, axis, 0, 0, tiled=True)  80.9 us
    all_to_all x4, blocking collectives, spread(): return lax.all_to_all(copies, axis, 0, 0, tiled=True)  68 us
    all_to_all x7, starting transfers between devices, spread(): return lax.all_to_all(copies, axis, 0, 0, tiled=True)  32.6 us
    all_to_all x3, blocking collectives, sum_groups(): lax.all_to_all(copies, 'col', 0, 0, axis_index_groups=groups, tiled=True)  30.4 us
    all_to_all x2, waiting for transfers between devices, sum_groups(): lax.all_to_all(copies, 'col', 0, 0, axis_index_groups=groups, tiled=True)  24.2 us
    all_to_all x1, blocking collectives, sum_scattered(): pieces = lax.all_to_all(pieces, 'col', 0, 0, tiled=True)  13.6 us
    all_to_all x2, starting transfers between devices, sum_groups(): lax.all_to_all(copies, 'col', 0, 0, axis_index_groups=groups, tiled=True)  13.5 us
    ppermute x3, starting transfers between devices, exchange(): lax.ppermute(value, axis, [(i, i ^ m) for i in range(size)])  8.98 us
  transfers between devices with their start and end apart: 13, of which 12 were waited for; matrix products, arithmetic and copies ran while one was open for 1% of the time, Pallas kernels for 0%

profile of v2, /device:TPU:1, one launch (start us, length us, event | category | flops | bytes accessed | tf_op | source)
XLA Modules:
  0.0 329.0 jit_solution(3194220281854049557)
XLA Ops:
  0.7 0.7 copy-done.13
  1.5 0.4 copy-done
  1.9 1.2 convolution_convert_fusion.1
  3.1 10.2 %all_to_all.90 = bf16[4,4,16,512]{3,2,1,0:T(8,128)(2,1)S(1)} all-to-all(bf16[4,4,16,512]{3,2,1,0:T(8,128)(2,1)S(1)} %broadcast_in_dim.35), channel_id=1, replica_groups={{0,1,2,3},{4,5,6,7},{8,9,10,11},{12,13,14,15},{16,17,18,19},{20,21,22,2..., dimensions={0} | all-to-all | bytes 524288 | tf_op jit(solution)/shard_map/all_to_all | solution.py:43
  13.3 0.8 broadcast_in_dim.36
  14.2 10.1 %all-to-all-start.1 = ((bf16[8,4,16,512]{3,2,1,0:T(8,128)(2,1)}), bf16[8,4,16,512]{3,2,1,0:T(8,128)(2,1)S(1)}, u32[]{:S(2)}, u32[]{:S(2)}) async-start(bf16[8,4,16,512]{3,2,1,0:T(8,128)(2,1)} %broadcast_in_dim.36), calls=%async_computation.1 | async-start | bytes 1048576 | tf_op jit(solution)/shard_map/all_to_all | solution.py:43
  24.4 15.0 %all-to-all-done.1 = bf16[8,4,16,512]{3,2,1,0:T(8,128)(2,1)S(1)} async-done(((bf16[8,4,16,512]{3,2,1,0:T(8,128)(2,1)}), bf16[8,4,16,512]{3,2,1,0:T(8,128)(2,1)S(1)}, u32[]{:S(2)}, u32[]{:S(2)}) %all-to-all-start.1) | async-done | bytes 524320 | tf_op jit(solution)/shard_map/all_to_all | solution.py:43
  39.8 21.9 %all_to_all.91 = bf16[16,4,16,128]{3,2,1,0:T(8,128)(2,1)S(1)} all-to-all(bf16[16,4,16,128]{3,2,1,0:T(8,128)(2,1)S(1)} %broadcast_in_dim.37), channel_id=1, replica_groups=mesh['row'=16,'col'=32] {'row'}, dimensions={0} | all-to-all | bytes 524288 | tf_op jit(solution)/shard_map/all_to_all | solution.py:67
  61.8 0.9 broadcast_in_dim.38
  62.7 4.0 %all-to-all-start.3 = ((bf16[32,4,16,128]{3,2,1,0:T(8,128)(2,1)}), bf16[32,4,16,128]{3,2,1,0:T(8,128)(2,1)S(1)}, u32[]{:S(2)}, u32[]{:S(2)}) async-start(bf16[32,4,16,128]{3,2,1,0:T(8,128)(2,1)} %broadcast_in_dim.38), calls=%async_computation.3 | async-start | bytes 1048576 | tf_op jit(solution)/shard_map/all_to_all | solution.py:67
  67.1 17.3 %all-to-all-done.3 = bf16[32,4,16,128]{3,2,1,0:T(8,128)(2,1)S(1)} async-done(((bf16[32,4,16,128]{3,2,1,0:T(8,128)(2,1)}), bf16[32,4,16,128]{3,2,1,0:T(8,128)(2,1)S(1)}, u32[]{:S(2)}, u32[]{:S(2)}) %all-to-all-start.3) | async-done | bytes 524320 | tf_op jit(solution)/shard_map/all_to_all | solution.py:67
  84.4 0.3 fusion
  84.8 0.7 copy-done.5
  85.8 8.6 %all_to_all.92 = bf16[4,2,16,512]{3,2,1,0:T(8,128)(2,1)S(1)} all-to-all(bf16[4,2,16,512]{3,2,1,0:T(8,128)(2,1)S(1)} %broadcast_in_dim.39), channel_id=1, replica_groups={{0,1,2,3},{4,5,6,7},{8,9,10,11},{12,13,14,15},{16,17,18,19},{20,21,22,2..., dimensions={0} | all-to-all | bytes 262144 | tf_op jit(solution)/shard_map/all_to_all | solution.py:43
  94.4 0.7 broadcast_in_dim.40
  95.1 3.4 %all-to-all-start.5 = ((bf16[8,2,16,512]{3,2,1,0:T(8,128)(2,1)}), bf16[8,2,16,512]{3,2,1,0:T(8,128)(2,1)S(1)}, u32[]{:S(2)}, u32[]{:S(2)}) async-start(bf16[8,2,16,512]{3,2,1,0:T(8,128)(2,1)} %broadcast_in_dim.40), calls=%async_computation.5 | async-start | bytes 524288 | tf_op jit(solution)/shard_map/all_to_all | solution.py:43
  98.6 9.2 %all-to-all-done.5 = bf16[8,2,16,512]{3,2,1,0:T(8,128)(2,1)S(1)} async-done(((bf16[8,2,16,512]{3,2,1,0:T(8,128)(2,1)}), bf16[8,2,16,512]{3,2,1,0:T(8,128)(2,1)S(1)}, u32[]{:S(2)}, u32[]{:S(2)}) %all-to-all-start.5) | async-done | bytes 262176 | tf_op jit(solution)/shard_map/all_to_all | solution.py:43
  108.0 0.7 broadcast_in_dim.41
  108.7 6.8 %all-to-all-start.6 = ((bf16[16,2,16,128]{3,2,1,0:T(8,128)(2,1)}), bf16[16,2,16,128]{3,2,1,0:T(8,128)(2,1)S(1)}, u32[]{:S(2)}, u32[]{:S(2)}) async-start(bf16[16,2,16,128]{3,2,1,0:T(8,128)(2,1)} %broadcast_in_dim.41), calls=%async_computation.6 | async-start | bytes 262144 | tf_op jit(solution)/shard_map/all_to_all | solution.py:67
  115.5 9.2 %all-to-all-done.6 = bf16[16,2,16,128]{3,2,1,0:T(8,128)(2,1)S(1)} async-done(((bf16[16,2,16,128]{3,2,1,0:T(8,128)(2,1)}), bf16[16,2,16,128]{3,2,1,0:T(8,128)(2,1)S(1)}, u32[]{:S(2)}, u32[]{:S(2)}) %all-to-all-start.6) | async-done | bytes 131104 | tf_op jit(solution)/shard_map/all_to_all | solution.py:67
  124.7 0.7 broadcast_in_dim.42
  125.4 3.9 %all-to-all-start.7 = ((bf16[32,2,16,128]{3,2,1,0:T(8,128)(2,1)}), bf16[32,2,16,128]{3,2,1,0:T(8,128)(2,1)S(1)}, u32[]{:S(2)}, u32[]{:S(2)}) async-start(bf16[32,2,16,128]{3,2,1,0:T(8,128)(2,1)} %broadcast_in_dim.42), calls=%async_computation.7 | async-start | bytes 524288 | tf_op jit(solution)/shard_map/all_to_all | solution.py:67
  129.3 0.7 copy-done.11
  130.3 11.8 %all-to-all-done.7 = bf16[32,2,16,128]{3,2,1,0:T(8,128)(2,1)S(1)} async-done(((bf16[32,2,16,128]{3,2,1,0:T(8,128)(2,1)}), bf16[32,2,16,128]{3,2,1,0:T(8,128)(2,1)S(1)}, u32[]{:S(2)}, u32[]{:S(2)}) %all-to-all-start.7) | async-done | bytes 262176 | tf_op jit(solution)/shard_map/all_to_all | solution.py:67
  142.4 0.4 copy-done.6
  143.2 0.5 broadcast.196
  143.7 0.8 reduce.23
  144.5 0.7 reshape.352
  145.2 3.9 %all-to-all-start.8 = ((bf16[32,2,192]{2,1,0:T(2,128)(2,1)}), bf16[32,2,192]{2,1,0:T(2,128)(2,1)S(1)}, u32[]{:S(2)}, u32[]{:S(2)}) async-start(bf16[32,2,192]{2,1,0:T(2,128)(2,1)} %reshape.352), calls=%async_computation.8 | async-start | bytes 65536 | tf_op jit(solution)/shard_map/all_to_all | solution.py:59
  149.1 8.6 %all-to-all-done.8 = bf16[32,2,192]{2,1,0:T(2,128)(2,1)S(1)} async-done(((bf16[32,2,192]{2,1,0:T(2,128)(2,1)}), bf16[32,2,192]{2,1,0:T(2,128)(2,1)S(1)}, u32[]{:S(2)}, u32[]{:S(2)}) %all-to-all-start.8) | async-done | bytes 24608 | tf_op jit(solution)/shard_map/all_to_all | solution.py:59
  157.9 0.8 reduce.24
  158.7 0.7 reshape.354
  159.4 3.9 %all-to-all-start.9 = ((bf16[32,2,192]{2,1,0:T(2,128)(2,1)}), bf16[32,2,192]{2,1,0:T(2,128)(2,1)S(1)}, u32[]{:S(2)}, u32[]{:S(2)}) async-start(bf16[32,2,192]{2,1,0:T(2,128)(2,1)} %reshape.354), calls=%async_computation.9 | async-start | bytes 65536 | tf_op jit(solution)/shard_map/all_to_all | solution.py:67
  163.3 8.6 %all-to-all-done.9 = bf16[32,2,192]{2,1,0:T(2,128)(2,1)S(1)} async-done(((bf16[32,2,192]{2,1,0:T(2,128)(2,1)}), bf16[32,2,192]{2,1,0:T(2,128)(2,1)S(1)}, u32[]{:S(2)}, u32[]{:S(2)}) %all-to-all-start.9) | async-done | bytes 24608 | tf_op jit(solution)/shard_map/all_to_all | solution.py:67
  172.2 0.7 copy-done.9
  173.1 16.2 %all_to_all.93 = bf16[16,1,16,384]{3,2,1,0:T(8,128)(2,1)S(1)} all-to-all(bf16[16,1,16,384]{3,2,1,0:T(8,128)(2,1)S(1)} %broadcast_in_dim.44), channel_id=1, replica_groups=mesh['row'=16,'col'=32] {'row'}, dimensions={0} | all-to-all | bytes 393216 | tf_op jit(solution)/shard_map/all_to_all | solution.py:67
  189.3 0.8 broadcast_in_dim.45
  190.1 3.9 %all-to-all-start.11 = ((bf16[32,1,16,384]{3,2,1,0:T(8,128)(2,1)}), bf16[32,1,16,384]{3,2,1,0:T(8,128)(2,1)S(1)}, u32[]{:S(2)}, u32[]{:S(2)}) async-start(bf16[32,1,16,384]{3,2,1,0:T(8,128)(2,1)} %broadcast_in_dim.45), calls=%async_computation.11 | async-start | bytes 786432 | tf_op jit(solution)/shard_map/all_to_all | solution.py:67
  194.0 0.5 fusion.41
  198.5 10.5 %all-to-all-done.11 = bf16[32,1,16,384]{3,2,1,0:T(8,128)(2,1)S(1)} async-done(((bf16[32,1,16,384]{3,2,1,0:T(8,128)(2,1)}), bf16[32,1,16,384]{3,2,1,0:T(8,128)(2,1)S(1)}, u32[]{:S(2)}, u32[]{:S(2)}) %all-to-all-start.11) | async-done | bytes 393248 | tf_op jit(solution)/shard_map/all_to_all | solution.py:67
  209.2 4.1 %collective-permute-start.2 = (bf16[2,16,512]{2,1,0:T(8,128)(2,1)S(1)}, bf16[2,16,512]{2,1,0:T(8,128)(2,1)S(1)}, u32[]{:S(2)}, u32[]{:S(2)}) collective-permute-start(bf16[2,16,512]{2,1,0:T(8,128)(2,1)S(1)} %convolution_convert_fusion.3), channel_id=1, source_target_pairs={{0,3},{1,2},{2,1},{3,0},{4,7},{5,6},{6,5},{7,4},{8,11},{9,10},{10,... | collective-permute-start | bytes 98312 | tf_op jit(solution)/shard_map/ppermute | solution.py:18
  213.3 2.5 collective-permute-start.1
  215.8 2.4 collective-permute-start
  218.2 1.3 collective-permute-done.1
  219.4 1.3 collective-permute-done
  220.8 11.6 %all_to_all.94 = bf16[8,2,16,512]{3,2,1,0:T(8,128)(2,1)S(1)} all-to-all(bf16[8,2,16,512]{3,2,1,0:T(8,128)(2,1)S(1)} %broadcast_in_dim.46), channel_id=1, replica_groups={{0,4,8,12,16,20,24,28},{1,5,9,13,17,21,25,29},{2,6,10,14,18,22,26,30},{..., dimensions={0} | all-to-all | bytes 524288 | tf_op jit(solution)/shard_map/all_to_all | solution.py:43
  232.4 0.6 copy-done.10
  233.3 17.9 %all_to_all.95 = bf16[16,2,16,256]{3,2,1,0:T(8,128)(2,1)S(1)} all-to-all(bf16[16,2,16,256]{3,2,1,0:T(8,128)(2,1)S(1)} %broadcast_in_dim.47), channel_id=1, replica_groups=mesh['row'=16,'col'=32] {'row'}, dimensions={0} | all-to-all | bytes 524288 | tf_op jit(solution)/shard_map/all_to_all | solution.py:67
  251.2 0.6 multiply_convert_fusion.11
  251.8 0.8 broadcast_in_dim.48
  252.7 3.9 %all-to-all-start.14 = ((bf16[32,2,16,256]{3,2,1,0:T(8,128)(2,1)}), bf16[32,2,16,256]{3,2,1,0:T(8,128)(2,1)S(1)}, u32[]{:S(2)}, u32[]{:S(2)}) async-start(bf16[32,2,16,256]{3,2,1,0:T(8,128)(2,1)} %broadcast_in_dim.48), calls=%async_computation.14 | async-start | bytes 1048576 | tf_op jit(solution)/shard_map/all_to_all | solution.py:67
  256.7 0.6 fusion.40
  267.5 6.7 %all-to-all-done.14 = bf16[32,2,16,256]{3,2,1,0:T(8,128)(2,1)S(1)} async-done(((bf16[32,2,16,256]{3,2,1,0:T(8,128)(2,1)}), bf16[32,2,16,256]{3,2,1,0:T(8,128)(2,1)S(1)}, u32[]{:S(2)}, u32[]{:S(2)}) %all-to-all-start.14) | async-done | bytes 524320 | tf_op jit(solution)/shard_map/all_to_all | solution.py:67
  274.5 1.0 reduce.25
  275.6 13.6 %all_to_all.96 = bf16[32,2,512]{2,1,0:T(2,128)(2,1)S(1)} all-to-all(bf16[32,2,512]{2,1,0:T(2,128)(2,1)S(1)} %reshape.356), channel_id=1, replica_groups=mesh['row'=16,'col'=32] {'col'}, dimensions={0} | all-to-all | bytes 131072 | tf_op jit(solution)/shard_map/all_to_all | solution.py:59
  289.4 1.0 reduce.26
  290.5 11.9 %all_to_all.97 = bf16[32,2,512]{2,1,0:T(2,128)(2,1)S(1)} all-to-all(bf16[32,2,512]{2,1,0:T(2,128)(2,1)S(1)} %reshape.358), channel_id=1, replica_groups=mesh['row'=16,'col'=32] {'col'}, dimensions={0} | all-to-all | bytes 131072 | tf_op jit(solution)/shard_map/all_to_all | solution.py:67
  302.4 0.3 convert_reduce_fusion.6
  302.8 0.7 copy-done.7
  303.7 0.9 broadcast_in_dim.50
  304.6 6.3 %all-to-all-start.17 = ((bf16[16,4,16,256]{3,2,1,0:T(8,128)(2,1)}), bf16[16,4,16,256]{3,2,1,0:T(8,128)(2,1)S(1)}, u32[]{:S(2)}, u32[]{:S(2)}) async-start(bf16[16,4,16,256]{3,2,1,0:T(8,128)(2,1)} %broadcast_in_dim.50), calls=%async_computation.17 | async-start | bytes 1048576 | tf_op jit(solution)/shard_map/all_to_all | solution.py:67
  310.9 0.6 fusion.16
  311.5 16.7 %all-to-all-done.17 = bf16[16,4,16,256]{3,2,1,0:T(8,128)(2,1)S(1)} async-done(((bf16[16,4,16,256]{3,2,1,0:T(8,128)(2,1)}), bf16[16,4,16,256]{3,2,1,0:T(8,128)(2,1)S(1)}, u32[]{:S(2)}, u32[]{:S(2)}) %all-to-all-start.17) | async-done | bytes 524320 | tf_op jit(solution)/shard_map/all_to_all | solution.py:67
  328.3 0.6 multiply_bitcast_fusion
  (88 shorter events, 4.8 us)
Async XLA Ops:
  0.6 1.2 copy-start
  0.7 0.7 copy-start.13
  14.2 25.2 %all-to-all-start.1 = ((bf16[8,4,16,512]{3,2,1,0:T(8,128)(2,1)}), bf16[8,4,16,512]{3,2,1,0:T(8,128)(2,1)S(1)}, u32[]{:S(2)}, u32[]{:S(2)}) async-start(bf16[8,4,16,512]{3,2,1,0:T(8,128)(2,1)} %broadcast_in_dim.36), calls=%async_computation.1 | async-start | bytes 1048576 | tf_op jit(solution)/shard_map/all_to_all | solution.py:43
  24.3 15.2 %copy-start.3 = (bf16[4,128,512]{2,1,0:T(8,128)(2,1)S(1)}, bf16[4,128,512]{2,1,0:T(8,128)(2,1)}, u32[]{:S(2)}) copy-start(bf16[4,128,512]{2,1,0:T(8,128)(2,1)} %param.19) | copy-start | bytes 1572868
  62.7 4.1 %copy-start.8 = (s32[4,32]{1,0:T(4,128)S(1)}, s32[4,32]{1,0:T(4,128)}, u32[]{:S(2)}) copy-start(s32[4,32]{1,0:T(4,128)} %param.29) | copy-start | bytes 1540
  62.7 4.3 %copy-start.12 = (s32[2]{0:T(128)S(1)}, s32[2]{0:T(128)}, u32[]{:S(2)}) copy-start(s32[2]{0:T(128)} %param.26) | copy-start | bytes 28
  62.7 21.7 %all-to-all-start.3 = ((bf16[32,4,16,128]{3,2,1,0:T(8,128)(2,1)}), bf16[32,4,16,128]{3,2,1,0:T(8,128)(2,1)S(1)}, u32[]{:S(2)}, u32[]{:S(2)}) async-start(bf16[32,4,16,128]{3,2,1,0:T(8,128)(2,1)} %broadcast_in_dim.38), calls=%async_computation.3 | async-start | bytes 1048576 | tf_op jit(solution)/shard_map/all_to_all | solution.py:67
  66.7 18.0 %copy-start.2 = (bf16[2,512,256]{2,1,0:T(8,128)(2,1)S(1)}, bf16[2,512,256]{2,1,0:T(8,128)(2,1)}, u32[]{:S(2)}) copy-start(bf16[2,512,256]{2,1,0:T(8,128)(2,1)} %param.16) | copy-start | bytes 1572868
  84.7 0.8 copy-start.5
  95.1 12.7 %all-to-all-start.5 = ((bf16[8,2,16,512]{3,2,1,0:T(8,128)(2,1)}), bf16[8,2,16,512]{3,2,1,0:T(8,128)(2,1)S(1)}, u32[]{:S(2)}, u32[]{:S(2)}) async-start(bf16[8,2,16,512]{3,2,1,0:T(8,128)(2,1)} %broadcast_in_dim.40), calls=%async_computation.5 | async-start | bytes 524288 | tf_op jit(solution)/shard_map/all_to_all | solution.py:43
  98.5 9.3 %copy-start.4 = (bf16[2,128,512]{2,1,0:T(8,128)(2,1)S(1)}, bf16[2,128,512]{2,1,0:T(8,128)(2,1)}, u32[]{:S(2)}) copy-start(bf16[2,128,512]{2,1,0:T(8,128)(2,1)} %param.18) | copy-start | bytes 786436
  108.7 16.0 %all-to-all-start.6 = ((bf16[16,2,16,128]{3,2,1,0:T(8,128)(2,1)}), bf16[16,2,16,128]{3,2,1,0:T(8,128)(2,1)S(1)}, u32[]{:S(2)}, u32[]{:S(2)}) async-start(bf16[16,2,16,128]{3,2,1,0:T(8,128)(2,1)} %broadcast_in_dim.41), calls=%async_computation.6 | async-start | bytes 262144 | tf_op jit(solution)/shard_map/all_to_all | solution.py:67
  124.7 17.7 %copy-start.1 = (bf16[768,384]{1,0:T(8,128)(2,1)S(1)}, bf16[768,384]{1,0:T(8,128)(2,1)}, u32[]{:S(2)}) copy-start(bf16[768,384]{1,0:T(8,128)(2,1)} %param.15) | copy-start | bytes 1769476
  125.4 16.7 %all-to-all-start.7 = ((bf16[32,2,16,128]{3,2,1,0:T(8,128)(2,1)}), bf16[32,2,16,128]{3,2,1,0:T(8,128)(2,1)S(1)}, u32[]{:S(2)}, u32[]{:S(2)}) async-start(bf16[32,2,16,128]{3,2,1,0:T(8,128)(2,1)} %broadcast_in_dim.42), calls=%async_computation.7 | async-start | bytes 524288 | tf_op jit(solution)/shard_map/all_to_all | solution.py:67
  129.3 0.7 copy-start.11
  142.1 0.7 copy-start.6
  145.2 12.5 %all-to-all-start.8 = ((bf16[32,2,192]{2,1,0:T(2,128)(2,1)}), bf16[32,2,192]{2,1,0:T(2,128)(2,1)S(1)}, u32[]{:S(2)}, u32[]{:S(2)}) async-start(bf16[32,2,192]{2,1,0:T(2,128)(2,1)} %reshape.352), calls=%async_computation.8 | async-start | bytes 65536 | tf_op jit(solution)/shard_map/all_to_all | solution.py:59
  159.4 12.5 %all-to-all-start.9 = ((bf16[32,2,192]{2,1,0:T(2,128)(2,1)}), bf16[32,2,192]{2,1,0:T(2,128)(2,1)S(1)}, u32[]{:S(2)}, u32[]{:S(2)}) async-start(bf16[32,2,192]{2,1,0:T(2,128)(2,1)} %reshape.354), calls=%async_computation.9 | async-start | bytes 65536 | tf_op jit(solution)/shard_map/all_to_all | solution.py:67
  172.1 0.7 copy-start.9
  190.1 19.0 %all-to-all-start.11 = ((bf16[32,1,16,384]{3,2,1,0:T(8,128)(2,1)}), bf16[32,1,16,384]{3,2,1,0:T(8,128)(2,1)S(1)}, u32[]{:S(2)}, u32[]{:S(2)}) async-start(bf16[32,1,16,384]{3,2,1,0:T(8,128)(2,1)} %broadcast_in_dim.45), calls=%async_computation.11 | async-start | bytes 786432 | tf_op jit(solution)/shard_map/all_to_all | solution.py:67
  209.2 9.0 %collective-permute-start.2 = (bf16[2,16,512]{2,1,0:T(8,128)(2,1)S(1)}, bf16[2,16,512]{2,1,0:T(8,128)(2,1)S(1)}, u32[]{:S(2)}, u32[]{:S(2)}) collective-permute-start(bf16[2,16,512]{2,1,0:T(8,128)(2,1)S(1)} %convolution_convert_fusion.3), channel_id=1, source_target_pairs={{0,3},{1,2},{2,1},{3,0},{4,7},{5,6},{6,5},{7,4},{8,11},{9,10},{10,... | collective-permute-start | bytes 98312 | tf_op jit(solution)/shard_map/ppermute | solution.py:18
  213.3 6.2 %collective-permute-start.1 = (bf16[2,16,512]{2,1,0:T(8,128)(2,1)S(1)}, bf16[2,16,512]{2,1,0:T(8,128)(2,1)S(1)}, u32[]{:S(2)}, u32[]{:S(2)}) collective-permute-start(bf16[2,16,512]{2,1,0:T(8,128)(2,1)S(1)} %convolution_convert_fusion.3), channel_id=1, source_target_pairs={{0,2},{1,3},{2,0},{3,1},{4,6},{5,7},{6,4},{7,5},{8,10},{9,11},{10,... | collective-permute-start | bytes 98312 | tf_op jit(solution)/shard_map/ppermute | solution.py:18
  215.8 5.0 %collective-permute-start = (bf16[2,16,512]{2,1,0:T(8,128)(2,1)S(1)}, bf16[2,16,512]{2,1,0:T(8,128)(2,1)S(1)}, u32[]{:S(2)}, u32[]{:S(2)}) collective-permute-start(bf16[2,16,512]{2,1,0:T(8,128)(2,1)S(1)} %convolution_convert_fusion.3), channel_id=1, source_target_pairs={{0,1},{1,0},{2,3},{3,2},{4,5},{5,4},{6,7},{7,6},{8,9},{9,8},{10,11... | collective-permute-start | bytes 98312 | tf_op jit(solution)/shard_map/ppermute | solution.py:18
  232.3 0.7 copy-start.10
  252.7 21.6 %all-to-all-start.14 = ((bf16[32,2,16,256]{3,2,1,0:T(8,128)(2,1)}), bf16[32,2,16,256]{3,2,1,0:T(8,128)(2,1)S(1)}, u32[]{:S(2)}, u32[]{:S(2)}) async-start(bf16[32,2,16,256]{3,2,1,0:T(8,128)(2,1)} %broadcast_in_dim.48), calls=%async_computation.14 | async-start | bytes 1048576 | tf_op jit(solution)/shard_map/all_to_all | solution.py:67
  302.8 0.7 copy-start.7
  304.6 23.7 %all-to-all-start.17 = ((bf16[16,4,16,256]{3,2,1,0:T(8,128)(2,1)}), bf16[16,4,16,256]{3,2,1,0:T(8,128)(2,1)S(1)}, u32[]{:S(2)}, u32[]{:S(2)}) async-start(bf16[16,4,16,256]{3,2,1,0:T(8,128)(2,1)} %broadcast_in_dim.50), calls=%async_computation.17 | async-start | bytes 1048576 | tf_op jit(solution)/shard_map/all_to_all | solution.py:67

commit v3 on v2

--- a/solution.py
+++ b/solution.py
@@ -11,20 +11,6 @@
 def level_mask(sizes, count, start):
     index = start + jnp.arange(count, dtype=jnp.int32)
     return (index[None, :] < sizes[:, None]).astype(F32)[:, None, :]
-
-
-def exchange(value, axis, masks):
-    size = lax.axis_size(axis)
-    return [lax.ppermute(value, axis, [(i, i ^ m) for i in range(size)]) for m in masks]
-
-
-def sum_stage(partial, axis, masks):
-    own = partial.astype(BF16)
-    parts = [own] + exchange(own, axis, masks)
-    parts = [part.astype(F32) for part in parts]
-    while len(parts) > 1:
-        parts = [parts[i] + parts[i + 1] for i in range(0, len(parts), 2)]
-    return parts[0]
 
 
 def near_groups():
@@ -46,10 +32,6 @@
 
 def sum_near_far(partial):
     return sum_groups(sum_groups(partial, near_groups()), far_groups())
-
-
-def sum_permutes_far(partial):
-    return sum_groups(sum_stage(partial, "col", (1, 2, 3)), far_groups())
 
 
 def sum_scattered(partial):
@@ -93,17 +75,31 @@
     return jnp.concatenate(placed, axis=-1)
 
 
-def child_rows(solved, blocks):
-    whole = spread(solved, "col")
-    _, parents, width, plocal = whole.shape
-    local_blocks = plocal // BLOCK
-    children = blocks.shape[0]
-    mine = lax.dynamic_slice_in_dim(blocks, lax.axis_index("col"), 1, 1)[:, 0]
-    picked = []
-    for c in range(children):
-        at = (mine[c] // local_blocks, c // 2, 0, (mine[c] % local_blocks) * BLOCK)
-        picked.append(lax.dynamic_slice(whole, at, (1, 1, width, BLOCK))[0])
-    return jnp.concatenate(picked, axis=0)
+def own_rows(coupling, blocks, parent_local):
+    whole = lax.all_gather(coupling, "col", axis=0)
+    local_blocks = parent_local // BLOCK
+    targets = lax.axis_index("col") * local_blocks + jnp.arange(local_blocks, dtype=jnp.int32)
+    hits = (blocks[:, None, :] == targets[None, :, None]).astype(jnp.int32)
+    listed = jnp.sum(hits, axis=-1)
+    at = jnp.sum(hits * jnp.arange(blocks.shape[1], dtype=jnp.int32), axis=-1)
+    rows = []
+    for c in range(blocks.shape[0]):
+        for b in range(local_blocks):
+            start = (at[c, b], c, 0, 0)
+            rows.append(lax.dynamic_slice(whole, start, (1, 1) + coupling.shape[1:])[0, 0])
+    rows = jnp.stack(rows).reshape((blocks.shape[0], parent_local) + coupling.shape[2:])
+    return rows, jnp.repeat(listed.astype(F32), BLOCK, axis=1)[:, None, :]
+
+
+def own_update(rows, listed, solved):
+    partial = times_rows(rows, solved) * listed
+    children, width, count = partial.shape
+    return sum_over_row(jnp.sum(partial.reshape(children // 2, 2, width, count), axis=1))
+
+
+def own_carried(rows, listed, solved, total):
+    taken = jnp.repeat(solved, 2, axis=0) * listed
+    return total(times_columns(rows, taken))
 
 
 def sweep(inverses, couplings, sources, pivots, sizes, lists):
@@ -112,23 +108,31 @@
     col_at = lax.axis_index("col")
     row_masks = []
     col_masks = []
+    moved = [None] * depth
     for level in range(depth):
         fronts, rows_here, cols_here = inverses[level].shape
         row_masks.append(level_mask(sizes[level], rows_here, row_at * rows_here))
         col_masks.append(level_mask(sizes[level], cols_here, col_at * cols_here))
+        if level > 0:
+            coupling = couplings[level]
+            if level > 1:
+                coupling, _ = lax.optimization_barrier((coupling, moved[level - 1]))
+            moved[level] = own_rows(coupling, lists[level], inverses[level - 1].shape[2])
     scaled = [None] * depth
     residual = sources[depth - 1]
-    forward = [sum_scattered, sum_near_far, sum_near_far]
-    backward = [sum_permutes_far, sum_scattered]
+    forward = [sum_near_far, sum_near_far, sum_scattered]
+    backward = [sum_near_far, sum_scattered]
     for level in range(depth - 1, -1, -1):
         solved = forward[level](times_rows(inverses[level], residual * col_masks[level]))
         solved = solved * row_masks[level]
         scaled[level] = solved * pivots[level][:, None, :]
-        if level > 0:
+        if level > 1:
             update = sum_over_row(times_rows(couplings[level], solved))
             residual = sources[level - 1] - place_updates(
                 update, lists[level], sources[level - 1].shape[-1]
             )
+        elif level > 0:
+            residual = sources[level - 1] - own_update(*moved[level], solved)
     outputs = [None] * depth
     carried = None
     for level in range(depth):
@@ -137,8 +141,7 @@
         solved = solved * col_masks[level]
         outputs[level] = solved
         if level + 1 < depth:
-            picked = child_rows(solved, lists[level + 1])
-            carried = backward[level](times_columns(couplings[level + 1], picked))
+            carried = own_carried(*moved[level + 1], solved, backward[level])
     return outputs
 
 

time: 331 us -> 416 us (1.26)
  waiting for transfers between devices: 116 us -> 192 us
  between operations: 15.4 us -> 40.7 us
  starting transfers between devices: 58.9 us -> 39.5 us
  blocking collectives: 112 us -> 100 us
  local copies, waits for them, and re-layouts: 15.8 us -> 21.9 us
  other arithmetic: 7.66 us -> 12.5 us
  matrix products: 3.01 us -> 7.57 us
    all_gather x0 -> x2, waiting for transfers between devices: none -> 100 us  [own_rows(): whole = lax.all_gather(coupling, 'col', axis=0)]
    all_to_all x7 -> x5, waiting for transfers between devices: 80.9 us -> 56.6 us  [spread(): return lax.all_to_all(copies, axis, 0, 0, tiled=True)]
    all_to_all x4 -> x3, blocking collectives: 68 us -> 48.1 us  [spread(): return lax.all_to_all(copies, axis, 0, 0, tiled=True)]
    all_to_all x3 -> x4, blocking collectives: 30.4 us -> 40.3 us  [sum_groups(): lax.all_to_all(copies, 'col', 0, 0, axis_index_groups=groups, tiled=True)]
    ppermute x3 -> x0, starting transfers between devices: 8.98 us -> none  [exchange(): lax.ppermute(value, axis, [(i, i ^ m) for i in range(size)])]
    all_to_all x2, starting transfers between devices: 13.5 us -> 6.8 us  [sum_groups(): lax.all_to_all(copies, 'col', 0, 0, axis_index_groups=groups, tiled=True)]
    unnamed x36 -> x34, local copies, waits for them, and re-layouts: 6.79 us -> 12.8 us
    all_to_all x7 -> x5, starting transfers between devices: 32.6 us -> 27.4 us  [spread(): return lax.all_to_all(copies, axis, 0, 0, tiled=True)]
  transfers between devices with their start and end apart: 13 -> 10, of which waited for: 12 -> 8; matrix products, arithmetic and copies ran while one was open for 1% -> 6% of each run, Pallas kernels for 0% -> 0%
where the time goes in v3:
time: 416 us; the launch traced here: 414 us
  waiting for transfers between devices  192 us (46%)
  blocking collectives  100 us (24%)
  between operations  40.7 us (10%)
  starting transfers between devices  39.5 us (9%)
  local copies, waits for them, and re-layouts  21.9 us (5%)
  other arithmetic  12.5 us (3%)
  matrix products  7.57 us (2%)
    all_gather x2, waiting for transfers between devices, own_rows(): whole = lax.all_gather(coupling, 'col', axis=0)  100 us
    all_to_all x5, waiting for transfers between devices, spread(): return lax.all_to_all(copies, axis, 0, 0, tiled=True)  56.6 us
    all_to_all x3, blocking collectives, spread(): return lax.all_to_all(copies, axis, 0, 0, tiled=True)  48.1 us
    all_to_all x4, blocking collectives, sum_groups(): lax.all_to_all(copies, 'col', 0, 0, axis_index_groups=groups, tiled=True)  40.3 us
    all_to_all x5, starting transfers between devices, spread(): return lax.all_to_all(copies, axis, 0, 0, tiled=True)  27.4 us
    all_to_all x2, waiting for transfers between devices, sum_groups(): lax.all_to_all(copies, 'col', 0, 0, axis_index_groups=groups, tiled=True)  25.7 us
    unnamed x34, local copies, waits for them, and re-layouts  12.8 us
    all_to_all x1, blocking collectives, sum_scattered(): pieces = lax.all_to_all(pieces, 'col', 0, 0, tiled=True)  11.8 us
  transfers between devices with their start and end apart: 10, of which 8 were waited for; matrix products, arithmetic and copies ran while one was open for 6% of the time, Pallas kernels for 0%

profile of v3, /device:TPU:1, one launch (start us, length us, event | category | flops | bytes accessed | tf_op | source)
XLA Modules:
  0.0 414.4 jit_solution(8695137431750966760)
XLA Ops:
  7.3 0.7 all-gather.5.cloned.1.call-update
  8.0 0.9 fusion.29
  20.7 100.2 %all-gather.5.cloned.1.call-done = bf16[64,128,512]{2,1,0:T(8,128)(2,1)} async-done(((bf16[2,128,512]{2,1,0:T(8,128)(2,1)}), bf16[64,128,512]{2,1,0:T(8,128)(2,1)}) %all-gather.5.cloned.1.call-update) | async-done | bytes 8388624 | tf_op jit(solution)/shard_map/all_gather | solution.py:79
  120.9 0.9 bitcast_dynamic-update-slice_fusion.13
  121.8 0.9 bitcast_dynamic-update-slice_fusion.12
  122.7 0.9 bitcast_dynamic-update-slice_fusion.11
  123.7 0.9 bitcast_dynamic-update-slice_fusion.10
  124.6 0.9 bitcast_dynamic-update-slice_fusion.9
  125.5 0.9 bitcast_dynamic-update-slice_fusion.8
  126.5 0.7 compare_convert_fusion.5
  127.2 1.2 convolution_convert_fusion.1
  129.0 1.0 reduce.22
  130.0 0.7 reshape.340
  130.7 5.2 %all-to-all-start = ((bf16[32,2,512]{2,1,0:T(2,128)(2,1)}), bf16[32,2,512]{2,1,0:T(2,128)(2,1)S(1)}, u32[]{:S(2)}, u32[]{:S(2)}) async-start(bf16[32,2,512]{2,1,0:T(2,128)(2,1)} %reshape.340), calls=%async_computation | async-start | bytes 131072 | tf_op jit(solution)/shard_map/all_to_all | solution.py:41
  135.9 8.8 %all-to-all-done = bf16[32,2,512]{2,1,0:T(2,128)(2,1)S(1)} async-done(((bf16[32,2,512]{2,1,0:T(2,128)(2,1)}), bf16[32,2,512]{2,1,0:T(2,128)(2,1)S(1)}, u32[]{:S(2)}, u32[]{:S(2)}) %all-to-all-start) | async-done | bytes 65568 | tf_op jit(solution)/shard_map/all_to_all | solution.py:41
  144.9 1.0 reduce.23
  146.0 0.7 reshape.342
  146.6 3.9 all-to-all-start.1
  150.5 0.7 compare_convert_fusion.1
  151.2 8.6 %all-to-all-done.1 = bf16[32,2,512]{2,1,0:T(2,128)(2,1)S(1)} async-done(((bf16[32,2,512]{2,1,0:T(2,128)(2,1)}), bf16[32,2,512]{2,1,0:T(2,128)(2,1)S(1)}, u32[]{:S(2)}, u32[]{:S(2)}) %all-to-all-start.1) | async-done | bytes 65568 | tf_op jit(solution)/shard_map/all_to_all | solution.py:49
  160.2 1.3 convolution_convert_fusion.7
  161.6 22.2 %all_to_all.80 = bf16[16,4,16,128]{3,2,1,0:T(8,128)(2,1)S(1)} all-to-all(bf16[16,4,16,128]{3,2,1,0:T(8,128)(2,1)S(1)} %broadcast_in_dim.38), channel_id=1, replica_groups=mesh['row'=16,'col'=32] {'row'}, dimensions={0} | all-to-all | bytes 524288 | tf_op jit(solution)/shard_map/all_to_all | solution.py:49
  183.8 0.9 broadcast_in_dim.39
  184.7 3.9 all-to-all-start.3
  188.6 0.8 compare_convert_fusion.6
  189.5 0.7 compare_convert_fusion.4
  190.3 21.6 %all-to-all-done.3 = bf16[32,4,16,128]{3,2,1,0:T(8,128)(2,1)S(1)} async-done(((bf16[32,4,16,128]{3,2,1,0:T(8,128)(2,1)}), bf16[32,4,16,128]{3,2,1,0:T(8,128)(2,1)S(1)}, u32[]{:S(2)}, u32[]{:S(2)}) %all-to-all-start.3) | async-done | bytes 524320 | tf_op jit(solution)/shard_map/all_to_all | solution.py:49
  212.2 1.3 convolution_convert_fusion.4
  213.5 10.3 %all_to_all.81 = bf16[4,2,16,512]{3,2,1,0:T(8,128)(2,1)S(1)} all-to-all(bf16[4,2,16,512]{3,2,1,0:T(8,128)(2,1)S(1)} %broadcast_in_dim.40), channel_id=1, replica_groups={{0,1,2,3},{4,5,6,7},{8,9,10,11},{12,13,14,15},{16,17,18,19},{20,21,22,2..., dimensions={0} | all-to-all | bytes 262144 | tf_op jit(solution)/shard_map/all_to_all | solution.py:29
  223.9 0.7 broadcast_in_dim.41
  224.6 3.4 all-to-all-start.5
  228.2 0.7 compare_convert_fusion
  228.9 13.1 %all-to-all-done.5 = bf16[8,2,16,512]{3,2,1,0:T(8,128)(2,1)S(1)} async-done(((bf16[8,2,16,512]{3,2,1,0:T(8,128)(2,1)}), bf16[8,2,16,512]{3,2,1,0:T(8,128)(2,1)S(1)}, u32[]{:S(2)}, u32[]{:S(2)}) %all-to-all-start.5) | async-done | bytes 262176 | tf_op jit(solution)/shard_map/all_to_all | solution.py:29
  242.4 0.7 broadcast_in_dim.43
  243.1 5.8 %all-to-all-start.6 = ((bf16[16,1,16,384]{3,2,1,0:T(8,128)(2,1)}), bf16[16,1,16,384]{3,2,1,0:T(8,128)(2,1)S(1)}, u32[]{:S(2)}, u32[]{:S(2)}) async-start(bf16[16,1,16,384]{3,2,1,0:T(8,128)(2,1)} %broadcast_in_dim.43), calls=%async_computation.6 | async-start | bytes 393216 | tf_op jit(solution)/shard_map/all_to_all | solution.py:49
  248.9 10.4 %all-to-all-done.6 = bf16[16,1,16,384]{3,2,1,0:T(8,128)(2,1)S(1)} async-done(((bf16[16,1,16,384]{3,2,1,0:T(8,128)(2,1)}), bf16[16,1,16,384]{3,2,1,0:T(8,128)(2,1)S(1)}, u32[]{:S(2)}, u32[]{:S(2)}) %all-to-all-start.6) | async-done | bytes 196640 | tf_op jit(solution)/shard_map/all_to_all | solution.py:49
  259.3 1.3 convolution_convert_fusion.5
  260.7 7.7 %all_to_all.82 = bf16[4,1,16,768]{3,2,1,0:T(8,128)(2,1)S(1)} all-to-all(bf16[4,1,16,768]{3,2,1,0:T(8,128)(2,1)S(1)} %broadcast_in_dim.44), channel_id=1, replica_groups={{0,1,2,3},{4,5,6,7},{8,9,10,11},{12,13,14,15},{16,17,18,19},{20,21,22,2..., dimensions={0} | all-to-all | bytes 196608 | tf_op jit(solution)/shard_map/all_to_all | solution.py:29
  268.4 0.7 broadcast_in_dim.45
  269.1 3.4 all-to-all-start.8
  272.5 12.6 %all-to-all-done.8 = bf16[8,1,16,768]{3,2,1,0:T(8,128)(2,1)S(1)} async-done(((bf16[8,1,16,768]{3,2,1,0:T(8,128)(2,1)}), bf16[8,1,16,768]{3,2,1,0:T(8,128)(2,1)S(1)}, u32[]{:S(2)}, u32[]{:S(2)}) %all-to-all-start.8) | async-done | bytes 196640 | tf_op jit(solution)/shard_map/all_to_all | solution.py:29
  285.1 1.3 convolution_convert_fusion.8
  286.4 14.0 %all_to_all.83 = bf16[16,1,16,384]{3,2,1,0:T(8,128)(2,1)S(1)} all-to-all(bf16[16,1,16,384]{3,2,1,0:T(8,128)(2,1)S(1)} %broadcast_in_dim.46), channel_id=1, replica_groups=mesh['row'=16,'col'=32] {'row'}, dimensions={0} | all-to-all | bytes 393216 | tf_op jit(solution)/shard_map/all_to_all | solution.py:49
  300.7 8.1 %all_to_all.84 = bf16[4,2,16,512]{3,2,1,0:T(8,128)(2,1)S(1)} all-to-all(bf16[4,2,16,512]{3,2,1,0:T(8,128)(2,1)S(1)} %broadcast_in_dim.47), channel_id=1, replica_groups={{0,1,2,3},{4,5,6,7},{8,9,10,11},{12,13,14,15},{16,17,18,19},{20,21,22,2..., dimensions={0} | all-to-all | bytes 262144 | tf_op jit(solution)/shard_map/all_to_all | solution.py:29
  308.8 14.2 %all_to_all.85 = bf16[8,2,16,512]{3,2,1,0:T(8,128)(2,1)S(1)} all-to-all(bf16[8,2,16,512]{3,2,1,0:T(8,128)(2,1)S(1)} %broadcast_in_dim.48), channel_id=1, replica_groups={{0,4,8,12,16,20,24,28},{1,5,9,13,17,21,25,29},{2,6,10,14,18,22,26,30},{..., dimensions={0} | all-to-all | bytes 524288 | tf_op jit(solution)/shard_map/all_to_all | solution.py:29
  323.3 0.7 broadcast_in_dim.49
  324.0 4.3 %all-to-all-start.12 = ((bf16[16,2,16,256]{3,2,1,0:T(8,128)(2,1)}), bf16[16,2,16,256]{3,2,1,0:T(8,128)(2,1)S(1)}, u32[]{:S(2)}, u32[]{:S(2)}) async-start(bf16[16,2,16,256]{3,2,1,0:T(8,128)(2,1)} %broadcast_in_dim.49), calls=%async_computation.12 | async-start | bytes 524288 | tf_op jit(solution)/shard_map/all_to_all | solution.py:49
  328.6 0.7 fusion.33
  344.7 0.9 bitcast_dynamic-update-slice_fusion.7
  345.6 0.9 bitcast_dynamic-update-slice_fusion.6
  346.5 0.9 bitcast_dynamic-update-slice_fusion.5
  347.4 0.9 bitcast_dynamic-update-slice_fusion.4
  348.4 0.9 bitcast_dynamic-update-slice_fusion.3
  349.3 0.9 bitcast_dynamic-update-slice_fusion.2
  350.2 0.9 bitcast_dynamic-update-slice_fusion.1
  351.1 0.9 bitcast_dynamic-update-slice_fusion
  352.3 1.0 reduce.24
  353.4 11.8 %all_to_all.86 = bf16[32,2,512]{2,1,0:T(2,128)(2,1)S(1)} all-to-all(bf16[32,2,512]{2,1,0:T(2,128)(2,1)S(1)} %reshape.344), channel_id=1, replica_groups=mesh['row'=16,'col'=32] {'col'}, dimensions={0} | all-to-all | bytes 131072 | tf_op jit(solution)/shard_map/all_to_all | solution.py:41
  365.5 1.0 reduce.25
  366.6 11.9 %all_to_all.87 = bf16[32,2,512]{2,1,0:T(2,128)(2,1)S(1)} all-to-all(bf16[32,2,512]{2,1,0:T(2,128)(2,1)S(1)} %reshape.346), channel_id=1, replica_groups=mesh['row'=16,'col'=32] {'col'}, dimensions={0} | all-to-all | bytes 131072 | tf_op jit(solution)/shard_map/all_to_all | solution.py:49
  379.1 0.9 broadcast_in_dim.53
  380.0 9.6 %all-to-all-start.15 = ((bf16[16,4,16,256]{3,2,1,0:T(8,128)(2,1)}), bf16[16,4,16,256]{3,2,1,0:T(8,128)(2,1)S(1)}, u32[]{:S(2)}, u32[]{:S(2)}) async-start(bf16[16,4,16,256]{3,2,1,0:T(8,128)(2,1)} %broadcast_in_dim.53), calls=%async_computation.15 | async-start | bytes 1048576 | tf_op jit(solution)/shard_map/all_to_all | solution.py:49
  390.8 16.1 %all-to-all-done.15 = bf16[16,4,16,256]{3,2,1,0:T(8,128)(2,1)S(1)} async-done(((bf16[16,4,16,256]{3,2,1,0:T(8,128)(2,1)}), bf16[16,4,16,256]{3,2,1,0:T(8,128)(2,1)S(1)}, u32[]{:S(2)}, u32[]{:S(2)}) %all-to-all-start.15) | async-done | bytes 524320 | tf_op jit(solution)/shard_map/all_to_all | solution.py:49
  407.0 0.6 multiply_bitcast_fusion
  (80 shorter events, 6.9 us)
Async XLA Ops:
  7.2 120.0 %copy-start = (bf16[4,512,256]{2,1,0:T(8,128)(2,1)S(1)}, bf16[4,512,256]{2,1,0:T(8,128)(2,1)}, u32[]{:S(2)}) copy-start(bf16[4,512,256]{2,1,0:T(8,128)(2,1)} %param.17) | copy-start | bytes 3145732
  7.2 321.2 %copy-start.3 = (s32[4,32]{1,0:T(4,128)S(1)}, s32[4,32]{1,0:T(4,128)}, u32[]{:S(2)}) copy-start(s32[4,32]{1,0:T(4,128)} %param.29) | copy-start | bytes 1540
  7.2 315.9 %copy-start.1 = (bf16[2,512,256]{2,1,0:T(8,128)(2,1)S(1)}, bf16[2,512,256]{2,1,0:T(8,128)(2,1)}, u32[]{:S(2)}) copy-start(bf16[2,512,256]{2,1,0:T(8,128)(2,1)} %param.16) | copy-start | bytes 1572868
  7.2 315.9 %copy-start.4 = (f32[2,512]{1,0:T(2,128)S(1)}, f32[2,512]{1,0:T(2,128)}, u32[]{:S(2)}) copy-start(f32[2,512]{1,0:T(2,128)} %param.24) | copy-start | bytes 12292
  7.2 371.7 %copy-start.2 = (f32[4,512]{1,0:T(4,128)S(1)}, f32[4,512]{1,0:T(4,128)}, u32[]{:S(2)}) copy-start(f32[4,512]{1,0:T(4,128)} %param.25) | copy-start | bytes 24580
  7.2 113.7 %all-gather.5.cloned.1.call-start = ((), (), s32[]{:S(2)}) async-start(), calls=%async_computation.16 | async-start | bytes 8650752 | tf_op jit(solution)/shard_map/all_gather | solution.py:79
  8.0 336.7 %all-gather.7.cloned.1.call-start = ((), (), s32[]{:S(2)}) async-start(), calls=%async_computation.17 | async-start | bytes 17301504 | tf_op jit(solution)/shard_map/all_gather | solution.py:79
  130.7 14.0 %all-to-all-start = ((bf16[32,2,512]{2,1,0:T(2,128)(2,1)}), bf16[32,2,512]{2,1,0:T(2,128)(2,1)S(1)}, u32[]{:S(2)}, u32[]{:S(2)}) async-start(bf16[32,2,512]{2,1,0:T(2,128)(2,1)} %reshape.340), calls=%async_computation | async-start | bytes 131072 | tf_op jit(solution)/shard_map/all_to_all | solution.py:41
  146.6 13.1 %all-to-all-start.1 = ((bf16[32,2,512]{2,1,0:T(2,128)(2,1)}), bf16[32,2,512]{2,1,0:T(2,128)(2,1)S(1)}, u32[]{:S(2)}, u32[]{:S(2)}) async-start(bf16[32,2,512]{2,1,0:T(2,128)(2,1)} %reshape.342), calls=%async_computation.1 | async-start | bytes 131072 | tf_op jit(solution)/shard_map/all_to_all | solution.py:49
  184.7 27.2 %all-to-all-start.3 = ((bf16[32,4,16,128]{3,2,1,0:T(8,128)(2,1)}), bf16[32,4,16,128]{3,2,1,0:T(8,128)(2,1)S(1)}, u32[]{:S(2)}, u32[]{:S(2)}) async-start(bf16[32,4,16,128]{3,2,1,0:T(8,128)(2,1)} %broadcast_in_dim.39), calls=%async_computation.3 | async-start | bytes 1048576 | tf_op jit(solution)/shard_map/all_to_all | solution.py:49
  224.6 17.4 %all-to-all-start.5 = ((bf16[8,2,16,512]{3,2,1,0:T(8,128)(2,1)}), bf16[8,2,16,512]{3,2,1,0:T(8,128)(2,1)S(1)}, u32[]{:S(2)}, u32[]{:S(2)}) async-start(bf16[8,2,16,512]{3,2,1,0:T(8,128)(2,1)} %broadcast_in_dim.41), calls=%async_computation.5 | async-start | bytes 524288 | tf_op jit(solution)/shard_map/all_to_all | solution.py:29
  243.1 16.1 %all-to-all-start.6 = ((bf16[16,1,16,384]{3,2,1,0:T(8,128)(2,1)}), bf16[16,1,16,384]{3,2,1,0:T(8,128)(2,1)S(1)}, u32[]{:S(2)}, u32[]{:S(2)}) async-start(bf16[16,1,16,384]{3,2,1,0:T(8,128)(2,1)} %broadcast_in_dim.43), calls=%async_computation.6 | async-start | bytes 393216 | tf_op jit(solution)/shard_map/all_to_all | solution.py:49
  269.1 16.0 %all-to-all-start.8 = ((bf16[8,1,16,768]{3,2,1,0:T(8,128)(2,1)}), bf16[8,1,16,768]{3,2,1,0:T(8,128)(2,1)S(1)}, u32[]{:S(2)}, u32[]{:S(2)}) async-start(bf16[8,1,16,768]{3,2,1,0:T(8,128)(2,1)} %broadcast_in_dim.45), calls=%async_computation.8 | async-start | bytes 393216 | tf_op jit(solution)/shard_map/all_to_all | solution.py:29
  324.0 20.5 %all-to-all-start.12 = ((bf16[16,2,16,256]{3,2,1,0:T(8,128)(2,1)}), bf16[16,2,16,256]{3,2,1,0:T(8,128)(2,1)S(1)}, u32[]{:S(2)}, u32[]{:S(2)}) async-start(bf16[16,2,16,256]{3,2,1,0:T(8,128)(2,1)} %broadcast_in_dim.49), calls=%async_computation.12 | async-start | bytes 524288 | tf_op jit(solution)/shard_map/all_to_all | solution.py:49
  380.0 26.9 %all-to-all-start.15 = ((bf16[16,4,16,256]{3,2,1,0:T(8,128)(2,1)}), bf16[16,4,16,256]{3,2,1,0:T(8,128)(2,1)S(1)}, u32[]{:S(2)}, u32[]{:S(2)}) async-start(bf16[16,4,16,256]{3,2,1,0:T(8,128)(2,1)} %broadcast_in_dim.53), calls=%async_computation.15 | async-start | bytes 1048576 | tf_op jit(solution)/shard_map/all_to_all | solution.py:49
Sparse Core Ops, SparseCore 0:
  11.2 109.6 all-gather.4
  126.6 161.1 all-gather.6

commit v4 on v0

v4 whole, which is shorter than its diff:
```python
import jax
import jax.numpy as jnp
from jax import lax
from jax.experimental import pallas as pl
from jax.experimental.pallas import tpu as pltpu
from jax.sharding import PartitionSpec as P

BLOCK = 128
NEAR = 4
BF16 = jnp.bfloat16
F32 = jnp.float32
VMEM_SPEC = pl.BlockSpec(memory_space=pltpu.VMEM)
SMEM_SPEC = pl.BlockSpec(memory_space=pltpu.SMEM)


def near_groups():
    size = lax.axis_size("col")
    return [[z * NEAR + x for x in range(NEAR)] for z in range(size // NEAR)]


def far_groups():
    size = lax.axis_size("col")
    return [[z * NEAR + x for z in range(size // NEAR)] for x in range(NEAR)]


def swap_near(pieces):
    return lax.all_to_all(pieces, "col", 0, 0, axis_index_groups=near_groups(), tiled=True)


def gather_near(value):
    return lax.all_gather(value, "col", axis_index_groups=near_groups(), axis=0)


def copies_of(value, size):
    return jnp.broadcast_to(value.astype(BF16)[None], (size,) + value.shape)


def spread_far(value):
    groups = far_groups()
    copies = copies_of(value, len(groups[0]))
    return lax.all_to_all(copies, "col", 0, 0, axis_index_groups=groups, tiled=True)


def spread_row(value):
    return lax.all_to_all(copies_of(value, lax.axis_size("row")), "row", 0, 0, tiled=True)


def sum_far(partial):
    return jnp.sum(spread_far(partial).astype(F32), axis=0)


def sum_row(partial):
    return jnp.sum(spread_row(partial).astype(F32), axis=0)


def level_mask(sizes, count, start):
    index = start + jnp.arange(count, dtype=jnp.int32)
    return (index[None, :] < sizes[:, None]).astype(F32)[:, None, :]


def dot(a, b, dims):
    return lax.dot_general(a, b, (dims, ((), ())), preferred_element_type=F32)


def place_kernel(here, blocks, whole, source, mask, inverse, out):
    parents = source.shape[0]
    held = source.shape[2] // BLOCK
    listed = blocks.shape[1]
    first = here[0] * held
    for p in range(parents):
        parts = []
        for b in range(held):
            parts.append(source[p, :, b * BLOCK : (b + 1) * BLOCK])
        residual = jnp.concatenate(parts, axis=-1)
        scratch_free = residual
        for c in (2 * p, 2 * p + 1):
            placed = []
            for b in range(held):
                def find(k, carry, c=c, b=b):
                    at, found = carry
                    hit = blocks[c, k] == first + b
                    return jnp.where(hit, k, at), jnp.where(hit, 1, found)

                at, found = lax.fori_loop(0, listed, find, (0, 0), unroll=True)
                lane = pl.multiple_of((at % NEAR) * BLOCK, BLOCK)
                tile = whole[at // NEAR, c, :, pl.ds(lane, BLOCK)].astype(F32)
                placed.append(tile * found.astype(F32))
            scratch_free = scratch_free - jnp.concatenate(placed, axis=-1)
        operand = (scratch_free * mask[p]).astype(BF16)
        width = inverse.shape[3]
        total = None
        for x in range(NEAR):
            part = dot(operand[:, x * width : (x + 1) * width], inverse[x, p], ((1,), (1,)))
            total = part if total is None else total + part
        out[p] = total


def place_and_solve(blocks, whole, source, mask, inverse):
    parents, width, _ = source.shape
    here = (lax.axis_index("col") // NEAR).reshape(1)
    return pl.pallas_call(
        place_kernel,
        out_shape=jax.ShapeDtypeStruct((parents, width, inverse.shape[2]), F32),
        in_specs=[SMEM_SPEC, SMEM_SPEC] + [VMEM_SPEC] * 4,
        out_specs=VMEM_SPEC,
        compiler_params=pltpu.CompilerParams(vmem_limit_bytes=32 << 20),
    )(here, blocks, whole, source, mask, inverse)


def pick_kernel(here, blocks, whole, coupling, out):
    children = blocks.shape[0]
    held = whole.shape[3] // BLOCK
    for c in range(children):
        total = None
        for x in range(NEAR):
            block = blocks[c, here[0] * NEAR + x]
            lane = pl.multiple_of((block % held) * BLOCK, BLOCK)
            tile = whole[block // held, c // 2, :, pl.ds(lane, BLOCK)]
            part = dot(tile, coupling[x, c], ((1,), (0,)))
            total = part if total is None else total + part
        out[c] = total


def pick_and_carry(blocks, whole, coupling):
    here = (lax.axis_index("col") // NEAR).reshape(1)
    return pl.pallas_call(
        pick_kernel,
        out_shape=jax.ShapeDtypeStruct((blocks.shape[0], whole.shape[2], coupling.shape[3]), F32),
        in_specs=[SMEM_SPEC, SMEM_SPEC] + [VMEM_SPEC] * 2,
        out_specs=VMEM_SPEC,
        compiler_params=pltpu.CompilerParams(vmem_limit_bytes=32 << 20),
    )(here, blocks, whole, coupling)


def update_of(coupling, solved):
    solved = solved.astype(BF16)
    parts = [
        jnp.einsum("fuk,fck->fcu", coupling[x], solved, preferred_element_type=F32)
        for x in range(NEAR)
    ]
    return jnp.concatenate(parts, axis=-1)


def transposed(inverse, vector):
    vector = vector.astype(BF16)
    parts = [
        jnp.einsum("fij,fci->fcj", inverse[x], vector, preferred_element_type=F32)
        for x in range(NEAR)
    ]
    return jnp.concatenate(parts, axis=-1)


def halves(value):
    high = value.astype(BF16)
    return high, (value - high.astype(F32)).astype(BF16)


def by_near(value):
    return value.reshape(NEAR, value.shape[0] // NEAR, value.shape[1])


def local(
    inverse_top,
    inverse_mid,
    inverse_low,
    coupling_mid,
    coupling_low,
    source_top,
    source_mid,
    source_low,
    pivots_top,
    pivots_mid,
    pivots_low,
    sizes_mid,
    sizes_low,
    blocks_mid,
    blocks_low,
):
    row_at = lax.axis_index("row")
    col_at = lax.axis_index("col")
    far_at = col_at // NEAR
    rhs = source_top.shape[1]
    width = rhs // NEAR
    n0, n1, n2 = source_top.shape[0], source_mid.shape[1], source_low.shape[1]
    k1, k2 = inverse_mid.shape[1], inverse_low.shape[1]
    top = jnp.full((1,), inverse_top.shape[0] * lax.axis_size("row"), jnp.int32)

    coupling_low_near = gather_near(coupling_low)
    inverse_mid_near = gather_near(inverse_mid)
    coupling_mid_near = gather_near(coupling_mid)
    inverse_top_near = gather_near(inverse_top)[:, None]

    row_mask_mid = level_mask(sizes_mid, k1, row_at * k1)
    row_mask_low = level_mask(sizes_low, k2, row_at * k2)
    col_mask_low = level_mask(sizes_low, n2, col_at * n2)
    wide_mask_mid = level_mask(sizes_mid, NEAR * n1, far_at * NEAR * n1)
    wide_mask_top = level_mask(top, NEAR * n0, far_at * NEAR * n0)

    source = jnp.swapaxes(source_low, 1, 2) * col_mask_low
    partial = jnp.einsum(
        "fij,fcj->cfi", inverse_low, source.astype(BF16), preferred_element_type=F32
    ).reshape(rhs, -1)
    others = jnp.concatenate([source_mid[0].T, source_mid[1].T, source_top.T], axis=-1)
    message = jnp.concatenate([partial.astype(BF16), *halves(others)], axis=-1)
    got = swap_near(by_near(message)).astype(F32)
    size = partial.shape[1]
    partial = jnp.sum(got[:, :, :size], axis=0)
    others = got[:, :, size : size + others.shape[1]] + got[:, :, size + others.shape[1] :]
    parts = jnp.swapaxes(others, 0, 1)
    wide_source_mid = jnp.stack(
        [parts[:, :, f * n1 : (f + 1) * n1].reshape(width, NEAR * n1) for f in range(2)]
    )
    wide_source_top = parts[:, :, 2 * n1 :].reshape(1, width, NEAR * n0)
    solved = sum_far(jnp.swapaxes(partial.reshape(width, -1, k2), 0, 1)) * row_mask_low
    scaled_low = solved * pivots_low[:, None, :]

    whole = spread_far(sum_row(update_of(coupling_low_near, solved)))
    partial = place_and_solve(blocks_low, whole, wide_source_mid, wide_mask_mid, inverse_mid_near)
    solved = sum_far(partial) * row_mask_mid
    scaled_mid = solved * pivots_mid[:, None, :]

    whole = spread_far(sum_row(update_of(coupling_mid_near, solved)))
    partial = place_and_solve(blocks_mid, whole, wide_source_top, wide_mask_top, inverse_top_near)
    scaled = sum_far(partial) * pivots_top[None, None, :]

    solution_top = sum_row(transposed(inverse_top_near, scaled))
    partial = pick_and_carry(blocks_mid, spread_far(solution_top), coupling_mid_near)
    residual = (scaled_mid - sum_far(partial)) * row_mask_mid
    solution_mid = sum_row(transposed(inverse_mid_near, residual)) * wide_mask_mid
    partial = pick_and_carry(blocks_low, spread_far(solution_mid), coupling_low_near)
    residual = (scaled_low - sum_far(partial)) * row_mask_low

    upper = jnp.concatenate(
        [
            solution_top[0].reshape(width, NEAR, n0),
            solution_mid[0].reshape(width, NEAR, n1),
            solution_mid[1].reshape(width, NEAR, n1),
        ],
        axis=-1,
    )
    upper = jnp.concatenate(halves(upper), axis=-1)
    flat = jnp.swapaxes(residual, 0, 1).reshape(width, -1).astype(BF16)
    size = flat.shape[1]
    message = jnp.concatenate([copies_of(flat, NEAR), jnp.swapaxes(upper, 0, 1)], axis=-1)
    got = swap_near(message).reshape(rhs, -1)
    upper = got[:, size:].astype(F32)
    upper = upper[:, : upper.shape[1] // 2] + upper[:, upper.shape[1] // 2 :]
    residual = got[:, :size].reshape(rhs, -1, k2)
    partial = jnp.einsum("fij,cfi->fcj", inverse_low, residual, preferred_element_type=F32)
    solution_low = sum_row(partial) * col_mask_low
    return (
        upper[:, :n0].T,
        jnp.stack([upper[:, n0 : n0 + n1].T, upper[:, n0 + n1 :].T]),
        jnp.swapaxes(solution_low, 1, 2),
    )


def solution(mesh):
    placed = (
        P("row", "col"),
        P(None, "row", "col"),
        P(None, "row", "col"),
        P(None, "col", "row"),
        P(None, "col", "row"),
        P("col", None),
        P(None, "col", None),
        P(None, "col", None),
        P("row"),
        P(None, "row"),
        P(None, "row"),
        P(),
        P(),
        P(),
        P(),
    )
    return jax.shard_map(
        local,
        mesh=mesh,
        in_specs=placed,
        out_specs=(P("col", None), P(None, "col", None), P(None, "col", None)),
        check_vma=False,
    )
```

time: 1270 us -> 309 us (0.24)
  waiting for transfers between devices: 802 us -> 131 us
  blocking collectives: 436 us -> 61.3 us
  starting transfers between devices: 0.25 us -> 66.5 us
    psum x5 -> x0, waiting for transfers between devices: 729 us -> none  [the longest x2 317 us: parent_coupling(): return lax.psum(partial_value, 'col')]
    psum x5 -> x0, blocking collectives: 336 us -> none  [the longest x2 130 us: diag_backward(): return lax.psum(partial_value, 'row') * mask_out]
    all_gather x3 -> x0, blocking collectives: 100 us -> none  [the longest x2 66.3 us: child_rows(): whole = lax.all_gather(solved, 'col', axis=1, tiled=True)]
    all_to_all x0 -> x11, waiting for transfers between devices: none -> 89.4 us  [the longest x4 48.6 us: spread_row(): lax.all_to_all(copies_of(value, lax.axis_size('row')), 'row', 0, 0, tiled...]
    all_to_all x0 -> x11, starting transfers between devices: none -> 66.4 us  [the longest x6 34.4 us: spread_far(): lax.all_to_all(copies, 'col', 0, 0, axis_index_groups=groups, tiled=True)]
    all_to_all x0 -> x5, blocking collectives: none -> 61.3 us  [the longest x3 34.9 us: spread_far(): lax.all_to_all(copies, 'col', 0, 0, axis_index_groups=groups, tiled=True)]
    all_gather x1 -> x4, waiting for transfers between devices: 72.9 us -> 38.7 us  [gather_near(): return lax.all_gather(value, 'col', axis_index_groups=near_groups(), axis=0)]
  transfers between devices with their start and end apart: 6 -> 15, of which waited for: 6 -> 14; matrix products, arithmetic and copies ran while one was open for 0% -> 6% of each run, Pallas kernels for 0% -> 1%
where the time goes in v4:
time: 309 us; the launch traced here: 307 us
  waiting for transfers between devices  131 us (42%)
  starting transfers between devices  66.5 us (22%)
  blocking collectives  61.3 us (20%)
  between operations  14.3 us (5%)
  matrix products  12.5 us (4%)
  local copies, waits for them, and re-layouts  11.7 us (4%)
  Pallas kernels  5.34 us (2%)
  other arithmetic  4.53 us (1%)
    all_to_all x4, waiting for transfers between devices, spread_row(): lax.all_to_all(copies_of(value, lax.axis_size('row')), 'row', 0, 0, tiled...  48.6 us
    all_gather x4, waiting for transfers between devices, gather_near(): return lax.all_gather(value, 'col', axis_index_groups=near_groups(), axis=0)  38.7 us
    all_to_all x6, waiting for transfers between devices, spread_far(): lax.all_to_all(copies, 'col', 0, 0, axis_index_groups=groups, tiled=True)  36.6 us
    all_to_all x3, blocking collectives, spread_far(): lax.all_to_all(copies, 'col', 0, 0, axis_index_groups=groups, tiled=True)  34.9 us
    all_to_all x6, starting transfers between devices, spread_far(): lax.all_to_all(copies, 'col', 0, 0, axis_index_groups=groups, tiled=True)  34.4 us
    all_to_all x4, starting transfers between devices, spread_row(): lax.all_to_all(copies_of(value, lax.axis_size('row')), 'row', 0, 0, tiled...  27.2 us
    all_to_all x1, blocking collectives, spread_row(): lax.all_to_all(copies_of(value, lax.axis_size('row')), 'row', 0, 0, tiled...  19.1 us
    dot_general x8, matrix products, update_of(): jnp.einsum('fuk,fck->fcu', coupling[x], solved, preferred_element_type=F32)  9.67 us
  transfers between devices with their start and end apart: 15, of which 14 were waited for; matrix products, arithmetic and copies ran while one was open for 6% of the time, Pallas kernels for 1%

profile of v4, /device:TPU:1, one launch (start us, length us, event | category | flops | bytes accessed | tf_op | source)
XLA Modules:
  0.0 307.0 jit_solution(3372104994586743459)
XLA Ops:
  7.2 0.7 all-gather.9.cloned.1.call-update
  8.0 0.7 all-gather.11.cloned.1.call-update
  8.7 0.7 all-gather.13.cloned.1.call-update
  9.4 0.7 compare_convert_fusion.5
  10.2 1.2 fusion
  11.7 0.7 pad_maximum_fusion
  12.4 4.8 %all-to-all-start = ((bf16[4,4,3840]{2,1,0:T(4,128)(2,1)}), bf16[4,4,3840]{2,1,0:T(4,128)(2,1)S(1)}, u32[]{:S(2)}, u32[]{:S(2)}) async-start(bf16[4,4,3840]{2,1,0:T(4,128)(2,1)} %pad_maximum_fusion), calls=%async_computation | async-start | bytes 245760 | tf_op jit(solution)/shard_map/all_to_all | solution.py:27
  17.2 0.6 all-gather.15.cloned.1.call-update
  17.8 4.2 %all-to-all-done = bf16[4,4,3840]{2,1,0:T(4,128)(2,1)S(1)} async-done(((bf16[4,4,3840]{2,1,0:T(4,128)(2,1)}), bf16[4,4,3840]{2,1,0:T(4,128)(2,1)S(1)}, u32[]{:S(2)}, u32[]{:S(2)}) %all-to-all-start) | async-done | bytes 122912 | tf_op jit(solution)/shard_map/all_to_all | solution.py:27
  22.0 0.7 broadcast_in_dim.34
  22.7 10.0 %all-to-all-start.1 = ((bf16[8,4,4,512]{3,2,1,0:T(4,128)(2,1)}), bf16[8,4,4,512]{3,2,1,0:T(4,128)(2,1)S(1)}, u32[]{:S(2)}, u32[]{:S(2)}) async-start(bf16[8,4,4,512]{3,2,1,0:T(4,128)(2,1)} %broadcast_in_dim.34), calls=%async_computation.1 | async-start | bytes 262144 | tf_op jit(solution)/shard_map/all_to_all | solution.py:41
  32.9 7.9 %all-to-all-done.1 = bf16[8,4,4,512]{3,2,1,0:T(4,128)(2,1)S(1)} async-done(((bf16[8,4,4,512]{3,2,1,0:T(4,128)(2,1)}), bf16[8,4,4,512]{3,2,1,0:T(4,128)(2,1)S(1)}, u32[]{:S(2)}, u32[]{:S(2)}) %all-to-all-start.1) | async-done | bytes 131104 | tf_op jit(solution)/shard_map/all_to_all | solution.py:41
  41.0 10.8 %all-gather.9.cloned.1.call-done = bf16[16,128,512]{2,1,0:T(8,128)(2,1)} async-done(((bf16[4,128,512]{2,1,0:T(8,128)(2,1)}), bf16[16,128,512]{2,1,0:T(8,128)(2,1)}) %all-gather.9.cloned.1.call-update) | async-done | bytes 2097168 | tf_op jit(solution)/shard_map/all_gather | solution.py:31
  51.8 1.3 convolution_convert_fusion.6
  53.1 1.3 convolution_convert_fusion.7
  54.4 1.3 convolution_convert_fusion.8
  55.7 1.3 convolution_convert_fusion.9
  57.0 0.8 broadcast_in_dim.35
  57.8 7.4 %all-to-all-start.2 = ((bf16[16,4,4,512]{3,2,1,0:T(4,128)(2,1)}), bf16[16,4,4,512]{3,2,1,0:T(4,128)(2,1)S(1)}, u32[]{:S(2)}, u32[]{:S(2)}) async-start(bf16[16,4,4,512]{3,2,1,0:T(4,128)(2,1)} %broadcast_in_dim.35), calls=%async_computation.2 | async-start | bytes 524288 | tf_op jit(solution)/shard_map/all_to_all | solution.py:45
  65.3 11.6 %all-to-all-done.2 = bf16[16,4,4,512]{3,2,1,0:T(4,128)(2,1)S(1)} async-done(((bf16[16,4,4,512]{3,2,1,0:T(4,128)(2,1)}), bf16[16,4,4,512]{3,2,1,0:T(4,128)(2,1)S(1)}, u32[]{:S(2)}, u32[]{:S(2)}) %all-to-all-start.2) | async-done | bytes 262176 | tf_op jit(solution)/shard_map/all_to_all | solution.py:45
  77.1 0.7 broadcast_in_dim.36
  77.7 7.1 %all-to-all-start.3 = ((bf16[8,4,4,512]{3,2,1,0:T(4,128)(2,1)}), bf16[8,4,4,512]{3,2,1,0:T(4,128)(2,1)S(1)}, u32[]{:S(2)}, u32[]{:S(2)}) async-start(bf16[8,4,4,512]{3,2,1,0:T(4,128)(2,1)} %broadcast_in_dim.36), calls=%async_computation.3 | async-start | bytes 262144 | tf_op jit(solution)/shard_map/all_to_all | solution.py:41
  84.9 5.3 %all-gather.11.cloned.1.call-done = bf16[8,512,256]{2,1,0:T(8,128)(2,1)} async-done(((bf16[2,512,256]{2,1,0:T(8,128)(2,1)}), bf16[8,512,256]{2,1,0:T(8,128)(2,1)}) %all-gather.11.cloned.1.call-update) | async-done | bytes 2097168 | tf_op jit(solution)/shard_map/all_gather | solution.py:31
  90.2 4.3 %all-to-all-done.3.whole = bf16[8,4,4,512]{3,2,1,0:T(4,128)(2,1)S(1)} async-done(((bf16[8,4,4,512]{3,2,1,0:T(4,128)(2,1)}), bf16[8,4,4,512]{3,2,1,0:T(4,128)(2,1)S(1)}, u32[]{:S(2)}, u32[]{:S(2)}) %all-to-all-start.3) | async-done | bytes 131104 | tf_op jit(solution)/shard_map/all_to_all | solution.py:41
  94.5 1.6 copy-done.3
  96.1 1.9 shard_map.166
  98.0 0.7 broadcast_in_dim.37
  98.7 3.4 %all-to-all-start.4 = ((bf16[8,2,4,512]{3,2,1,0:T(4,128)(2,1)}), bf16[8,2,4,512]{3,2,1,0:T(4,128)(2,1)S(1)}, u32[]{:S(2)}, u32[]{:S(2)}) async-start(bf16[8,2,4,512]{3,2,1,0:T(4,128)(2,1)} %broadcast_in_dim.37), calls=%async_computation.4 | async-start | bytes 131072 | tf_op jit(solution)/shard_map/all_to_all | solution.py:41
  102.1 7.0 %all-to-all-done.4 = bf16[8,2,4,512]{3,2,1,0:T(4,128)(2,1)S(1)} async-done(((bf16[8,2,4,512]{3,2,1,0:T(4,128)(2,1)}), bf16[8,2,4,512]{3,2,1,0:T(4,128)(2,1)S(1)}, u32[]{:S(2)}, u32[]{:S(2)}) %all-to-all-start.4) | async-done | bytes 65568 | tf_op jit(solution)/shard_map/all_to_all | solution.py:41
  109.2 11.6 %all-gather.13.cloned.1.call-done = bf16[8,128,512]{2,1,0:T(8,128)(2,1)} async-done(((bf16[2,128,512]{2,1,0:T(8,128)(2,1)}), bf16[8,128,512]{2,1,0:T(8,128)(2,1)}) %all-gather.13.cloned.1.call-update) | async-done | bytes 1048592 | tf_op jit(solution)/shard_map/all_gather | solution.py:31
  120.8 1.1 convolution_convert_fusion.14
  121.9 1.1 convolution_convert_fusion.15
  123.0 1.1 convolution_convert_fusion.16
  124.2 1.1 convolution_convert_fusion.17
  125.4 0.7 broadcast_in_dim.38
  126.0 8.3 %all-to-all-start.5 = ((bf16[16,2,4,512]{3,2,1,0:T(4,128)(2,1)}), bf16[16,2,4,512]{3,2,1,0:T(4,128)(2,1)S(1)}, u32[]{:S(2)}, u32[]{:S(2)}) async-start(bf16[16,2,4,512]{3,2,1,0:T(4,128)(2,1)} %broadcast_in_dim.38), calls=%async_computation.5 | async-start | bytes 262144 | tf_op jit(solution)/shard_map/all_to_all | solution.py:45
  134.4 9.2 %all-to-all-done.5 = bf16[16,2,4,512]{3,2,1,0:T(4,128)(2,1)S(1)} async-done(((bf16[16,2,4,512]{3,2,1,0:T(4,128)(2,1)}), bf16[16,2,4,512]{3,2,1,0:T(4,128)(2,1)S(1)}, u32[]{:S(2)}, u32[]{:S(2)}) %all-to-all-start.5) | async-done | bytes 131104 | tf_op jit(solution)/shard_map/all_to_all | solution.py:45
  143.6 0.7 broadcast_in_dim.39
  144.3 7.1 %all-to-all-start.6 = ((bf16[8,2,4,512]{3,2,1,0:T(4,128)(2,1)}), bf16[8,2,4,512]{3,2,1,0:T(4,128)(2,1)S(1)}, u32[]{:S(2)}, u32[]{:S(2)}) async-start(bf16[8,2,4,512]{3,2,1,0:T(4,128)(2,1)} %broadcast_in_dim.39), calls=%async_computation.6 | async-start | bytes 131072 | tf_op jit(solution)/shard_map/all_to_all | solution.py:41
  151.4 11.0 %all-gather.15.cloned.1.call-done = bf16[3072,384]{1,0:T(8,128)(2,1)} async-done(((bf16[768,384]{1,0:T(8,128)(2,1)}), bf16[3072,384]{1,0:T(8,128)(2,1)}) %all-gather.15.cloned.1.call-update) | async-done | bytes 2359312 | tf_op jit(solution)/shard_map/all_gather | solution.py:31
  162.4 1.7 copy-done.1
  164.1 1.7 shard_map.167
  165.8 14.1 %all_to_all.80 = bf16[8,1,4,768]{3,2,1,0:T(4,128)(2,1)S(1)} all-to-all(bf16[8,1,4,768]{3,2,1,0:T(4,128)(2,1)S(1)} %broadcast_in_dim.42), channel_id=1, replica_groups={{0,4,8,12,16,20,24,28},{1,5,9,13,17,21,25,29},{2,6,10,14,18,22,26,30},{..., dimensions={0} | all-to-all | bytes 98304 | tf_op jit(solution)/shard_map/all_to_all | solution.py:41
  180.9 19.1 %all_to_all.81 = bf16[16,1,4,1536]{3,2,1,0:T(4,128)(2,1)S(1)} all-to-all(bf16[16,1,4,1536]{3,2,1,0:T(4,128)(2,1)S(1)} %broadcast_in_dim.43), channel_id=1, replica_groups=mesh['row'=16,'col'=32] {'row'}, dimensions={0} | all-to-all | bytes 393216 | tf_op jit(solution)/shard_map/all_to_all | solution.py:45
  200.1 11.3 %all_to_all.82.whole = bf16[8,1,4,1536]{3,2,1,0:T(4,128)(2,1)S(1)} all-to-all(bf16[8,1,4,1536]{3,2,1,0:T(4,128)(2,1)S(1)} %broadcast_in_dim.44), channel_id=1, replica_groups={{0,4,8,12,16,20,24,28},{1,5,9,13,17,21,25,29},{2,6,10,14,18,22,26,30},{..., dimensions={0} | all-to-all | bytes 196608 | tf_op jit(solution)/shard_map/all_to_all | solution.py:41
  211.4 0.8 shard_map.168
  212.2 9.5 %all_to_all.83 = bf16[8,2,4,512]{3,2,1,0:T(4,128)(2,1)S(1)} all-to-all(bf16[8,2,4,512]{3,2,1,0:T(4,128)(2,1)S(1)} %broadcast_in_dim.45), channel_id=1, replica_groups={{0,4,8,12,16,20,24,28},{1,5,9,13,17,21,25,29},{2,6,10,14,18,22,26,30},{..., dimensions={0} | all-to-all | bytes 131072 | tf_op jit(solution)/shard_map/all_to_all | solution.py:41
  222.6 0.8 broadcast_in_dim.46
  223.4 5.0 %all-to-all-start.11 = ((bf16[16,2,4,1024]{3,2,1,0:T(4,128)(2,1)}), bf16[16,2,4,1024]{3,2,1,0:T(4,128)(2,1)S(1)}, u32[]{:S(2)}, u32[]{:S(2)}) async-start(bf16[16,2,4,1024]{3,2,1,0:T(4,128)(2,1)} %broadcast_in_dim.46), calls=%async_computation.11 | async-start | bytes 524288 | tf_op jit(solution)/shard_map/all_to_all | solution.py:45
  228.5 11.7 %all-to-all-done.11 = bf16[16,2,4,1024]{3,2,1,0:T(4,128)(2,1)S(1)} async-done(((bf16[16,2,4,1024]{3,2,1,0:T(4,128)(2,1)}), bf16[16,2,4,1024]{3,2,1,0:T(4,128)(2,1)S(1)}, u32[]{:S(2)}, u32[]{:S(2)}) %all-to-all-start.11) | async-done | bytes 262176 | tf_op jit(solution)/shard_map/all_to_all | solution.py:45
  240.5 0.7 broadcast_in_dim.47
  241.1 3.4 %all-to-all-start.12 = ((bf16[8,2,4,1024]{3,2,1,0:T(4,128)(2,1)}), bf16[8,2,4,1024]{3,2,1,0:T(4,128)(2,1)S(1)}, u32[]{:S(2)}, u32[]{:S(2)}) async-start(bf16[8,2,4,1024]{3,2,1,0:T(4,128)(2,1)} %broadcast_in_dim.47), calls=%async_computation.12 | async-start | bytes 262144 | tf_op jit(solution)/shard_map/all_to_all | solution.py:41
  244.6 9.2 %all-to-all-done.12.whole = bf16[8,2,4,1024]{3,2,1,0:T(4,128)(2,1)S(1)} async-done(((bf16[8,2,4,1024]{3,2,1,0:T(4,128)(2,1)}), bf16[8,2,4,1024]{3,2,1,0:T(4,128)(2,1)S(1)}, u32[]{:S(2)}, u32[]{:S(2)}) %all-to-all-start.12) | async-done | bytes 131104 | tf_op jit(solution)/shard_map/all_to_all | solution.py:41
  253.8 0.9 shard_map.169
  254.8 0.7 broadcast_in_dim.48
  255.5 3.4 %all-to-all-start.13 = ((bf16[8,4,4,512]{3,2,1,0:T(4,128)(2,1)}), bf16[8,4,4,512]{3,2,1,0:T(4,128)(2,1)S(1)}, u32[]{:S(2)}, u32[]{:S(2)}) async-start(bf16[8,4,4,512]{3,2,1,0:T(4,128)(2,1)} %broadcast_in_dim.48), calls=%async_computation.13 | async-start | bytes 262144 | tf_op jit(solution)/shard_map/all_to_all | solution.py:41
  259.0 8.1 %all-to-all-done.13 = bf16[8,4,4,512]{3,2,1,0:T(4,128)(2,1)S(1)} async-done(((bf16[8,4,4,512]{3,2,1,0:T(4,128)(2,1)}), bf16[8,4,4,512]{3,2,1,0:T(4,128)(2,1)S(1)}, u32[]{:S(2)}, u32[]{:S(2)}) %all-to-all-start.13) | async-done | bytes 131104 | tf_op jit(solution)/shard_map/all_to_all | solution.py:41
  267.4 7.4 %all_to_all.84 = bf16[4,4,3840]{2,1,0:T(4,128)(2,1)S(1)} all-to-all(bf16[4,4,3840]{2,1,0:T(4,128)(2,1)S(1)} %pad_maximum_fusion.1), channel_id=1, replica_groups={{0,1,2,3},{4,5,6,7},{8,9,10,11},{12,13,14,15},{16,17,18,19},{20,21,22,2..., dimensions={0} | all-to-all | bytes 245760 | tf_op jit(solution)/shard_map/all_to_all | solution.py:27
  275.1 0.9 broadcast_in_dim.50
  275.9 6.5 %all-to-all-start.15 = ((bf16[16,4,16,256]{3,2,1,0:T(8,128)(2,1)}), bf16[16,4,16,256]{3,2,1,0:T(8,128)(2,1)S(1)}, u32[]{:S(2)}, u32[]{:S(2)}) async-start(bf16[16,4,16,256]{3,2,1,0:T(8,128)(2,1)} %broadcast_in_dim.50), calls=%async_computation.15 | async-start | bytes 1048576 | tf_op jit(solution)/shard_map/all_to_all | solution.py:45
  282.5 0.6 pad_maximum_fusion.3
  283.1 0.6 slice_bitcast_fusion
  283.7 16.1 %all-to-all-done.15 = bf16[16,4,16,256]{3,2,1,0:T(8,128)(2,1)S(1)} async-done(((bf16[16,4,16,256]{3,2,1,0:T(8,128)(2,1)}), bf16[16,4,16,256]{3,2,1,0:T(8,128)(2,1)S(1)}, u32[]{:S(2)}, u32[]{:S(2)}) %all-to-all-start.15) | async-done | bytes 524320 | tf_op jit(solution)/shard_map/all_to_all | solution.py:45
  299.8 0.6 multiply_bitcast_fusion
  (112 shorter events, 4.2 us)
Async XLA Ops:
  7.2 3.0 copy-start
  7.2 4.3 %copy-start.8 = (f32[2,256,16]{1,2,0:T(8,128)S(1)}, f32[2,256,16]{1,2,0:T(8,128)}, u32[]{:S(2)}) copy-start(f32[2,256,16]{1,2,0:T(8,128)} %param.21) | copy-start | bytes 98308
  7.2 4.4 %copy-start.9 = (f32[384,16]{0,1:T(8,128)S(1)}, f32[384,16]{0,1:T(8,128)}, u32[]{:S(2)}) copy-start(f32[384,16]{0,1:T(8,128)} %param.20) | copy-start | bytes 73732
  7.2 44.6 %all-gather.9.cloned.1.call-start = ((), (), s32[]{:S(2)}) async-start(), calls=%async_computation.16 | async-start | bytes 2621440 | tf_op jit(solution)/shard_map/all_gather | solution.py:31
  7.9 82.3 %all-gather.11.cloned.1.call-start = ((), (), s32[]{:S(2)}) async-start(), calls=%async_computation.17 | async-start | bytes 2621440 | tf_op jit(solution)/shard_map/all_gather | solution.py:31
  8.7 24.1 %copy-start.14 = (s32[4]{0:T(128)S(1)}, s32[4]{0:T(128)}, u32[]{:S(2)}) copy-start(s32[4]{0:T(128)} %param.27) | copy-start | bytes 52
  8.7 112.1 %all-gather.13.cloned.1.call-start = ((), (), s32[]{:S(2)}) async-start(), calls=%async_computation.18 | async-start | bytes 1310720 | tf_op jit(solution)/shard_map/all_gather | solution.py:31
  12.4 9.6 %all-to-all-start = ((bf16[4,4,3840]{2,1,0:T(4,128)(2,1)}), bf16[4,4,3840]{2,1,0:T(4,128)(2,1)S(1)}, u32[]{:S(2)}, u32[]{:S(2)}) async-start(bf16[4,4,3840]{2,1,0:T(4,128)(2,1)} %pad_maximum_fusion), calls=%async_computation | async-start | bytes 245760 | tf_op jit(solution)/shard_map/all_to_all | solution.py:27
  17.2 145.2 %all-gather.15.cloned.1.call-start = ((), (), s32[]{:S(2)}) async-start(), calls=%async_computation.19 | async-start | bytes 2949120 | tf_op jit(solution)/shard_map/all_gather | solution.py:31
  17.8 47.5 %copy-start.11 = (s32[2]{0:T(128)S(1)}, s32[2]{0:T(128)}, u32[]{:S(2)}) copy-start(s32[2]{0:T(128)} %param.26) | copy-start | bytes 28
  22.7 18.1 %all-to-all-start.1 = ((bf16[8,4,4,512]{3,2,1,0:T(4,128)(2,1)}), bf16[8,4,4,512]{3,2,1,0:T(4,128)(2,1)S(1)}, u32[]{:S(2)}, u32[]{:S(2)}) async-start(bf16[8,4,4,512]{3,2,1,0:T(4,128)(2,1)} %broadcast_in_dim.34), calls=%async_computation.1 | async-start | bytes 262144 | tf_op jit(solution)/shard_map/all_to_all | solution.py:41
  32.9 61.6 %copy-start.6 = (s32[4,32]{1,0:T(4,128)S(1)}, s32[4,32]{1,0:T(4,128)}, u32[]{:S(2)}) copy-start(s32[4,32]{1,0:T(4,128)} %blocks.7) | copy-start | bytes 1540
  57.8 19.1 %all-to-all-start.2 = ((bf16[16,4,4,512]{3,2,1,0:T(4,128)(2,1)}), bf16[16,4,4,512]{3,2,1,0:T(4,128)(2,1)S(1)}, u32[]{:S(2)}, u32[]{:S(2)}) async-start(bf16[16,4,4,512]{3,2,1,0:T(4,128)(2,1)} %broadcast_in_dim.35), calls=%async_computation.2 | async-start | bytes 524288 | tf_op jit(solution)/shard_map/all_to_all | solution.py:45
  77.7 16.7 %all-to-all-start.3 = ((bf16[8,4,4,512]{3,2,1,0:T(4,128)(2,1)}), bf16[8,4,4,512]{3,2,1,0:T(4,128)(2,1)S(1)}, u32[]{:S(2)}, u32[]{:S(2)}) async-start(bf16[8,4,4,512]{3,2,1,0:T(4,128)(2,1)} %broadcast_in_dim.36), calls=%async_computation.3 | async-start | bytes 262144 | tf_op jit(solution)/shard_map/all_to_all | solution.py:41
  94.5 1.6 copy-start.3
  96.1 66.3 %copy-start.7 = (s32[2,32]{1,0:T(2,128)S(1)}, s32[2,32]{1,0:T(2,128)}, u32[]{:S(2)}) copy-start(s32[2,32]{1,0:T(2,128)} %blocks.6) | copy-start | bytes 772
  98.7 10.5 %all-to-all-start.4 = ((bf16[8,2,4,512]{3,2,1,0:T(4,128)(2,1)}), bf16[8,2,4,512]{3,2,1,0:T(4,128)(2,1)S(1)}, u32[]{:S(2)}, u32[]{:S(2)}) async-start(bf16[8,2,4,512]{3,2,1,0:T(4,128)(2,1)} %broadcast_in_dim.37), calls=%async_computation.4 | async-start | bytes 131072 | tf_op jit(solution)/shard_map/all_to_all | solution.py:41
  123.0 56.9 %copy-start.13 = (f32[768]{0:T(1024)S(1)}, f32[768]{0:T(1024)}, u32[]{:S(2)}) copy-start(f32[768]{0:T(1024)} %param.23) | copy-start | bytes 9220
  126.0 17.5 %all-to-all-start.5 = ((bf16[16,2,4,512]{3,2,1,0:T(4,128)(2,1)}), bf16[16,2,4,512]{3,2,1,0:T(4,128)(2,1)S(1)}, u32[]{:S(2)}, u32[]{:S(2)}) async-start(bf16[16,2,4,512]{3,2,1,0:T(4,128)(2,1)} %broadcast_in_dim.38), calls=%async_computation.5 | async-start | bytes 262144 | tf_op jit(solution)/shard_map/all_to_all | solution.py:45
  144.3 18.1 %all-to-all-start.6 = ((bf16[8,2,4,512]{3,2,1,0:T(4,128)(2,1)}), bf16[8,2,4,512]{3,2,1,0:T(4,128)(2,1)S(1)}, u32[]{:S(2)}, u32[]{:S(2)}) async-start(bf16[8,2,4,512]{3,2,1,0:T(4,128)(2,1)} %broadcast_in_dim.39), calls=%async_computation.6 | async-start | bytes 131072 | tf_op jit(solution)/shard_map/all_to_all | solution.py:41
  162.4 1.7 copy-start.1
  165.8 45.6 %copy-start.5 = (bf16[8,128,512]{2,1,0:T(8,128)(2,1)S(1)}, bf16[8,128,512]{2,1,0:T(8,128)(2,1)}, u32[]{:S(2)}) copy-start(bf16[8,128,512]{2,1,0:T(8,128)(2,1)} %all-gather.13.cloned.1.call-done) | copy-start | bytes 3145732
  180.1 41.7 %copy-start.12 = (f32[2,512]{1,0:T(2,128)S(1)}, f32[2,512]{1,0:T(2,128)}, u32[]{:S(2)}) copy-start(f32[2,512]{1,0:T(2,128)} %param.24) | copy-start | bytes 12292
  180.3 41.5 %copy-start.4 = (bf16[8,512,256]{2,1,0:T(8,128)(2,1)S(1)}, bf16[8,512,256]{2,1,0:T(8,128)(2,1)}, u32[]{:S(2)}) copy-start(bf16[8,512,256]{2,1,0:T(8,128)(2,1)} %all-gather.11.cloned.1.call-done) | copy-start | bytes 6291460
  221.7 32.1 %copy-start.2 = (bf16[16,128,512]{2,1,0:T(8,128)(2,1)S(1)}, bf16[16,128,512]{2,1,0:T(8,128)(2,1)}, u32[]{:S(2)}) copy-start(bf16[16,128,512]{2,1,0:T(8,128)(2,1)} %all-gather.9.cloned.1.call-done) | copy-start | bytes 6291460
  223.4 16.8 %all-to-all-start.11 = ((bf16[16,2,4,1024]{3,2,1,0:T(4,128)(2,1)}), bf16[16,2,4,1024]{3,2,1,0:T(4,128)(2,1)S(1)}, u32[]{:S(2)}, u32[]{:S(2)}) async-start(bf16[16,2,4,1024]{3,2,1,0:T(4,128)(2,1)} %broadcast_in_dim.46), calls=%async_computation.11 | async-start | bytes 524288 | tf_op jit(solution)/shard_map/all_to_all | solution.py:45
  228.5 38.8 %copy-start.10 = (f32[4,512]{1,0:T(4,128)S(1)}, f32[4,512]{1,0:T(4,128)}, u32[]{:S(2)}) copy-start(f32[4,512]{1,0:T(4,128)} %param.25) | copy-start | bytes 24580
  241.1 12.7 %all-to-all-start.12 = ((bf16[8,2,4,1024]{3,2,1,0:T(4,128)(2,1)}), bf16[8,2,4,1024]{3,2,1,0:T(4,128)(2,1)S(1)}, u32[]{:S(2)}, u32[]{:S(2)}) async-start(bf16[8,2,4,1024]{3,2,1,0:T(4,128)(2,1)} %broadcast_in_dim.47), calls=%async_computation.12 | async-start | bytes 262144 | tf_op jit(solution)/shard_map/all_to_all | solution.py:41
  255.5 11.6 %all-to-all-start.13 = ((bf16[8,4,4,512]{3,2,1,0:T(4,128)(2,1)}), bf16[8,4,4,512]{3,2,1,0:T(4,128)(2,1)S(1)}, u32[]{:S(2)}, u32[]{:S(2)}) async-start(bf16[8,4,4,512]{3,2,1,0:T(4,128)(2,1)} %broadcast_in_dim.48), calls=%async_computation.13 | async-start | bytes 262144 | tf_op jit(solution)/shard_map/all_to_all | solution.py:41
  275.9 23.8 %all-to-all-start.15 = ((bf16[16,4,16,256]{3,2,1,0:T(8,128)(2,1)}), bf16[16,4,16,256]{3,2,1,0:T(8,128)(2,1)S(1)}, u32[]{:S(2)}, u32[]{:S(2)}) async-start(bf16[16,4,16,256]{3,2,1,0:T(8,128)(2,1)} %broadcast_in_dim.50), calls=%async_computation.15 | async-start | bytes 1048576 | tf_op jit(solution)/shard_map/all_to_all | solution.py:45
Sparse Core Ops, SparseCore 0:
  10.1 41.6 all-gather.8
  53.9 36.2 all-gather.10
  92.3 28.4 all-gather.12
  122.7 39.6 all-gather.14

commit v5 on v4

v5 whole, which is shorter than its diff:
```python
import functools

import jax
import jax.numpy as jnp
from jax import lax
from jax.experimental import pallas as pl
from jax.experimental.pallas import tpu as pltpu
from jax.sharding import PartitionSpec as P

BLOCK = 128
NEAR = 4
BF16 = jnp.bfloat16
F32 = jnp.float32
VMEM_SPEC = pl.BlockSpec(memory_space=pltpu.VMEM)
SMEM_SPEC = pl.BlockSpec(memory_space=pltpu.SMEM)


def near_groups():
    size = lax.axis_size("col")
    return [[z * NEAR + x for x in range(NEAR)] for z in range(size // NEAR)]


def far_groups():
    size = lax.axis_size("col")
    return [[z * NEAR + x for z in range(size // NEAR)] for x in range(NEAR)]


def swap_near(pieces):
    return lax.all_to_all(pieces, "col", 0, 0, axis_index_groups=near_groups(), tiled=True)


def far_size():
    return lax.axis_size("col") // NEAR


def gather_near(value):
    size = lax.axis_size("col")
    parts = [value]
    for m in range(1, NEAR):
        parts.append(lax.ppermute(value, "col", [(i, i ^ m) for i in range(size)]))
    return parts


def gather_beside(value, message):
    value, message = lax.optimization_barrier((value, message))
    return gather_near(value), message


def xor_order(value):
    near = lax.axis_index("col") % NEAR
    for bit in (1, 2):
        swapped = jnp.stack([value[i ^ bit] for i in range(NEAR)])
        value = jnp.where((near & bit) != 0, swapped, value)
    return value


def copies_of(value, size):
    return jnp.broadcast_to(value.astype(BF16)[None], (size,) + value.shape)


def send_far(copies):
    groups = far_groups()
    return lax.all_to_all(copies, "col", 0, 0, axis_index_groups=groups, tiled=True)


def send_row(copies):
    return lax.all_to_all(copies, "row", 0, 0, tiled=True)


def level_mask_xor(sizes, count):
    near, far = lax.axis_index("col") % NEAR, lax.axis_index("col") // NEAR
    slots = near ^ jnp.arange(NEAR, dtype=jnp.int32)
    index = (far * NEAR + slots)[:, None] * count + jnp.arange(count, dtype=jnp.int32)
    return (index.reshape(1, -1) < sizes[:, None]).astype(F32)[:, None, :]


def update_table(blocks, held):
    near, far = lax.axis_index("col") % NEAR, lax.axis_index("col") // NEAR
    slots = near ^ jnp.arange(NEAR, dtype=jnp.int32)
    targets = (far * NEAR + slots)[:, None] * held + jnp.arange(held, dtype=jnp.int32)
    hits = (blocks[:, None, :] == targets.reshape(1, -1, 1)).astype(jnp.int32)
    return jnp.sum(hits * jnp.arange(1, blocks.shape[1] + 1, dtype=jnp.int32), axis=-1) - 1


def level_mask(sizes, count, start):
    index = start + jnp.arange(count, dtype=jnp.int32)
    return (index[None, :] < sizes[:, None]).astype(F32)[:, None, :]


def dot(a, b, dims):
    return lax.dot_general(a, b, (dims, ((), ())), preferred_element_type=F32)


def call(kernel, out_shape, scalars, arrays, **static):
    return pl.pallas_call(
        functools.partial(kernel, **static),
        out_shape=out_shape,
        in_specs=[SMEM_SPEC] * len(scalars) + [VMEM_SPEC] * len(arrays),
        out_specs=jax.tree.map(lambda _: VMEM_SPEC, out_shape),
        compiler_params=pltpu.CompilerParams(vmem_limit_bytes=16 << 20),
    )(*scalars, *arrays)


def arrived(parts, f):
    terms = [parts[i, f].astype(F32) for i in range(parts.shape[0])]
    while len(terms) > 1:
        terms = [terms[i] + terms[i + 1] for i in range(0, len(terms), 2)]
    return terms[0]


def write_copies(out, f, value):
    value = value.astype(BF16)
    for i in range(out.shape[0]):
        out[i, f] = value


def shape_of(*dims, dtype=BF16):
    return jax.ShapeDtypeStruct(dims, dtype)


def update_kernel(parts, mask, pivots, c0, c1, c2, c3, out, scaled):
    for f in range(parts.shape[1]):
        solved = arrived(parts, f) * mask[f]
        scaled[f] = solved * pivots[f]
        operand = solved.astype(BF16)
        update = [dot(operand, c[f], ((1,), (1,))) for c in (c0, c1, c2, c3)]
        write_copies(out, f, jnp.concatenate(update, axis=-1))


def update_of(parts, mask, pivots, couplings):
    _, fronts, width, count = parts.shape
    rows = lax.axis_size("row")
    out = (
        shape_of(rows, fronts, width, NEAR * couplings[0].shape[1]),
        shape_of(fronts, width, count, dtype=F32),
    )
    return call(update_kernel, out, [], [parts, mask, pivots[:, None, :], *couplings])


def relay_kernel(parts, out):
    for f in range(parts.shape[1]):
        write_copies(out, f, arrived(parts, f))


def relay(parts):
    return call(relay_kernel, shape_of(far_size(), *parts.shape[1:]), [], [parts])


def solved_kernel(parts, mask, out, solved):
    for f in range(parts.shape[1]):
        value = arrived(parts, f) * mask[f]
        solved[f] = value
        write_copies(out, f, value)


def relay_solved(parts, mask):
    shape = parts.shape[1:]
    out = (shape_of(far_size(), *shape), shape_of(*shape, dtype=F32))
    return call(solved_kernel, out, [], [parts, mask])


def place_kernel(here, table, whole, source, mask, i0, i1, i2, i3, out, *, base):
    near = here[1]
    n = i0.shape[2]
    held = n // BLOCK
    for p in range(i0.shape[0]):
        total = None
        for m, inverse in enumerate((i0, i1, i2, i3)):
            tiles = []
            for b in range(held):
                start = base + p * n + b * BLOCK
                tile = source[near ^ m, :, start : start + BLOCK]
                for c in (2 * p, 2 * p + 1):
                    at = table[c, m * held + b]
                    found = jnp.where(at >= 0, 1.0, 0.0).astype(F32)
                    at = jnp.maximum(at, 0)
                    lane = pl.multiple_of(((at % NEAR) ^ near) * BLOCK, BLOCK)
                    placed = whole[at // NEAR, c, :, pl.ds(lane, BLOCK)].astype(F32)
                    tile = tile - placed * found
                tiles.append(tile)
            operand = jnp.concatenate(tiles, axis=-1) * mask[p, :, m * n : (m + 1) * n]
            part = dot(operand.astype(BF16), inverse[p], ((1,), (1,)))
            total = part if total is None else total + part
        write_copies(out, p, total)


def place_and_solve(here, table, whole, source, mask, inverses, base):
    parents, count, _ = inverses[0].shape
    out = shape_of(far_size(), parents, whole.shape[2], count)
    arrays = [whole, source, mask, *inverses]
    return call(place_kernel, out, [here, table], arrays, base=base)


def root_kernel(parts, pivots, i0, i1, i2, i3, out):
    operand = (arrived(parts, 0) * pivots[...]).astype(BF16)
    pieces = [dot(operand, i[0], ((1,), (0,))) for i in (i0, i1, i2, i3)]
    write_copies(out, 0, jnp.concatenate(pieces, axis=-1))


def root_back(parts, pivots, inverses):
    out = shape_of(lax.axis_size("row"), 1, parts.shape[2], NEAR * inverses[0].shape[2])
    return call(root_kernel, out, [], [parts, pivots[None, :], *inverses])


def back_kernel(parts, scaled, mask, i0, i1, i2, i3, out):
    for p in range(parts.shape[1]):
        operand = ((scaled[p] - arrived(parts, p)) * mask[p]).astype(BF16)
        pieces = [dot(operand, i[p], ((1,), (0,))) for i in (i0, i1, i2, i3)]
        write_copies(out, p, jnp.concatenate(pieces, axis=-1))


def back(parts, scaled, mask, inverses):
    fronts, _, n = inverses[0].shape
    out = shape_of(lax.axis_size("row"), fronts, parts.shape[2], NEAR * n)
    return call(back_kernel, out, [], [parts, scaled, mask, *inverses])


def pick_kernel(here, blocks, whole, c0, c1, c2, c3, out):
    far, near = here[0], here[1]
    held = whole.shape[3] // BLOCK // NEAR
    for c in range(blocks.shape[0]):
        total = None
        for m, coupling in enumerate((c0, c1, c2, c3)):
            block = blocks[c, far * NEAR + (near ^ m)]
            owner = block // held
            slot = (owner % NEAR) ^ near
            lane = pl.multiple_of((slot * held + block % held) * BLOCK, BLOCK)
            tile = whole[owner // NEAR, c // 2, :, pl.ds(lane, BLOCK)]
            part = dot(tile, coupling[c], ((1,), (0,)))
            total = part if total is None else total + part
        write_copies(out, c, total)


def pick_and_carry(here, blocks, whole, couplings):
    children, _, count = couplings[0].shape
    out = shape_of(far_size(), children, whole.shape[2], count)
    return call(pick_kernel, out, [here, blocks], [whole, *couplings])


def halves(value):
    high = value.astype(BF16)
    return high, (value - high.astype(F32)).astype(BF16)


def by_near(value):
    return value.reshape(NEAR, value.shape[0] // NEAR, value.shape[1])


def local(
    inverse_top,
    inverse_mid,
    inverse_low,
    coupling_mid,
    coupling_low,
    source_top,
    source_mid,
    source_low,
    pivots_top,
    pivots_mid,
    pivots_low,
    sizes_mid,
    sizes_low,
    blocks_mid,
    blocks_low,
):
    row_at = lax.axis_index("row")
    col_at = lax.axis_index("col")
    far_at = col_at // NEAR
    rhs = source_top.shape[1]
    width = rhs // NEAR
    n0, n1, n2 = source_top.shape[0], source_mid.shape[1], source_low.shape[1]
    k1, k2 = inverse_mid.shape[1], inverse_low.shape[1]
    top = jnp.full((1,), inverse_top.shape[0] * lax.axis_size("row"), jnp.int32)

    here = jnp.stack([far_at, col_at % NEAR]).astype(jnp.int32)
    table_low = update_table(blocks_low, n1 // BLOCK)
    table_mid = update_table(blocks_mid, n0 // BLOCK)
    row_mask_mid = level_mask(sizes_mid, k1, row_at * k1)
    row_mask_low = level_mask(sizes_low, k2, row_at * k2)
    col_mask_low = level_mask(sizes_low, n2, col_at * n2)
    wide_mask_mid = level_mask_xor(sizes_mid, n1)
    wide_mask_top = level_mask_xor(top, n0)

    source = jnp.swapaxes(source_low, 1, 2) * col_mask_low
    partial = jnp.einsum(
        "fij,fcj->cfi", inverse_low, source.astype(BF16), preferred_element_type=F32
    ).reshape(rhs, -1)
    others = jnp.concatenate([source_mid[0].T, source_mid[1].T, source_top.T], axis=-1)
    message = jnp.concatenate([partial.astype(BF16), *halves(others)], axis=-1)
    coupling_low_near, message = gather_beside(coupling_low, message)
    got = swap_near(by_near(message)).astype(F32)
    size = partial.shape[1]
    partial = jnp.sum(got[:, :, :size], axis=0)
    others = got[:, :, size : size + others.shape[1]] + got[:, :, size + others.shape[1] :]
    partial = jnp.swapaxes(partial.reshape(width, -1, k2), 0, 1)
    inverse_mid_near, message = gather_beside(inverse_mid, copies_of(partial, far_size()))
    parts = send_far(message)

    message, scaled_low = update_of(parts, row_mask_low, pivots_low, coupling_low_near)
    coupling_mid_near, message = gather_beside(coupling_mid, message)
    message = relay(send_row(message))
    inverse_top_near, message = gather_beside(inverse_top[None], message)
    whole = send_far(message)
    parts = send_far(
        place_and_solve(here, table_low, whole, others, wide_mask_mid, inverse_mid_near, 0)
    )

    message, scaled_mid = update_of(parts, row_mask_mid, pivots_mid, coupling_mid_near)
    whole = send_far(relay(send_row(message)))
    parts = send_far(
        place_and_solve(here, table_mid, whole, others, wide_mask_top, inverse_top_near, 2 * n1)
    )

    message, solution_top = relay_solved(
        send_row(root_back(parts, pivots_top, inverse_top_near)), wide_mask_top
    )
    parts = send_far(pick_and_carry(here, blocks_mid, send_far(message), coupling_mid_near))
    message, solution_mid = relay_solved(
        send_row(back(parts, scaled_mid, row_mask_mid, inverse_mid_near)), wide_mask_mid
    )
    parts = send_far(pick_and_carry(here, blocks_low, send_far(message), coupling_low_near))
    residual = (scaled_low - jnp.sum(parts.astype(F32), axis=0)) * row_mask_low

    upper = jnp.concatenate(
        [
            solution_top[0].reshape(width, NEAR, n0),
            solution_mid[0].reshape(width, NEAR, n1),
            solution_mid[1].reshape(width, NEAR, n1),
        ],
        axis=-1,
    )
    upper = xor_order(jnp.swapaxes(jnp.concatenate(halves(upper), axis=-1), 0, 1))
    flat = jnp.swapaxes(residual, 0, 1).reshape(width, -1).astype(BF16)
    size = flat.shape[1]
    message = jnp.concatenate([copies_of(flat, NEAR), upper], axis=-1)
    got = swap_near(message).reshape(rhs, -1)
    upper = got[:, size:].astype(F32)
    upper = upper[:, : upper.shape[1] // 2] + upper[:, upper.shape[1] // 2 :]
    residual = got[:, :size].reshape(rhs, -1, k2)
    partial = jnp.einsum("fij,cfi->fcj", inverse_low, residual, preferred_element_type=F32)
    parts = send_row(copies_of(partial, lax.axis_size("row")))
    solution_low = jnp.sum(parts.astype(F32), axis=0) * col_mask_low
    return (
        upper[:, :n0].T,
        jnp.stack([upper[:, n0 : n0 + n1].T, upper[:, n0 + n1 :].T]),
        jnp.swapaxes(solution_low, 1, 2),
    )


def solution(mesh):
    placed = (
        P("row", "col"),
        P(None, "row", "col"),
        P(None, "row", "col"),
        P(None, "col", "row"),
        P(None, "col", "row"),
        P("col", None),
        P(None, "col", None),
        P(None, "col", None),
        P("row"),
        P(None, "row"),
        P(None, "row"),
        P(),
        P(),
        P(),
        P(),
    )
    return jax.shard_map(
        local,
        mesh=mesh,
        in_specs=placed,
        out_specs=(P("col", None), P(None, "col", None), P(None, "col", None)),
        check_vma=False,
    )
```

time: 309 us -> 312 us (level)
  starting transfers between devices: 66.5 us -> 125 us
  waiting for transfers between devices: 131 us -> 96.4 us
  blocking collectives: 61.3 us -> 42.9 us
  between operations: 14.3 us -> 1.41 us
  matrix products: 12.5 us -> 0.61 us
  local copies, waits for them, and re-layouts: 11.7 us -> 22.8 us
  Pallas kernels: 5.34 us -> 13.1 us
    ppermute x0 -> x12, starting transfers between devices: none -> 39.4 us  [gather_near(): parts.append(lax.ppermute(value, 'col', [(i, i ^ m) for i in range(size)]))]
    all_gather x4 -> x0, waiting for transfers between devices: 38.7 us -> none  [gather_near(): return lax.all_gather(value, 'col', axis_index_groups=near_groups(), axis=0)]
    all_to_all x10 -> x11, starting transfers between devices: 61.6 us -> 81.5 us  [the longest x4 48.5 us: send_row(): return lax.all_to_all(copies, 'row', 0, 0, tiled=True)]
    all_to_all x4 -> x3, blocking collectives: 54 us -> 35.8 us  [the longest x2 20.9 us: send_far(): lax.all_to_all(copies, 'col', 0, 0, axis_index_groups=groups, tiled=True)]
    all_to_all x10 -> x11, waiting for transfers between devices: 85.2 us -> 69 us  [the longest x7 37.6 us: send_far(): lax.all_to_all(copies, 'col', 0, 0, axis_index_groups=groups, tiled=True)]
    all_to_all x1, waiting for transfers between devices: 4.2 us -> 17.8 us  [swap_near(): lax.all_to_all(pieces, 'col', 0, 0, axis_index_groups=near_groups(), tile...]
    unnamed x34 -> x111, local copies, waits for them, and re-layouts: 3.37 us -> 16.1 us
    dot_general x16 -> x0, matrix products: 11.1 us -> none  [the longest x8 9.67 us: update_of(): jnp.einsum('fuk,fck->fcu', coupling[x], solved, preferred_element_type=F32)]
  transfers between devices with their start and end apart: 15 -> 24, of which waited for: 14 -> 12; matrix products, arithmetic and copies ran while one was open for 6% -> 4% of each run, Pallas kernels for 1% -> 2%
where the time goes in v5:
time: 312 us; the launch traced here: 310 us
  starting transfers between devices  125 us (40%)
  waiting for transfers between devices  96.4 us (31%)
  blocking collectives  42.9 us (14%)
  local copies, waits for them, and re-layouts  22.8 us (7%)
  Pallas kernels  13.1 us (4%)
  other arithmetic  7.49 us (2%)
    all_to_all x4, starting transfers between devices, send_row(): return lax.all_to_all(copies, 'row', 0, 0, tiled=True)  48.5 us
    ppermute x12, starting transfers between devices, gather_near(): parts.append(lax.ppermute(value, 'col', [(i, i ^ m) for i in range(size)]))  39.4 us
    all_to_all x7, waiting for transfers between devices, send_far(): lax.all_to_all(copies, 'col', 0, 0, axis_index_groups=groups, tiled=True)  37.6 us
    all_to_all x7, starting transfers between devices, send_far(): lax.all_to_all(copies, 'col', 0, 0, axis_index_groups=groups, tiled=True)  33 us
    all_to_all x4, waiting for transfers between devices, send_row(): return lax.all_to_all(copies, 'row', 0, 0, tiled=True)  31.5 us
    all_to_all x2, blocking collectives, send_far(): lax.all_to_all(copies, 'col', 0, 0, axis_index_groups=groups, tiled=True)  20.9 us
    all_to_all x1, waiting for transfers between devices, swap_near(): lax.all_to_all(pieces, 'col', 0, 0, axis_index_groups=near_groups(), tile...  17.8 us
    unnamed x111, local copies, waits for them, and re-layouts  16.1 us
  transfers between devices with their start and end apart: 24, of which 12 were waited for; matrix products, arithmetic and copies ran while one was open for 4% of the time, Pallas kernels for 2%

profile of v5, /device:TPU:1, one launch (start us, length us, event | category | flops | bytes accessed | tf_op | source)
XLA Modules:
  0.0 309.6 jit_solution(16094513509667614982)
XLA Ops:
  0.7 0.8 slice_bitcast_fusion.4
  3.5 3.9 %collective-permute-start = (bf16[4,128,512]{2,1,0:T(8,128)(2,1)S(1)}, bf16[4,128,512]{2,1,0:T(8,128)(2,1)S(1)}, u32[]{:S(2)}, u32[]{:S(2)}) collective-permute-start(bf16[4,128,512]{2,1,0:T(8,128)(2,1)S(1)} %copy-done.4), channel_id=1, source_target_pairs={{0,1},{1,0},{2,3},{3,2},{4,5},{5,4},{6,7},{7,6},{8,9},{9,8},{10,11... | collective-permute-start | bytes 1572872 | tf_op jit(solution)/shard_map/ppermute | solution.py:40
  7.4 4.4 %collective-permute-start.1 = (bf16[4,128,512]{2,1,0:T(8,128)(2,1)S(1)}, bf16[4,128,512]{2,1,0:T(8,128)(2,1)S(1)}, u32[]{:S(2)}, u32[]{:S(2)}) collective-permute-start(bf16[4,128,512]{2,1,0:T(8,128)(2,1)S(1)} %copy-done.4), channel_id=1, source_target_pairs={{0,2},{1,3},{2,0},{3,1},{4,6},{5,7},{6,4},{7,5},{8,10},{9,11},{10,... | collective-permute-start | bytes 1572872 | tf_op jit(solution)/shard_map/ppermute | solution.py:40
  11.8 1.9 collective-permute-start.2
  13.7 0.7 reshape.294
  14.4 3.9 %all-to-all-start = ((bf16[4,4,3840]{2,1,0:T(4,128)(2,1)}), bf16[4,4,3840]{2,1,0:T(4,128)(2,1)S(1)}, u32[]{:S(2)}, u32[]{:S(2)}) async-start(bf16[4,4,3840]{2,1,0:T(4,128)(2,1)} %reshape.294), calls=%async_computation | async-start | bytes 245760 | tf_op jit(solution)/shard_map/all_to_all | solution.py:29
  19.6 17.8 %all-to-all-done = bf16[4,4,3840]{2,1,0:T(4,128)(2,1)S(1)} async-done(((bf16[4,4,3840]{2,1,0:T(4,128)(2,1)}), bf16[4,4,3840]{2,1,0:T(4,128)(2,1)S(1)}, u32[]{:S(2)}, u32[]{:S(2)}) %all-to-all-start) | async-done | bytes 122912 | tf_op jit(solution)/shard_map/all_to_all | solution.py:29
  37.4 0.7 copy-done.39
  38.1 0.7 broadcast_in_dim.14
  38.8 12.3 %all-to-all-start.1 = ((bf16[8,4,4,512]{3,2,1,0:T(4,128)(2,1)}), bf16[8,4,4,512]{3,2,1,0:T(4,128)(2,1)S(1)}, u32[]{:S(2)}, u32[]{:S(2)}) async-start(bf16[8,4,4,512]{3,2,1,0:T(4,128)(2,1)} %broadcast_in_dim.14), calls=%async_computation.1 | async-start | bytes 262144 | tf_op jit(solution)/shard_map/all_to_all | solution.py:63
  52.5 6.6 %all-to-all-done.1.parts = bf16[8,4,4,512]{3,2,1,0:T(4,128)(2,1)S(1)} async-done(((bf16[8,4,4,512]{3,2,1,0:T(4,128)(2,1)}), bf16[8,4,4,512]{3,2,1,0:T(4,128)(2,1)S(1)}, u32[]{:S(2)}, u32[]{:S(2)}) %all-to-all-start.1) | async-done | bytes 131104 | tf_op jit(solution)/shard_map/all_to_all | solution.py:63
  60.1 0.8 copy-done.10
  60.9 0.7 copy-done.24
  62.2 10.7 %all-to-all-start.2 = ((bf16[16,4,4,512]{3,2,1,0:T(4,128)(2,1)}), bf16[16,4,4,512]{3,2,1,0:T(4,128)(2,1)}, u32[]{:S(2)}, u32[]{:S(2)}) async-start(bf16[16,4,4,512]{3,2,1,0:T(4,128)(2,1)} %copy-done.24), calls=%async_computation.2 | async-start | bytes 524288 | tf_op jit(solution)/shard_map/all_to_all | solution.py:67
  73.1 1.9 collective-permute-start.3
  75.1 3.3 %collective-permute-start.4 = (bf16[2,512,256]{2,1,0:T(8,128)(2,1)S(1)}, bf16[2,512,256]{2,1,0:T(8,128)(2,1)S(1)}, u32[]{:S(2)}, u32[]{:S(2)}) collective-permute-start(bf16[2,512,256]{2,1,0:T(8,128)(2,1)S(1)} %copy-done.2), channel_id=1, source_target_pairs={{0,2},{1,3},{2,0},{3,1},{4,6},{5,7},{6,4},{7,5},{8,10},{9,11},{10,... | collective-permute-start | bytes 1572872 | tf_op jit(solution)/shard_map/ppermute | solution.py:40
  78.4 4.4 %collective-permute-start.5 = (bf16[2,512,256]{2,1,0:T(8,128)(2,1)S(1)}, bf16[2,512,256]{2,1,0:T(8,128)(2,1)}, u32[]{:S(2)}, u32[]{:S(2)}) collective-permute-start(bf16[2,512,256]{2,1,0:T(8,128)(2,1)S(1)} %copy-done.2), channel_id=1, source_target_pairs={{0,3},{1,2},{2,1},{3,0},{4,7},{5,6},{6,5},{7,4},{8,11},{9,10},{10,... | collective-permute-start | bytes 1572872 | tf_op jit(solution)/shard_map/ppermute | solution.py:40
  82.8 1.9 collective-permute-start.6
  84.8 1.6 shard_map.167
  86.4 3.4 %all-to-all-start.3 = ((bf16[8,4,4,512]{3,2,1,0:T(4,128)(2,1)}), bf16[8,4,4,512]{3,2,1,0:T(4,128)(2,1)S(1)}, u32[]{:S(2)}, u32[]{:S(2)}) async-start(bf16[8,4,4,512]{3,2,1,0:T(4,128)(2,1)} %shard_map.167), calls=%async_computation.3 | async-start | bytes 262144 | tf_op jit(solution)/shard_map/all_to_all | solution.py:63
  89.9 3.3 %collective-permute-start.7 = (bf16[2,128,512]{2,1,0:T(8,128)(2,1)}, bf16[2,128,512]{2,1,0:T(8,128)(2,1)}, u32[]{:S(2)}, u32[]{:S(2)}) collective-permute-start(bf16[2,128,512]{2,1,0:T(8,128)(2,1)} %c0.2), channel_id=1, source_target_pairs={{0,2},{1,3},{2,0},{3,1},{4,6},{5,7},{6,4},{7,5},{8,10},{9,11},{10,... | collective-permute-start | bytes 786440 | tf_op jit(solution)/shard_map/ppermute | solution.py:40
  93.2 0.8 copy-done.12
  93.9 4.4 %collective-permute-start.8 = (bf16[2,128,512]{2,1,0:T(8,128)(2,1)}, bf16[2,128,512]{2,1,0:T(8,128)(2,1)}, u32[]{:S(2)}, u32[]{:S(2)}) collective-permute-start(bf16[2,128,512]{2,1,0:T(8,128)(2,1)} %c0.2), channel_id=1, source_target_pairs={{0,3},{1,2},{2,1},{3,0},{4,7},{5,6},{6,5},{7,4},{8,11},{9,10},{10,... | collective-permute-start | bytes 786440 | tf_op jit(solution)/shard_map/ppermute | solution.py:40
  98.3 0.9 slice_add_fusion.1.source
  99.6 0.8 copy-done.15
  100.4 3.7 %collective-permute-start.10 = (bf16[1,768,384]{2,1,0:T(8,128)(2,1)S(1)}, bf16[1,768,384]{2,1,0:T(8,128)(2,1)S(1)}, u32[]{:S(2)}, u32[]{:S(2)}) collective-permute-start(bf16[1,768,384]{2,1,0:T(8,128)(2,1)S(1)} %bitcast.47), channel_id=1, source_target_pairs={{0,2},{1,3},{2,0},{3,1},{4,6},{5,7},{6,4},{7,5},{8,10},{9,11},{10,... | collective-permute-start | bytes 1769480 | tf_op jit(solution)/shard_map/ppermute | solution.py:40
  104.1 1.8 collective-permute-done.5.i3
  105.9 4.4 %collective-permute-start.11 = (bf16[1,768,384]{2,1,0:T(8,128)(2,1)S(1)}, bf16[1,768,384]{2,1,0:T(8,128)(2,1)S(1)}, u32[]{:S(2)}, u32[]{:S(2)}) collective-permute-start(bf16[1,768,384]{2,1,0:T(8,128)(2,1)S(1)} %bitcast.48), channel_id=1, source_target_pairs={{0,3},{1,2},{2,1},{3,0},{4,7},{5,6},{6,5},{7,4},{8,11},{9,10},{10,... | collective-permute-start | bytes 1769480 | tf_op jit(solution)/shard_map/ppermute | solution.py:40
  110.3 1.0 copy-done.13
  111.3 1.0 copy-done.16
  112.4 1.7 shard_map.168
  115.9 3.5 %all-to-all-start.4 = ((bf16[8,2,4,512]{3,2,1,0:T(4,128)(2,1)}), bf16[8,2,4,512]{3,2,1,0:T(4,128)(2,1)S(1)}, u32[]{:S(2)}, u32[]{:S(2)}) async-start(bf16[8,2,4,512]{3,2,1,0:T(4,128)(2,1)} %copy-done.22), calls=%async_computation.4 | async-start | bytes 131072 | tf_op jit(solution)/shard_map/all_to_all | solution.py:63
  119.4 1.9 collective-permute-start.9
  122.0 7.4 %collective-permute-done.8.c3 = bf16[2,128,512]{2,1,0:T(8,128)(2,1)} collective-permute-done((bf16[2,128,512]{2,1,0:T(8,128)(2,1)}, bf16[2,128,512]{2,1,0:T(8,128)(2,1)}, u32[]{:S(2)}, u32[]{:S(2)}) %collective-permute-start.8) | collective-permute-done | bytes 262176 | tf_op jit(solution)/shard_map/ppermute | solution.py:40
  129.5 0.9 copy-done.18
  130.4 1.5 shard_map.169
  133.2 26.5 %all-to-all-start.5 = ((bf16[16,2,4,512]{3,2,1,0:T(4,128)(2,1)}), bf16[16,2,4,512]{3,2,1,0:T(4,128)(2,1)S(1)}, u32[]{:S(2)}, u32[]{:S(2)}) async-start(bf16[16,2,4,512]{3,2,1,0:T(4,128)(2,1)} %copy-done.26), calls=%async_computation.5 | async-start | bytes 262144 | tf_op jit(solution)/shard_map/all_to_all | solution.py:67
  159.7 1.6 fusion.5
  161.3 1.3 copy.28
  163.2 0.7 fusion.6
  163.8 0.7 reshape.297.mask
  164.5 4.3 %all-to-all-done.5.parts = bf16[16,2,4,512]{3,2,1,0:T(4,128)(2,1)S(1)} async-done(((bf16[16,2,4,512]{3,2,1,0:T(4,128)(2,1)}), bf16[16,2,4,512]{3,2,1,0:T(4,128)(2,1)S(1)}, u32[]{:S(2)}, u32[]{:S(2)}) %all-to-all-start.5) | async-done | bytes 131104 | tf_op jit(solution)/shard_map/all_to_all | solution.py:67
  169.5 3.5 %all-to-all-start.6 = ((bf16[8,2,4,512]{3,2,1,0:T(4,128)(2,1)}), bf16[8,2,4,512]{3,2,1,0:T(4,128)(2,1)S(1)}, u32[]{:S(2)}, u32[]{:S(2)}) async-start(bf16[8,2,4,512]{3,2,1,0:T(4,128)(2,1)} %copy-done.23), calls=%async_computation.6 | async-start | bytes 131072 | tf_op jit(solution)/shard_map/all_to_all | solution.py:63
  173.7 7.1 %all-to-all-done.6.whole = bf16[8,2,4,512]{3,2,1,0:T(4,128)(2,1)S(1)} async-done(((bf16[8,2,4,512]{3,2,1,0:T(4,128)(2,1)}), bf16[8,2,4,512]{3,2,1,0:T(4,128)(2,1)S(1)}, u32[]{:S(2)}, u32[]{:S(2)}) %all-to-all-start.6) | async-done | bytes 65568 | tf_op jit(solution)/shard_map/all_to_all | solution.py:63
  180.7 1.3 shard_map.171
  182.7 3.5 %all-to-all-start.7 = ((bf16[8,1,4,768]{3,2,1,0:T(4,128)(2,1)}), bf16[8,1,4,768]{3,2,1,0:T(4,128)(2,1)S(1)}, u32[]{:S(2)}, u32[]{:S(2)}) async-start(bf16[8,1,4,768]{3,2,1,0:T(4,128)(2,1)} %copy-done.25), calls=%async_computation.7 | async-start | bytes 98304 | tf_op jit(solution)/shard_map/all_to_all | solution.py:63
  186.2 7.0 %all-to-all-done.7.parts = bf16[8,1,4,768]{3,2,1,0:T(4,128)(2,1)S(1)} async-done(((bf16[8,1,4,768]{3,2,1,0:T(4,128)(2,1)}), bf16[8,1,4,768]{3,2,1,0:T(4,128)(2,1)S(1)}, u32[]{:S(2)}, u32[]{:S(2)}) %all-to-all-start.7) | async-done | bytes 49184 | tf_op jit(solution)/shard_map/all_to_all | solution.py:63
  193.6 14.8 %all_to_all.80.parts = bf16[16,1,4,1536]{3,2,1,0:T(4,128)(2,1)S(1)} all-to-all(bf16[16,1,4,1536]{3,2,1,0:T(4,128)(2,1)S(1)} %shard_map.172), channel_id=1, replica_groups=mesh['row'=16,'col'=32] {'row'}, dimensions={0} | all-to-all | bytes 393216 | tf_op jit(solution)/shard_map/all_to_all | solution.py:67
  208.5 11.4 %all_to_all.81.whole = bf16[8,1,4,1536]{3,2,1,0:T(4,128)(2,1)S(1)} all-to-all(bf16[8,1,4,1536]{3,2,1,0:T(4,128)(2,1)S(1)} %get-tuple-element.30), channel_id=1, replica_groups={{0,4,8,12,16,20,24,28},{1,5,9,13,17,21,25,29},{2,6,10,14,18,22,26,30},{..., dimensions={0} | all-to-all | bytes 196608 | tf_op jit(solution)/shard_map/all_to_all | solution.py:63
  219.9 1.5 shard_map.174
  221.4 9.5 %all_to_all.82.parts = bf16[8,2,4,512]{3,2,1,0:T(4,128)(2,1)S(1)} all-to-all(bf16[8,2,4,512]{3,2,1,0:T(4,128)(2,1)S(1)} %shard_map.174), channel_id=1, replica_groups={{0,4,8,12,16,20,24,28},{1,5,9,13,17,21,25,29},{2,6,10,14,18,22,26,30},{..., dimensions={0} | all-to-all | bytes 131072 | tf_op jit(solution)/shard_map/all_to_all | solution.py:63
  230.9 2.1 shard_map.175
  233.1 5.1 %all-to-all-start.11 = ((bf16[16,2,4,1024]{3,2,1,0:T(4,128)(2,1)}), bf16[16,2,4,1024]{3,2,1,0:T(4,128)(2,1)S(1)}, u32[]{:S(2)}, u32[]{:S(2)}) async-start(bf16[16,2,4,1024]{3,2,1,0:T(4,128)(2,1)} %shard_map.175), calls=%async_computation.11 | async-start | bytes 524288 | tf_op jit(solution)/shard_map/all_to_all | solution.py:67
  238.9 11.1 %all-to-all-done.11.parts = bf16[16,2,4,1024]{3,2,1,0:T(4,128)(2,1)S(1)} async-done(((bf16[16,2,4,1024]{3,2,1,0:T(4,128)(2,1)}), bf16[16,2,4,1024]{3,2,1,0:T(4,128)(2,1)S(1)}, u32[]{:S(2)}, u32[]{:S(2)}) %all-to-all-start.11) | async-done | bytes 262176 | tf_op jit(solution)/shard_map/all_to_all | solution.py:67
  250.0 0.7 shard_map.176
  250.7 3.5 %all-to-all-start.12 = ((bf16[8,2,4,1024]{3,2,1,0:T(4,128)(2,1)}), bf16[8,2,4,1024]{3,2,1,0:T(4,128)(2,1)S(1)}, u32[]{:S(2)}, u32[]{:S(2)}) async-start(bf16[8,2,4,1024]{3,2,1,0:T(4,128)(2,1)} %get-tuple-element.32), calls=%async_computation.12 | async-start | bytes 262144 | tf_op jit(solution)/shard_map/all_to_all | solution.py:63
  254.7 8.8 %all-to-all-done.12.whole = bf16[8,2,4,1024]{3,2,1,0:T(4,128)(2,1)S(1)} async-done(((bf16[8,2,4,1024]{3,2,1,0:T(4,128)(2,1)}), bf16[8,2,4,1024]{3,2,1,0:T(4,128)(2,1)S(1)}, u32[]{:S(2)}, u32[]{:S(2)}) %all-to-all-start.12) | async-done | bytes 131104 | tf_op jit(solution)/shard_map/all_to_all | solution.py:63
  263.6 1.6 shard_map.177
  265.2 3.4 %all-to-all-start.13 = ((bf16[8,4,4,512]{3,2,1,0:T(4,128)(2,1)}), bf16[8,4,4,512]{3,2,1,0:T(4,128)(2,1)S(1)}, u32[]{:S(2)}, u32[]{:S(2)}) async-start(bf16[8,4,4,512]{3,2,1,0:T(4,128)(2,1)} %shard_map.177), calls=%async_computation.13 | async-start | bytes 262144 | tf_op jit(solution)/shard_map/all_to_all | solution.py:63
  268.7 8.1 %all-to-all-done.13 = bf16[8,4,4,512]{3,2,1,0:T(4,128)(2,1)S(1)} async-done(((bf16[8,4,4,512]{3,2,1,0:T(4,128)(2,1)}), bf16[8,4,4,512]{3,2,1,0:T(4,128)(2,1)S(1)}, u32[]{:S(2)}, u32[]{:S(2)}) %all-to-all-start.13) | async-done | bytes 131104 | tf_op jit(solution)/shard_map/all_to_all | solution.py:63
  277.0 7.2 %all_to_all.83 = bf16[4,4,3840]{2,1,0:T(4,128)(2,1)S(1)} all-to-all(bf16[4,4,3840]{2,1,0:T(4,128)(2,1)S(1)} %pad_maximum_fusion.1), channel_id=1, replica_groups={{0,1,2,3},{4,5,6,7},{8,9,10,11},{12,13,14,15},{16,17,18,19},{20,21,22,2..., dimensions={0} | all-to-all | bytes 245760 | tf_op jit(solution)/shard_map/all_to_all | solution.py:29
  284.5 0.9 broadcast_in_dim.20
  285.3 6.2 %all-to-all-start.15 = ((bf16[16,4,16,256]{3,2,1,0:T(8,128)(2,1)}), bf16[16,4,16,256]{3,2,1,0:T(8,128)(2,1)S(1)}, u32[]{:S(2)}, u32[]{:S(2)}) async-start(bf16[16,4,16,256]{3,2,1,0:T(8,128)(2,1)} %broadcast_in_dim.20), calls=%async_computation.15 | async-start | bytes 1048576 | tf_op jit(solution)/shard_map/all_to_all | solution.py:67
  292.8 16.1 %all-to-all-done.15 = bf16[16,4,16,256]{3,2,1,0:T(8,128)(2,1)S(1)} async-done(((bf16[16,4,16,256]{3,2,1,0:T(8,128)(2,1)}), bf16[16,4,16,256]{3,2,1,0:T(8,128)(2,1)S(1)}, u32[]{:S(2)}, u32[]{:S(2)}) %all-to-all-start.15) | async-done | bytes 524320 | tf_op jit(solution)/shard_map/all_to_all | solution.py:67
  (175 shorter events, 17.6 us)
Async XLA Ops:
  0.6 1.6 copy-start
  0.6 0.8 copy-start.40
  1.5 0.9 copy-start.41
  2.4 1.0 copy-start.4
  3.5 55.6 %collective-permute-start = (bf16[4,128,512]{2,1,0:T(8,128)(2,1)S(1)}, bf16[4,128,512]{2,1,0:T(8,128)(2,1)S(1)}, u32[]{:S(2)}, u32[]{:S(2)}) collective-permute-start(bf16[4,128,512]{2,1,0:T(8,128)(2,1)S(1)} %copy-done.4), channel_id=1, source_target_pairs={{0,1},{1,0},{2,3},{3,2},{4,5},{5,4},{6,7},{7,6},{8,9},{9,8},{10,11... | collective-permute-start | bytes 1572872 | tf_op jit(solution)/shard_map/ppermute | solution.py:40
  7.4 51.7 %collective-permute-start.1 = (bf16[4,128,512]{2,1,0:T(8,128)(2,1)S(1)}, bf16[4,128,512]{2,1,0:T(8,128)(2,1)S(1)}, u32[]{:S(2)}, u32[]{:S(2)}) collective-permute-start(bf16[4,128,512]{2,1,0:T(8,128)(2,1)S(1)} %copy-done.4), channel_id=1, source_target_pairs={{0,2},{1,3},{2,0},{3,1},{4,6},{5,7},{6,4},{7,5},{8,10},{9,11},{10,... | collective-permute-start | bytes 1572872 | tf_op jit(solution)/shard_map/ppermute | solution.py:40
  11.8 47.3 %collective-permute-start.2 = (bf16[4,128,512]{2,1,0:T(8,128)(2,1)S(1)}, bf16[4,128,512]{2,1,0:T(8,128)(2,1)S(1)}, u32[]{:S(2)}, u32[]{:S(2)}) collective-permute-start(bf16[4,128,512]{2,1,0:T(8,128)(2,1)S(1)} %copy-done.4), channel_id=1, source_target_pairs={{0,3},{1,2},{2,1},{3,0},{4,7},{5,6},{6,5},{7,4},{8,11},{9,10},{10,... | collective-permute-start | bytes 1572872 | tf_op jit(solution)/shard_map/ppermute | solution.py:40
  14.4 23.0 %all-to-all-start = ((bf16[4,4,3840]{2,1,0:T(4,128)(2,1)}), bf16[4,4,3840]{2,1,0:T(4,128)(2,1)S(1)}, u32[]{:S(2)}, u32[]{:S(2)}) async-start(bf16[4,4,3840]{2,1,0:T(4,128)(2,1)} %reshape.294), calls=%async_computation | async-start | bytes 245760 | tf_op jit(solution)/shard_map/all_to_all | solution.py:29
  19.4 55.6 %copy-start.44 = (s32[512]{0:T(512)}, s32[512]{0:T(512)S(1)}, u32[]{:S(2)}) copy-start(s32[512]{0:T(512)S(1)} %iota_add_fusion.2) | copy-start | bytes 6148
  37.4 0.7 copy-start.39
  38.8 20.3 %all-to-all-start.1 = ((bf16[8,4,4,512]{3,2,1,0:T(4,128)(2,1)}), bf16[8,4,4,512]{3,2,1,0:T(4,128)(2,1)S(1)}, u32[]{:S(2)}, u32[]{:S(2)}) async-start(bf16[8,4,4,512]{3,2,1,0:T(4,128)(2,1)} %broadcast_in_dim.14), calls=%async_computation.1 | async-start | bytes 262144 | tf_op jit(solution)/shard_map/all_to_all | solution.py:63
  51.1 0.7 copy-start.46
  59.1 0.8 copy-start.6
  59.1 1.0 copy-start.8
  59.1 13.8 %copy-start.35 = (s32[4,32]{1,0:T(4,128)S(1)}, s32[4,32]{1,0:T(4,128)}, u32[]{:S(2)}) copy-start(s32[4,32]{1,0:T(4,128)} %blocks.3) | copy-start | bytes 1540
  60.1 0.8 copy-start.10
  60.9 0.7 copy-start.24
  62.2 11.0 %copy-start.2 = (bf16[2,512,256]{2,1,0:T(8,128)(2,1)S(1)}, bf16[2,512,256]{2,1,0:T(8,128)(2,1)}, u32[]{:S(2)}) copy-start(bf16[2,512,256]{2,1,0:T(8,128)(2,1)} %i0.1) | copy-start | bytes 1572868
  62.2 38.2 %copy-start.1 = (bf16[768,384]{1,0:T(8,128)(2,1)S(1)}, bf16[768,384]{1,0:T(8,128)(2,1)}, u32[]{:S(2)}) copy-start(bf16[768,384]{1,0:T(8,128)(2,1)} %param.15) | copy-start | bytes 1769476
  62.2 22.6 %all-to-all-start.2 = ((bf16[16,4,4,512]{3,2,1,0:T(4,128)(2,1)}), bf16[16,4,4,512]{3,2,1,0:T(4,128)(2,1)}, u32[]{:S(2)}, u32[]{:S(2)}) async-start(bf16[16,4,4,512]{3,2,1,0:T(4,128)(2,1)} %copy-done.24), calls=%async_computation.2 | async-start | bytes 524288 | tf_op jit(solution)/shard_map/all_to_all | solution.py:67
  73.1 20.0 %collective-permute-start.3 = (bf16[2,512,256]{2,1,0:T(8,128)(2,1)S(1)}, bf16[2,512,256]{2,1,0:T(8,128)(2,1)S(1)}, u32[]{:S(2)}, u32[]{:S(2)}) collective-permute-start(bf16[2,512,256]{2,1,0:T(8,128)(2,1)S(1)} %copy-done.2), channel_id=1, source_target_pairs={{0,1},{1,0},{2,3},{3,2},{4,5},{5,4},{6,7},{7,6},{8,9},{9,8},{10,11... | collective-permute-start | bytes 1572872 | tf_op jit(solution)/shard_map/ppermute | solution.py:40
  75.1 54.3 %copy-start.27 = (f32[2,1,512]{2,1,0:T(1,128)}, f32[2,1,512]{2,1,0:T(1,128)S(1)}, u32[]{:S(2)}) copy-start(f32[2,1,512]{2,1,0:T(1,128)S(1)} %compare_convert_fusion.2.mask) | copy-start | bytes 12292
  75.1 24.5 %collective-permute-start.4 = (bf16[2,512,256]{2,1,0:T(8,128)(2,1)S(1)}, bf16[2,512,256]{2,1,0:T(8,128)(2,1)S(1)}, u32[]{:S(2)}, u32[]{:S(2)}) collective-permute-start(bf16[2,512,256]{2,1,0:T(8,128)(2,1)S(1)} %copy-done.2), channel_id=1, source_target_pairs={{0,2},{1,3},{2,0},{3,1},{4,6},{5,7},{6,4},{7,5},{8,10},{9,11},{10,... | collective-permute-start | bytes 1572872 | tf_op jit(solution)/shard_map/ppermute | solution.py:40
  78.4 27.5 %collective-permute-start.5 = (bf16[2,512,256]{2,1,0:T(8,128)(2,1)S(1)}, bf16[2,512,256]{2,1,0:T(8,128)(2,1)}, u32[]{:S(2)}, u32[]{:S(2)}) collective-permute-start(bf16[2,512,256]{2,1,0:T(8,128)(2,1)S(1)} %copy-done.2), channel_id=1, source_target_pairs={{0,3},{1,2},{2,1},{3,0},{4,7},{5,6},{6,5},{7,4},{8,11},{9,10},{10,... | collective-permute-start | bytes 1572872 | tf_op jit(solution)/shard_map/ppermute | solution.py:40
  82.8 36.6 %collective-permute-start.6 = (bf16[2,128,512]{2,1,0:T(8,128)(2,1)}, bf16[2,128,512]{2,1,0:T(8,128)(2,1)}, u32[]{:S(2)}, u32[]{:S(2)}) collective-permute-start(bf16[2,128,512]{2,1,0:T(8,128)(2,1)} %c0.2), channel_id=1, source_target_pairs={{0,1},{1,0},{2,3},{3,2},{4,5},{5,4},{6,7},{7,6},{8,9},{9,8},{10,11... | collective-permute-start | bytes 786440 | tf_op jit(solution)/shard_map/ppermute | solution.py:40
  86.4 23.9 %all-to-all-start.3 = ((bf16[8,4,4,512]{3,2,1,0:T(4,128)(2,1)}), bf16[8,4,4,512]{3,2,1,0:T(4,128)(2,1)S(1)}, u32[]{:S(2)}, u32[]{:S(2)}) async-start(bf16[8,4,4,512]{3,2,1,0:T(4,128)(2,1)} %shard_map.167), calls=%async_computation.3 | async-start | bytes 262144 | tf_op jit(solution)/shard_map/all_to_all | solution.py:63
  89.9 32.2 %collective-permute-start.7 = (bf16[2,128,512]{2,1,0:T(8,128)(2,1)}, bf16[2,128,512]{2,1,0:T(8,128)(2,1)}, u32[]{:S(2)}, u32[]{:S(2)}) collective-permute-start(bf16[2,128,512]{2,1,0:T(8,128)(2,1)} %c0.2), channel_id=1, source_target_pairs={{0,2},{1,3},{2,0},{3,1},{4,6},{5,7},{6,4},{7,5},{8,10},{9,11},{10,... | collective-permute-start | bytes 786440 | tf_op jit(solution)/shard_map/ppermute | solution.py:40
  93.2 0.8 copy-start.12
  93.9 35.5 %collective-permute-start.8 = (bf16[2,128,512]{2,1,0:T(8,128)(2,1)}, bf16[2,128,512]{2,1,0:T(8,128)(2,1)}, u32[]{:S(2)}, u32[]{:S(2)}) collective-permute-start(bf16[2,128,512]{2,1,0:T(8,128)(2,1)} %c0.2), channel_id=1, source_target_pairs={{0,3},{1,2},{2,1},{3,0},{4,7},{5,6},{6,5},{7,4},{8,11},{9,10},{10,... | collective-permute-start | bytes 786440 | tf_op jit(solution)/shard_map/ppermute | solution.py:40
  99.6 0.8 copy-start.15
  100.4 73.3 %collective-permute-start.10 = (bf16[1,768,384]{2,1,0:T(8,128)(2,1)S(1)}, bf16[1,768,384]{2,1,0:T(8,128)(2,1)S(1)}, u32[]{:S(2)}, u32[]{:S(2)}) collective-permute-start(bf16[1,768,384]{2,1,0:T(8,128)(2,1)S(1)} %bitcast.47), channel_id=1, source_target_pairs={{0,2},{1,3},{2,0},{3,1},{4,6},{5,7},{6,4},{7,5},{8,10},{9,11},{10,... | collective-permute-start | bytes 1769480 | tf_op jit(solution)/shard_map/ppermute | solution.py:40
  105.9 67.8 %collective-permute-start.11 = (bf16[1,768,384]{2,1,0:T(8,128)(2,1)S(1)}, bf16[1,768,384]{2,1,0:T(8,128)(2,1)S(1)}, u32[]{:S(2)}, u32[]{:S(2)}) collective-permute-start(bf16[1,768,384]{2,1,0:T(8,128)(2,1)S(1)} %bitcast.48), channel_id=1, source_target_pairs={{0,3},{1,2},{2,1},{3,0},{4,7},{5,6},{6,5},{7,4},{8,11},{9,10},{10,... | collective-permute-start | bytes 1769480 | tf_op jit(solution)/shard_map/ppermute | solution.py:40
  110.3 1.0 copy-start.13
  111.3 1.0 copy-start.16
  115.9 5.4 %copy-start.51 = (s32[4]{0:T(128)S(1)}, s32[4]{0:T(128)}, u32[]{:S(2)}) copy-start(s32[4]{0:T(128)} %get-tuple-element.53) | copy-start | bytes 52
  115.9 13.6 %all-to-all-start.4 = ((bf16[8,2,4,512]{3,2,1,0:T(4,128)(2,1)}), bf16[8,2,4,512]{3,2,1,0:T(4,128)(2,1)S(1)}, u32[]{:S(2)}, u32[]{:S(2)}) async-start(bf16[8,2,4,512]{3,2,1,0:T(4,128)(2,1)} %copy-done.22), calls=%async_computation.4 | async-start | bytes 131072 | tf_op jit(solution)/shard_map/all_to_all | solution.py:63
  119.4 2.0 copy-start.50
  119.4 54.2 %collective-permute-start.9 = (bf16[1,768,384]{2,1,0:T(8,128)(2,1)S(1)}, bf16[1,768,384]{2,1,0:T(8,128)(2,1)S(1)}, u32[]{:S(2)}, u32[]{:S(2)}) collective-permute-start(bf16[1,768,384]{2,1,0:T(8,128)(2,1)S(1)} %bitcast.49), channel_id=1, source_target_pairs={{0,1},{1,0},{2,3},{3,2},{4,5},{5,4},{6,7},{7,6},{8,9},{9,8},{10,11... | collective-permute-start | bytes 1769480 | tf_op jit(solution)/shard_map/ppermute | solution.py:40
  129.5 1.0 copy-start.18
  133.2 26.5 %copy-start.37 = (s32[2,32]{1,0:T(2,128)S(1)}, s32[2,32]{1,0:T(2,128)}, u32[]{:S(2)}) copy-start(s32[2,32]{1,0:T(2,128)} %blocks.2) | copy-start | bytes 772
  133.2 35.7 %all-to-all-start.5 = ((bf16[16,2,4,512]{3,2,1,0:T(4,128)(2,1)}), bf16[16,2,4,512]{3,2,1,0:T(4,128)(2,1)S(1)}, u32[]{:S(2)}, u32[]{:S(2)}) async-start(bf16[16,2,4,512]{3,2,1,0:T(4,128)(2,1)} %copy-done.26), calls=%async_computation.5 | async-start | bytes 262144 | tf_op jit(solution)/shard_map/all_to_all | solution.py:67
  169.5 11.2 %copy-start.21 = (f32[4,4,896]{2,1,0:T(4,128)S(1)}, f32[4,4,896]{2,1,0:T(4,128)}, u32[]{:S(2)}) copy-start(f32[4,4,896]{2,1,0:T(4,128)} %copy-done.20) | copy-start | bytes 172036
  169.5 11.2 %all-to-all-start.6 = ((bf16[8,2,4,512]{3,2,1,0:T(4,128)(2,1)}), bf16[8,2,4,512]{3,2,1,0:T(4,128)(2,1)S(1)}, u32[]{:S(2)}, u32[]{:S(2)}) async-start(bf16[8,2,4,512]{3,2,1,0:T(4,128)(2,1)} %copy-done.23), calls=%async_computation.6 | async-start | bytes 131072 | tf_op jit(solution)/shard_map/all_to_all | solution.py:63
  173.0 7.7 %copy-start.34 = (s32[2]{0:T(128)S(1)}, s32[2]{0:T(128)}, u32[]{:S(2)}) copy-start(s32[2]{0:T(128)} %copy-done.33) | copy-start | bytes 28
  182.7 3.5 %copy-start.49 = (f32[768]{0:T(1024)S(1)}, f32[768]{0:T(1024)}, u32[]{:S(2)}) copy-start(f32[768]{0:T(1024)} %param.23) | copy-start | bytes 9220
  182.7 10.5 %all-to-all-start.7 = ((bf16[8,1,4,768]{3,2,1,0:T(4,128)(2,1)}), bf16[8,1,4,768]{3,2,1,0:T(4,128)(2,1)S(1)}, u32[]{:S(2)}, u32[]{:S(2)}) async-start(bf16[8,1,4,768]{3,2,1,0:T(4,128)(2,1)} %copy-done.25), calls=%async_computation.7 | async-start | bytes 98304 | tf_op jit(solution)/shard_map/all_to_all | solution.py:63
  193.5 26.3 %copy-start.19 = (bf16[2,128,512]{2,1,0:T(8,128)(2,1)S(1)}, bf16[2,128,512]{2,1,0:T(8,128)(2,1)}, u32[]{:S(2)}) copy-start(bf16[2,128,512]{2,1,0:T(8,128)(2,1)} %c0.2) | copy-start | bytes 786436
  193.6 26.3 %copy-start.38 = (s32[2,32]{1,0:T(2,128)S(1)}, s32[2,32]{1,0:T(2,128)}, u32[]{:S(2)}) copy-start(s32[2,32]{1,0:T(2,128)} %blocks.2) | copy-start | bytes 772
  208.4 22.5 %copy-start.17 = (bf16[2,512,256]{2,1,0:T(8,128)(2,1)S(1)}, bf16[2,512,256]{2,1,0:T(8,128)(2,1)}, u32[]{:S(2)}) copy-start(bf16[2,512,256]{2,1,0:T(8,128)(2,1)} %copy-done.15) | copy-start | bytes 1572868
  219.9 11.0 %copy-start.3 = (bf16[2,512,256]{2,1,0:T(8,128)(2,1)S(1)}, bf16[2,512,256]{2,1,0:T(8,128)(2,1)}, u32[]{:S(2)}) copy-start(bf16[2,512,256]{2,1,0:T(8,128)(2,1)} %i0.1) | copy-start | bytes 1572868
  219.9 11.0 %copy-start.14 = (bf16[2,512,256]{2,1,0:T(8,128)(2,1)S(1)}, bf16[2,512,256]{2,1,0:T(8,128)(2,1)}, u32[]{:S(2)}) copy-start(bf16[2,512,256]{2,1,0:T(8,128)(2,1)} %copy-done.12) | copy-start | bytes 1572868
  221.4 9.6 %copy-start.28 = (f32[2,1,512]{2,1,0:T(1,128)S(1)}, f32[2,1,512]{2,1,0:T(1,128)}, u32[]{:S(2)}) copy-start(f32[2,1,512]{2,1,0:T(1,128)} %copy-done.27) | copy-start | bytes 12292
  221.4 9.6 %copy-start.32 = (f32[2,4,512]{2,1,0:T(4,128)S(1)}, f32[2,4,512]{2,1,0:T(4,128)}, u32[]{:S(2)}) copy-start(f32[2,4,512]{2,1,0:T(4,128)} %copy-done.31) | copy-start | bytes 49156
  233.0 30.5 %copy-start.11 = (bf16[4,128,512]{2,1,0:T(8,128)(2,1)S(1)}, bf16[4,128,512]{2,1,0:T(8,128)(2,1)}, u32[]{:S(2)}) copy-start(bf16[4,128,512]{2,1,0:T(8,128)(2,1)} %copy-done.10) | copy-start | bytes 1572868
  233.1 17.0 %all-to-all-start.11 = ((bf16[16,2,4,1024]{3,2,1,0:T(4,128)(2,1)}), bf16[16,2,4,1024]{3,2,1,0:T(4,128)(2,1)S(1)}, u32[]{:S(2)}, u32[]{:S(2)}) async-start(bf16[16,2,4,1024]{3,2,1,0:T(4,128)(2,1)} %shard_map.175), calls=%async_computation.11 | async-start | bytes 524288 | tf_op jit(solution)/shard_map/all_to_all | solution.py:67
  238.9 24.6 %copy-start.9 = (bf16[4,128,512]{2,1,0:T(8,128)(2,1)S(1)}, bf16[4,128,512]{2,1,0:T(8,128)(2,1)}, u32[]{:S(2)}) copy-start(bf16[4,128,512]{2,1,0:T(8,128)(2,1)} %copy-done.8) | copy-start | bytes 1572868
  250.7 12.8 %copy-start.7 = (bf16[4,128,512]{2,1,0:T(8,128)(2,1)S(1)}, bf16[4,128,512]{2,1,0:T(8,128)(2,1)}, u32[]{:S(2)}) copy-start(bf16[4,128,512]{2,1,0:T(8,128)(2,1)} %copy-done.6) | copy-start | bytes 1572868
  250.7 12.8 %all-to-all-start.12 = ((bf16[8,2,4,1024]{3,2,1,0:T(4,128)(2,1)}), bf16[8,2,4,1024]{3,2,1,0:T(4,128)(2,1)S(1)}, u32[]{:S(2)}, u32[]{:S(2)}) async-start(bf16[8,2,4,1024]{3,2,1,0:T(4,128)(2,1)} %get-tuple-element.32), calls=%async_computation.12 | async-start | bytes 262144 | tf_op jit(solution)/shard_map/all_to_all | solution.py:63
  254.2 9.3 %copy-start.5 = (bf16[4,128,512]{2,1,0:T(8,128)(2,1)S(1)}, bf16[4,128,512]{2,1,0:T(8,128)(2,1)}, u32[]{:S(2)}) copy-start(bf16[4,128,512]{2,1,0:T(8,128)(2,1)} %c0.3) | copy-start | bytes 1572868
  254.7 8.9 %copy-start.36 = (s32[4,32]{1,0:T(4,128)S(1)}, s32[4,32]{1,0:T(4,128)}, u32[]{:S(2)}) copy-start(s32[4,32]{1,0:T(4,128)} %blocks.3) | copy-start | bytes 1540
  265.2 11.6 %all-to-all-start.13 = ((bf16[8,4,4,512]{3,2,1,0:T(4,128)(2,1)}), bf16[8,4,4,512]{3,2,1,0:T(4,128)(2,1)S(1)}, u32[]{:S(2)}, u32[]{:S(2)}) async-start(bf16[8,4,4,512]{3,2,1,0:T(4,128)(2,1)} %shard_map.177), calls=%async_computation.13 | async-start | bytes 262144 | tf_op jit(solution)/shard_map/all_to_all | solution.py:63
  268.7 8.2 %copy-start.30 = (f32[4,4,512]{2,1,0:T(4,128)S(1)}, f32[4,4,512]{2,1,0:T(4,128)}, u32[]{:S(2)}) copy-start(f32[4,4,512]{2,1,0:T(4,128)} %copy-done.29) | copy-start | bytes 98308
  285.3 23.6 %all-to-all-start.15 = ((bf16[16,4,16,256]{3,2,1,0:T(8,128)(2,1)}), bf16[16,4,16,256]{3,2,1,0:T(8,128)(2,1)S(1)}, u32[]{:S(2)}, u32[]{:S(2)}) async-start(bf16[16,4,16,256]{3,2,1,0:T(8,128)(2,1)} %broadcast_in_dim.20), calls=%async_computation.15 | async-start | bytes 1048576 | tf_op jit(solution)/shard_map/all_to_all | solution.py:67
  292.8 16.2 %copy-start.43 = (f32[4,256]{1,0:T(4,128)S(1)}, f32[4,256]{1,0:T(4,128)}, u32[]{:S(2)}) copy-start(f32[4,256]{1,0:T(4,128)} %copy-done.42) | copy-start | bytes 12292
  (14 other events, 8.8 us)

commit v6 on v5

v6 whole, which is shorter than its diff:
```python
import functools

import jax
import jax.numpy as jnp
from jax import lax
from jax.experimental import pallas as pl
from jax.experimental.pallas import tpu as pltpu
from jax.sharding import PartitionSpec as P

BLOCK = 128
NEAR = 4
BF16 = jnp.bfloat16
F32 = jnp.float32
VMEM_SPEC = pl.BlockSpec(memory_space=pltpu.VMEM)
SMEM_SPEC = pl.BlockSpec(memory_space=pltpu.SMEM)


def near_groups():
    size = lax.axis_size("col")
    return [[z * NEAR + x for x in range(NEAR)] for z in range(size // NEAR)]


def far_groups():
    size = lax.axis_size("col")
    return [[z * NEAR + x for z in range(size // NEAR)] for x in range(NEAR)]


def swap_near(pieces):
    return lax.all_to_all(pieces, "col", 0, 0, axis_index_groups=near_groups(), tiled=True)


def far_size():
    return lax.axis_size("col") // NEAR


def gather_near(value):
    return lax.all_gather(value, "col", axis_index_groups=near_groups(), axis=0)


def copies_of(value, size):
    return jnp.broadcast_to(value.astype(BF16)[None], (size,) + value.shape)


def send_far(copies):
    groups = far_groups()
    return lax.all_to_all(copies, "col", 0, 0, axis_index_groups=groups, tiled=True)


def send_row(copies):
    return lax.all_to_all(copies, "row", 0, 0, tiled=True)


def update_table(blocks, far_at, held):
    targets = far_at * NEAR * held + jnp.arange(NEAR * held, dtype=jnp.int32)
    hits = (blocks[:, None, :] == targets[None, :, None]).astype(jnp.int32)
    return jnp.sum(hits * jnp.arange(1, blocks.shape[1] + 1, dtype=jnp.int32), axis=-1) - 1


def send_col(copies):
    return lax.all_to_all(copies, "col", 0, 0, tiled=True)


def level_mask(sizes, count, start):
    index = start + jnp.arange(count, dtype=jnp.int32)
    return (index[None, :] < sizes[:, None]).astype(F32)[:, None, :]


def dot(a, b, dims):
    return lax.dot_general(a, b, (dims, ((), ())), preferred_element_type=F32)


def call(kernel, out_shape, scalars, arrays, **static):
    return pl.pallas_call(
        functools.partial(kernel, **static),
        out_shape=out_shape,
        in_specs=[SMEM_SPEC] * len(scalars) + [VMEM_SPEC] * len(arrays),
        out_specs=jax.tree.map(lambda _: VMEM_SPEC, out_shape),
        compiler_params=pltpu.CompilerParams(vmem_limit_bytes=16 << 20),
    )(*scalars, *arrays)


def arrived(parts, f):
    terms = [parts[i, f].astype(F32) for i in range(parts.shape[0])]
    while len(terms) > 1:
        terms = [terms[i] + terms[i + 1] for i in range(0, len(terms), 2)]
    return terms[0]


def write_copies(out, f, value):
    value = value.astype(BF16)
    for i in range(out.shape[0]):
        out[i, f] = value


def shape_of(*dims, dtype=BF16):
    return jax.ShapeDtypeStruct(dims, dtype)


def first_kernel(parts, mask, pivots, out, scaled):
    for f in range(parts.shape[1]):
        solved = arrived(parts, f) * mask[f]
        scaled[f] = solved * pivots[f]
        write_copies(out, f, solved)


def first_solved(parts, mask, pivots):
    shape = parts.shape[1:]
    out = (shape_of(NEAR, *shape), shape_of(*shape, dtype=F32))
    return call(first_kernel, out, [], [parts, mask, pivots[:, None, :]])


def first_update_kernel(parts, coupling, out):
    for f in range(coupling.shape[0]):
        pieces = [parts[x, f].astype(F32) for x in range(NEAR)]
        operand = jnp.concatenate(pieces, axis=0).astype(BF16)
        write_copies(out, f, dot(operand, coupling[f], ((1,), (1,))))


def first_update(parts, coupling):
    fronts, count, _ = coupling.shape
    out = shape_of(lax.axis_size("row"), fronts, NEAR * parts.shape[2], count)
    return call(first_update_kernel, out, [], [parts, coupling])


def scatter_kernel(parts, out):
    width = out.shape[2]
    for f in range(parts.shape[1]):
        value = arrived(parts, f)
        for x in range(NEAR):
            share = value[x * width : (x + 1) * width].astype(BF16)
            for z in range(out.shape[0] // NEAR):
                out[z * NEAR + x, f] = share


def relay_scattered(parts):
    _, fronts, rhs, count = parts.shape
    out = shape_of(lax.axis_size("col"), fronts, rhs // NEAR, count)
    return call(scatter_kernel, out, [], [parts])


def update_kernel(parts, mask, pivots, coupling, out, scaled):
    for f in range(parts.shape[1]):
        solved = arrived(parts, f) * mask[f]
        scaled[f] = solved * pivots[f]
        operand = solved.astype(BF16)
        update = [dot(operand, coupling[x, f], ((1,), (1,))) for x in range(NEAR)]
        write_copies(out, f, jnp.concatenate(update, axis=-1))


def update_of(parts, mask, pivots, coupling):
    _, fronts, width, count = parts.shape
    rows = lax.axis_size("row")
    out = (
        shape_of(rows, fronts, width, NEAR * coupling.shape[2]),
        shape_of(fronts, width, count, dtype=F32),
    )
    return call(update_kernel, out, [], [parts, mask, pivots[:, None, :], coupling])


def relay_kernel(parts, out):
    for f in range(parts.shape[1]):
        write_copies(out, f, arrived(parts, f))


def relay(parts):
    return call(relay_kernel, shape_of(far_size(), *parts.shape[1:]), [], [parts])


def solved_kernel(parts, mask, out, solved):
    for f in range(parts.shape[1]):
        value = arrived(parts, f) * mask[f]
        solved[f] = value
        write_copies(out, f, value)


def relay_solved(parts, mask):
    shape = parts.shape[1:]
    out = (shape_of(far_size(), *shape), shape_of(*shape, dtype=F32))
    return call(solved_kernel, out, [], [parts, mask])


def place_kernel(table, whole, source, mask, inverse, out, *, base):
    n = inverse.shape[2]
    held = n // BLOCK
    count = out.shape[3]
    spread = whole.shape[3] // BLOCK
    for p in range(out.shape[1]):
        total = None
        for x in range(NEAR):
            tiles = []
            for b in range(held):
                start = base + p * n + b * BLOCK
                tile = source[x, :, start : start + BLOCK]
                for c in (2 * p, 2 * p + 1):
                    at = table[c, x * held + b]
                    found = jnp.where(at >= 0, 1.0, 0.0).astype(F32)
                    at = jnp.maximum(at, 0)
                    if spread == 1:
                        placed = whole[at, c]
                    else:
                        lane = pl.multiple_of((at % spread) * BLOCK, BLOCK)
                        placed = whole[at // spread, c, :, pl.ds(lane, BLOCK)]
                    tile = tile - placed.astype(F32) * found
                tiles.append(tile)
            operand = jnp.concatenate(tiles, axis=-1) * mask[p, :, x * n : (x + 1) * n]
            rows = inverse[x, p * count : (p + 1) * count]
            part = dot(operand.astype(BF16), rows, ((1,), (1,)))
            total = part if total is None else total + part
        write_copies(out, p, total)


def place_and_solve(table, whole, source, mask, inverse, parents, count, base):
    out = shape_of(far_size(), parents, whole.shape[2], count)
    return call(place_kernel, out, [table], [whole, source, mask, inverse], base=base)


def root_kernel(parts, pivots, inverse, out):
    operand = (arrived(parts, 0) * pivots[...]).astype(BF16)
    pieces = [dot(operand, inverse[x], ((1,), (0,))) for x in range(NEAR)]
    write_copies(out, 0, jnp.concatenate(pieces, axis=-1))


def root_back(parts, pivots, inverse):
    out = shape_of(lax.axis_size("row"), 1, parts.shape[2], NEAR * inverse.shape[2])
    return call(root_kernel, out, [], [parts, pivots[None, :], inverse])


def back_kernel(parts, scaled, mask, inverse, out):
    count = parts.shape[3]
    for p in range(parts.shape[1]):
        operand = ((scaled[p] - arrived(parts, p)) * mask[p]).astype(BF16)
        pieces = [
            dot(operand, inverse[x, p * count : (p + 1) * count], ((1,), (0,)))
            for x in range(NEAR)
        ]
        write_copies(out, p, jnp.concatenate(pieces, axis=-1))


def back(parts, scaled, mask, inverse):
    _, fronts, width, _ = parts.shape
    out = shape_of(lax.axis_size("row"), fronts, width, NEAR * inverse.shape[2])
    return call(back_kernel, out, [], [parts, scaled, mask, inverse])


def pick_kernel(far, blocks, whole, coupling, out):
    held = whole.shape[3] // BLOCK
    for c in range(blocks.shape[0]):
        total = None
        for x in range(NEAR):
            block = blocks[c, far[0] * NEAR + x]
            lane = pl.multiple_of((block % held) * BLOCK, BLOCK)
            tile = whole[block // held, c // 2, :, pl.ds(lane, BLOCK)]
            part = dot(tile, coupling[x, c], ((1,), (0,)))
            total = part if total is None else total + part
        write_copies(out, c, total)


def pick_and_carry(far, blocks, whole, coupling):
    _, children, _, count = coupling.shape
    out = shape_of(far_size(), children, whole.shape[2], count)
    return call(pick_kernel, out, [far, blocks], [whole, coupling])


def halves(value):
    high = value.astype(BF16)
    return high, (value - high.astype(F32)).astype(BF16)


def by_near(value):
    return value.reshape(NEAR, value.shape[0] // NEAR, value.shape[1])


def local(
    inverse_top,
    inverse_mid,
    inverse_low,
    coupling_mid,
    coupling_low,
    source_top,
    source_mid,
    source_low,
    pivots_top,
    pivots_mid,
    pivots_low,
    sizes_mid,
    sizes_low,
    blocks_mid,
    blocks_low,
):
    row_at = lax.axis_index("row")
    col_at = lax.axis_index("col")
    far_at = col_at // NEAR
    rhs = source_top.shape[1]
    width = rhs // NEAR
    n0, n1, n2 = source_top.shape[0], source_mid.shape[1], source_low.shape[1]
    k1, k2 = inverse_mid.shape[1], inverse_low.shape[1]
    top = jnp.full((1,), inverse_top.shape[0] * lax.axis_size("row"), jnp.int32)

    others = jnp.concatenate([source_mid[0].T, source_mid[1].T, source_top.T], axis=-1)
    halved = jnp.concatenate(halves(others), axis=-1).reshape(-1, n1)
    packed = jnp.concatenate([inverse_mid.reshape(-1, n1), halved], axis=0)
    packed, coupling_mid = lax.optimization_barrier((packed, coupling_mid))
    packed_near = gather_near(packed)
    coupling_mid_near = gather_near(coupling_mid)
    inverse_top_near = gather_near(inverse_top)
    coupling_low_near = gather_near(coupling_low)

    far = far_at.reshape(1)
    table_low = update_table(blocks_low, far_at, n1 // BLOCK)
    table_mid = update_table(blocks_mid, far_at, n0 // BLOCK)
    row_mask_mid = level_mask(sizes_mid, k1, row_at * k1)
    row_mask_low = level_mask(sizes_low, k2, row_at * k2)
    col_mask_low = level_mask(sizes_low, n2, col_at * n2)
    wide_mask_mid = level_mask(sizes_mid, NEAR * n1, far_at * NEAR * n1)
    wide_mask_top = level_mask(top, NEAR * n0, far_at * NEAR * n0)

    source = jnp.swapaxes(source_low, 1, 2) * col_mask_low
    partial = jnp.einsum(
        "fij,fcj->cfi", inverse_low, source.astype(BF16), preferred_element_type=F32
    ).reshape(rhs, -1)
    got = swap_near(by_near(partial.astype(BF16))).astype(F32)
    partial = jnp.swapaxes(jnp.sum(got, axis=0).reshape(width, -1, k2), 0, 1)
    parts = send_far(copies_of(partial, far_size()))
    message, scaled_low = first_solved(parts, row_mask_low, pivots_low)
    message = first_update(swap_near(message), coupling_low)
    whole = send_col(relay_scattered(send_row(message)))

    halved = packed_near[:, 2 * k1 :].reshape(NEAR, rhs, -1)
    halved = lax.dynamic_slice_in_dim(halved, (col_at % NEAR) * width, width, 1).astype(F32)
    size = halved.shape[2] // 2
    others = halved[:, :, :size] + halved[:, :, size:]
    parts = send_far(
        place_and_solve(table_low, whole, others, wide_mask_mid, packed_near, 2, k1, 0)
    )

    message, scaled_mid = update_of(parts, row_mask_mid, pivots_mid, coupling_mid_near)
    whole = send_far(relay(send_row(message)))
    k0 = inverse_top.shape[0]
    parts = send_far(
        place_and_solve(table_mid, whole, others, wide_mask_top, inverse_top_near, 1, k0, 2 * n1)
    )

    message, solution_top = relay_solved(
        send_row(root_back(parts, pivots_top, inverse_top_near)), wide_mask_top
    )
    parts = send_far(pick_and_carry(far, blocks_mid, send_far(message), coupling_mid_near))
    message, solution_mid = relay_solved(
        send_row(back(parts, scaled_mid, row_mask_mid, packed_near)), wide_mask_mid
    )
    parts = send_far(pick_and_carry(far, blocks_low, send_far(message), coupling_low_near))
    residual = (scaled_low - jnp.sum(parts.astype(F32), axis=0)) * row_mask_low

    upper = jnp.concatenate(
        [
            solution_top[0].reshape(width, NEAR, n0),
            solution_mid[0].reshape(width, NEAR, n1),
            solution_mid[1].reshape(width, NEAR, n1),
        ],
        axis=-1,
    )
    upper = jnp.swapaxes(jnp.concatenate(halves(upper), axis=-1), 0, 1)
    flat = jnp.swapaxes(residual, 0, 1).reshape(width, -1).astype(BF16)
    size = flat.shape[1]
    message = jnp.concatenate([copies_of(flat, NEAR), upper], axis=-1)
    got = swap_near(message).reshape(rhs, -1)
    upper = got[:, size:].astype(F32)
    upper = upper[:, : upper.shape[1] // 2] + upper[:, upper.shape[1] // 2 :]
    residual = got[:, :size].reshape(rhs, -1, k2)
    partial = jnp.einsum("fij,cfi->fcj", inverse_low, residual, preferred_element_type=F32)
    parts = send_row(copies_of(partial, lax.axis_size("row")))
    solution_low = jnp.sum(parts.astype(F32), axis=0) * col_mask_low
    return (
        upper[:, :n0].T,
        jnp.stack([upper[:, n0 : n0 + n1].T, upper[:, n0 + n1 :].T]),
        jnp.swapaxes(solution_low, 1, 2),
    )


def solution(mesh):
    placed = (
        P("row", "col"),
        P(None, "row", "col"),
        P(None, "row", "col"),
        P(None, "col", "row"),
        P(None, "col", "row"),
        P("col", None),
        P(None, "col", None),
        P(None, "col", None),
        P("row"),
        P(None, "row"),
        P(None, "row"),
        P(),
        P(),
        P(),
        P(),
    )
    return jax.shard_map(
        local,
        mesh=mesh,
        in_specs=placed,
        out_specs=(P("col", None), P(None, "col", None), P(None, "col", None)),
        check_vma=False,
    )
```

time: 312 us -> 278 us (0.89)
  starting transfers between devices: 125 us -> 67.1 us
  waiting for transfers between devices: 96.4 us -> 115 us
  between operations: 1.41 us -> 14.2 us
  local copies, waits for them, and re-layouts: 22.8 us -> 14.1 us
  blocking collectives: 42.9 us -> 47.1 us
    ppermute x12 -> x0, starting transfers between devices: 39.4 us -> none  [gather_near(): parts.append(lax.ppermute(value, 'col', [(i, i ^ m) for i in range(size)]))]
    all_to_all x4, starting transfers between devices: 48.5 us -> 28 us  [send_row(): return lax.all_to_all(copies, 'row', 0, 0, tiled=True)]
    all_to_all x4, waiting for transfers between devices: 31.5 us -> 48.2 us  [send_row(): return lax.all_to_all(copies, 'row', 0, 0, tiled=True)]
    ppermute x12 -> x0, waiting for transfers between devices: 9.62 us -> none  [gather_near(): parts.append(lax.ppermute(value, 'col', [(i, i ^ m) for i in range(size)]))]
    all_to_all x0 -> x1, waiting for transfers between devices: none -> 9.3 us  [send_col(): return lax.all_to_all(copies, 'col', 0, 0, tiled=True)]
    all_to_all x1 -> x2, waiting for transfers between devices: 17.8 us -> 8.81 us  [swap_near(): lax.all_to_all(pieces, 'col', 0, 0, axis_index_groups=near_groups(), tile...]
    unnamed x111 -> x38, local copies, waits for them, and re-layouts: 16.1 us -> 8.81 us
    all_to_all x7 -> x6, starting transfers between devices: 33 us -> 26.9 us  [send_far(): lax.all_to_all(copies, 'col', 0, 0, axis_index_groups=groups, tiled=True)]
  transfers between devices with their start and end apart: 24 -> 17, of which waited for: 12 -> 14; matrix products, arithmetic and copies ran while one was open for 4% -> 2% of each run, Pallas kernels for 2% -> 4%
where the time goes in v6:
time: 278 us; the launch traced here: 276 us
  waiting for transfers between devices  115 us (41%)
  starting transfers between devices  67.1 us (24%)
  blocking collectives  47.1 us (17%)
  between operations  14.2 us (5%)
  local copies, waits for them, and re-layouts  14.1 us (5%)
  Pallas kernels  11.7 us (4%)
  other arithmetic  6.01 us (2%)
    all_to_all x4, waiting for transfers between devices, send_row(): return lax.all_to_all(copies, 'row', 0, 0, tiled=True)  48.2 us
    all_to_all x6, waiting for transfers between devices, send_far(): lax.all_to_all(copies, 'col', 0, 0, axis_index_groups=groups, tiled=True)  42.9 us
    all_to_all x4, starting transfers between devices, send_row(): return lax.all_to_all(copies, 'row', 0, 0, tiled=True)  28 us
    all_to_all x6, starting transfers between devices, send_far(): lax.all_to_all(copies, 'col', 0, 0, axis_index_groups=groups, tiled=True)  26.9 us
    all_to_all x2, blocking collectives, send_far(): lax.all_to_all(copies, 'col', 0, 0, axis_index_groups=groups, tiled=True)  20.8 us
    all_to_all x1, blocking collectives, send_row(): return lax.all_to_all(copies, 'row', 0, 0, tiled=True)  18.8 us
    pallas_call x13, Pallas kernels, call(): pl.pallas_call(functools.partial(kernel, **static), out_shape=out_shape,...  11.7 us
    all_to_all x1, waiting for transfers between devices, send_col(): return lax.all_to_all(copies, 'col', 0, 0, tiled=True)  9.3 us
  transfers between devices with their start and end apart: 17, of which 14 were waited for; matrix products, arithmetic and copies ran while one was open for 2% of the time, Pallas kernels for 4%

profile of v6, /device:TPU:1, one launch (start us, length us, event | category | flops | bytes accessed | tf_op | source)
XLA Modules:
  0.0 276.1 jit_solution(16302223864705521156)
XLA Ops:
  7.2 0.8 slice_bitcast_fusion.4
  8.1 0.7 fusion.3
  8.8 0.7 subtract_convert_fusion.1
  9.6 1.9 pad_maximum_fusion
  11.7 0.7 all-gather.11.cloned.1.call-update
  12.4 0.7 all-gather.13.cloned.1.call-update
  13.2 0.4 fusion
  13.6 0.7 convert_element_type.126
  14.3 4.8 %all-to-all-start = ((bf16[4,4,2048]{2,1,0:T(4,128)(2,1)}), bf16[4,4,2048]{2,1,0:T(4,128)(2,1)S(1)}, u32[]{:S(2)}, u32[]{:S(2)}) async-start(bf16[4,4,2048]{2,1,0:T(4,128)(2,1)} %convert_element_type.126), calls=%async_computation | async-start | bytes 131072 | tf_op jit(solution)/shard_map/all_to_all | solution.py:29
  19.2 0.6 all-gather.15.cloned.1.call-update
  19.8 3.9 %all-to-all-done = bf16[4,4,2048]{2,1,0:T(4,128)(2,1)S(1)} async-done(((bf16[4,4,2048]{2,1,0:T(4,128)(2,1)}), bf16[4,4,2048]{2,1,0:T(4,128)(2,1)S(1)}, u32[]{:S(2)}, u32[]{:S(2)}) %all-to-all-start) | async-done | bytes 65568 | tf_op jit(solution)/shard_map/all_to_all | solution.py:29
  23.7 0.7 broadcast_in_dim.12
  24.4 10.0 %all-to-all-start.1 = ((bf16[8,4,4,512]{3,2,1,0:T(4,128)(2,1)}), bf16[8,4,4,512]{3,2,1,0:T(4,128)(2,1)S(1)}, u32[]{:S(2)}, u32[]{:S(2)}) async-start(bf16[8,4,4,512]{3,2,1,0:T(4,128)(2,1)} %broadcast_in_dim.12), calls=%async_computation.1 | async-start | bytes 262144 | tf_op jit(solution)/shard_map/all_to_all | solution.py:46
  34.5 7.9 %all-to-all-done.1.parts = bf16[8,4,4,512]{3,2,1,0:T(4,128)(2,1)S(1)} async-done(((bf16[8,4,4,512]{3,2,1,0:T(4,128)(2,1)}), bf16[8,4,4,512]{3,2,1,0:T(4,128)(2,1)S(1)}, u32[]{:S(2)}, u32[]{:S(2)}) %all-to-all-start.1) | async-done | bytes 131104 | tf_op jit(solution)/shard_map/all_to_all | solution.py:46
  42.4 0.7 shard_map.166
  43.1 3.3 %all-to-all-start.2 = ((bf16[4,4,4,512]{3,2,1,0:T(4,128)(2,1)}), bf16[4,4,4,512]{3,2,1,0:T(4,128)(2,1)S(1)}, u32[]{:S(2)}, u32[]{:S(2)}) async-start(bf16[4,4,4,512]{3,2,1,0:T(4,128)(2,1)} %get-tuple-element.14), calls=%async_computation.2 | async-start | bytes 131072 | tf_op jit(solution)/shard_map/all_to_all | solution.py:29
  46.6 4.9 %all-to-all-done.2.parts = bf16[4,4,4,512]{3,2,1,0:T(4,128)(2,1)S(1)} async-done(((bf16[4,4,4,512]{3,2,1,0:T(4,128)(2,1)}), bf16[4,4,4,512]{3,2,1,0:T(4,128)(2,1)S(1)}, u32[]{:S(2)}, u32[]{:S(2)}) %all-to-all-start.2) | async-done | bytes 65568 | tf_op jit(solution)/shard_map/all_to_all | solution.py:29
  51.6 1.0 shard_map.167
  52.5 11.6 %all-to-all-start.3 = ((bf16[16,4,16,128]{3,2,1,0:T(8,128)(2,1)}), bf16[16,4,16,128]{3,2,1,0:T(8,128)(2,1)S(1)}, u32[]{:S(2)}, u32[]{:S(2)}) async-start(bf16[16,4,16,128]{3,2,1,0:T(8,128)(2,1)} %shard_map.167), calls=%async_computation.3 | async-start | bytes 524288 | tf_op jit(solution)/shard_map/all_to_all | solution.py:50
  64.3 11.6 %all-to-all-done.3.parts = bf16[16,4,16,128]{3,2,1,0:T(8,128)(2,1)S(1)} async-done(((bf16[16,4,16,128]{3,2,1,0:T(8,128)(2,1)}), bf16[16,4,16,128]{3,2,1,0:T(8,128)(2,1)S(1)}, u32[]{:S(2)}, u32[]{:S(2)}) %all-to-all-start.3) | async-done | bytes 262176 | tf_op jit(solution)/shard_map/all_to_all | solution.py:50
  75.9 0.7 shard_map.168
  76.6 4.0 %all-to-all-start.4 = ((bf16[32,4,4,128]{3,2,1,0:T(4,128)(2,1)}), bf16[32,4,4,128]{3,2,1,0:T(4,128)(2,1)S(1)}, u32[]{:S(2)}, u32[]{:S(2)}) async-start(bf16[32,4,4,128]{3,2,1,0:T(4,128)(2,1)} %shard_map.168), calls=%async_computation.4 | async-start | bytes 262144 | tf_op jit(solution)/shard_map/all_to_all | solution.py:60
  80.6 1.0 slice.56
  81.9 9.3 %all-to-all-done.4.whole = bf16[32,4,4,128]{3,2,1,0:T(4,128)(2,1)S(1)} async-done(((bf16[32,4,4,128]{3,2,1,0:T(4,128)(2,1)}), bf16[32,4,4,128]{3,2,1,0:T(4,128)(2,1)S(1)}, u32[]{:S(2)}, u32[]{:S(2)}) %all-to-all-start.4) | async-done | bytes 131104 | tf_op jit(solution)/shard_map/all_to_all | solution.py:60
  91.2 1.7 copy-done.1
  92.8 1.9 shard_map.169
  94.7 3.4 %all-to-all-start.5 = ((bf16[8,2,4,512]{3,2,1,0:T(4,128)(2,1)}), bf16[8,2,4,512]{3,2,1,0:T(4,128)(2,1)S(1)}, u32[]{:S(2)}, u32[]{:S(2)}) async-start(bf16[8,2,4,512]{3,2,1,0:T(4,128)(2,1)} %shard_map.169), calls=%async_computation.5 | async-start | bytes 131072 | tf_op jit(solution)/shard_map/all_to_all | solution.py:46
  98.2 6.9 %all-to-all-done.5.parts = bf16[8,2,4,512]{3,2,1,0:T(4,128)(2,1)S(1)} async-done(((bf16[8,2,4,512]{3,2,1,0:T(4,128)(2,1)}), bf16[8,2,4,512]{3,2,1,0:T(4,128)(2,1)S(1)}, u32[]{:S(2)}, u32[]{:S(2)}) %all-to-all-start.5) | async-done | bytes 65568 | tf_op jit(solution)/shard_map/all_to_all | solution.py:46
  105.1 1.3 copy-done.5
  106.4 1.0 shard_map.170
  107.4 4.9 %all-to-all-start.6 = ((bf16[16,2,4,512]{3,2,1,0:T(4,128)(2,1)}), bf16[16,2,4,512]{3,2,1,0:T(4,128)(2,1)S(1)}, u32[]{:S(2)}, u32[]{:S(2)}) async-start(bf16[16,2,4,512]{3,2,1,0:T(4,128)(2,1)} %get-tuple-element.17), calls=%async_computation.6 | async-start | bytes 262144 | tf_op jit(solution)/shard_map/all_to_all | solution.py:50
  112.8 8.7 %all-to-all-done.6.parts = bf16[16,2,4,512]{3,2,1,0:T(4,128)(2,1)S(1)} async-done(((bf16[16,2,4,512]{3,2,1,0:T(4,128)(2,1)}), bf16[16,2,4,512]{3,2,1,0:T(4,128)(2,1)S(1)}, u32[]{:S(2)}, u32[]{:S(2)}) %all-to-all-start.6) | async-done | bytes 131104 | tf_op jit(solution)/shard_map/all_to_all | solution.py:50
  121.6 0.7 shard_map.171
  122.2 3.4 %all-to-all-start.7 = ((bf16[8,2,4,512]{3,2,1,0:T(4,128)(2,1)}), bf16[8,2,4,512]{3,2,1,0:T(4,128)(2,1)S(1)}, u32[]{:S(2)}, u32[]{:S(2)}) async-start(bf16[8,2,4,512]{3,2,1,0:T(4,128)(2,1)} %shard_map.171), calls=%async_computation.7 | async-start | bytes 131072 | tf_op jit(solution)/shard_map/all_to_all | solution.py:46
  125.6 4.0 %all-gather.13.cloned.1.call-done = bf16[3072,384]{1,0:T(8,128)(2,1)} async-done(((bf16[768,384]{1,0:T(8,128)(2,1)}), bf16[3072,384]{1,0:T(8,128)(2,1)}) %all-gather.13.cloned.1.call-update) | async-done | bytes 2359312 | tf_op jit(solution)/shard_map/all_gather | solution.py:37
  129.6 3.7 %all-to-all-done.7.whole = bf16[8,2,4,512]{3,2,1,0:T(4,128)(2,1)S(1)} async-done(((bf16[8,2,4,512]{3,2,1,0:T(4,128)(2,1)}), bf16[8,2,4,512]{3,2,1,0:T(4,128)(2,1)S(1)}, u32[]{:S(2)}, u32[]{:S(2)}) %all-to-all-start.7) | async-done | bytes 65568 | tf_op jit(solution)/shard_map/all_to_all | solution.py:46
  133.3 1.7 copy-done.3
  135.0 1.9 shard_map.172
  136.9 3.4 %all-to-all-start.8 = ((bf16[8,1,4,768]{3,2,1,0:T(4,128)(2,1)}), bf16[8,1,4,768]{3,2,1,0:T(4,128)(2,1)S(1)}, u32[]{:S(2)}, u32[]{:S(2)}) async-start(bf16[8,1,4,768]{3,2,1,0:T(4,128)(2,1)} %shard_map.172), calls=%async_computation.8 | async-start | bytes 98304 | tf_op jit(solution)/shard_map/all_to_all | solution.py:46
  140.3 7.0 %all-to-all-done.8.parts = bf16[8,1,4,768]{3,2,1,0:T(4,128)(2,1)S(1)} async-done(((bf16[8,1,4,768]{3,2,1,0:T(4,128)(2,1)}), bf16[8,1,4,768]{3,2,1,0:T(4,128)(2,1)S(1)}, u32[]{:S(2)}, u32[]{:S(2)}) %all-to-all-start.8) | async-done | bytes 49184 | tf_op jit(solution)/shard_map/all_to_all | solution.py:46
  147.3 1.8 copy-done.4
  149.2 0.4 shard_map.173
  149.6 18.8 %all_to_all.85.parts = bf16[16,1,4,1536]{3,2,1,0:T(4,128)(2,1)S(1)} all-to-all(bf16[16,1,4,1536]{3,2,1,0:T(4,128)(2,1)S(1)} %shard_map.173), channel_id=1, replica_groups=mesh['row'=16,'col'=32] {'row'}, dimensions={0} | all-to-all | bytes 393216 | tf_op jit(solution)/shard_map/all_to_all | solution.py:50
  168.4 11.3 %all_to_all.86.whole = bf16[8,1,4,1536]{3,2,1,0:T(4,128)(2,1)S(1)} all-to-all(bf16[8,1,4,1536]{3,2,1,0:T(4,128)(2,1)S(1)} %get-tuple-element.18), channel_id=1, replica_groups={{0,4,8,12,16,20,24,28},{1,5,9,13,17,21,25,29},{2,6,10,14,18,22,26,30},{..., dimensions={0} | all-to-all | bytes 196608 | tf_op jit(solution)/shard_map/all_to_all | solution.py:46
  179.7 0.8 shard_map.175
  180.5 9.5 %all_to_all.87.parts = bf16[8,2,4,512]{3,2,1,0:T(4,128)(2,1)S(1)} all-to-all(bf16[8,2,4,512]{3,2,1,0:T(4,128)(2,1)S(1)} %shard_map.175), channel_id=1, replica_groups={{0,4,8,12,16,20,24,28},{1,5,9,13,17,21,25,29},{2,6,10,14,18,22,26,30},{..., dimensions={0} | all-to-all | bytes 131072 | tf_op jit(solution)/shard_map/all_to_all | solution.py:46
  190.0 0.4 shard_map.176
  190.4 0.7 copy-done.9
  191.1 5.0 %all-to-all-start.12 = ((bf16[16,2,4,1024]{3,2,1,0:T(4,128)(2,1)}), bf16[16,2,4,1024]{3,2,1,0:T(4,128)(2,1)S(1)}, u32[]{:S(2)}, u32[]{:S(2)}) async-start(bf16[16,2,4,1024]{3,2,1,0:T(4,128)(2,1)} %copy-done.9), calls=%async_computation.12 | async-start | bytes 524288 | tf_op jit(solution)/shard_map/all_to_all | solution.py:50
  196.2 11.8 %all-to-all-done.12.parts = bf16[16,2,4,1024]{3,2,1,0:T(4,128)(2,1)S(1)} async-done(((bf16[16,2,4,1024]{3,2,1,0:T(4,128)(2,1)}), bf16[16,2,4,1024]{3,2,1,0:T(4,128)(2,1)S(1)}, u32[]{:S(2)}, u32[]{:S(2)}) %all-to-all-start.12) | async-done | bytes 262176 | tf_op jit(solution)/shard_map/all_to_all | solution.py:50
  208.0 0.7 shard_map.177
  208.7 3.4 %all-to-all-start.13 = ((bf16[8,2,4,1024]{3,2,1,0:T(4,128)(2,1)}), bf16[8,2,4,1024]{3,2,1,0:T(4,128)(2,1)S(1)}, u32[]{:S(2)}, u32[]{:S(2)}) async-start(bf16[8,2,4,1024]{3,2,1,0:T(4,128)(2,1)} %get-tuple-element.20), calls=%async_computation.13 | async-start | bytes 262144 | tf_op jit(solution)/shard_map/all_to_all | solution.py:46
  212.2 9.2 %all-to-all-done.13.whole = bf16[8,2,4,1024]{3,2,1,0:T(4,128)(2,1)S(1)} async-done(((bf16[8,2,4,1024]{3,2,1,0:T(4,128)(2,1)}), bf16[8,2,4,1024]{3,2,1,0:T(4,128)(2,1)S(1)}, u32[]{:S(2)}, u32[]{:S(2)}) %all-to-all-start.13) | async-done | bytes 131104 | tf_op jit(solution)/shard_map/all_to_all | solution.py:46
  221.4 1.6 copy-done.7
  223.0 1.6 shard_map.178
  224.6 3.4 %all-to-all-start.14 = ((bf16[8,4,4,512]{3,2,1,0:T(4,128)(2,1)}), bf16[8,4,4,512]{3,2,1,0:T(4,128)(2,1)S(1)}, u32[]{:S(2)}, u32[]{:S(2)}) async-start(bf16[8,4,4,512]{3,2,1,0:T(4,128)(2,1)} %shard_map.178), calls=%async_computation.14 | async-start | bytes 262144 | tf_op jit(solution)/shard_map/all_to_all | solution.py:46
  228.0 8.1 %all-to-all-done.14 = bf16[8,4,4,512]{3,2,1,0:T(4,128)(2,1)S(1)} async-done(((bf16[8,4,4,512]{3,2,1,0:T(4,128)(2,1)}), bf16[8,4,4,512]{3,2,1,0:T(4,128)(2,1)S(1)}, u32[]{:S(2)}, u32[]{:S(2)}) %all-to-all-start.14) | async-done | bytes 131104 | tf_op jit(solution)/shard_map/all_to_all | solution.py:46
  236.4 7.5 %all_to_all.88 = bf16[4,4,3840]{2,1,0:T(4,128)(2,1)S(1)} all-to-all(bf16[4,4,3840]{2,1,0:T(4,128)(2,1)S(1)} %pad_maximum_fusion.1), channel_id=1, replica_groups={{0,1,2,3},{4,5,6,7},{8,9,10,11},{12,13,14,15},{16,17,18,19},{20,21,22,2..., dimensions={0} | all-to-all | bytes 245760 | tf_op jit(solution)/shard_map/all_to_all | solution.py:29
  244.1 0.9 broadcast_in_dim.17
  245.0 6.5 %all-to-all-start.16 = ((bf16[16,4,16,256]{3,2,1,0:T(8,128)(2,1)}), bf16[16,4,16,256]{3,2,1,0:T(8,128)(2,1)S(1)}, u32[]{:S(2)}, u32[]{:S(2)}) async-start(bf16[16,4,16,256]{3,2,1,0:T(8,128)(2,1)} %broadcast_in_dim.17), calls=%async_computation.16 | async-start | bytes 1048576 | tf_op jit(solution)/shard_map/all_to_all | solution.py:50
  251.5 0.6 pad_maximum_fusion.4
  252.1 0.6 slice_bitcast_fusion
  252.7 16.1 %all-to-all-done.16 = bf16[16,4,16,256]{3,2,1,0:T(8,128)(2,1)S(1)} async-done(((bf16[16,4,16,256]{3,2,1,0:T(8,128)(2,1)}), bf16[16,4,16,256]{3,2,1,0:T(8,128)(2,1)S(1)}, u32[]{:S(2)}, u32[]{:S(2)}) %all-to-all-start.16) | async-done | bytes 524320 | tf_op jit(solution)/shard_map/all_to_all | solution.py:50
  268.9 0.6 multiply_bitcast_fusion
  (87 shorter events, 2.6 us)
Async XLA Ops:
  7.2 6.0 %copy-start = (bf16[4,512,256]{2,1,0:T(8,128)(2,1)S(1)}, bf16[4,512,256]{2,1,0:T(8,128)(2,1)}, u32[]{:S(2)}) copy-start(bf16[4,512,256]{2,1,0:T(8,128)(2,1)} %param.17) | copy-start | bytes 3145732
  7.2 5.9 %copy-start.14 = (s32[4]{0:T(128)S(1)}, s32[4]{0:T(128)}, u32[]{:S(2)}) copy-start(s32[4]{0:T(128)} %param.27) | copy-start | bytes 52
  7.2 6.0 %copy-start.12 = (f32[4,256,16]{1,2,0:T(8,128)S(1)}, f32[4,256,16]{1,2,0:T(8,128)}, u32[]{:S(2)}) copy-start(f32[4,256,16]{1,2,0:T(8,128)} %param.22) | copy-start | bytes 196612
  7.2 73.4 %all-gather.9.cloned.1.call-start = ((), (), s32[]{:S(2)}) async-start(), calls=%async_computation.17 | async-start | bytes 2908160 | tf_op jit(solution)/shard_map/all_gather | solution.py:37
  11.6 22.8 %copy-start.13 = (f32[4,512]{1,0:T(4,128)S(1)}, f32[4,512]{1,0:T(4,128)}, u32[]{:S(2)}) copy-start(f32[4,512]{1,0:T(4,128)} %param.25) | copy-start | bytes 24580
  11.6 34.8 %copy-start.10 = (s32[4,32]{1,0:T(4,128)S(1)}, s32[4,32]{1,0:T(4,128)}, u32[]{:S(2)}) copy-start(s32[4,32]{1,0:T(4,128)} %blocks.3) | copy-start | bytes 1540
  11.6 40.0 %copy-start.8 = (bf16[4,128,512]{2,1,0:T(8,128)(2,1)S(1)}, bf16[4,128,512]{2,1,0:T(8,128)(2,1)}, u32[]{:S(2)}) copy-start(bf16[4,128,512]{2,1,0:T(8,128)(2,1)} %coupling.1) | copy-start | bytes 1572868
  11.6 86.6 %all-gather.11.cloned.1.call-start = ((), (), s32[]{:S(2)}) async-start(), calls=%async_computation.18 | async-start | bytes 1310720 | tf_op jit(solution)/shard_map/all_gather | solution.py:37
  12.4 117.2 %all-gather.13.cloned.1.call-start = ((), (), s32[]{:S(2)}) async-start(), calls=%async_computation.19 | async-start | bytes 2949120 | tf_op jit(solution)/shard_map/all_gather | solution.py:37
  13.2 51.0 %copy-start.17 = (s32[2]{0:T(128)S(1)}, s32[2]{0:T(128)}, u32[]{:S(2)}) copy-start(s32[2]{0:T(128)} %param.26) | copy-start | bytes 28
  14.3 9.3 %all-to-all-start = ((bf16[4,4,2048]{2,1,0:T(4,128)(2,1)}), bf16[4,4,2048]{2,1,0:T(4,128)(2,1)S(1)}, u32[]{:S(2)}, u32[]{:S(2)}) async-start(bf16[4,4,2048]{2,1,0:T(4,128)(2,1)} %convert_element_type.126), calls=%async_computation | async-start | bytes 131072 | tf_op jit(solution)/shard_map/all_to_all | solution.py:29
  19.2 193.0 %all-gather.15.cloned.1.call-start = ((), (), s32[]{:S(2)}) async-start(), calls=%async_computation.20 | async-start | bytes 2621440 | tf_op jit(solution)/shard_map/all_gather | solution.py:37
  24.4 18.1 %all-to-all-start.1 = ((bf16[8,4,4,512]{3,2,1,0:T(4,128)(2,1)}), bf16[8,4,4,512]{3,2,1,0:T(4,128)(2,1)S(1)}, u32[]{:S(2)}, u32[]{:S(2)}) async-start(bf16[8,4,4,512]{3,2,1,0:T(4,128)(2,1)} %broadcast_in_dim.12), calls=%async_computation.1 | async-start | bytes 262144 | tf_op jit(solution)/shard_map/all_to_all | solution.py:46
  43.1 8.4 %all-to-all-start.2 = ((bf16[4,4,4,512]{3,2,1,0:T(4,128)(2,1)}), bf16[4,4,4,512]{3,2,1,0:T(4,128)(2,1)S(1)}, u32[]{:S(2)}, u32[]{:S(2)}) async-start(bf16[4,4,4,512]{3,2,1,0:T(4,128)(2,1)} %get-tuple-element.14), calls=%async_computation.2 | async-start | bytes 131072 | tf_op jit(solution)/shard_map/all_to_all | solution.py:29
  52.5 23.3 %all-to-all-start.3 = ((bf16[16,4,16,128]{3,2,1,0:T(8,128)(2,1)}), bf16[16,4,16,128]{3,2,1,0:T(8,128)(2,1)S(1)}, u32[]{:S(2)}, u32[]{:S(2)}) async-start(bf16[16,4,16,128]{3,2,1,0:T(8,128)(2,1)} %shard_map.167), calls=%async_computation.3 | async-start | bytes 524288 | tf_op jit(solution)/shard_map/all_to_all | solution.py:50
  76.6 21.5 %copy-start.16 = (f32[2,512]{1,0:T(2,128)S(1)}, f32[2,512]{1,0:T(2,128)}, u32[]{:S(2)}) copy-start(f32[2,512]{1,0:T(2,128)} %param.24) | copy-start | bytes 12292
  76.6 14.6 %all-to-all-start.4 = ((bf16[32,4,4,128]{3,2,1,0:T(4,128)(2,1)}), bf16[32,4,4,128]{3,2,1,0:T(4,128)(2,1)S(1)}, u32[]{:S(2)}, u32[]{:S(2)}) async-start(bf16[32,4,4,128]{3,2,1,0:T(4,128)(2,1)} %shard_map.168), calls=%async_computation.4 | async-start | bytes 262144 | tf_op jit(solution)/shard_map/all_to_all | solution.py:60
  91.2 1.7 copy-start.1
  92.8 19.5 %copy-start.11 = (s32[2,32]{1,0:T(2,128)S(1)}, s32[2,32]{1,0:T(2,128)}, u32[]{:S(2)}) copy-start(s32[2,32]{1,0:T(2,128)} %blocks.2) | copy-start | bytes 772
  94.7 10.4 %all-to-all-start.5 = ((bf16[8,2,4,512]{3,2,1,0:T(4,128)(2,1)}), bf16[8,2,4,512]{3,2,1,0:T(4,128)(2,1)S(1)}, u32[]{:S(2)}, u32[]{:S(2)}) async-start(bf16[8,2,4,512]{3,2,1,0:T(4,128)(2,1)} %shard_map.169), calls=%async_computation.5 | async-start | bytes 131072 | tf_op jit(solution)/shard_map/all_to_all | solution.py:46
  105.1 1.3 copy-start.5
  106.4 33.9 %copy-start.15 = (f32[768]{0:T(1024)S(1)}, f32[768]{0:T(1024)}, u32[]{:S(2)}) copy-start(f32[768]{0:T(1024)} %param.23) | copy-start | bytes 9220
  107.4 14.1 %all-to-all-start.6 = ((bf16[16,2,4,512]{3,2,1,0:T(4,128)(2,1)}), bf16[16,2,4,512]{3,2,1,0:T(4,128)(2,1)S(1)}, u32[]{:S(2)}, u32[]{:S(2)}) async-start(bf16[16,2,4,512]{3,2,1,0:T(4,128)(2,1)} %get-tuple-element.17), calls=%async_computation.6 | async-start | bytes 262144 | tf_op jit(solution)/shard_map/all_to_all | solution.py:50
  122.2 11.1 %all-to-all-start.7 = ((bf16[8,2,4,512]{3,2,1,0:T(4,128)(2,1)}), bf16[8,2,4,512]{3,2,1,0:T(4,128)(2,1)S(1)}, u32[]{:S(2)}, u32[]{:S(2)}) async-start(bf16[8,2,4,512]{3,2,1,0:T(4,128)(2,1)} %shard_map.171), calls=%async_computation.7 | async-start | bytes 131072 | tf_op jit(solution)/shard_map/all_to_all | solution.py:46
  133.3 1.7 copy-start.3
  136.9 10.4 %all-to-all-start.8 = ((bf16[8,1,4,768]{3,2,1,0:T(4,128)(2,1)}), bf16[8,1,4,768]{3,2,1,0:T(4,128)(2,1)S(1)}, u32[]{:S(2)}, u32[]{:S(2)}) async-start(bf16[8,1,4,768]{3,2,1,0:T(4,128)(2,1)} %shard_map.172), calls=%async_computation.8 | async-start | bytes 98304 | tf_op jit(solution)/shard_map/all_to_all | solution.py:46
  140.3 49.7 %copy-start.2 = (bf16[4544,256]{1,0:T(8,128)(2,1)S(1)}, bf16[4544,256]{1,0:T(8,128)(2,1)}, u32[]{:S(2)}) copy-start(bf16[4544,256]{1,0:T(8,128)(2,1)} %all-gather.9.cloned.1.call-done) | copy-start | bytes 6979588
  147.3 1.8 copy-start.4
  149.2 30.6 %copy-start.6 = (bf16[8,128,512]{2,1,0:T(8,128)(2,1)S(1)}, bf16[8,128,512]{2,1,0:T(8,128)(2,1)}, u32[]{:S(2)}) copy-start(bf16[8,128,512]{2,1,0:T(8,128)(2,1)} %all-gather.11.cloned.1.call-done) | copy-start | bytes 3145732
  190.4 0.7 copy-start.9
  191.1 16.8 %all-to-all-start.12 = ((bf16[16,2,4,1024]{3,2,1,0:T(4,128)(2,1)}), bf16[16,2,4,1024]{3,2,1,0:T(4,128)(2,1)S(1)}, u32[]{:S(2)}, u32[]{:S(2)}) async-start(bf16[16,2,4,1024]{3,2,1,0:T(4,128)(2,1)} %copy-done.9), calls=%async_computation.12 | async-start | bytes 524288 | tf_op jit(solution)/shard_map/all_to_all | solution.py:50
  208.7 12.7 %all-to-all-start.13 = ((bf16[8,2,4,1024]{3,2,1,0:T(4,128)(2,1)}), bf16[8,2,4,1024]{3,2,1,0:T(4,128)(2,1)S(1)}, u32[]{:S(2)}, u32[]{:S(2)}) async-start(bf16[8,2,4,1024]{3,2,1,0:T(4,128)(2,1)} %get-tuple-element.20), calls=%async_computation.13 | async-start | bytes 262144 | tf_op jit(solution)/shard_map/all_to_all | solution.py:46
  221.4 1.6 copy-start.7
  224.6 11.6 %all-to-all-start.14 = ((bf16[8,4,4,512]{3,2,1,0:T(4,128)(2,1)}), bf16[8,4,4,512]{3,2,1,0:T(4,128)(2,1)S(1)}, u32[]{:S(2)}, u32[]{:S(2)}) async-start(bf16[8,4,4,512]{3,2,1,0:T(4,128)(2,1)} %shard_map.178), calls=%async_computation.14 | async-start | bytes 262144 | tf_op jit(solution)/shard_map/all_to_all | solution.py:46
  245.0 23.8 %all-to-all-start.16 = ((bf16[16,4,16,256]{3,2,1,0:T(8,128)(2,1)}), bf16[16,4,16,256]{3,2,1,0:T(8,128)(2,1)S(1)}, u32[]{:S(2)}, u32[]{:S(2)}) async-start(bf16[16,4,16,256]{3,2,1,0:T(8,128)(2,1)} %broadcast_in_dim.17), calls=%async_computation.16 | async-start | bytes 1048576 | tf_op jit(solution)/shard_map/all_to_all | solution.py:50
Sparse Core Ops, SparseCore 0:
  11.7 44.2 all-gather.8
  58.1 28.8 all-gather.10
  89.1 40.5 all-gather.12
  131.6 36.2 all-gather.14

commit v7 on v6

--- a/solution.py
+++ b/solution.py
@@ -69,14 +69,30 @@
     return lax.dot_general(a, b, (dims, ((), ())), preferred_element_type=F32)
 
 
-def call(kernel, out_shape, scalars, arrays, **static):
+def call(kernel, out_shape, scalars, arrays, fetched=(), **static):
+    specs = [SMEM_SPEC] * len(scalars) + [VMEM_SPEC] * len(arrays)
+    specs += [pl.BlockSpec(memory_space=pl.ANY)] * len(fetched)
+    scratch = []
+    for array in fetched:
+        scratch += [pltpu.VMEM(array.shape, array.dtype), pltpu.SemaphoreType.DMA((array.shape[0],))]
     return pl.pallas_call(
         functools.partial(kernel, **static),
         out_shape=out_shape,
-        in_specs=[SMEM_SPEC] * len(scalars) + [VMEM_SPEC] * len(arrays),
+        in_specs=specs,
         out_specs=jax.tree.map(lambda _: VMEM_SPEC, out_shape),
+        scratch_shapes=scratch,
         compiler_params=pltpu.CompilerParams(vmem_limit_bytes=16 << 20),
-    )(*scalars, *arrays)
+    )(*scalars, *arrays, *fetched)
+
+
+def fetch(array, held, semaphores):
+    pieces = [
+        pltpu.make_async_copy(array.at[x], held.at[x], semaphores.at[x])
+        for x in range(array.shape[0])
+    ]
+    for piece in pieces:
+        piece.start()
+    return pieces
 
 
 def arrived(parts, f):
@@ -96,30 +112,54 @@
     return jax.ShapeDtypeStruct(dims, dtype)
 
 
-def first_kernel(parts, mask, pivots, out, scaled):
-    for f in range(parts.shape[1]):
-        solved = arrived(parts, f) * mask[f]
-        scaled[f] = solved * pivots[f]
-        write_copies(out, f, solved)
-
-
-def first_solved(parts, mask, pivots):
-    shape = parts.shape[1:]
-    out = (shape_of(NEAR, *shape), shape_of(*shape, dtype=F32))
-    return call(first_kernel, out, [], [parts, mask, pivots[:, None, :]])
-
-
-def first_update_kernel(parts, coupling, out):
-    for f in range(coupling.shape[0]):
-        pieces = [parts[x, f].astype(F32) for x in range(NEAR)]
+def total_kernel(parts, out):
+    terms = [parts[i].astype(F32) for i in range(parts.shape[0])]
+    while len(terms) > 1:
+        terms = [terms[i] + terms[i + 1] for i in range(0, len(terms), 2)]
+    value = terms[0].astype(BF16)
+    for i in range(out.shape[0]):
+        out[i] = value
+
+
+def relay_pieces(parts):
+    return call(total_kernel, shape_of(*parts.shape), [], [parts])
+
+
+def first_update_kernel(near, parts, mask, pivots, coupling, out, scaled):
+    fronts = coupling.shape[0]
+    pieces = parts.shape[0] // fronts
+    share = pieces // NEAR
+    for f in range(fronts):
+        solved = [parts[f * pieces + g].astype(F32) for g in range(pieces)]
+        operand = (jnp.concatenate(solved, axis=0) * mask[f]).astype(BF16)
+        write_copies(out, f, dot(operand, coupling[f], ((1,), (1,))))
+        first = f * pieces + near[0] * share
+        solved = [parts[first + g].astype(F32) for g in range(share)]
+        scaled[f] = jnp.concatenate(solved, axis=0) * mask[f] * pivots[f]
+
+
+def first_update(near, parts, mask, pivots, coupling):
+    fronts, count, solved = coupling.shape
+    rhs = parts.shape[0] * parts.shape[1] // fronts
+    out = (
+        shape_of(lax.axis_size("row"), fronts, rhs, count),
+        shape_of(fronts, rhs // NEAR, solved, dtype=F32),
+    )
+    return call(first_update_kernel, out, [near], [parts, mask, pivots[:, None, :], coupling])
+
+
+def last_kernel(got, inverse, out):
+    count = inverse.shape[1]
+    for f in range(inverse.shape[0]):
+        pieces = [got[x, :, f * count : (f + 1) * count].astype(F32) for x in range(NEAR)]
         operand = jnp.concatenate(pieces, axis=0).astype(BF16)
-        write_copies(out, f, dot(operand, coupling[f], ((1,), (1,))))
-
-
-def first_update(parts, coupling):
-    fronts, count, _ = coupling.shape
-    out = shape_of(lax.axis_size("row"), fronts, NEAR * parts.shape[2], count)
-    return call(first_update_kernel, out, [], [parts, coupling])
+        write_copies(out, f, dot(operand, inverse[f], ((1,), (0,))))
+
+
+def last_product(got, inverse):
+    fronts, _, n = inverse.shape
+    out = shape_of(lax.axis_size("row"), fronts, NEAR * got.shape[1], n)
+    return call(last_kernel, out, [], [got, inverse])
 
 
 def scatter_kernel(parts, out):
@@ -179,7 +219,8 @@
     return call(solved_kernel, out, [], [parts, mask])
 
 
-def place_kernel(table, whole, source, mask, inverse, out, *, base):
+def place_kernel(table, whole, source, mask, inverse_at, out, inverse, semaphores, *, base):
+    copies = fetch(inverse_at, inverse, semaphores)
     n = inverse.shape[2]
     held = n // BLOCK
     count = out.shape[3]
@@ -203,6 +244,8 @@
                     tile = tile - placed.astype(F32) * found
                 tiles.append(tile)
             operand = jnp.concatenate(tiles, axis=-1) * mask[p, :, x * n : (x + 1) * n]
+            if p == 0:
+                copies[x].wait()
             rows = inverse[x, p * count : (p + 1) * count]
             part = dot(operand.astype(BF16), rows, ((1,), (1,)))
             total = part if total is None else total + part
@@ -211,18 +254,22 @@
 
 def place_and_solve(table, whole, source, mask, inverse, parents, count, base):
     out = shape_of(far_size(), parents, whole.shape[2], count)
-    return call(place_kernel, out, [table], [whole, source, mask, inverse], base=base)
-
-
-def root_kernel(parts, pivots, inverse, out):
+    return call(place_kernel, out, [table], [whole, source, mask], [inverse], base=base)
+
+
+def root_kernel(parts, pivots, inverse_at, out, inverse, semaphores):
+    copies = fetch(inverse_at, inverse, semaphores)
     operand = (arrived(parts, 0) * pivots[...]).astype(BF16)
-    pieces = [dot(operand, inverse[x], ((1,), (0,))) for x in range(NEAR)]
+    pieces = []
+    for x in range(NEAR):
+        copies[x].wait()
+        pieces.append(dot(operand, inverse[x], ((1,), (0,))))
     write_copies(out, 0, jnp.concatenate(pieces, axis=-1))
 
 
 def root_back(parts, pivots, inverse):
     out = shape_of(lax.axis_size("row"), 1, parts.shape[2], NEAR * inverse.shape[2])
-    return call(root_kernel, out, [], [parts, pivots[None, :], inverse])
+    return call(root_kernel, out, [], [parts, pivots[None, :]], [inverse])
 
 
 def back_kernel(parts, scaled, mask, inverse, out):
@@ -264,10 +311,6 @@
 def halves(value):
     high = value.astype(BF16)
     return high, (value - high.astype(F32)).astype(BF16)
-
-
-def by_near(value):
-    return value.reshape(NEAR, value.shape[0] // NEAR, value.shape[1])
 
 
 def local(
@@ -296,16 +339,7 @@
     k1, k2 = inverse_mid.shape[1], inverse_low.shape[1]
     top = jnp.full((1,), inverse_top.shape[0] * lax.axis_size("row"), jnp.int32)
 
-    others = jnp.concatenate([source_mid[0].T, source_mid[1].T, source_top.T], axis=-1)
-    halved = jnp.concatenate(halves(others), axis=-1).reshape(-1, n1)
-    packed = jnp.concatenate([inverse_mid.reshape(-1, n1), halved], axis=0)
-    packed, coupling_mid = lax.optimization_barrier((packed, coupling_mid))
-    packed_near = gather_near(packed)
-    coupling_mid_near = gather_near(coupling_mid)
-    inverse_top_near = gather_near(inverse_top)
-    coupling_low_near = gather_near(coupling_low)
-
-    far = far_at.reshape(1)
+    far, near = far_at.reshape(1), (col_at % NEAR).reshape(1)
     table_low = update_table(blocks_low, far_at, n1 // BLOCK)
     table_mid = update_table(blocks_mid, far_at, n0 // BLOCK)
     row_mask_mid = level_mask(sizes_mid, k1, row_at * k1)
@@ -316,22 +350,35 @@
 
     source = jnp.swapaxes(source_low, 1, 2) * col_mask_low
     partial = jnp.einsum(
-        "fij,fcj->cfi", inverse_low, source.astype(BF16), preferred_element_type=F32
-    ).reshape(rhs, -1)
-    got = swap_near(by_near(partial.astype(BF16))).astype(F32)
-    partial = jnp.swapaxes(jnp.sum(got, axis=0).reshape(width, -1, k2), 0, 1)
-    parts = send_far(copies_of(partial, far_size()))
-    message, scaled_low = first_solved(parts, row_mask_low, pivots_low)
-    message = first_update(swap_near(message), coupling_low)
+        "fij,fcj->fci", inverse_low, source.astype(BF16), preferred_element_type=F32
+    )
+    message = partial.astype(BF16).reshape(lax.axis_size("col"), -1, k2)
+
+    coupling_mid_near = gather_near(coupling_mid)
+    inverse_mid, source_mid, source_top, message = lax.optimization_barrier(
+        (inverse_mid, source_mid, source_top, message)
+    )
+    others = jnp.concatenate([source_mid[0].T, source_mid[1].T, source_top.T], axis=-1)
+    halved = jnp.concatenate(halves(others), axis=-1).reshape(-1, n1)
+    packed = jnp.concatenate([inverse_mid.reshape(-1, n1), halved], axis=0)
+    packed, inverse_top, coupling_low_late = lax.optimization_barrier(
+        (packed, inverse_top, coupling_low)
+    )
+    packed_near = gather_near(packed)
+    inverse_top_near = gather_near(inverse_top)
+    coupling_low_near = gather_near(coupling_low_late)
+
+    parts = send_col(relay_pieces(send_col(message)))
+    message, scaled_low = first_update(near, parts, row_mask_low, pivots_low, coupling_low)
     whole = send_col(relay_scattered(send_row(message)))
 
     halved = packed_near[:, 2 * k1 :].reshape(NEAR, rhs, -1)
     halved = lax.dynamic_slice_in_dim(halved, (col_at % NEAR) * width, width, 1).astype(F32)
     size = halved.shape[2] // 2
     others = halved[:, :, :size] + halved[:, :, size:]
-    parts = send_far(
-        place_and_solve(table_low, whole, others, wide_mask_mid, packed_near, 2, k1, 0)
-    )
+    message = place_and_solve(table_low, whole, others, wide_mask_mid, packed_near, 2, k1, 0)
+    coupling_mid_near, message = lax.optimization_barrier((coupling_mid_near, message))
+    parts = send_far(message)
 
     message, scaled_mid = update_of(parts, row_mask_mid, pivots_mid, coupling_mid_near)
     whole = send_far(relay(send_row(message)))
@@ -343,7 +390,9 @@
     message, solution_top = relay_solved(
         send_row(root_back(parts, pivots_top, inverse_top_near)), wide_mask_top
     )
-    parts = send_far(pick_and_carry(far, blocks_mid, send_far(message), coupling_mid_near))
+    message = pick_and_carry(far, blocks_mid, send_far(message), coupling_mid_near)
+    coupling_low_near, message = lax.optimization_barrier((coupling_low_near, message))
+    parts = send_far(message)
     message, solution_mid = relay_solved(
         send_row(back(parts, scaled_mid, row_mask_mid, packed_near)), wide_mask_mid
     )
@@ -362,12 +411,10 @@
     flat = jnp.swapaxes(residual, 0, 1).reshape(width, -1).astype(BF16)
     size = flat.shape[1]
     message = jnp.concatenate([copies_of(flat, NEAR), upper], axis=-1)
-    got = swap_near(message).reshape(rhs, -1)
-    upper = got[:, size:].astype(F32)
+    got = swap_near(message)
+    parts = send_row(last_product(got, inverse_low))
+    upper = got[:, :, size:].astype(F32).reshape(rhs, -1)
     upper = upper[:, : upper.shape[1] // 2] + upper[:, upper.shape[1] // 2 :]
-    residual = got[:, :size].reshape(rhs, -1, k2)
-    partial = jnp.einsum("fij,cfi->fcj", inverse_low, residual, preferred_element_type=F32)
-    parts = send_row(copies_of(partial, lax.axis_size("row")))
     solution_low = jnp.sum(parts.astype(F32), axis=0) * col_mask_low
     return (
         upper[:, :n0].T,

time: 278 us -> 281 us (1.011)
  Pallas kernels: 11.7 us -> 15.9 us
    all_to_all x1 -> x3, starting transfers between devices: 3.98 us -> 21.6 us  [send_col(): return lax.all_to_all(copies, 'col', 0, 0, tiled=True)]
    all_to_all x1 -> x3, waiting for transfers between devices: 9.3 us -> 26 us  [send_col(): return lax.all_to_all(copies, 'col', 0, 0, tiled=True)]
    all_to_all x6 -> x5, starting transfers between devices: 26.9 us -> 16.9 us  [send_far(): lax.all_to_all(copies, 'col', 0, 0, axis_index_groups=groups, tiled=True)]
    all_to_all x2 -> x0, waiting for transfers between devices: 8.81 us -> none  [swap_near(): lax.all_to_all(pieces, 'col', 0, 0, axis_index_groups=near_groups(), tile...]
    all_to_all x2 -> x0, starting transfers between devices: 8.13 us -> none  [swap_near(): lax.all_to_all(pieces, 'col', 0, 0, axis_index_groups=near_groups(), tile...]
    all_to_all x6 -> x5, waiting for transfers between devices: 42.9 us -> 37 us  [send_far(): lax.all_to_all(copies, 'col', 0, 0, axis_index_groups=groups, tiled=True)]
    pallas_call x13 -> x14, Pallas kernels: 11.7 us -> 15.9 us  [call(): pl.pallas_call(functools.partial(kernel, **static), out_shape=out_shape,...]
    all_to_all x4, starting transfers between devices: 28 us -> 31.2 us  [send_row(): return lax.all_to_all(copies, 'row', 0, 0, tiled=True)]
  transfers between devices with their start and end apart: 17 -> 16, of which waited for: 14 -> 13; matrix products, arithmetic and copies ran while one was open for 2% -> 1% of each run, Pallas kernels for 4% -> 4%
where the time goes in v7:
time: 281 us; the launch traced here: 279 us
  waiting for transfers between devices  115 us (41%)
  starting transfers between devices  69.8 us (25%)
  blocking collectives  45.5 us (16%)
  Pallas kernels  15.9 us (6%)
  between operations  14.2 us (5%)
  local copies, waits for them, and re-layouts  11.3 us (4%)
  other arithmetic  5.66 us (2%)
    all_to_all x4, waiting for transfers between devices, send_row(): return lax.all_to_all(copies, 'row', 0, 0, tiled=True)  48.1 us
    all_to_all x5, waiting for transfers between devices, send_far(): lax.all_to_all(copies, 'col', 0, 0, axis_index_groups=groups, tiled=True)  37 us
    all_to_all x4, starting transfers between devices, send_row(): return lax.all_to_all(copies, 'row', 0, 0, tiled=True)  31.2 us
    all_to_all x3, waiting for transfers between devices, send_col(): return lax.all_to_all(copies, 'col', 0, 0, tiled=True)  26 us
    all_to_all x3, starting transfers between devices, send_col(): return lax.all_to_all(copies, 'col', 0, 0, tiled=True)  21.6 us
    all_to_all x2, blocking collectives, send_far(): lax.all_to_all(copies, 'col', 0, 0, axis_index_groups=groups, tiled=True)  20.8 us
    all_to_all x1, blocking collectives, send_row(): return lax.all_to_all(copies, 'row', 0, 0, tiled=True)  17.3 us
    all_to_all x5, starting transfers between devices, send_far(): lax.all_to_all(copies, 'col', 0, 0, axis_index_groups=groups, tiled=True)  16.9 us
  transfers between devices with their start and end apart: 16, of which 13 were waited for; matrix products, arithmetic and copies ran while one was open for 1% of the time, Pallas kernels for 4%

profile of v7, /device:TPU:1, one launch (start us, length us, event | category | flops | bytes accessed | tf_op | source)
XLA Modules:
  0.0 279.3 jit_solution(543437982551563615)
XLA Ops:
  7.2 0.8 compare_convert_fusion.5
  8.0 1.6 convolution_convert_fusion
  9.7 0.7 reshape.232
  10.3 0.7 slice_bitcast_fusion.4
  11.1 0.7 fusion
  11.8 0.7 subtract_convert_fusion.1
  12.7 0.9 pad_maximum_fusion
  13.7 0.7 all-gather.11.cloned.1.call-update
  14.4 0.7 all-gather.15.cloned.1.call-update
  15.1 13.7 %all-to-all-start = ((bf16[32,2,512]{2,1,0:T(2,128)(2,1)}), bf16[32,2,512]{2,1,0:T(2,128)(2,1)S(1)}, u32[]{:S(2)}, u32[]{:S(2)}) async-start(bf16[32,2,512]{2,1,0:T(2,128)(2,1)} %reshape.232), calls=%async_computation | async-start | bytes 131072 | tf_op jit(solution)/shard_map/all_to_all | solution.py:60
  28.9 0.5 all-gather.9.cloned.1.call-update
  29.5 8.1 %all-to-all-done.parts = bf16[32,2,512]{2,1,0:T(2,128)(2,1)S(1)} async-done(((bf16[32,2,512]{2,1,0:T(2,128)(2,1)}), bf16[32,2,512]{2,1,0:T(2,128)(2,1)S(1)}, u32[]{:S(2)}, u32[]{:S(2)}) %all-to-all-start) | async-done | bytes 65568 | tf_op jit(solution)/shard_map/all_to_all | solution.py:60
  37.6 0.7 shard_map.166
  38.3 3.9 %all-to-all-start.1 = ((bf16[32,2,512]{2,1,0:T(2,128)(2,1)}), bf16[32,2,512]{2,1,0:T(2,128)(2,1)S(1)}, u32[]{:S(2)}, u32[]{:S(2)}) async-start(bf16[32,2,512]{2,1,0:T(2,128)(2,1)} %shard_map.166), calls=%async_computation.1 | async-start | bytes 131072 | tf_op jit(solution)/shard_map/all_to_all | solution.py:60
  42.2 0.2 select_reduce_fusion
  42.5 8.6 %all-to-all-done.1.parts = bf16[32,2,512]{2,1,0:T(2,128)(2,1)S(1)} async-done(((bf16[32,2,512]{2,1,0:T(2,128)(2,1)}), bf16[32,2,512]{2,1,0:T(2,128)(2,1)S(1)}, u32[]{:S(2)}, u32[]{:S(2)}) %all-to-all-start.1) | async-done | bytes 65568 | tf_op jit(solution)/shard_map/all_to_all | solution.py:60
  51.1 1.0 shard_map.167
  52.1 10.4 %all-to-all-start.2 = ((bf16[16,4,16,128]{3,2,1,0:T(8,128)(2,1)}), bf16[16,4,16,128]{3,2,1,0:T(8,128)(2,1)S(1)}, u32[]{:S(2)}, u32[]{:S(2)}) async-start(bf16[16,4,16,128]{3,2,1,0:T(8,128)(2,1)} %get-tuple-element.28), calls=%async_computation.2 | async-start | bytes 524288 | tf_op jit(solution)/shard_map/all_to_all | solution.py:50
  62.5 11.6 %all-to-all-done.2.parts = bf16[16,4,16,128]{3,2,1,0:T(8,128)(2,1)S(1)} async-done(((bf16[16,4,16,128]{3,2,1,0:T(8,128)(2,1)}), bf16[16,4,16,128]{3,2,1,0:T(8,128)(2,1)S(1)}, u32[]{:S(2)}, u32[]{:S(2)}) %all-to-all-start.2) | async-done | bytes 262176 | tf_op jit(solution)/shard_map/all_to_all | solution.py:50
  74.1 0.7 shard_map.168
  74.8 4.0 %all-to-all-start.3 = ((bf16[32,4,4,128]{3,2,1,0:T(4,128)(2,1)}), bf16[32,4,4,128]{3,2,1,0:T(4,128)(2,1)S(1)}, u32[]{:S(2)}, u32[]{:S(2)}) async-start(bf16[32,4,4,128]{3,2,1,0:T(4,128)(2,1)} %shard_map.168), calls=%async_computation.3 | async-start | bytes 262144 | tf_op jit(solution)/shard_map/all_to_all | solution.py:60
  78.9 1.0 slice.52
  79.8 0.2 reshape.236
  80.1 9.3 %all-to-all-done.3.whole = bf16[32,4,4,128]{3,2,1,0:T(4,128)(2,1)S(1)} async-done(((bf16[32,4,4,128]{3,2,1,0:T(4,128)(2,1)}), bf16[32,4,4,128]{3,2,1,0:T(4,128)(2,1)S(1)}, u32[]{:S(2)}, u32[]{:S(2)}) %all-to-all-start.3) | async-done | bytes 131104 | tf_op jit(solution)/shard_map/all_to_all | solution.py:60
  89.4 1.7 copy-done
  91.1 2.4 shard_map.169
  93.5 3.4 %all-to-all-start.4 = ((bf16[8,2,4,512]{3,2,1,0:T(4,128)(2,1)}), bf16[8,2,4,512]{3,2,1,0:T(4,128)(2,1)S(1)}, u32[]{:S(2)}, u32[]{:S(2)}) async-start(bf16[8,2,4,512]{3,2,1,0:T(4,128)(2,1)} %shard_map.169), calls=%async_computation.4 | async-start | bytes 131072 | tf_op jit(solution)/shard_map/all_to_all | solution.py:46
  97.0 7.1 %all-to-all-done.4.parts = bf16[8,2,4,512]{3,2,1,0:T(4,128)(2,1)S(1)} async-done(((bf16[8,2,4,512]{3,2,1,0:T(4,128)(2,1)}), bf16[8,2,4,512]{3,2,1,0:T(4,128)(2,1)S(1)}, u32[]{:S(2)}, u32[]{:S(2)}) %all-to-all-start.4) | async-done | bytes 65568 | tf_op jit(solution)/shard_map/all_to_all | solution.py:46
  104.0 1.2 copy-done.5
  105.3 1.0 shard_map.170
  106.3 9.3 %all-to-all-start.5 = ((bf16[16,2,4,512]{3,2,1,0:T(4,128)(2,1)}), bf16[16,2,4,512]{3,2,1,0:T(4,128)(2,1)S(1)}, u32[]{:S(2)}, u32[]{:S(2)}) async-start(bf16[16,2,4,512]{3,2,1,0:T(4,128)(2,1)} %get-tuple-element.32), calls=%async_computation.5 | async-start | bytes 262144 | tf_op jit(solution)/shard_map/all_to_all | solution.py:50
  115.7 0.3 fusion.3
  116.1 8.7 %all-to-all-done.5.parts = bf16[16,2,4,512]{3,2,1,0:T(4,128)(2,1)S(1)} async-done(((bf16[16,2,4,512]{3,2,1,0:T(4,128)(2,1)}), bf16[16,2,4,512]{3,2,1,0:T(4,128)(2,1)S(1)}, u32[]{:S(2)}, u32[]{:S(2)}) %all-to-all-start.5) | async-done | bytes 131104 | tf_op jit(solution)/shard_map/all_to_all | solution.py:50
  124.8 0.7 shard_map.171
  125.5 3.4 %all-to-all-start.6 = ((bf16[8,2,4,512]{3,2,1,0:T(4,128)(2,1)}), bf16[8,2,4,512]{3,2,1,0:T(4,128)(2,1)S(1)}, u32[]{:S(2)}, u32[]{:S(2)}) async-start(bf16[8,2,4,512]{3,2,1,0:T(4,128)(2,1)} %shard_map.171), calls=%async_computation.6 | async-start | bytes 131072 | tf_op jit(solution)/shard_map/all_to_all | solution.py:46
  128.8 2.2 all-gather.15.cloned.1.call-done
  131.1 5.5 %all-to-all-done.6.whole = bf16[8,2,4,512]{3,2,1,0:T(4,128)(2,1)S(1)} async-done(((bf16[8,2,4,512]{3,2,1,0:T(4,128)(2,1)}), bf16[8,2,4,512]{3,2,1,0:T(4,128)(2,1)S(1)}, u32[]{:S(2)}, u32[]{:S(2)}) %all-to-all-start.6) | async-done | bytes 65568 | tf_op jit(solution)/shard_map/all_to_all | solution.py:46
  136.6 1.7 copy-done.2
  138.2 2.7 shard_map.172
  141.0 3.4 %all-to-all-start.7 = ((bf16[8,1,4,768]{3,2,1,0:T(4,128)(2,1)}), bf16[8,1,4,768]{3,2,1,0:T(4,128)(2,1)S(1)}, u32[]{:S(2)}, u32[]{:S(2)}) async-start(bf16[8,1,4,768]{3,2,1,0:T(4,128)(2,1)} %shard_map.172), calls=%async_computation.7 | async-start | bytes 98304 | tf_op jit(solution)/shard_map/all_to_all | solution.py:46
  144.4 6.9 %all-to-all-done.7.parts = bf16[8,1,4,768]{3,2,1,0:T(4,128)(2,1)S(1)} async-done(((bf16[8,1,4,768]{3,2,1,0:T(4,128)(2,1)}), bf16[8,1,4,768]{3,2,1,0:T(4,128)(2,1)S(1)}, u32[]{:S(2)}, u32[]{:S(2)}) %all-to-all-start.7) | async-done | bytes 49184 | tf_op jit(solution)/shard_map/all_to_all | solution.py:46
  151.3 1.7 copy-done.3
  153.0 1.4 shard_map.173
  154.4 17.3 %all_to_all.80.parts = bf16[16,1,4,1536]{3,2,1,0:T(4,128)(2,1)S(1)} all-to-all(bf16[16,1,4,1536]{3,2,1,0:T(4,128)(2,1)S(1)} %shard_map.173), channel_id=1, replica_groups=mesh['row'=16,'col'=32] {'row'}, dimensions={0} | all-to-all | bytes 393216 | tf_op jit(solution)/shard_map/all_to_all | solution.py:50
  171.7 11.3 %all_to_all.81.whole = bf16[8,1,4,1536]{3,2,1,0:T(4,128)(2,1)S(1)} all-to-all(bf16[8,1,4,1536]{3,2,1,0:T(4,128)(2,1)S(1)} %get-tuple-element.34), channel_id=1, replica_groups={{0,4,8,12,16,20,24,28},{1,5,9,13,17,21,25,29},{2,6,10,14,18,22,26,30},{..., dimensions={0} | all-to-all | bytes 196608 | tf_op jit(solution)/shard_map/all_to_all | solution.py:46
  183.0 0.8 shard_map.175
  183.8 9.5 %all_to_all.82.parts = bf16[8,2,4,512]{3,2,1,0:T(4,128)(2,1)S(1)} all-to-all(bf16[8,2,4,512]{3,2,1,0:T(4,128)(2,1)S(1)} %shard_map.175), channel_id=1, replica_groups={{0,4,8,12,16,20,24,28},{1,5,9,13,17,21,25,29},{2,6,10,14,18,22,26,30},{..., dimensions={0} | all-to-all | bytes 131072 | tf_op jit(solution)/shard_map/all_to_all | solution.py:46
  193.3 1.1 shard_map.176
  194.4 5.0 %all-to-all-start.11 = ((bf16[16,2,4,1024]{3,2,1,0:T(4,128)(2,1)}), bf16[16,2,4,1024]{3,2,1,0:T(4,128)(2,1)S(1)}, u32[]{:S(2)}, u32[]{:S(2)}) async-start(bf16[16,2,4,1024]{3,2,1,0:T(4,128)(2,1)} %shard_map.176), calls=%async_computation.11 | async-start | bytes 524288 | tf_op jit(solution)/shard_map/all_to_all | solution.py:50
  199.5 11.8 %all-to-all-done.11.parts = bf16[16,2,4,1024]{3,2,1,0:T(4,128)(2,1)S(1)} async-done(((bf16[16,2,4,1024]{3,2,1,0:T(4,128)(2,1)}), bf16[16,2,4,1024]{3,2,1,0:T(4,128)(2,1)S(1)}, u32[]{:S(2)}, u32[]{:S(2)}) %all-to-all-start.11) | async-done | bytes 262176 | tf_op jit(solution)/shard_map/all_to_all | solution.py:50
  211.3 0.7 shard_map.177
  212.0 3.5 %all-to-all-start.12 = ((bf16[8,2,4,1024]{3,2,1,0:T(4,128)(2,1)}), bf16[8,2,4,1024]{3,2,1,0:T(4,128)(2,1)S(1)}, u32[]{:S(2)}, u32[]{:S(2)}) async-start(bf16[8,2,4,1024]{3,2,1,0:T(4,128)(2,1)} %get-tuple-element.37), calls=%async_computation.12 | async-start | bytes 262144 | tf_op jit(solution)/shard_map/all_to_all | solution.py:46
  215.5 9.3 %all-to-all-done.12.whole = bf16[8,2,4,1024]{3,2,1,0:T(4,128)(2,1)S(1)} async-done(((bf16[8,2,4,1024]{3,2,1,0:T(4,128)(2,1)}), bf16[8,2,4,1024]{3,2,1,0:T(4,128)(2,1)S(1)}, u32[]{:S(2)}, u32[]{:S(2)}) %all-to-all-start.12) | async-done | bytes 131104 | tf_op jit(solution)/shard_map/all_to_all | solution.py:46
  224.8 1.6 copy-done.7
  226.4 1.6 shard_map.178
  228.0 3.4 %all-to-all-start.13 = ((bf16[8,4,4,512]{3,2,1,0:T(4,128)(2,1)}), bf16[8,4,4,512]{3,2,1,0:T(4,128)(2,1)S(1)}, u32[]{:S(2)}, u32[]{:S(2)}) async-start(bf16[8,4,4,512]{3,2,1,0:T(4,128)(2,1)} %shard_map.178), calls=%async_computation.13 | async-start | bytes 262144 | tf_op jit(solution)/shard_map/all_to_all | solution.py:46
  231.5 8.2 %all-to-all-done.13 = bf16[8,4,4,512]{3,2,1,0:T(4,128)(2,1)S(1)} async-done(((bf16[8,4,4,512]{3,2,1,0:T(4,128)(2,1)}), bf16[8,4,4,512]{3,2,1,0:T(4,128)(2,1)S(1)}, u32[]{:S(2)}, u32[]{:S(2)}) %all-to-all-start.13) | async-done | bytes 131104 | tf_op jit(solution)/shard_map/all_to_all | solution.py:46
  239.8 7.4 %all_to_all.83.got = bf16[4,4,3840]{2,1,0:T(4,128)(2,1)S(1)} all-to-all(bf16[4,4,3840]{2,1,0:T(4,128)(2,1)S(1)} %pad_maximum_fusion.1), channel_id=1, replica_groups={{0,1,2,3},{4,5,6,7},{8,9,10,11},{12,13,14,15},{16,17,18,19},{20,21,22,2..., dimensions={0} | all-to-all | bytes 245760 | tf_op jit(solution)/shard_map/all_to_all | solution.py:29
  247.2 1.1 shard_map.179
  248.3 6.5 %all-to-all-start.15 = ((bf16[16,4,16,256]{3,2,1,0:T(8,128)(2,1)}), bf16[16,4,16,256]{3,2,1,0:T(8,128)(2,1)S(1)}, u32[]{:S(2)}, u32[]{:S(2)}) async-start(bf16[16,4,16,256]{3,2,1,0:T(8,128)(2,1)} %shard_map.179), calls=%async_computation.15 | async-start | bytes 1048576 | tf_op jit(solution)/shard_map/all_to_all | solution.py:50
  254.8 0.6 pad_maximum_fusion.5
  255.5 0.6 slice_bitcast_fusion
  256.1 16.0 %all-to-all-done.15 = bf16[16,4,16,256]{3,2,1,0:T(8,128)(2,1)S(1)} async-done(((bf16[16,4,16,256]{3,2,1,0:T(8,128)(2,1)}), bf16[16,4,16,256]{3,2,1,0:T(8,128)(2,1)S(1)}, u32[]{:S(2)}, u32[]{:S(2)}) %all-to-all-start.15) | async-done | bytes 524320 | tf_op jit(solution)/shard_map/all_to_all | solution.py:50
  272.2 0.6 multiply_bitcast_fusion
  (72 shorter events, 1.3 us)
Async XLA Ops:
  7.2 5.5 %copy-start.11 = (bf16[2,512,256]{2,1,0:T(8,128)(2,1)S(1)}, bf16[2,512,256]{2,1,0:T(8,128)(2,1)}, u32[]{:S(2)}) copy-start(bf16[2,512,256]{2,1,0:T(8,128)(2,1)} %param.16) | copy-start | bytes 1572868
  7.2 71.7 %all-gather.13.cloned.1.call-start = ((), (), s32[]{:S(2)}) async-start(), calls=%async_computation.18 | async-start | bytes 2908160 | tf_op jit(solution)/shard_map/all_gather | solution.py:37
  9.6 19.8 %copy-start.13 = (s32[4]{0:T(128)S(1)}, s32[4]{0:T(128)}, u32[]{:S(2)}) copy-start(s32[4]{0:T(128)} %param.27) | copy-start | bytes 52
  9.6 32.6 %copy-start.12 = (f32[4,512]{1,0:T(4,128)S(1)}, f32[4,512]{1,0:T(4,128)}, u32[]{:S(2)}) copy-start(f32[4,512]{1,0:T(4,128)} %param.25) | copy-start | bytes 24580
  9.7 32.6 %copy-start.9 = (s32[4,32]{1,0:T(4,128)S(1)}, s32[4,32]{1,0:T(4,128)}, u32[]{:S(2)}) copy-start(s32[4,32]{1,0:T(4,128)} %blocks.3) | copy-start | bytes 1540
  9.7 41.4 %copy-start.8 = (bf16[4,128,512]{2,1,0:T(8,128)(2,1)S(1)}, bf16[4,128,512]{2,1,0:T(8,128)(2,1)}, u32[]{:S(2)}) copy-start(bf16[4,128,512]{2,1,0:T(8,128)(2,1)} %coupling.1) | copy-start | bytes 1572868
  12.7 49.8 %copy-start.16 = (s32[2]{0:T(128)S(1)}, s32[2]{0:T(128)}, u32[]{:S(2)}) copy-start(s32[2]{0:T(128)} %param.26) | copy-start | bytes 28
  13.6 79.9 %all-gather.11.cloned.1.call-start = ((), (), s32[]{:S(2)}) async-start(), calls=%async_computation.17 | async-start | bytes 1310720 | tf_op jit(solution)/shard_map/all_gather | solution.py:37
  14.4 116.7 %all-gather.15.cloned.1.call-start = ((), (), s32[]{:S(2)}) async-start(), calls=%async_computation.19 | async-start | bytes 2949120 | tf_op jit(solution)/shard_map/all_gather | solution.py:37
  15.1 22.6 %all-to-all-start = ((bf16[32,2,512]{2,1,0:T(2,128)(2,1)}), bf16[32,2,512]{2,1,0:T(2,128)(2,1)S(1)}, u32[]{:S(2)}, u32[]{:S(2)}) async-start(bf16[32,2,512]{2,1,0:T(2,128)(2,1)} %reshape.232), calls=%async_computation | async-start | bytes 131072 | tf_op jit(solution)/shard_map/all_to_all | solution.py:60
  28.8 155.0 %all-gather.9.cloned.1.call-start = ((), (), s32[]{:S(2)}) async-start(), calls=%async_computation.16 | async-start | bytes 2621440 | tf_op jit(solution)/shard_map/all_gather | solution.py:37
  38.3 12.7 %all-to-all-start.1 = ((bf16[32,2,512]{2,1,0:T(2,128)(2,1)}), bf16[32,2,512]{2,1,0:T(2,128)(2,1)S(1)}, u32[]{:S(2)}, u32[]{:S(2)}) async-start(bf16[32,2,512]{2,1,0:T(2,128)(2,1)} %shard_map.166), calls=%async_computation.1 | async-start | bytes 131072 | tf_op jit(solution)/shard_map/all_to_all | solution.py:60
  52.1 22.1 %all-to-all-start.2 = ((bf16[16,4,16,128]{3,2,1,0:T(8,128)(2,1)}), bf16[16,4,16,128]{3,2,1,0:T(8,128)(2,1)S(1)}, u32[]{:S(2)}, u32[]{:S(2)}) async-start(bf16[16,4,16,128]{3,2,1,0:T(8,128)(2,1)} %get-tuple-element.28), calls=%async_computation.2 | async-start | bytes 524288 | tf_op jit(solution)/shard_map/all_to_all | solution.py:50
  74.8 22.1 %copy-start.15 = (f32[2,512]{1,0:T(2,128)S(1)}, f32[2,512]{1,0:T(2,128)}, u32[]{:S(2)}) copy-start(f32[2,512]{1,0:T(2,128)} %param.24) | copy-start | bytes 12292
  74.8 14.6 %all-to-all-start.3 = ((bf16[32,4,4,128]{3,2,1,0:T(4,128)(2,1)}), bf16[32,4,4,128]{3,2,1,0:T(4,128)(2,1)S(1)}, u32[]{:S(2)}, u32[]{:S(2)}) async-start(bf16[32,4,4,128]{3,2,1,0:T(4,128)(2,1)} %shard_map.168), calls=%async_computation.3 | async-start | bytes 262144 | tf_op jit(solution)/shard_map/all_to_all | solution.py:60
  89.4 1.7 copy-start
  91.1 24.6 %copy-start.10 = (s32[2,32]{1,0:T(2,128)S(1)}, s32[2,32]{1,0:T(2,128)}, u32[]{:S(2)}) copy-start(s32[2,32]{1,0:T(2,128)} %blocks.2) | copy-start | bytes 772
  93.5 10.5 %all-to-all-start.4 = ((bf16[8,2,4,512]{3,2,1,0:T(4,128)(2,1)}), bf16[8,2,4,512]{3,2,1,0:T(4,128)(2,1)S(1)}, u32[]{:S(2)}, u32[]{:S(2)}) async-start(bf16[8,2,4,512]{3,2,1,0:T(4,128)(2,1)} %shard_map.169), calls=%async_computation.4 | async-start | bytes 131072 | tf_op jit(solution)/shard_map/all_to_all | solution.py:46
  104.0 1.2 copy-start.5
  105.3 39.1 %copy-start.14 = (f32[768]{0:T(1024)S(1)}, f32[768]{0:T(1024)}, u32[]{:S(2)}) copy-start(f32[768]{0:T(1024)} %param.23) | copy-start | bytes 9220
  106.3 18.5 %all-to-all-start.5 = ((bf16[16,2,4,512]{3,2,1,0:T(4,128)(2,1)}), bf16[16,2,4,512]{3,2,1,0:T(4,128)(2,1)S(1)}, u32[]{:S(2)}, u32[]{:S(2)}) async-start(bf16[16,2,4,512]{3,2,1,0:T(4,128)(2,1)} %get-tuple-element.32), calls=%async_computation.5 | async-start | bytes 262144 | tf_op jit(solution)/shard_map/all_to_all | solution.py:50
  125.5 11.1 %all-to-all-start.6 = ((bf16[8,2,4,512]{3,2,1,0:T(4,128)(2,1)}), bf16[8,2,4,512]{3,2,1,0:T(4,128)(2,1)S(1)}, u32[]{:S(2)}, u32[]{:S(2)}) async-start(bf16[8,2,4,512]{3,2,1,0:T(4,128)(2,1)} %shard_map.171), calls=%async_computation.6 | async-start | bytes 131072 | tf_op jit(solution)/shard_map/all_to_all | solution.py:46
  136.6 1.7 copy-start.2
  138.2 44.8 %copy-start.6 = (bf16[8,128,512]{2,1,0:T(8,128)(2,1)S(1)}, bf16[8,128,512]{2,1,0:T(8,128)(2,1)}, u32[]{:S(2)}) copy-start(bf16[8,128,512]{2,1,0:T(8,128)(2,1)} %all-gather.11.cloned.1.call-done) | copy-start | bytes 3145732
  141.0 10.3 %all-to-all-start.7 = ((bf16[8,1,4,768]{3,2,1,0:T(4,128)(2,1)}), bf16[8,1,4,768]{3,2,1,0:T(4,128)(2,1)S(1)}, u32[]{:S(2)}, u32[]{:S(2)}) async-start(bf16[8,1,4,768]{3,2,1,0:T(4,128)(2,1)} %shard_map.172), calls=%async_computation.7 | async-start | bytes 98304 | tf_op jit(solution)/shard_map/all_to_all | solution.py:46
  144.4 49.0 %copy-start.1 = (bf16[4544,256]{1,0:T(8,128)(2,1)S(1)}, bf16[4544,256]{1,0:T(8,128)(2,1)}, u32[]{:S(2)}) copy-start(bf16[4544,256]{1,0:T(8,128)(2,1)} %all-gather.13.cloned.1.call-done) | copy-start | bytes 6979588
  151.3 1.7 copy-start.3
  194.4 16.8 %all-to-all-start.11 = ((bf16[16,2,4,1024]{3,2,1,0:T(4,128)(2,1)}), bf16[16,2,4,1024]{3,2,1,0:T(4,128)(2,1)S(1)}, u32[]{:S(2)}, u32[]{:S(2)}) async-start(bf16[16,2,4,1024]{3,2,1,0:T(4,128)(2,1)} %shard_map.176), calls=%async_computation.11 | async-start | bytes 524288 | tf_op jit(solution)/shard_map/all_to_all | solution.py:50
  212.0 35.2 %copy-start.4 = (bf16[4,512,256]{2,1,0:T(8,128)(2,1)S(1)}, bf16[4,512,256]{2,1,0:T(8,128)(2,1)}, u32[]{:S(2)}) copy-start(bf16[4,512,256]{2,1,0:T(8,128)(2,1)} %inverse.1) | copy-start | bytes 3145732
  212.0 12.8 %all-to-all-start.12 = ((bf16[8,2,4,1024]{3,2,1,0:T(4,128)(2,1)}), bf16[8,2,4,1024]{3,2,1,0:T(4,128)(2,1)S(1)}, u32[]{:S(2)}, u32[]{:S(2)}) async-start(bf16[8,2,4,1024]{3,2,1,0:T(4,128)(2,1)} %get-tuple-element.37), calls=%async_computation.12 | async-start | bytes 262144 | tf_op jit(solution)/shard_map/all_to_all | solution.py:46
  224.8 1.6 copy-start.7
  228.0 11.6 %all-to-all-start.13 = ((bf16[8,4,4,512]{3,2,1,0:T(4,128)(2,1)}), bf16[8,4,4,512]{3,2,1,0:T(4,128)(2,1)S(1)}, u32[]{:S(2)}, u32[]{:S(2)}) async-start(bf16[8,4,4,512]{3,2,1,0:T(4,128)(2,1)} %shard_map.178), calls=%async_computation.13 | async-start | bytes 262144 | tf_op jit(solution)/shard_map/all_to_all | solution.py:46
  248.3 23.8 %all-to-all-start.15 = ((bf16[16,4,16,256]{3,2,1,0:T(8,128)(2,1)}), bf16[16,4,16,256]{3,2,1,0:T(8,128)(2,1)S(1)}, u32[]{:S(2)}, u32[]{:S(2)}) async-start(bf16[16,4,16,256]{3,2,1,0:T(8,128)(2,1)} %shard_map.179), calls=%async_computation.15 | async-start | bytes 1048576 | tf_op jit(solution)/shard_map/all_to_all | solution.py:50
Sparse Core Ops, SparseCore 0:
  13.7 44.2 all-gather.12
  60.2 28.9 all-gather.10
  91.2 39.7 all-gather.14
  133.0 36.2 all-gather.8

commit v8 on v7

--- a/solution.py
+++ b/solution.py
@@ -75,13 +75,14 @@
     scratch = []
     for array in fetched:
         scratch += [pltpu.VMEM(array.shape, array.dtype), pltpu.SemaphoreType.DMA((array.shape[0],))]
+    limit = None if fetched else 16 << 20
     return pl.pallas_call(
         functools.partial(kernel, **static),
         out_shape=out_shape,
         in_specs=specs,
         out_specs=jax.tree.map(lambda _: VMEM_SPEC, out_shape),
         scratch_shapes=scratch,
-        compiler_params=pltpu.CompilerParams(vmem_limit_bytes=16 << 20),
+        compiler_params=pltpu.CompilerParams(vmem_limit_bytes=limit),
     )(*scalars, *arrays, *fetched)
 
 
@@ -93,6 +94,37 @@
     for piece in pieces:
         piece.start()
     return pieces
+
+
+def pack_kernel(others, inverse, out, held, semaphores):
+    rows, n = inverse.shape
+    first = pltpu.make_async_copy(inverse, out.at[pl.ds(0, rows)], semaphores.at[0])
+    first.start()
+    rhs = others.shape[0]
+    blocks = others.shape[1] // n
+    for k in range(blocks):
+        value = others[:, k * n : (k + 1) * n]
+        high = value.astype(BF16)
+        held[k * rhs : (k + 1) * rhs] = high
+        low = (value - high.astype(F32)).astype(BF16)
+        held[(blocks + k) * rhs : (blocks + k + 1) * rhs] = low
+    second = pltpu.make_async_copy(held, out.at[pl.ds(rows, held.shape[0])], semaphores.at[1])
+    second.start()
+    first.wait()
+    second.wait()
+
+
+def pack(others, inverse):
+    rows, n = inverse.shape
+    more = 2 * others.shape[0] * others.shape[1] // n
+    anywhere = pl.BlockSpec(memory_space=pl.ANY)
+    return pl.pallas_call(
+        pack_kernel,
+        out_shape=shape_of(rows + more, n),
+        in_specs=[VMEM_SPEC, anywhere],
+        out_specs=anywhere,
+        scratch_shapes=[pltpu.VMEM((more, n), BF16), pltpu.SemaphoreType.DMA((2,))],
+    )(others, inverse)
 
 
 def arrived(parts, f):
@@ -217,6 +249,13 @@
     shape = parts.shape[1:]
     out = (shape_of(far_size(), *shape), shape_of(*shape, dtype=F32))
     return call(solved_kernel, out, [], [parts, mask])
+
+
+def source_tile(source, x, start):
+    blocks, n = source.shape[1] // 2, source.shape[3]
+    k, lanes = start // n, slice(start % n, start % n + BLOCK)
+    high = source[x, k, :, lanes].astype(F32)
+    return high + source[x, blocks + k, :, lanes].astype(F32)
 
 
 def place_kernel(table, whole, source, mask, inverse_at, out, inverse, semaphores, *, base):
@@ -231,7 +270,7 @@
             tiles = []
             for b in range(held):
                 start = base + p * n + b * BLOCK
-                tile = source[x, :, start : start + BLOCK]
+                tile = source_tile(source, x, start)
                 for c in (2 * p, 2 * p + 1):
                     at = table[c, x * held + b]
                     found = jnp.where(at >= 0, 1.0, 0.0).astype(F32)
@@ -289,7 +328,7 @@
     return call(back_kernel, out, [], [parts, scaled, mask, inverse])
 
 
-def pick_kernel(far, blocks, whole, coupling, out):
+def pick_kernel(far, blocks, whole, coupling, out, copies=None):
     held = whole.shape[3] // BLOCK
     for c in range(blocks.shape[0]):
         total = None
@@ -297,6 +336,8 @@
             block = blocks[c, far[0] * NEAR + x]
             lane = pl.multiple_of((block % held) * BLOCK, BLOCK)
             tile = whole[block // held, c // 2, :, pl.ds(lane, BLOCK)]
+            if copies is not None and c == 0:
+                copies[x].wait()
             part = dot(tile, coupling[x, c], ((1,), (0,)))
             total = part if total is None else total + part
         write_copies(out, c, total)
@@ -306,6 +347,17 @@
     _, children, _, count = coupling.shape
     out = shape_of(far_size(), children, whole.shape[2], count)
     return call(pick_kernel, out, [far, blocks], [whole, coupling])
+
+
+def pick_fetched_kernel(far, blocks, whole, coupling_at, out, coupling, semaphores):
+    copies = fetch(coupling_at, coupling, semaphores)
+    pick_kernel(far, blocks, whole, coupling, out, copies)
+
+
+def pick_fetched(far, blocks, whole, coupling):
+    _, children, _, count = coupling.shape
+    out = shape_of(far_size(), children, whole.shape[2], count)
+    return call(pick_fetched_kernel, out, [far, blocks], [whole], [coupling])
 
 
 def halves(value):
@@ -359,8 +411,8 @@
         (inverse_mid, source_mid, source_top, message)
     )
     others = jnp.concatenate([source_mid[0].T, source_mid[1].T, source_top.T], axis=-1)
-    halved = jnp.concatenate(halves(others), axis=-1).reshape(-1, n1)
-    packed = jnp.concatenate([inverse_mid.reshape(-1, n1), halved], axis=0)
+    others = jnp.pad(others, ((0, 0), (0, -others.shape[1] % n1)))
+    packed = pack(others, inverse_mid.reshape(-1, n1))
     packed, inverse_top, coupling_low_late = lax.optimization_barrier(
         (packed, inverse_top, coupling_low)
     )
@@ -372,12 +424,9 @@
     message, scaled_low = first_update(near, parts, row_mask_low, pivots_low, coupling_low)
     whole = send_col(relay_scattered(send_row(message)))
 
-    halved = packed_near[:, 2 * k1 :].reshape(NEAR, rhs, -1)
-    halved = lax.dynamic_slice_in_dim(halved, (col_at % NEAR) * width, width, 1).astype(F32)
-    size = halved.shape[2] // 2
-    others = halved[:, :, :size] + halved[:, :, size:]
+    others = packed_near[:, 2 * k1 :].reshape(NEAR, -1, rhs, n1)
+    others = lax.dynamic_slice_in_dim(others, (col_at % NEAR) * width, width, 2)
     message = place_and_solve(table_low, whole, others, wide_mask_mid, packed_near, 2, k1, 0)
-    coupling_mid_near, message = lax.optimization_barrier((coupling_mid_near, message))
     parts = send_far(message)
 
     message, scaled_mid = update_of(parts, row_mask_mid, pivots_mid, coupling_mid_near)
@@ -391,12 +440,11 @@
         send_row(root_back(parts, pivots_top, inverse_top_near)), wide_mask_top
     )
     message = pick_and_carry(far, blocks_mid, send_far(message), coupling_mid_near)
-    coupling_low_near, message = lax.optimization_barrier((coupling_low_near, message))
     parts = send_far(message)
     message, solution_mid = relay_solved(
         send_row(back(parts, scaled_mid, row_mask_mid, packed_near)), wide_mask_mid
     )
-    parts = send_far(pick_and_carry(far, blocks_low, send_far(message), coupling_low_near))
+    parts = send_far(pick_fetched(far, blocks_low, send_far(message), coupling_low_near))
     residual = (scaled_low - jnp.sum(parts.astype(F32), axis=0)) * row_mask_low
 
     upper = jnp.concatenate(

time: 281 us -> 300 us (1.068)
  Pallas kernels: 15.9 us -> 39.9 us
  local copies, waits for them, and re-layouts: 11.3 us -> 8.27 us
  waiting for transfers between devices: 115 us -> 112 us
    pallas_call x0 -> x1, Pallas kernels: none -> 17.9 us  [pack(): pl.pallas_call(pack_kernel, out_shape=shape_of(rows + more, n), in_specs=...]
    pallas_call x14, Pallas kernels: 15.9 us -> 22.1 us  [call(): pl.pallas_call(functools.partial(kernel, **static), out_shape=out_shape,...]
    all_to_all x5, waiting for transfers between devices: 37 us -> 32.3 us  [send_far(): lax.all_to_all(copies, 'col', 0, 0, axis_index_groups=groups, tiled=True)]
    all_to_all x4, starting transfers between devices: 31.2 us -> 27 us  [send_row(): return lax.all_to_all(copies, 'row', 0, 0, tiled=True)]
    unnamed x34 -> x38, local copies, waits for them, and re-layouts: 7.86 us -> 3.82 us
    all_gather x4, waiting for transfers between devices: 2.26 us -> 5.76 us  [gather_near(): return lax.all_gather(value, 'col', axis_index_groups=near_groups(), axis=0)]
  transfers between devices with their start and end apart: 16 -> 16, of which waited for: 13 -> 13; matrix products, arithmetic and copies ran while one was open for 1% -> 2% of each run, Pallas kernels for 4% -> 6%
where the time goes in v8:
time: 300 us; the launch traced here: 298 us
  waiting for transfers between devices  112 us (37%)
  starting transfers between devices  67.9 us (23%)
  blocking collectives  47.4 us (16%)
  Pallas kernels  39.9 us (13%)
  between operations  14.2 us (5%)
  local copies, waits for them, and re-layouts  8.27 us (3%)
  other arithmetic  6.9 us (2%)
    all_to_all x4, waiting for transfers between devices, send_row(): return lax.all_to_all(copies, 'row', 0, 0, tiled=True)  46.7 us
    all_to_all x5, waiting for transfers between devices, send_far(): lax.all_to_all(copies, 'col', 0, 0, axis_index_groups=groups, tiled=True)  32.3 us
    all_to_all x4, starting transfers between devices, send_row(): return lax.all_to_all(copies, 'row', 0, 0, tiled=True)  27 us
    all_to_all x3, waiting for transfers between devices, send_col(): return lax.all_to_all(copies, 'col', 0, 0, tiled=True)  25.3 us
    pallas_call x14, Pallas kernels, call(): pl.pallas_call(functools.partial(kernel, **static), out_shape=out_shape,...  22.1 us
    all_to_all x3, starting transfers between devices, send_col(): return lax.all_to_all(copies, 'col', 0, 0, tiled=True)  21.4 us
    all_to_all x2, blocking collectives, send_far(): lax.all_to_all(copies, 'col', 0, 0, axis_index_groups=groups, tiled=True)  20.8 us
    all_to_all x5, starting transfers between devices, send_far(): lax.all_to_all(copies, 'col', 0, 0, axis_index_groups=groups, tiled=True)  19.3 us
  transfers between devices with their start and end apart: 16, of which 13 were waited for; matrix products, arithmetic and copies ran while one was open for 2% of the time, Pallas kernels for 6%

profile of v8, /device:TPU:1, one launch (start us, length us, event | category | flops | bytes accessed | tf_op | source)
XLA Modules:
  0.0 298.3 jit_solution(1446940259918567290)
XLA Ops:
  7.2 0.7 compare_convert_fusion.5
  8.0 1.7 convolution_convert_fusion
  9.7 0.7 reshape.229
  10.3 0.7 slice_bitcast_fusion.4
  11.1 1.4 select_maximum_fusion.others
  12.5 17.9 %shard_map.169 = bf16[1152,256]{1,0:T(8,128)(2,1)} custom-call(f32[16,1024]{1,0:T(8,128)} %select_maximum_fusion.others, bf16[1024,256]{1,0:T(8,128)(2,1)} %bitcast.48), custom_call_target="tpu_custom_call" | custom-call | tf_op jit(solution)/shard_map/pallas_call | solution.py:121
  30.4 0.7 all-gather.11.cloned.1.call-update
  31.1 0.7 all-gather.13.cloned.1.call-update
  31.8 13.7 %all-to-all-start = ((bf16[32,2,512]{2,1,0:T(2,128)(2,1)}), bf16[32,2,512]{2,1,0:T(2,128)(2,1)S(1)}, u32[]{:S(2)}, u32[]{:S(2)}) async-start(bf16[32,2,512]{2,1,0:T(2,128)(2,1)} %reshape.229), calls=%async_computation | async-start | bytes 131072 | tf_op jit(solution)/shard_map/all_to_all | solution.py:60
  46.2 8.2 %all-to-all-done.parts = bf16[32,2,512]{2,1,0:T(2,128)(2,1)S(1)} async-done(((bf16[32,2,512]{2,1,0:T(2,128)(2,1)}), bf16[32,2,512]{2,1,0:T(2,128)(2,1)S(1)}, u32[]{:S(2)}, u32[]{:S(2)}) %all-to-all-start) | async-done | bytes 65568 | tf_op jit(solution)/shard_map/all_to_all | solution.py:60
  54.4 0.7 shard_map.166
  55.1 3.9 %all-to-all-start.1 = ((bf16[32,2,512]{2,1,0:T(2,128)(2,1)}), bf16[32,2,512]{2,1,0:T(2,128)(2,1)S(1)}, u32[]{:S(2)}, u32[]{:S(2)}) async-start(bf16[32,2,512]{2,1,0:T(2,128)(2,1)} %shard_map.166), calls=%async_computation.1 | async-start | bytes 131072 | tf_op jit(solution)/shard_map/all_to_all | solution.py:60
  59.1 8.7 %all-to-all-done.1.parts = bf16[32,2,512]{2,1,0:T(2,128)(2,1)S(1)} async-done(((bf16[32,2,512]{2,1,0:T(2,128)(2,1)}), bf16[32,2,512]{2,1,0:T(2,128)(2,1)S(1)}, u32[]{:S(2)}, u32[]{:S(2)}) %all-to-all-start.1) | async-done | bytes 65568 | tf_op jit(solution)/shard_map/all_to_all | solution.py:60
  67.8 1.0 shard_map.167
  68.8 10.5 %all-to-all-start.2 = ((bf16[16,4,16,128]{3,2,1,0:T(8,128)(2,1)}), bf16[16,4,16,128]{3,2,1,0:T(8,128)(2,1)S(1)}, u32[]{:S(2)}, u32[]{:S(2)}) async-start(bf16[16,4,16,128]{3,2,1,0:T(8,128)(2,1)} %get-tuple-element.20), calls=%async_computation.2 | async-start | bytes 524288 | tf_op jit(solution)/shard_map/all_to_all | solution.py:50
  79.5 0.7 compare_convert_fusion.mask
  80.2 10.8 %all-to-all-done.2.parts = bf16[16,4,16,128]{3,2,1,0:T(8,128)(2,1)S(1)} async-done(((bf16[16,4,16,128]{3,2,1,0:T(8,128)(2,1)}), bf16[16,4,16,128]{3,2,1,0:T(8,128)(2,1)S(1)}, u32[]{:S(2)}, u32[]{:S(2)}) %all-to-all-start.2) | async-done | bytes 262176 | tf_op jit(solution)/shard_map/all_to_all | solution.py:50
  91.0 0.7 shard_map.168
  91.7 3.8 %all-to-all-start.3 = ((bf16[32,4,4,128]{3,2,1,0:T(4,128)(2,1)}), bf16[32,4,4,128]{3,2,1,0:T(4,128)(2,1)S(1)}, u32[]{:S(2)}, u32[]{:S(2)}) async-start(bf16[32,4,4,128]{3,2,1,0:T(4,128)(2,1)} %shard_map.168), calls=%async_computation.3 | async-start | bytes 262144 | tf_op jit(solution)/shard_map/all_to_all | solution.py:60
  96.1 1.0 slice.44
  97.1 0.7 constant_dynamic-slice_fusion.source
  97.8 8.4 %all-to-all-done.3.whole = bf16[32,4,4,128]{3,2,1,0:T(4,128)(2,1)S(1)} async-done(((bf16[32,4,4,128]{3,2,1,0:T(4,128)(2,1)}), bf16[32,4,4,128]{3,2,1,0:T(4,128)(2,1)S(1)}, u32[]{:S(2)}, u32[]{:S(2)}) %all-to-all-start.3) | async-done | bytes 131104 | tf_op jit(solution)/shard_map/all_to_all | solution.py:60
  106.2 0.7 copy-done.9
  106.8 3.7 %shard_map.170 = bf16[8,2,4,512]{3,2,1,0:T(4,128)(2,1)} custom-call(s32[4,8]{1,0:T(4,128)} %broadcast_add_fusion.table, bf16[32,4,4,128]{3,2,1,0:T(4,128)(2,1)} %copy-done.9, bf16[4,8,4,256]{3,2,1,0:T(4,128)(2,1)} %constant_dynamic-slice_fusion.source, f32[2,1,1024]{2,1,0:T(1,128)} %compare_convert_fusion.mask, bf16[4,1152,256]{2,1,0:T(8,128)(2,1)} %bitcast.39), custom_call_target="tpu_custom_call" | custom-call | tf_op jit(solution)/shard_map/pallas_call | solution.py:79
  110.5 3.4 %all-to-all-start.4 = ((bf16[8,2,4,512]{3,2,1,0:T(4,128)(2,1)}), bf16[8,2,4,512]{3,2,1,0:T(4,128)(2,1)S(1)}, u32[]{:S(2)}, u32[]{:S(2)}) async-start(bf16[8,2,4,512]{3,2,1,0:T(4,128)(2,1)} %shard_map.170), calls=%async_computation.4 | async-start | bytes 131072 | tf_op jit(solution)/shard_map/all_to_all | solution.py:46
  114.0 7.0 %all-to-all-done.4.parts = bf16[8,2,4,512]{3,2,1,0:T(4,128)(2,1)S(1)} async-done(((bf16[8,2,4,512]{3,2,1,0:T(4,128)(2,1)}), bf16[8,2,4,512]{3,2,1,0:T(4,128)(2,1)S(1)}, u32[]{:S(2)}, u32[]{:S(2)}) %all-to-all-start.4) | async-done | bytes 65568 | tf_op jit(solution)/shard_map/all_to_all | solution.py:46
  121.0 1.2 copy-done.2
  122.3 1.0 shard_map.171
  123.3 4.9 %all-to-all-start.5 = ((bf16[16,2,4,512]{3,2,1,0:T(4,128)(2,1)}), bf16[16,2,4,512]{3,2,1,0:T(4,128)(2,1)S(1)}, u32[]{:S(2)}, u32[]{:S(2)}) async-start(bf16[16,2,4,512]{3,2,1,0:T(4,128)(2,1)} %get-tuple-element.25), calls=%async_computation.5 | async-start | bytes 262144 | tf_op jit(solution)/shard_map/all_to_all | solution.py:50
  128.7 0.6 compare_convert_fusion.2.mask
  129.3 8.2 %all-to-all-done.5.parts = bf16[16,2,4,512]{3,2,1,0:T(4,128)(2,1)S(1)} async-done(((bf16[16,2,4,512]{3,2,1,0:T(4,128)(2,1)}), bf16[16,2,4,512]{3,2,1,0:T(4,128)(2,1)S(1)}, u32[]{:S(2)}, u32[]{:S(2)}) %all-to-all-start.5) | async-done | bytes 131104 | tf_op jit(solution)/shard_map/all_to_all | solution.py:50
  137.5 0.6 shard_map.172
  138.1 3.4 %all-to-all-start.6 = ((bf16[8,2,4,512]{3,2,1,0:T(4,128)(2,1)}), bf16[8,2,4,512]{3,2,1,0:T(4,128)(2,1)S(1)}, u32[]{:S(2)}, u32[]{:S(2)}) async-start(bf16[8,2,4,512]{3,2,1,0:T(4,128)(2,1)} %shard_map.172), calls=%async_computation.6 | async-start | bytes 131072 | tf_op jit(solution)/shard_map/all_to_all | solution.py:46
  141.5 0.6 broadcast_add_fusion.1.table
  142.0 5.7 %all-gather.13.cloned.1.call-done = bf16[3072,384]{1,0:T(8,128)(2,1)} async-done(((bf16[768,384]{1,0:T(8,128)(2,1)}), bf16[3072,384]{1,0:T(8,128)(2,1)}) %all-gather.13.cloned.1.call-update) | async-done | bytes 2359312 | tf_op jit(solution)/shard_map/all_gather | solution.py:37
  147.8 1.4 all-to-all-done.6.whole
  149.2 0.6 copy-done.10
  149.8 3.7 %shard_map.173 = bf16[8,1,4,768]{3,2,1,0:T(4,128)(2,1)} custom-call(s32[2,12]{1,0:T(2,128)} %broadcast_add_fusion.1.table, bf16[8,2,4,512]{3,2,1,0:T(4,128)(2,1)} %copy-done.10, bf16[4,8,4,256]{3,2,1,0:T(4,128)(2,1)} %constant_dynamic-slice_fusion.source, f32[1,1,1536]{2,1,0:T(1,128)} %compare_convert_fusion.2.mask, bf16[4,768,384]{2,1,0:T(8,128)(2,1)} %bitcast.45), custom_call_target="tpu_custom_call" | custom-call | tf_op jit(solution)/shard_map/pallas_call | solution.py:79
  153.5 5.8 %all-to-all-start.7 = ((bf16[8,1,4,768]{3,2,1,0:T(4,128)(2,1)}), bf16[8,1,4,768]{3,2,1,0:T(4,128)(2,1)S(1)}, u32[]{:S(2)}, u32[]{:S(2)}) async-start(bf16[8,1,4,768]{3,2,1,0:T(4,128)(2,1)} %shard_map.173), calls=%async_computation.7 | async-start | bytes 98304 | tf_op jit(solution)/shard_map/all_to_all | solution.py:46
  159.4 0.6 broadcast_in_dim.10.pivots
  160.0 6.5 %all-to-all-done.7.parts = bf16[8,1,4,768]{3,2,1,0:T(4,128)(2,1)S(1)} async-done(((bf16[8,1,4,768]{3,2,1,0:T(4,128)(2,1)}), bf16[8,1,4,768]{3,2,1,0:T(4,128)(2,1)S(1)}, u32[]{:S(2)}, u32[]{:S(2)}) %all-to-all-start.7) | async-done | bytes 49184 | tf_op jit(solution)/shard_map/all_to_all | solution.py:46
  166.4 0.6 copy-done.11
  167.1 3.5 %shard_map.174 = bf16[16,1,4,1536]{3,2,1,0:T(4,128)(2,1)} custom-call(bf16[8,1,4,768]{3,2,1,0:T(4,128)(2,1)} %copy-done.11, f32[1,768]{1,0:T(1,128)} %broadcast_in_dim.10.pivots, bf16[4,768,384]{2,1,0:T(8,128)(2,1)} %bitcast.46), custom_call_target="tpu_custom_call" | custom-call | tf_op jit(solution)/shard_map/pallas_call | solution.py:79
  170.5 19.2 %all_to_all.80.parts = bf16[16,1,4,1536]{3,2,1,0:T(4,128)(2,1)S(1)} all-to-all(bf16[16,1,4,1536]{3,2,1,0:T(4,128)(2,1)} %shard_map.174), channel_id=1, replica_groups=mesh['row'=16,'col'=32] {'row'}, dimensions={0} | all-to-all | bytes 393216 | tf_op jit(solution)/shard_map/all_to_all | solution.py:50
  189.8 11.3 %all_to_all.81.whole = bf16[8,1,4,1536]{3,2,1,0:T(4,128)(2,1)S(1)} all-to-all(bf16[8,1,4,1536]{3,2,1,0:T(4,128)(2,1)S(1)} %get-tuple-element.27), channel_id=1, replica_groups={{0,4,8,12,16,20,24,28},{1,5,9,13,17,21,25,29},{2,6,10,14,18,22,26,30},{..., dimensions={0} | all-to-all | bytes 196608 | tf_op jit(solution)/shard_map/all_to_all | solution.py:46
  201.1 0.8 shard_map.176
  201.8 9.5 %all_to_all.82.parts = bf16[8,2,4,512]{3,2,1,0:T(4,128)(2,1)S(1)} all-to-all(bf16[8,2,4,512]{3,2,1,0:T(4,128)(2,1)S(1)} %shard_map.176), channel_id=1, replica_groups={{0,4,8,12,16,20,24,28},{1,5,9,13,17,21,25,29},{2,6,10,14,18,22,26,30},{..., dimensions={0} | all-to-all | bytes 131072 | tf_op jit(solution)/shard_map/all_to_all | solution.py:46
  211.4 1.1 shard_map.177
  212.5 5.1 %all-to-all-start.11 = ((bf16[16,2,4,1024]{3,2,1,0:T(4,128)(2,1)}), bf16[16,2,4,1024]{3,2,1,0:T(4,128)(2,1)S(1)}, u32[]{:S(2)}, u32[]{:S(2)}) async-start(bf16[16,2,4,1024]{3,2,1,0:T(4,128)(2,1)} %shard_map.177), calls=%async_computation.11 | async-start | bytes 524288 | tf_op jit(solution)/shard_map/all_to_all | solution.py:50
  217.6 11.8 %all-to-all-done.11.parts = bf16[16,2,4,1024]{3,2,1,0:T(4,128)(2,1)S(1)} async-done(((bf16[16,2,4,1024]{3,2,1,0:T(4,128)(2,1)}), bf16[16,2,4,1024]{3,2,1,0:T(4,128)(2,1)S(1)}, u32[]{:S(2)}, u32[]{:S(2)}) %all-to-all-start.11) | async-done | bytes 262176 | tf_op jit(solution)/shard_map/all_to_all | solution.py:50
  229.4 0.7 shard_map.178
  230.1 3.4 %all-to-all-start.12 = ((bf16[8,2,4,1024]{3,2,1,0:T(4,128)(2,1)}), bf16[8,2,4,1024]{3,2,1,0:T(4,128)(2,1)S(1)}, u32[]{:S(2)}, u32[]{:S(2)}) async-start(bf16[8,2,4,1024]{3,2,1,0:T(4,128)(2,1)} %get-tuple-element.29), calls=%async_computation.12 | async-start | bytes 262144 | tf_op jit(solution)/shard_map/all_to_all | solution.py:46
  233.6 9.3 %all-to-all-done.12.whole = bf16[8,2,4,1024]{3,2,1,0:T(4,128)(2,1)S(1)} async-done(((bf16[8,2,4,1024]{3,2,1,0:T(4,128)(2,1)}), bf16[8,2,4,1024]{3,2,1,0:T(4,128)(2,1)S(1)}, u32[]{:S(2)}, u32[]{:S(2)}) %all-to-all-start.12) | async-done | bytes 131104 | tf_op jit(solution)/shard_map/all_to_all | solution.py:46
  242.8 0.6 copy-done.8
  243.5 3.5 %shard_map.179 = bf16[8,4,4,512]{3,2,1,0:T(4,128)(2,1)} custom-call(s32[1]{0:T(128)} %bitcast.1.far, s32[4,32]{1,0:T(4,128)} %blocks.3, bf16[8,2,4,1024]{3,2,1,0:T(4,128)(2,1)} %copy-done.8, bf16[4,4,128,512]{3,2,1,0:T(8,128)(2,1)} %bitcast.47), custom_call_target="tpu_custom_call" | custom-call | tf_op jit(solution)/shard_map/pallas_call | solution.py:79
  246.9 3.4 %all-to-all-start.13 = ((bf16[8,4,4,512]{3,2,1,0:T(4,128)(2,1)}), bf16[8,4,4,512]{3,2,1,0:T(4,128)(2,1)S(1)}, u32[]{:S(2)}, u32[]{:S(2)}) async-start(bf16[8,4,4,512]{3,2,1,0:T(4,128)(2,1)} %shard_map.179), calls=%async_computation.13 | async-start | bytes 262144 | tf_op jit(solution)/shard_map/all_to_all | solution.py:46
  250.4 8.2 %all-to-all-done.13 = bf16[8,4,4,512]{3,2,1,0:T(4,128)(2,1)S(1)} async-done(((bf16[8,4,4,512]{3,2,1,0:T(4,128)(2,1)}), bf16[8,4,4,512]{3,2,1,0:T(4,128)(2,1)S(1)}, u32[]{:S(2)}, u32[]{:S(2)}) %all-to-all-start.13) | async-done | bytes 131104 | tf_op jit(solution)/shard_map/all_to_all | solution.py:46
  258.8 7.4 %all_to_all.83.got = bf16[4,4,3840]{2,1,0:T(4,128)(2,1)S(1)} all-to-all(bf16[4,4,3840]{2,1,0:T(4,128)(2,1)S(1)} %pad_maximum_fusion), channel_id=1, replica_groups={{0,1,2,3},{4,5,6,7},{8,9,10,11},{12,13,14,15},{16,17,18,19},{20,21,22,2..., dimensions={0} | all-to-all | bytes 245760 | tf_op jit(solution)/shard_map/all_to_all | solution.py:29
  266.1 1.1 shard_map.180
  267.2 6.5 %all-to-all-start.15 = ((bf16[16,4,16,256]{3,2,1,0:T(8,128)(2,1)}), bf16[16,4,16,256]{3,2,1,0:T(8,128)(2,1)S(1)}, u32[]{:S(2)}, u32[]{:S(2)}) async-start(bf16[16,4,16,256]{3,2,1,0:T(8,128)(2,1)} %shard_map.180), calls=%async_computation.15 | async-start | bytes 1048576 | tf_op jit(solution)/shard_map/all_to_all | solution.py:50
  273.8 0.6 pad_maximum_fusion.2
  274.4 0.6 slice_bitcast_fusion
  275.0 16.0 %all-to-all-done.15 = bf16[16,4,16,256]{3,2,1,0:T(8,128)(2,1)S(1)} async-done(((bf16[16,4,16,256]{3,2,1,0:T(8,128)(2,1)}), bf16[16,4,16,256]{3,2,1,0:T(8,128)(2,1)S(1)}, u32[]{:S(2)}, u32[]{:S(2)}) %all-to-all-start.15) | async-done | bytes 524320 | tf_op jit(solution)/shard_map/all_to_all | solution.py:50
  291.1 0.6 multiply_bitcast_fusion
  (71 shorter events, 2.7 us)
Async XLA Ops:
  7.2 89.0 %all-gather.9.cloned.1.call-start = ((), (), s32[]{:S(2)}) async-start(), calls=%async_computation.16 | async-start | bytes 2949120 | tf_op jit(solution)/shard_map/all_gather | solution.py:37
  8.0 51.0 %copy-start.14 = (s32[4]{0:T(128)S(1)}, s32[4]{0:T(128)}, u32[]{:S(2)}) copy-start(s32[4]{0:T(128)} %param.27) | copy-start | bytes 52
  8.0 51.0 %copy-start.12 = (f32[4,512]{1,0:T(4,128)S(1)}, f32[4,512]{1,0:T(4,128)}, u32[]{:S(2)}) copy-start(f32[4,512]{1,0:T(4,128)} %param.25) | copy-start | bytes 24580
  8.0 59.8 %copy-start.4 = (bf16[4,128,512]{2,1,0:T(8,128)(2,1)S(1)}, bf16[4,128,512]{2,1,0:T(8,128)(2,1)}, u32[]{:S(2)}) copy-start(bf16[4,128,512]{2,1,0:T(8,128)(2,1)} %coupling.1) | copy-start | bytes 1572868
  12.4 66.9 %copy-start.13 = (s32[4,32]{1,0:T(4,128)S(1)}, s32[4,32]{1,0:T(4,128)}, u32[]{:S(2)}) copy-start(s32[4,32]{1,0:T(4,128)} %blocks.3) | copy-start | bytes 1540
  12.5 67.1 %copy-start.18 = (s32[2]{0:T(128)S(1)}, s32[2]{0:T(128)}, u32[]{:S(2)}) copy-start(s32[2]{0:T(128)} %param.26) | copy-start | bytes 28
  30.4 83.6 %all-gather.11.cloned.1.call-start = ((), (), s32[]{:S(2)}) async-start(), calls=%async_computation.17 | async-start | bytes 1310720 | tf_op jit(solution)/shard_map/all_gather | solution.py:37
  31.1 116.7 %all-gather.13.cloned.1.call-start = ((), (), s32[]{:S(2)}) async-start(), calls=%async_computation.18 | async-start | bytes 2949120 | tf_op jit(solution)/shard_map/all_gather | solution.py:37
  31.8 22.6 %all-to-all-start = ((bf16[32,2,512]{2,1,0:T(2,128)(2,1)}), bf16[32,2,512]{2,1,0:T(2,128)(2,1)S(1)}, u32[]{:S(2)}, u32[]{:S(2)}) async-start(bf16[32,2,512]{2,1,0:T(2,128)(2,1)} %reshape.229), calls=%async_computation | async-start | bytes 131072 | tf_op jit(solution)/shard_map/all_to_all | solution.py:60
  45.6 188.0 %all-gather.15.cloned.1.call-start = ((), (), s32[]{:S(2)}) async-start(), calls=%async_computation.19 | async-start | bytes 2621440 | tf_op jit(solution)/shard_map/all_gather | solution.py:37
  55.1 12.7 %all-to-all-start.1 = ((bf16[32,2,512]{2,1,0:T(2,128)(2,1)}), bf16[32,2,512]{2,1,0:T(2,128)(2,1)S(1)}, u32[]{:S(2)}, u32[]{:S(2)}) async-start(bf16[32,2,512]{2,1,0:T(2,128)(2,1)} %shard_map.166), calls=%async_computation.1 | async-start | bytes 131072 | tf_op jit(solution)/shard_map/all_to_all | solution.py:60
  68.8 45.2 %copy-start.17 = (f32[2,512]{1,0:T(2,128)S(1)}, f32[2,512]{1,0:T(2,128)}, u32[]{:S(2)}) copy-start(f32[2,512]{1,0:T(2,128)} %param.24) | copy-start | bytes 12292
  68.8 22.2 %all-to-all-start.2 = ((bf16[16,4,16,128]{3,2,1,0:T(8,128)(2,1)}), bf16[16,4,16,128]{3,2,1,0:T(8,128)(2,1)S(1)}, u32[]{:S(2)}, u32[]{:S(2)}) async-start(bf16[16,4,16,128]{3,2,1,0:T(8,128)(2,1)} %get-tuple-element.20), calls=%async_computation.2 | async-start | bytes 524288 | tf_op jit(solution)/shard_map/all_to_all | solution.py:50
  91.7 14.5 %all-to-all-start.3 = ((bf16[32,4,4,128]{3,2,1,0:T(4,128)(2,1)}), bf16[32,4,4,128]{3,2,1,0:T(4,128)(2,1)S(1)}, u32[]{:S(2)}, u32[]{:S(2)}) async-start(bf16[32,4,4,128]{3,2,1,0:T(4,128)(2,1)} %shard_map.168), calls=%async_computation.3 | async-start | bytes 262144 | tf_op jit(solution)/shard_map/all_to_all | solution.py:60
  96.1 32.1 %copy-start.7 = (s32[2,32]{1,0:T(2,128)S(1)}, s32[2,32]{1,0:T(2,128)}, u32[]{:S(2)}) copy-start(s32[2,32]{1,0:T(2,128)} %blocks.2) | copy-start | bytes 772
  106.2 0.7 copy-start.9
  110.5 48.9 %copy-start.16 = (f32[768]{0:T(1024)S(1)}, f32[768]{0:T(1024)}, u32[]{:S(2)}) copy-start(f32[768]{0:T(1024)} %param.23) | copy-start | bytes 9220
  110.5 10.5 %all-to-all-start.4 = ((bf16[8,2,4,512]{3,2,1,0:T(4,128)(2,1)}), bf16[8,2,4,512]{3,2,1,0:T(4,128)(2,1)S(1)}, u32[]{:S(2)}, u32[]{:S(2)}) async-start(bf16[8,2,4,512]{3,2,1,0:T(4,128)(2,1)} %shard_map.170), calls=%async_computation.4 | async-start | bytes 131072 | tf_op jit(solution)/shard_map/all_to_all | solution.py:46
  121.0 1.2 copy-start.2
  123.3 14.2 %all-to-all-start.5 = ((bf16[16,2,4,512]{3,2,1,0:T(4,128)(2,1)}), bf16[16,2,4,512]{3,2,1,0:T(4,128)(2,1)S(1)}, u32[]{:S(2)}, u32[]{:S(2)}) async-start(bf16[16,2,4,512]{3,2,1,0:T(4,128)(2,1)} %get-tuple-element.25), calls=%async_computation.5 | async-start | bytes 262144 | tf_op jit(solution)/shard_map/all_to_all | solution.py:50
  138.1 11.1 %all-to-all-start.6 = ((bf16[8,2,4,512]{3,2,1,0:T(4,128)(2,1)}), bf16[8,2,4,512]{3,2,1,0:T(4,128)(2,1)S(1)}, u32[]{:S(2)}, u32[]{:S(2)}) async-start(bf16[8,2,4,512]{3,2,1,0:T(4,128)(2,1)} %shard_map.172), calls=%async_computation.6 | async-start | bytes 131072 | tf_op jit(solution)/shard_map/all_to_all | solution.py:46
  149.2 0.6 copy-start.10
  149.8 39.9 %copy-start.6 = (f32[1,1,1536]{2,1,0:T(1,128)S(1)}, f32[1,1,1536]{2,1,0:T(1,128)}, u32[]{:S(2)}) copy-start(f32[1,1,1536]{2,1,0:T(1,128)} %compare_convert_fusion.2.mask) | copy-start | bytes 18436
  153.5 47.5 %copy-start.3 = (bf16[8,128,512]{2,1,0:T(8,128)(2,1)S(1)}, bf16[8,128,512]{2,1,0:T(8,128)(2,1)}, u32[]{:S(2)}) copy-start(bf16[8,128,512]{2,1,0:T(8,128)(2,1)} %all-gather.11.cloned.1.call-done) | copy-start | bytes 3145732
  153.5 12.9 %all-to-all-start.7 = ((bf16[8,1,4,768]{3,2,1,0:T(4,128)(2,1)}), bf16[8,1,4,768]{3,2,1,0:T(4,128)(2,1)S(1)}, u32[]{:S(2)}, u32[]{:S(2)}) async-start(bf16[8,1,4,768]{3,2,1,0:T(4,128)(2,1)} %shard_map.173), calls=%async_computation.7 | async-start | bytes 98304 | tf_op jit(solution)/shard_map/all_to_all | solution.py:46
  160.0 51.4 %copy-start = (bf16[4608,256]{1,0:T(8,128)(2,1)S(1)}, bf16[4608,256]{1,0:T(8,128)(2,1)}, u32[]{:S(2)}) copy-start(bf16[4608,256]{1,0:T(8,128)(2,1)} %all-gather.9.cloned.1.call-done) | copy-start | bytes 7077892
  166.4 0.6 copy-start.11
  189.7 27.8 %copy-start.15 = (s32[4]{0:T(128)S(1)}, s32[4]{0:T(128)}, u32[]{:S(2)}) copy-start(s32[4]{0:T(128)} %param.27) | copy-start | bytes 52
  189.8 39.7 %copy-start.5 = (f32[2,1,1024]{2,1,0:T(1,128)S(1)}, f32[2,1,1024]{2,1,0:T(1,128)}, u32[]{:S(2)}) copy-start(f32[2,1,1024]{2,1,0:T(1,128)} %compare_convert_fusion.mask) | copy-start | bytes 24580
  212.5 53.7 %copy-start.1 = (bf16[4,512,256]{2,1,0:T(8,128)(2,1)S(1)}, bf16[4,512,256]{2,1,0:T(8,128)(2,1)}, u32[]{:S(2)}) copy-start(bf16[4,512,256]{2,1,0:T(8,128)(2,1)} %inverse.1) | copy-start | bytes 3145732
  212.5 17.0 %all-to-all-start.11 = ((bf16[16,2,4,1024]{3,2,1,0:T(4,128)(2,1)}), bf16[16,2,4,1024]{3,2,1,0:T(4,128)(2,1)S(1)}, u32[]{:S(2)}, u32[]{:S(2)}) async-start(bf16[16,2,4,1024]{3,2,1,0:T(4,128)(2,1)} %shard_map.177), calls=%async_computation.11 | async-start | bytes 524288 | tf_op jit(solution)/shard_map/all_to_all | solution.py:50
  230.1 12.7 %all-to-all-start.12 = ((bf16[8,2,4,1024]{3,2,1,0:T(4,128)(2,1)}), bf16[8,2,4,1024]{3,2,1,0:T(4,128)(2,1)S(1)}, u32[]{:S(2)}, u32[]{:S(2)}) async-start(bf16[8,2,4,1024]{3,2,1,0:T(4,128)(2,1)} %get-tuple-element.29), calls=%async_computation.12 | async-start | bytes 262144 | tf_op jit(solution)/shard_map/all_to_all | solution.py:46
  242.8 0.6 copy-start.8
  246.9 11.6 %all-to-all-start.13 = ((bf16[8,4,4,512]{3,2,1,0:T(4,128)(2,1)}), bf16[8,4,4,512]{3,2,1,0:T(4,128)(2,1)S(1)}, u32[]{:S(2)}, u32[]{:S(2)}) async-start(bf16[8,4,4,512]{3,2,1,0:T(4,128)(2,1)} %shard_map.179), calls=%async_computation.13 | async-start | bytes 262144 | tf_op jit(solution)/shard_map/all_to_all | solution.py:46
  267.2 23.8 %all-to-all-start.15 = ((bf16[16,4,16,256]{3,2,1,0:T(8,128)(2,1)}), bf16[16,4,16,256]{3,2,1,0:T(8,128)(2,1)S(1)}, u32[]{:S(2)}, u32[]{:S(2)}) async-start(bf16[16,4,16,256]{3,2,1,0:T(8,128)(2,1)} %shard_map.180), calls=%async_computation.15 | async-start | bytes 1048576 | tf_op jit(solution)/shard_map/all_to_all | solution.py:50
Sparse Core Ops, SparseCore 0:
  30.5 44.5 all-gather.8
  77.2 28.8 all-gather.10
  108.2 39.5 all-gather.12
  149.7 36.2 all-gather.14

commit v9 on v7

--- a/solution.py
+++ b/solution.py
@@ -69,30 +69,26 @@
     return lax.dot_general(a, b, (dims, ((), ())), preferred_element_type=F32)
 
 
-def call(kernel, out_shape, scalars, arrays, fetched=(), **static):
-    specs = [SMEM_SPEC] * len(scalars) + [VMEM_SPEC] * len(arrays)
-    specs += [pl.BlockSpec(memory_space=pl.ANY)] * len(fetched)
-    scratch = []
-    for array in fetched:
-        scratch += [pltpu.VMEM(array.shape, array.dtype), pltpu.SemaphoreType.DMA((array.shape[0],))]
+def call(kernel, out_shape, scalars, arrays, **static):
     return pl.pallas_call(
         functools.partial(kernel, **static),
         out_shape=out_shape,
-        in_specs=specs,
+        in_specs=[SMEM_SPEC] * len(scalars) + [VMEM_SPEC] * len(arrays),
         out_specs=jax.tree.map(lambda _: VMEM_SPEC, out_shape),
-        scratch_shapes=scratch,
         compiler_params=pltpu.CompilerParams(vmem_limit_bytes=16 << 20),
-    )(*scalars, *arrays, *fetched)
-
-
-def fetch(array, held, semaphores):
-    pieces = [
-        pltpu.make_async_copy(array.at[x], held.at[x], semaphores.at[x])
-        for x in range(array.shape[0])
-    ]
-    for piece in pieces:
-        piece.start()
-    return pieces
+    )(*scalars, *arrays)
+
+
+LANES = 128
+
+
+def tall(operand):
+    missing = jnp.zeros((LANES - operand.shape[0], operand.shape[1]), F32)
+    return jnp.concatenate([operand, missing], axis=0).astype(BF16)
+
+
+def times_tall(matrix, operand):
+    return dot(matrix, operand, ((1,), (1,)))
 
 
 def arrived(parts, f):
@@ -131,8 +127,8 @@
     share = pieces // NEAR
     for f in range(fronts):
         solved = [parts[f * pieces + g].astype(F32) for g in range(pieces)]
-        operand = (jnp.concatenate(solved, axis=0) * mask[f]).astype(BF16)
-        write_copies(out, f, dot(operand, coupling[f], ((1,), (1,))))
+        operand = tall(jnp.concatenate(solved, axis=0) * mask[f])
+        write_copies(out, f, times_tall(coupling[f], operand).T[: out.shape[2]])
         first = f * pieces + near[0] * share
         solved = [parts[first + g].astype(F32) for g in range(share)]
         scaled[f] = jnp.concatenate(solved, axis=0) * mask[f] * pivots[f]
@@ -182,8 +178,8 @@
     for f in range(parts.shape[1]):
         solved = arrived(parts, f) * mask[f]
         scaled[f] = solved * pivots[f]
-        operand = solved.astype(BF16)
-        update = [dot(operand, coupling[x, f], ((1,), (1,))) for x in range(NEAR)]
+        operand = tall(solved)
+        update = [times_tall(coupling[x, f], operand).T[: out.shape[2]] for x in range(NEAR)]
         write_copies(out, f, jnp.concatenate(update, axis=-1))
 
 
@@ -219,8 +215,7 @@
     return call(solved_kernel, out, [], [parts, mask])
 
 
-def place_kernel(table, whole, source, mask, inverse_at, out, inverse, semaphores, *, base):
-    copies = fetch(inverse_at, inverse, semaphores)
+def place_kernel(table, whole, source, mask, inverse, out, *, base):
     n = inverse.shape[2]
     held = n // BLOCK
     count = out.shape[3]
@@ -244,32 +239,26 @@
                     tile = tile - placed.astype(F32) * found
                 tiles.append(tile)
             operand = jnp.concatenate(tiles, axis=-1) * mask[p, :, x * n : (x + 1) * n]
-            if p == 0:
-                copies[x].wait()
             rows = inverse[x, p * count : (p + 1) * count]
-            part = dot(operand.astype(BF16), rows, ((1,), (1,)))
+            part = times_tall(rows, tall(operand))
             total = part if total is None else total + part
-        write_copies(out, p, total)
+        write_copies(out, p, total.T[: out.shape[2]])
 
 
 def place_and_solve(table, whole, source, mask, inverse, parents, count, base):
     out = shape_of(far_size(), parents, whole.shape[2], count)
-    return call(place_kernel, out, [table], [whole, source, mask], [inverse], base=base)
-
-
-def root_kernel(parts, pivots, inverse_at, out, inverse, semaphores):
-    copies = fetch(inverse_at, inverse, semaphores)
+    return call(place_kernel, out, [table], [whole, source, mask, inverse], base=base)
+
+
+def root_kernel(parts, pivots, inverse, out):
     operand = (arrived(parts, 0) * pivots[...]).astype(BF16)
-    pieces = []
-    for x in range(NEAR):
-        copies[x].wait()
-        pieces.append(dot(operand, inverse[x], ((1,), (0,))))
+    pieces = [dot(operand, inverse[x], ((1,), (0,))) for x in range(NEAR)]
     write_copies(out, 0, jnp.concatenate(pieces, axis=-1))
 
 
 def root_back(parts, pivots, inverse):
     out = shape_of(lax.axis_size("row"), 1, parts.shape[2], NEAR * inverse.shape[2])
-    return call(root_kernel, out, [], [parts, pivots[None, :]], [inverse])
+    return call(root_kernel, out, [], [parts, pivots[None, :], inverse])
 
 
 def back_kernel(parts, scaled, mask, inverse, out):
@@ -377,7 +366,6 @@
     size = halved.shape[2] // 2
     others = halved[:, :, :size] + halved[:, :, size:]
     message = place_and_solve(table_low, whole, others, wide_mask_mid, packed_near, 2, k1, 0)
-    coupling_mid_near, message = lax.optimization_barrier((coupling_mid_near, message))
     parts = send_far(message)
 
     message, scaled_mid = update_of(parts, row_mask_mid, pivots_mid, coupling_mid_near)
@@ -391,7 +379,6 @@
         send_row(root_back(parts, pivots_top, inverse_top_near)), wide_mask_top
     )
     message = pick_and_carry(far, blocks_mid, send_far(message), coupling_mid_near)
-    coupling_low_near, message = lax.optimization_barrier((coupling_low_near, message))
     parts = send_far(message)
     message, solution_mid = relay_solved(
         send_row(back(parts, scaled_mid, row_mask_mid, packed_near)), wide_mask_mid

time: 281 us -> 279 us (level)
    all_to_all x5, waiting for transfers between devices: 37 us -> 32.2 us  [send_far(): lax.all_to_all(copies, 'col', 0, 0, axis_index_groups=groups, tiled=True)]
    all_gather x4, waiting for transfers between devices: 2.26 us -> 6.94 us  [gather_near(): return lax.all_gather(value, 'col', axis_index_groups=near_groups(), axis=0)]
    all_to_all x4, starting transfers between devices: 31.2 us -> 26.7 us  [send_row(): return lax.all_to_all(copies, 'row', 0, 0, tiled=True)]
    all_to_all x5, starting transfers between devices: 16.9 us -> 19.9 us  [send_far(): lax.all_to_all(copies, 'col', 0, 0, axis_index_groups=groups, tiled=True)]
where the time goes in v9:
time: 279 us; the launch traced here: 278 us
  waiting for transfers between devices  115 us (41%)
  starting transfers between devices  68.3 us (24%)
  blocking collectives  47 us (17%)
  between operations  14.2 us (5%)
  Pallas kernels  14 us (5%)
  local copies, waits for them, and re-layouts  11.5 us (4%)
  other arithmetic  5.65 us (2%)
    all_to_all x4, waiting for transfers between devices, send_row(): return lax.all_to_all(copies, 'row', 0, 0, tiled=True)  48.2 us
    all_to_all x5, waiting for transfers between devices, send_far(): lax.all_to_all(copies, 'col', 0, 0, axis_index_groups=groups, tiled=True)  32.2 us
    all_to_all x4, starting transfers between devices, send_row(): return lax.all_to_all(copies, 'row', 0, 0, tiled=True)  26.7 us
    all_to_all x3, waiting for transfers between devices, send_col(): return lax.all_to_all(copies, 'col', 0, 0, tiled=True)  26 us
    all_to_all x3, starting transfers between devices, send_col(): return lax.all_to_all(copies, 'col', 0, 0, tiled=True)  21.6 us
    all_to_all x2, blocking collectives, send_far(): lax.all_to_all(copies, 'col', 0, 0, axis_index_groups=groups, tiled=True)  20.8 us
    all_to_all x5, starting transfers between devices, send_far(): lax.all_to_all(copies, 'col', 0, 0, axis_index_groups=groups, tiled=True)  19.9 us
    all_to_all x1, blocking collectives, send_row(): return lax.all_to_all(copies, 'row', 0, 0, tiled=True)  18.8 us
  transfers between devices with their start and end apart: 16, of which 13 were waited for; matrix products, arithmetic and copies ran while one was open for 1% of the time, Pallas kernels for 4%

profile of v9, /device:TPU:1, one launch (start us, length us, event | category | flops | bytes accessed | tf_op | source)
XLA Modules:
  0.0 277.6 jit_solution(9414326589539012466)
XLA Ops:
  7.2 0.8 compare_convert_fusion.5
  8.0 1.6 convolution_convert_fusion
  9.7 0.7 reshape.232
  10.3 0.7 slice_bitcast_fusion.4
  11.1 0.7 fusion
  11.8 0.7 subtract_convert_fusion.1
  12.7 0.9 pad_maximum_fusion
  13.7 0.7 all-gather.11.cloned.1.call-update
  14.4 0.7 all-gather.13.cloned.1.call-update
  15.1 13.7 %all-to-all-start = ((bf16[32,2,512]{2,1,0:T(2,128)(2,1)}), bf16[32,2,512]{2,1,0:T(2,128)(2,1)S(1)}, u32[]{:S(2)}, u32[]{:S(2)}) async-start(bf16[32,2,512]{2,1,0:T(2,128)(2,1)} %reshape.232), calls=%async_computation | async-start | bytes 131072 | tf_op jit(solution)/shard_map/all_to_all | solution.py:60
  28.9 0.5 all-gather.15.cloned.1.call-update
  29.5 8.1 %all-to-all-done.parts = bf16[32,2,512]{2,1,0:T(2,128)(2,1)S(1)} async-done(((bf16[32,2,512]{2,1,0:T(2,128)(2,1)}), bf16[32,2,512]{2,1,0:T(2,128)(2,1)S(1)}, u32[]{:S(2)}, u32[]{:S(2)}) %all-to-all-start) | async-done | bytes 65568 | tf_op jit(solution)/shard_map/all_to_all | solution.py:60
  37.6 0.7 shard_map.166
  38.3 3.9 %all-to-all-start.1 = ((bf16[32,2,512]{2,1,0:T(2,128)(2,1)}), bf16[32,2,512]{2,1,0:T(2,128)(2,1)S(1)}, u32[]{:S(2)}, u32[]{:S(2)}) async-start(bf16[32,2,512]{2,1,0:T(2,128)(2,1)} %shard_map.166), calls=%async_computation.1 | async-start | bytes 131072 | tf_op jit(solution)/shard_map/all_to_all | solution.py:60
  42.2 0.2 select_reduce_fusion
  42.5 8.6 %all-to-all-done.1.parts = bf16[32,2,512]{2,1,0:T(2,128)(2,1)S(1)} async-done(((bf16[32,2,512]{2,1,0:T(2,128)(2,1)}), bf16[32,2,512]{2,1,0:T(2,128)(2,1)S(1)}, u32[]{:S(2)}, u32[]{:S(2)}) %all-to-all-start.1) | async-done | bytes 65568 | tf_op jit(solution)/shard_map/all_to_all | solution.py:60
  51.1 1.1 shard_map.167
  52.1 10.4 %all-to-all-start.2 = ((bf16[16,4,16,128]{3,2,1,0:T(8,128)(2,1)}), bf16[16,4,16,128]{3,2,1,0:T(8,128)(2,1)S(1)}, u32[]{:S(2)}, u32[]{:S(2)}) async-start(bf16[16,4,16,128]{3,2,1,0:T(8,128)(2,1)} %get-tuple-element.20), calls=%async_computation.2 | async-start | bytes 524288 | tf_op jit(solution)/shard_map/all_to_all | solution.py:50
  62.6 11.6 %all-to-all-done.2.parts = bf16[16,4,16,128]{3,2,1,0:T(8,128)(2,1)S(1)} async-done(((bf16[16,4,16,128]{3,2,1,0:T(8,128)(2,1)}), bf16[16,4,16,128]{3,2,1,0:T(8,128)(2,1)S(1)}, u32[]{:S(2)}, u32[]{:S(2)}) %all-to-all-start.2) | async-done | bytes 262176 | tf_op jit(solution)/shard_map/all_to_all | solution.py:50
  74.2 0.7 shard_map.168
  74.9 4.0 %all-to-all-start.3 = ((bf16[32,4,4,128]{3,2,1,0:T(4,128)(2,1)}), bf16[32,4,4,128]{3,2,1,0:T(4,128)(2,1)S(1)}, u32[]{:S(2)}, u32[]{:S(2)}) async-start(bf16[32,4,4,128]{3,2,1,0:T(4,128)(2,1)} %shard_map.168), calls=%async_computation.3 | async-start | bytes 262144 | tf_op jit(solution)/shard_map/all_to_all | solution.py:60
  78.9 1.0 slice.52
  79.9 0.2 reshape.236
  80.2 9.3 %all-to-all-done.3.whole = bf16[32,4,4,128]{3,2,1,0:T(4,128)(2,1)S(1)} async-done(((bf16[32,4,4,128]{3,2,1,0:T(4,128)(2,1)}), bf16[32,4,4,128]{3,2,1,0:T(4,128)(2,1)S(1)}, u32[]{:S(2)}, u32[]{:S(2)}) %all-to-all-start.3) | async-done | bytes 131104 | tf_op jit(solution)/shard_map/all_to_all | solution.py:60
  89.5 1.7 copy-done
  91.2 2.0 shard_map.169
  93.2 3.4 %all-to-all-start.4 = ((bf16[8,2,4,512]{3,2,1,0:T(4,128)(2,1)}), bf16[8,2,4,512]{3,2,1,0:T(4,128)(2,1)S(1)}, u32[]{:S(2)}, u32[]{:S(2)}) async-start(bf16[8,2,4,512]{3,2,1,0:T(4,128)(2,1)} %shard_map.169), calls=%async_computation.4 | async-start | bytes 131072 | tf_op jit(solution)/shard_map/all_to_all | solution.py:46
  96.6 6.9 %all-to-all-done.4.parts = bf16[8,2,4,512]{3,2,1,0:T(4,128)(2,1)S(1)} async-done(((bf16[8,2,4,512]{3,2,1,0:T(4,128)(2,1)}), bf16[8,2,4,512]{3,2,1,0:T(4,128)(2,1)S(1)}, u32[]{:S(2)}, u32[]{:S(2)}) %all-to-all-start.4) | async-done | bytes 65568 | tf_op jit(solution)/shard_map/all_to_all | solution.py:46
  103.6 1.2 copy-done.5
  104.8 1.1 shard_map.170
  105.9 4.9 %all-to-all-start.5 = ((bf16[16,2,4,512]{3,2,1,0:T(4,128)(2,1)}), bf16[16,2,4,512]{3,2,1,0:T(4,128)(2,1)S(1)}, u32[]{:S(2)}, u32[]{:S(2)}) async-start(bf16[16,2,4,512]{3,2,1,0:T(4,128)(2,1)} %get-tuple-element.25), calls=%async_computation.5 | async-start | bytes 262144 | tf_op jit(solution)/shard_map/all_to_all | solution.py:50
  110.8 0.3 fusion.3
  111.3 8.7 %all-to-all-done.5.parts = bf16[16,2,4,512]{3,2,1,0:T(4,128)(2,1)S(1)} async-done(((bf16[16,2,4,512]{3,2,1,0:T(4,128)(2,1)}), bf16[16,2,4,512]{3,2,1,0:T(4,128)(2,1)S(1)}, u32[]{:S(2)}, u32[]{:S(2)}) %all-to-all-start.5) | async-done | bytes 131104 | tf_op jit(solution)/shard_map/all_to_all | solution.py:50
  120.1 0.7 shard_map.171
  120.7 3.4 %all-to-all-start.6 = ((bf16[8,2,4,512]{3,2,1,0:T(4,128)(2,1)}), bf16[8,2,4,512]{3,2,1,0:T(4,128)(2,1)S(1)}, u32[]{:S(2)}, u32[]{:S(2)}) async-start(bf16[8,2,4,512]{3,2,1,0:T(4,128)(2,1)} %shard_map.171), calls=%async_computation.6 | async-start | bytes 131072 | tf_op jit(solution)/shard_map/all_to_all | solution.py:46
  124.1 6.9 %all-gather.13.cloned.1.call-done = bf16[3072,384]{1,0:T(8,128)(2,1)} async-done(((bf16[768,384]{1,0:T(8,128)(2,1)}), bf16[3072,384]{1,0:T(8,128)(2,1)}) %all-gather.13.cloned.1.call-update) | async-done | bytes 2359312 | tf_op jit(solution)/shard_map/all_gather | solution.py:37
  131.0 0.8 all-to-all-done.6.whole
  131.8 1.7 copy-done.2
  133.5 2.0 shard_map.172
  135.5 6.3 %all-to-all-start.7 = ((bf16[8,1,4,768]{3,2,1,0:T(4,128)(2,1)}), bf16[8,1,4,768]{3,2,1,0:T(4,128)(2,1)S(1)}, u32[]{:S(2)}, u32[]{:S(2)}) async-start(bf16[8,1,4,768]{3,2,1,0:T(4,128)(2,1)} %shard_map.172), calls=%async_computation.7 | async-start | bytes 98304 | tf_op jit(solution)/shard_map/all_to_all | solution.py:46
  141.8 7.0 %all-to-all-done.7.parts = bf16[8,1,4,768]{3,2,1,0:T(4,128)(2,1)S(1)} async-done(((bf16[8,1,4,768]{3,2,1,0:T(4,128)(2,1)}), bf16[8,1,4,768]{3,2,1,0:T(4,128)(2,1)S(1)}, u32[]{:S(2)}, u32[]{:S(2)}) %all-to-all-start.7) | async-done | bytes 49184 | tf_op jit(solution)/shard_map/all_to_all | solution.py:46
  148.8 1.8 copy-done.3
  150.6 0.4 shard_map.173
  151.1 18.8 %all_to_all.80.parts = bf16[16,1,4,1536]{3,2,1,0:T(4,128)(2,1)S(1)} all-to-all(bf16[16,1,4,1536]{3,2,1,0:T(4,128)(2,1)S(1)} %shard_map.173), channel_id=1, replica_groups=mesh['row'=16,'col'=32] {'row'}, dimensions={0} | all-to-all | bytes 393216 | tf_op jit(solution)/shard_map/all_to_all | solution.py:50
  169.9 11.3 %all_to_all.81.whole = bf16[8,1,4,1536]{3,2,1,0:T(4,128)(2,1)S(1)} all-to-all(bf16[8,1,4,1536]{3,2,1,0:T(4,128)(2,1)S(1)} %get-tuple-element.27), channel_id=1, replica_groups={{0,4,8,12,16,20,24,28},{1,5,9,13,17,21,25,29},{2,6,10,14,18,22,26,30},{..., dimensions={0} | all-to-all | bytes 196608 | tf_op jit(solution)/shard_map/all_to_all | solution.py:46
  181.2 0.8 shard_map.175
  182.0 9.5 %all_to_all.82.parts = bf16[8,2,4,512]{3,2,1,0:T(4,128)(2,1)S(1)} all-to-all(bf16[8,2,4,512]{3,2,1,0:T(4,128)(2,1)S(1)} %shard_map.175), channel_id=1, replica_groups={{0,4,8,12,16,20,24,28},{1,5,9,13,17,21,25,29},{2,6,10,14,18,22,26,30},{..., dimensions={0} | all-to-all | bytes 131072 | tf_op jit(solution)/shard_map/all_to_all | solution.py:46
  191.5 1.1 shard_map.176
  192.6 5.0 %all-to-all-start.11 = ((bf16[16,2,4,1024]{3,2,1,0:T(4,128)(2,1)}), bf16[16,2,4,1024]{3,2,1,0:T(4,128)(2,1)S(1)}, u32[]{:S(2)}, u32[]{:S(2)}) async-start(bf16[16,2,4,1024]{3,2,1,0:T(4,128)(2,1)} %shard_map.176), calls=%async_computation.11 | async-start | bytes 524288 | tf_op jit(solution)/shard_map/all_to_all | solution.py:50
  197.7 11.8 %all-to-all-done.11.parts = bf16[16,2,4,1024]{3,2,1,0:T(4,128)(2,1)S(1)} async-done(((bf16[16,2,4,1024]{3,2,1,0:T(4,128)(2,1)}), bf16[16,2,4,1024]{3,2,1,0:T(4,128)(2,1)S(1)}, u32[]{:S(2)}, u32[]{:S(2)}) %all-to-all-start.11) | async-done | bytes 262176 | tf_op jit(solution)/shard_map/all_to_all | solution.py:50
  209.5 0.7 shard_map.177
  210.2 3.5 %all-to-all-start.12 = ((bf16[8,2,4,1024]{3,2,1,0:T(4,128)(2,1)}), bf16[8,2,4,1024]{3,2,1,0:T(4,128)(2,1)S(1)}, u32[]{:S(2)}, u32[]{:S(2)}) async-start(bf16[8,2,4,1024]{3,2,1,0:T(4,128)(2,1)} %get-tuple-element.29), calls=%async_computation.12 | async-start | bytes 262144 | tf_op jit(solution)/shard_map/all_to_all | solution.py:46
  213.7 9.3 %all-to-all-done.12.whole = bf16[8,2,4,1024]{3,2,1,0:T(4,128)(2,1)S(1)} async-done(((bf16[8,2,4,1024]{3,2,1,0:T(4,128)(2,1)}), bf16[8,2,4,1024]{3,2,1,0:T(4,128)(2,1)S(1)}, u32[]{:S(2)}, u32[]{:S(2)}) %all-to-all-start.12) | async-done | bytes 131104 | tf_op jit(solution)/shard_map/all_to_all | solution.py:46
  223.0 1.6 copy-done.7
  224.6 1.6 shard_map.178
  226.2 3.4 %all-to-all-start.13 = ((bf16[8,4,4,512]{3,2,1,0:T(4,128)(2,1)}), bf16[8,4,4,512]{3,2,1,0:T(4,128)(2,1)S(1)}, u32[]{:S(2)}, u32[]{:S(2)}) async-start(bf16[8,4,4,512]{3,2,1,0:T(4,128)(2,1)} %shard_map.178), calls=%async_computation.13 | async-start | bytes 262144 | tf_op jit(solution)/shard_map/all_to_all | solution.py:46
  229.7 8.2 %all-to-all-done.13 = bf16[8,4,4,512]{3,2,1,0:T(4,128)(2,1)S(1)} async-done(((bf16[8,4,4,512]{3,2,1,0:T(4,128)(2,1)}), bf16[8,4,4,512]{3,2,1,0:T(4,128)(2,1)S(1)}, u32[]{:S(2)}, u32[]{:S(2)}) %all-to-all-start.13) | async-done | bytes 131104 | tf_op jit(solution)/shard_map/all_to_all | solution.py:46
  238.0 7.4 %all_to_all.83.got = bf16[4,4,3840]{2,1,0:T(4,128)(2,1)S(1)} all-to-all(bf16[4,4,3840]{2,1,0:T(4,128)(2,1)S(1)} %pad_maximum_fusion.1), channel_id=1, replica_groups={{0,1,2,3},{4,5,6,7},{8,9,10,11},{12,13,14,15},{16,17,18,19},{20,21,22,2..., dimensions={0} | all-to-all | bytes 245760 | tf_op jit(solution)/shard_map/all_to_all | solution.py:29
  245.4 1.1 shard_map.179
  246.5 6.5 %all-to-all-start.15 = ((bf16[16,4,16,256]{3,2,1,0:T(8,128)(2,1)}), bf16[16,4,16,256]{3,2,1,0:T(8,128)(2,1)S(1)}, u32[]{:S(2)}, u32[]{:S(2)}) async-start(bf16[16,4,16,256]{3,2,1,0:T(8,128)(2,1)} %shard_map.179), calls=%async_computation.15 | async-start | bytes 1048576 | tf_op jit(solution)/shard_map/all_to_all | solution.py:50
  253.1 0.6 pad_maximum_fusion.5
  253.7 0.6 slice_bitcast_fusion
  254.3 16.0 %all-to-all-done.15 = bf16[16,4,16,256]{3,2,1,0:T(8,128)(2,1)S(1)} async-done(((bf16[16,4,16,256]{3,2,1,0:T(8,128)(2,1)}), bf16[16,4,16,256]{3,2,1,0:T(8,128)(2,1)S(1)}, u32[]{:S(2)}, u32[]{:S(2)}) %all-to-all-start.15) | async-done | bytes 524320 | tf_op jit(solution)/shard_map/all_to_all | solution.py:50
  270.4 0.6 multiply_bitcast_fusion
  (72 shorter events, 1.3 us)
Async XLA Ops:
  7.2 5.5 %copy-start.11 = (bf16[2,512,256]{2,1,0:T(8,128)(2,1)S(1)}, bf16[2,512,256]{2,1,0:T(8,128)(2,1)}, u32[]{:S(2)}) copy-start(bf16[2,512,256]{2,1,0:T(8,128)(2,1)} %param.16) | copy-start | bytes 1572868
  7.2 71.8 %all-gather.9.cloned.1.call-start = ((), (), s32[]{:S(2)}) async-start(), calls=%async_computation.16 | async-start | bytes 2908160 | tf_op jit(solution)/shard_map/all_gather | solution.py:37
  9.6 19.8 %copy-start.13 = (s32[4]{0:T(128)S(1)}, s32[4]{0:T(128)}, u32[]{:S(2)}) copy-start(s32[4]{0:T(128)} %param.27) | copy-start | bytes 52
  9.6 32.6 %copy-start.12 = (f32[4,512]{1,0:T(4,128)S(1)}, f32[4,512]{1,0:T(4,128)}, u32[]{:S(2)}) copy-start(f32[4,512]{1,0:T(4,128)} %param.25) | copy-start | bytes 24580
  9.7 32.6 %copy-start.9 = (s32[4,32]{1,0:T(4,128)S(1)}, s32[4,32]{1,0:T(4,128)}, u32[]{:S(2)}) copy-start(s32[4,32]{1,0:T(4,128)} %blocks.3) | copy-start | bytes 1540
  9.7 41.4 %copy-start.8 = (bf16[4,128,512]{2,1,0:T(8,128)(2,1)S(1)}, bf16[4,128,512]{2,1,0:T(8,128)(2,1)}, u32[]{:S(2)}) copy-start(bf16[4,128,512]{2,1,0:T(8,128)(2,1)} %coupling.1) | copy-start | bytes 1572868
  12.7 49.8 %copy-start.16 = (s32[2]{0:T(128)S(1)}, s32[2]{0:T(128)}, u32[]{:S(2)}) copy-start(s32[2]{0:T(128)} %param.26) | copy-start | bytes 28
  13.6 83.0 %all-gather.11.cloned.1.call-start = ((), (), s32[]{:S(2)}) async-start(), calls=%async_computation.17 | async-start | bytes 1310720 | tf_op jit(solution)/shard_map/all_gather | solution.py:37
  14.4 116.6 %all-gather.13.cloned.1.call-start = ((), (), s32[]{:S(2)}) async-start(), calls=%async_computation.18 | async-start | bytes 2949120 | tf_op jit(solution)/shard_map/all_gather | solution.py:37
  15.1 22.6 %all-to-all-start = ((bf16[32,2,512]{2,1,0:T(2,128)(2,1)}), bf16[32,2,512]{2,1,0:T(2,128)(2,1)S(1)}, u32[]{:S(2)}, u32[]{:S(2)}) async-start(bf16[32,2,512]{2,1,0:T(2,128)(2,1)} %reshape.232), calls=%async_computation | async-start | bytes 131072 | tf_op jit(solution)/shard_map/all_to_all | solution.py:60
  28.8 184.9 %all-gather.15.cloned.1.call-start = ((), (), s32[]{:S(2)}) async-start(), calls=%async_computation.19 | async-start | bytes 2621440 | tf_op jit(solution)/shard_map/all_gather | solution.py:37
  38.3 12.7 %all-to-all-start.1 = ((bf16[32,2,512]{2,1,0:T(2,128)(2,1)}), bf16[32,2,512]{2,1,0:T(2,128)(2,1)S(1)}, u32[]{:S(2)}, u32[]{:S(2)}) async-start(bf16[32,2,512]{2,1,0:T(2,128)(2,1)} %shard_map.166), calls=%async_computation.1 | async-start | bytes 131072 | tf_op jit(solution)/shard_map/all_to_all | solution.py:60
  52.1 22.1 %all-to-all-start.2 = ((bf16[16,4,16,128]{3,2,1,0:T(8,128)(2,1)}), bf16[16,4,16,128]{3,2,1,0:T(8,128)(2,1)S(1)}, u32[]{:S(2)}, u32[]{:S(2)}) async-start(bf16[16,4,16,128]{3,2,1,0:T(8,128)(2,1)} %get-tuple-element.20), calls=%async_computation.2 | async-start | bytes 524288 | tf_op jit(solution)/shard_map/all_to_all | solution.py:50
  74.9 21.7 %copy-start.15 = (f32[2,512]{1,0:T(2,128)S(1)}, f32[2,512]{1,0:T(2,128)}, u32[]{:S(2)}) copy-start(f32[2,512]{1,0:T(2,128)} %param.24) | copy-start | bytes 12292
  74.9 14.6 %all-to-all-start.3 = ((bf16[32,4,4,128]{3,2,1,0:T(4,128)(2,1)}), bf16[32,4,4,128]{3,2,1,0:T(4,128)(2,1)S(1)}, u32[]{:S(2)}, u32[]{:S(2)}) async-start(bf16[32,4,4,128]{3,2,1,0:T(4,128)(2,1)} %shard_map.168), calls=%async_computation.3 | async-start | bytes 262144 | tf_op jit(solution)/shard_map/all_to_all | solution.py:60
  89.5 1.7 copy-start
  91.2 19.7 %copy-start.10 = (s32[2,32]{1,0:T(2,128)S(1)}, s32[2,32]{1,0:T(2,128)}, u32[]{:S(2)}) copy-start(s32[2,32]{1,0:T(2,128)} %blocks.2) | copy-start | bytes 772
  93.2 10.4 %all-to-all-start.4 = ((bf16[8,2,4,512]{3,2,1,0:T(4,128)(2,1)}), bf16[8,2,4,512]{3,2,1,0:T(4,128)(2,1)S(1)}, u32[]{:S(2)}, u32[]{:S(2)}) async-start(bf16[8,2,4,512]{3,2,1,0:T(4,128)(2,1)} %shard_map.169), calls=%async_computation.4 | async-start | bytes 131072 | tf_op jit(solution)/shard_map/all_to_all | solution.py:46
  103.6 1.2 copy-start.5
  104.8 37.0 %copy-start.14 = (f32[768]{0:T(1024)S(1)}, f32[768]{0:T(1024)}, u32[]{:S(2)}) copy-start(f32[768]{0:T(1024)} %param.23) | copy-start | bytes 9220
  105.9 14.1 %all-to-all-start.5 = ((bf16[16,2,4,512]{3,2,1,0:T(4,128)(2,1)}), bf16[16,2,4,512]{3,2,1,0:T(4,128)(2,1)S(1)}, u32[]{:S(2)}, u32[]{:S(2)}) async-start(bf16[16,2,4,512]{3,2,1,0:T(4,128)(2,1)} %get-tuple-element.25), calls=%async_computation.5 | async-start | bytes 262144 | tf_op jit(solution)/shard_map/all_to_all | solution.py:50
  120.7 11.1 %all-to-all-start.6 = ((bf16[8,2,4,512]{3,2,1,0:T(4,128)(2,1)}), bf16[8,2,4,512]{3,2,1,0:T(4,128)(2,1)S(1)}, u32[]{:S(2)}, u32[]{:S(2)}) async-start(bf16[8,2,4,512]{3,2,1,0:T(4,128)(2,1)} %shard_map.171), calls=%async_computation.6 | async-start | bytes 131072 | tf_op jit(solution)/shard_map/all_to_all | solution.py:46
  131.8 1.7 copy-start.2
  133.5 47.8 %copy-start.6 = (bf16[8,128,512]{2,1,0:T(8,128)(2,1)S(1)}, bf16[8,128,512]{2,1,0:T(8,128)(2,1)}, u32[]{:S(2)}) copy-start(bf16[8,128,512]{2,1,0:T(8,128)(2,1)} %all-gather.11.cloned.1.call-done) | copy-start | bytes 3145732
  135.5 13.3 %all-to-all-start.7 = ((bf16[8,1,4,768]{3,2,1,0:T(4,128)(2,1)}), bf16[8,1,4,768]{3,2,1,0:T(4,128)(2,1)S(1)}, u32[]{:S(2)}, u32[]{:S(2)}) async-start(bf16[8,1,4,768]{3,2,1,0:T(4,128)(2,1)} %shard_map.172), calls=%async_computation.7 | async-start | bytes 98304 | tf_op jit(solution)/shard_map/all_to_all | solution.py:46
  141.8 49.7 %copy-start.1 = (bf16[4544,256]{1,0:T(8,128)(2,1)S(1)}, bf16[4544,256]{1,0:T(8,128)(2,1)}, u32[]{:S(2)}) copy-start(bf16[4544,256]{1,0:T(8,128)(2,1)} %all-gather.9.cloned.1.call-done) | copy-start | bytes 6979588
  148.8 1.8 copy-start.3
  192.6 16.8 %all-to-all-start.11 = ((bf16[16,2,4,1024]{3,2,1,0:T(4,128)(2,1)}), bf16[16,2,4,1024]{3,2,1,0:T(4,128)(2,1)S(1)}, u32[]{:S(2)}, u32[]{:S(2)}) async-start(bf16[16,2,4,1024]{3,2,1,0:T(4,128)(2,1)} %shard_map.176), calls=%async_computation.11 | async-start | bytes 524288 | tf_op jit(solution)/shard_map/all_to_all | solution.py:50
  210.2 35.3 %copy-start.4 = (bf16[4,512,256]{2,1,0:T(8,128)(2,1)S(1)}, bf16[4,512,256]{2,1,0:T(8,128)(2,1)}, u32[]{:S(2)}) copy-start(bf16[4,512,256]{2,1,0:T(8,128)(2,1)} %inverse.1) | copy-start | bytes 3145732
  210.2 12.8 %all-to-all-start.12 = ((bf16[8,2,4,1024]{3,2,1,0:T(4,128)(2,1)}), bf16[8,2,4,1024]{3,2,1,0:T(4,128)(2,1)S(1)}, u32[]{:S(2)}, u32[]{:S(2)}) async-start(bf16[8,2,4,1024]{3,2,1,0:T(4,128)(2,1)} %get-tuple-element.29), calls=%async_computation.12 | async-start | bytes 262144 | tf_op jit(solution)/shard_map/all_to_all | solution.py:46
  223.0 1.6 copy-start.7
  226.2 11.6 %all-to-all-start.13 = ((bf16[8,4,4,512]{3,2,1,0:T(4,128)(2,1)}), bf16[8,4,4,512]{3,2,1,0:T(4,128)(2,1)S(1)}, u32[]{:S(2)}, u32[]{:S(2)}) async-start(bf16[8,4,4,512]{3,2,1,0:T(4,128)(2,1)} %shard_map.178), calls=%async_computation.13 | async-start | bytes 262144 | tf_op jit(solution)/shard_map/all_to_all | solution.py:46
  246.5 23.8 %all-to-all-start.15 = ((bf16[16,4,16,256]{3,2,1,0:T(8,128)(2,1)}), bf16[16,4,16,256]{3,2,1,0:T(8,128)(2,1)S(1)}, u32[]{:S(2)}, u32[]{:S(2)}) async-start(bf16[16,4,16,256]{3,2,1,0:T(8,128)(2,1)} %shard_map.179), calls=%async_computation.15 | async-start | bytes 1048576 | tf_op jit(solution)/shard_map/all_to_all | solution.py:50
Sparse Core Ops, SparseCore 0:
  13.7 44.2 all-gather.8
  60.2 28.8 all-gather.10
  91.2 39.7 all-gather.12
  132.9 36.2 all-gather.14

commit v10 on v9

--- a/solution.py
+++ b/solution.py
@@ -35,6 +35,11 @@
 
 def gather_near(value):
     return lax.all_gather(value, "col", axis_index_groups=near_groups(), axis=0)
+
+
+def settled(array, message):
+    zero = lax.slice(message, (0,) * message.ndim, (1,) * message.ndim).reshape(()) * 0
+    return array + zero.astype(array.dtype)
 
 
 def copies_of(value, size):
@@ -359,17 +364,21 @@
 
     parts = send_col(relay_pieces(send_col(message)))
     message, scaled_low = first_update(near, parts, row_mask_low, pivots_low, coupling_low)
-    whole = send_col(relay_scattered(send_row(message)))
+    message = relay_scattered(send_row(message))
+    staged_mid = settled(packed_near, message)
+    whole = send_col(message)
 
     halved = packed_near[:, 2 * k1 :].reshape(NEAR, rhs, -1)
     halved = lax.dynamic_slice_in_dim(halved, (col_at % NEAR) * width, width, 1).astype(F32)
     size = halved.shape[2] // 2
     others = halved[:, :, :size] + halved[:, :, size:]
-    message = place_and_solve(table_low, whole, others, wide_mask_mid, packed_near, 2, k1, 0)
+    message = place_and_solve(table_low, whole, others, wide_mask_mid, staged_mid, 2, k1, 0)
+    coupling_mid_near = settled(coupling_mid_near, message)
     parts = send_far(message)
 
     message, scaled_mid = update_of(parts, row_mask_mid, pivots_mid, coupling_mid_near)
     whole = send_far(relay(send_row(message)))
+    inverse_top_near = settled(inverse_top_near, whole)
     k0 = inverse_top.shape[0]
     parts = send_far(
         place_and_solve(table_mid, whole, others, wide_mask_top, inverse_top_near, 1, k0, 2 * n1)
@@ -381,8 +390,9 @@
     message = pick_and_carry(far, blocks_mid, send_far(message), coupling_mid_near)
     parts = send_far(message)
     message, solution_mid = relay_solved(
-        send_row(back(parts, scaled_mid, row_mask_mid, packed_near)), wide_mask_mid
-    )
+        send_row(back(parts, scaled_mid, row_mask_mid, staged_mid)), wide_mask_mid
+    )
+    coupling_low_near = settled(coupling_low_near, message)
     parts = send_far(pick_and_carry(far, blocks_low, send_far(message), coupling_low_near))
     residual = (scaled_low - jnp.sum(parts.astype(F32), axis=0)) * row_mask_low
 

time: 279 us -> 280 us (level)
  other arithmetic: 5.65 us -> 14 us
  waiting for transfers between devices: 115 us -> 107 us
  between operations: 14.2 us -> 17 us
    all_gather x4, waiting for transfers between devices: 6.94 us -> 0.08 us  [gather_near(): return lax.all_gather(value, 'col', axis_index_groups=near_groups(), axis=0)]
    add x0 -> x4, other arithmetic: none -> 6.76 us  [settled(): return array + zero.astype(array.dtype)]
    unnamed x34 -> x44, local copies, waits for them, and re-layouts: 8 us -> 1.34 us
    slice x0 -> x4, local copies, waits for them, and re-layouts: none -> 4.07 us  [settled(): lax.slice(message, (0,) * message.ndim, (1,) * message.ndim).reshape(()) * 0]
  transfers between devices with their start and end apart: 16 -> 16, of which waited for: 13 -> 12; matrix products, arithmetic and copies ran while one was open for 1% -> 6% of each run, Pallas kernels for 4% -> 4%
where the time goes in v10:
time: 280 us; the launch traced here: 278 us
  waiting for transfers between devices  107 us (38%)
  starting transfers between devices  68 us (24%)
  blocking collectives  47.3 us (17%)
  between operations  17 us (6%)
  other arithmetic  14 us (5%)
  Pallas kernels  13.3 us (5%)
  local copies, waits for them, and re-layouts  9.56 us (3%)
    all_to_all x4, waiting for transfers between devices, send_row(): return lax.all_to_all(copies, 'row', 0, 0, tiled=True)  48.1 us
    all_to_all x5, waiting for transfers between devices, send_far(): lax.all_to_all(copies, 'col', 0, 0, axis_index_groups=groups, tiled=True)  33.6 us
    all_to_all x4, starting transfers between devices, send_row(): return lax.all_to_all(copies, 'row', 0, 0, tiled=True)  26.7 us
    all_to_all x3, waiting for transfers between devices, send_col(): return lax.all_to_all(copies, 'col', 0, 0, tiled=True)  23.5 us
    all_to_all x3, starting transfers between devices, send_col(): return lax.all_to_all(copies, 'col', 0, 0, tiled=True)  21.4 us
    all_to_all x2, blocking collectives, send_far(): lax.all_to_all(copies, 'col', 0, 0, axis_index_groups=groups, tiled=True)  20.8 us
    all_to_all x5, starting transfers between devices, send_far(): lax.all_to_all(copies, 'col', 0, 0, axis_index_groups=groups, tiled=True)  19.7 us
    all_to_all x1, blocking collectives, send_row(): return lax.all_to_all(copies, 'row', 0, 0, tiled=True)  19.1 us
  transfers between devices with their start and end apart: 16, of which 12 were waited for; matrix products, arithmetic and copies ran while one was open for 6% of the time, Pallas kernels for 4%

profile of v10, /device:TPU:1, one launch (start us, length us, event | category | flops | bytes accessed | tf_op | source)
XLA Modules:
  0.0 277.9 jit_solution(3008120366798143386)
XLA Ops:
  7.2 0.7 compare_convert_fusion.5
  8.0 1.7 convolution_convert_fusion
  9.6 0.7 reshape.244
  10.3 0.7 slice_bitcast_fusion.4
  11.0 0.7 fusion
  11.8 0.7 subtract_convert_fusion.1
  12.7 2.0 pad_maximum_fusion
  14.7 0.7 all-gather.11.cloned.1.call-update
  15.4 0.7 all-gather.13.cloned.1.call-update
  16.1 13.7 %all-to-all-start = ((bf16[32,2,512]{2,1,0:T(2,128)(2,1)}), bf16[32,2,512]{2,1,0:T(2,128)(2,1)S(1)}, u32[]{:S(2)}, u32[]{:S(2)}) async-start(bf16[32,2,512]{2,1,0:T(2,128)(2,1)} %reshape.244), calls=%async_computation | async-start | bytes 131072 | tf_op jit(solution)/shard_map/all_to_all | solution.py:65
  30.8 7.9 %all-to-all-done.parts = bf16[32,2,512]{2,1,0:T(2,128)(2,1)S(1)} async-done(((bf16[32,2,512]{2,1,0:T(2,128)(2,1)}), bf16[32,2,512]{2,1,0:T(2,128)(2,1)S(1)}, u32[]{:S(2)}, u32[]{:S(2)}) %all-to-all-start) | async-done | bytes 65568 | tf_op jit(solution)/shard_map/all_to_all | solution.py:65
  38.7 0.7 shard_map.166
  39.4 3.9 %all-to-all-start.1 = ((bf16[32,2,512]{2,1,0:T(2,128)(2,1)}), bf16[32,2,512]{2,1,0:T(2,128)(2,1)S(1)}, u32[]{:S(2)}, u32[]{:S(2)}) async-start(bf16[32,2,512]{2,1,0:T(2,128)(2,1)} %shard_map.166), calls=%async_computation.1 | async-start | bytes 131072 | tf_op jit(solution)/shard_map/all_to_all | solution.py:65
  43.3 8.8 %all-to-all-done.1.parts = bf16[32,2,512]{2,1,0:T(2,128)(2,1)S(1)} async-done(((bf16[32,2,512]{2,1,0:T(2,128)(2,1)}), bf16[32,2,512]{2,1,0:T(2,128)(2,1)S(1)}, u32[]{:S(2)}, u32[]{:S(2)}) %all-to-all-start.1) | async-done | bytes 65568 | tf_op jit(solution)/shard_map/all_to_all | solution.py:65
  52.1 1.1 shard_map.167
  53.2 0.6 copy-done.5
  53.8 10.4 %all-to-all-start.2 = ((bf16[16,4,16,128]{3,2,1,0:T(8,128)(2,1)}), bf16[16,4,16,128]{3,2,1,0:T(8,128)(2,1)S(1)}, u32[]{:S(2)}, u32[]{:S(2)}) async-start(bf16[16,4,16,128]{3,2,1,0:T(8,128)(2,1)} %get-tuple-element.20), calls=%async_computation.2 | async-start | bytes 524288 | tf_op jit(solution)/shard_map/all_to_all | solution.py:55
  64.4 11.5 %all-to-all-done.2.parts = bf16[16,4,16,128]{3,2,1,0:T(8,128)(2,1)S(1)} async-done(((bf16[16,4,16,128]{3,2,1,0:T(8,128)(2,1)}), bf16[16,4,16,128]{3,2,1,0:T(8,128)(2,1)S(1)}, u32[]{:S(2)}, u32[]{:S(2)}) %all-to-all-start.2) | async-done | bytes 262176 | tf_op jit(solution)/shard_map/all_to_all | solution.py:55
  75.9 0.7 shard_map.168
  76.6 1.2 slice.71
  77.7 3.9 %all-to-all-start.3 = ((bf16[32,4,4,128]{3,2,1,0:T(4,128)(2,1)}), bf16[32,4,4,128]{3,2,1,0:T(4,128)(2,1)S(1)}, u32[]{:S(2)}, u32[]{:S(2)}) async-start(bf16[32,4,4,128]{3,2,1,0:T(4,128)(2,1)} %shard_map.168), calls=%async_computation.3 | async-start | bytes 262144 | tf_op jit(solution)/shard_map/all_to_all | solution.py:65
  82.3 1.0 slice.68
  83.3 1.8 broadcast_add_fusion.1.inverse
  85.4 6.8 %all-to-all-done.3.whole = bf16[32,4,4,128]{3,2,1,0:T(4,128)(2,1)S(1)} async-done(((bf16[32,4,4,128]{3,2,1,0:T(4,128)(2,1)}), bf16[32,4,4,128]{3,2,1,0:T(4,128)(2,1)S(1)}, u32[]{:S(2)}, u32[]{:S(2)}) %all-to-all-start.3) | async-done | bytes 131104 | tf_op jit(solution)/shard_map/all_to_all | solution.py:65
  92.2 2.0 shard_map.169
  94.2 1.2 slice.72
  95.4 3.4 %all-to-all-start.4 = ((bf16[8,2,4,512]{3,2,1,0:T(4,128)(2,1)}), bf16[8,2,4,512]{3,2,1,0:T(4,128)(2,1)S(1)}, u32[]{:S(2)}, u32[]{:S(2)}) async-start(bf16[8,2,4,512]{3,2,1,0:T(4,128)(2,1)} %shard_map.169), calls=%async_computation.4 | async-start | bytes 131072 | tf_op jit(solution)/shard_map/all_to_all | solution.py:51
  99.4 1.3 broadcast_add_fusion.3
  100.7 5.1 %all-to-all-done.4.parts = bf16[8,2,4,512]{3,2,1,0:T(4,128)(2,1)S(1)} async-done(((bf16[8,2,4,512]{3,2,1,0:T(4,128)(2,1)}), bf16[8,2,4,512]{3,2,1,0:T(4,128)(2,1)S(1)}, u32[]{:S(2)}, u32[]{:S(2)}) %all-to-all-start.4) | async-done | bytes 65568 | tf_op jit(solution)/shard_map/all_to_all | solution.py:51
  105.8 1.1 shard_map.170
  106.9 4.9 %all-to-all-start.5 = ((bf16[16,2,4,512]{3,2,1,0:T(4,128)(2,1)}), bf16[16,2,4,512]{3,2,1,0:T(4,128)(2,1)S(1)}, u32[]{:S(2)}, u32[]{:S(2)}) async-start(bf16[16,2,4,512]{3,2,1,0:T(4,128)(2,1)} %get-tuple-element.25), calls=%async_computation.5 | async-start | bytes 262144 | tf_op jit(solution)/shard_map/all_to_all | solution.py:55
  112.3 8.7 %all-to-all-done.5.parts = bf16[16,2,4,512]{3,2,1,0:T(4,128)(2,1)S(1)} async-done(((bf16[16,2,4,512]{3,2,1,0:T(4,128)(2,1)}), bf16[16,2,4,512]{3,2,1,0:T(4,128)(2,1)S(1)}, u32[]{:S(2)}, u32[]{:S(2)}) %all-to-all-start.5) | async-done | bytes 131104 | tf_op jit(solution)/shard_map/all_to_all | solution.py:55
  121.1 0.7 shard_map.171
  121.7 3.4 %all-to-all-start.6 = ((bf16[8,2,4,512]{3,2,1,0:T(4,128)(2,1)}), bf16[8,2,4,512]{3,2,1,0:T(4,128)(2,1)S(1)}, u32[]{:S(2)}, u32[]{:S(2)}) async-start(bf16[8,2,4,512]{3,2,1,0:T(4,128)(2,1)} %shard_map.171), calls=%async_computation.6 | async-start | bytes 131072 | tf_op jit(solution)/shard_map/all_to_all | solution.py:51
  125.1 0.6 broadcast_add_fusion.5.table
  125.7 7.1 %all-to-all-done.6.whole = bf16[8,2,4,512]{3,2,1,0:T(4,128)(2,1)S(1)} async-done(((bf16[8,2,4,512]{3,2,1,0:T(4,128)(2,1)}), bf16[8,2,4,512]{3,2,1,0:T(4,128)(2,1)S(1)}, u32[]{:S(2)}, u32[]{:S(2)}) %all-to-all-start.6) | async-done | bytes 65568 | tf_op jit(solution)/shard_map/all_to_all | solution.py:51
  134.0 1.9 broadcast_add_fusion
  135.9 1.4 shard_map.172
  137.3 0.6 copy-done.4
  137.9 6.2 %all-to-all-start.7 = ((bf16[8,1,4,768]{3,2,1,0:T(4,128)(2,1)}), bf16[8,1,4,768]{3,2,1,0:T(4,128)(2,1)S(1)}, u32[]{:S(2)}, u32[]{:S(2)}) async-start(bf16[8,1,4,768]{3,2,1,0:T(4,128)(2,1)} %copy-done.4), calls=%async_computation.7 | async-start | bytes 98304 | tf_op jit(solution)/shard_map/all_to_all | solution.py:51
  144.2 0.7 broadcast_in_dim.10.pivots
  144.8 6.4 %all-to-all-done.7.parts = bf16[8,1,4,768]{3,2,1,0:T(4,128)(2,1)S(1)} async-done(((bf16[8,1,4,768]{3,2,1,0:T(4,128)(2,1)}), bf16[8,1,4,768]{3,2,1,0:T(4,128)(2,1)S(1)}, u32[]{:S(2)}, u32[]{:S(2)}) %all-to-all-start.7) | async-done | bytes 49184 | tf_op jit(solution)/shard_map/all_to_all | solution.py:51
  151.6 19.1 %all_to_all.80.parts = bf16[16,1,4,1536]{3,2,1,0:T(4,128)(2,1)S(1)} all-to-all(bf16[16,1,4,1536]{3,2,1,0:T(4,128)(2,1)S(1)} %shard_map.173), channel_id=1, replica_groups=mesh['row'=16,'col'=32] {'row'}, dimensions={0} | all-to-all | bytes 393216 | tf_op jit(solution)/shard_map/all_to_all | solution.py:55
  170.8 11.3 %all_to_all.81.whole = bf16[8,1,4,1536]{3,2,1,0:T(4,128)(2,1)S(1)} all-to-all(bf16[8,1,4,1536]{3,2,1,0:T(4,128)(2,1)S(1)} %get-tuple-element.27), channel_id=1, replica_groups={{0,4,8,12,16,20,24,28},{1,5,9,13,17,21,25,29},{2,6,10,14,18,22,26,30},{..., dimensions={0} | all-to-all | bytes 196608 | tf_op jit(solution)/shard_map/all_to_all | solution.py:51
  182.1 0.8 shard_map.175
  182.9 9.5 %all_to_all.82.parts = bf16[8,2,4,512]{3,2,1,0:T(4,128)(2,1)S(1)} all-to-all(bf16[8,2,4,512]{3,2,1,0:T(4,128)(2,1)S(1)} %shard_map.175), channel_id=1, replica_groups={{0,4,8,12,16,20,24,28},{1,5,9,13,17,21,25,29},{2,6,10,14,18,22,26,30},{..., dimensions={0} | all-to-all | bytes 131072 | tf_op jit(solution)/shard_map/all_to_all | solution.py:51
  192.4 1.1 shard_map.176
  193.5 5.0 %all-to-all-start.11 = ((bf16[16,2,4,1024]{3,2,1,0:T(4,128)(2,1)}), bf16[16,2,4,1024]{3,2,1,0:T(4,128)(2,1)S(1)}, u32[]{:S(2)}, u32[]{:S(2)}) async-start(bf16[16,2,4,1024]{3,2,1,0:T(4,128)(2,1)} %shard_map.176), calls=%async_computation.11 | async-start | bytes 524288 | tf_op jit(solution)/shard_map/all_to_all | solution.py:55
  198.6 11.8 %all-to-all-done.11.parts = bf16[16,2,4,1024]{3,2,1,0:T(4,128)(2,1)S(1)} async-done(((bf16[16,2,4,1024]{3,2,1,0:T(4,128)(2,1)}), bf16[16,2,4,1024]{3,2,1,0:T(4,128)(2,1)S(1)}, u32[]{:S(2)}, u32[]{:S(2)}) %all-to-all-start.11) | async-done | bytes 262176 | tf_op jit(solution)/shard_map/all_to_all | solution.py:55
  210.3 0.7 shard_map.177
  211.0 1.2 slice.59
  212.2 3.4 %all-to-all-start.12 = ((bf16[8,2,4,1024]{3,2,1,0:T(4,128)(2,1)}), bf16[8,2,4,1024]{3,2,1,0:T(4,128)(2,1)S(1)}, u32[]{:S(2)}, u32[]{:S(2)}) async-start(bf16[8,2,4,1024]{3,2,1,0:T(4,128)(2,1)} %get-tuple-element.29), calls=%async_computation.12 | async-start | bytes 262144 | tf_op jit(solution)/shard_map/all_to_all | solution.py:51
  216.3 1.7 broadcast_add_fusion.2
  218.1 6.8 %all-to-all-done.12.whole = bf16[8,2,4,1024]{3,2,1,0:T(4,128)(2,1)S(1)} async-done(((bf16[8,2,4,1024]{3,2,1,0:T(4,128)(2,1)}), bf16[8,2,4,1024]{3,2,1,0:T(4,128)(2,1)S(1)}, u32[]{:S(2)}, u32[]{:S(2)}) %all-to-all-start.12) | async-done | bytes 131104 | tf_op jit(solution)/shard_map/all_to_all | solution.py:51
  224.9 1.6 shard_map.178
  226.5 3.4 %all-to-all-start.13 = ((bf16[8,4,4,512]{3,2,1,0:T(4,128)(2,1)}), bf16[8,4,4,512]{3,2,1,0:T(4,128)(2,1)S(1)}, u32[]{:S(2)}, u32[]{:S(2)}) async-start(bf16[8,4,4,512]{3,2,1,0:T(4,128)(2,1)} %shard_map.178), calls=%async_computation.13 | async-start | bytes 262144 | tf_op jit(solution)/shard_map/all_to_all | solution.py:51
  230.0 8.2 %all-to-all-done.13 = bf16[8,4,4,512]{3,2,1,0:T(4,128)(2,1)S(1)} async-done(((bf16[8,4,4,512]{3,2,1,0:T(4,128)(2,1)}), bf16[8,4,4,512]{3,2,1,0:T(4,128)(2,1)S(1)}, u32[]{:S(2)}, u32[]{:S(2)}) %all-to-all-start.13) | async-done | bytes 131104 | tf_op jit(solution)/shard_map/all_to_all | solution.py:51
  238.3 7.4 %all_to_all.83.got = bf16[4,4,3840]{2,1,0:T(4,128)(2,1)S(1)} all-to-all(bf16[4,4,3840]{2,1,0:T(4,128)(2,1)S(1)} %pad_maximum_fusion.1), channel_id=1, replica_groups={{0,1,2,3},{4,5,6,7},{8,9,10,11},{12,13,14,15},{16,17,18,19},{20,21,22,2..., dimensions={0} | all-to-all | bytes 245760 | tf_op jit(solution)/shard_map/all_to_all | solution.py:29
  245.7 1.1 shard_map.179
  246.8 6.5 %all-to-all-start.15 = ((bf16[16,4,16,256]{3,2,1,0:T(8,128)(2,1)}), bf16[16,4,16,256]{3,2,1,0:T(8,128)(2,1)S(1)}, u32[]{:S(2)}, u32[]{:S(2)}) async-start(bf16[16,4,16,256]{3,2,1,0:T(8,128)(2,1)} %shard_map.179), calls=%async_computation.15 | async-start | bytes 1048576 | tf_op jit(solution)/shard_map/all_to_all | solution.py:55
  253.3 0.6 pad_maximum_fusion.5
  254.0 0.6 slice_bitcast_fusion
  254.6 16.0 %all-to-all-done.15 = bf16[16,4,16,256]{3,2,1,0:T(8,128)(2,1)S(1)} async-done(((bf16[16,4,16,256]{3,2,1,0:T(8,128)(2,1)}), bf16[16,4,16,256]{3,2,1,0:T(8,128)(2,1)S(1)}, u32[]{:S(2)}, u32[]{:S(2)}) %all-to-all-start.15) | async-done | bytes 524320 | tf_op jit(solution)/shard_map/all_to_all | solution.py:55
  270.7 0.6 multiply_bitcast_fusion
  (90 shorter events, 3.6 us)
Async XLA Ops:
  7.2 75.1 %all-gather.9.cloned.1.call-start = ((), (), s32[]{:S(2)}) async-start(), calls=%async_computation.16 | async-start | bytes 2908160 | tf_op jit(solution)/shard_map/all_gather | solution.py:37
  8.0 3.1 %copy-start.13 = (f32[4,256]{1,0:T(4,128)}, f32[4,256]{1,0:T(4,128)S(1)}, u32[]{:S(2)}) copy-start(f32[4,256]{1,0:T(4,128)S(1)} %compare_convert_fusion.5) | copy-start | bytes 12292
  8.0 22.5 %copy-start.18 = (s32[4]{0:T(128)S(1)}, s32[4]{0:T(128)}, u32[]{:S(2)}) copy-start(s32[4]{0:T(128)} %param.27) | copy-start | bytes 52
  8.0 22.6 %copy-start.9 = (s32[4,32]{1,0:T(4,128)S(1)}, s32[4,32]{1,0:T(4,128)}, u32[]{:S(2)}) copy-start(s32[4,32]{1,0:T(4,128)} %blocks.3) | copy-start | bytes 1540
  9.6 33.6 %copy-start.17 = (f32[4,512]{1,0:T(4,128)S(1)}, f32[4,512]{1,0:T(4,128)}, u32[]{:S(2)}) copy-start(f32[4,512]{1,0:T(4,128)} %param.25) | copy-start | bytes 24580
  9.6 42.5 %copy-start.3 = (bf16[4,128,512]{2,1,0:T(8,128)(2,1)S(1)}, bf16[4,128,512]{2,1,0:T(8,128)(2,1)}, u32[]{:S(2)}) copy-start(bf16[4,128,512]{2,1,0:T(8,128)(2,1)} %coupling.1) | copy-start | bytes 1572868
  12.6 51.5 %copy-start.20 = (f32[2,512]{1,0:T(2,128)S(1)}, f32[2,512]{1,0:T(2,128)}, u32[]{:S(2)}) copy-start(f32[2,512]{1,0:T(2,128)} %param.24) | copy-start | bytes 12292
  12.6 51.6 %copy-start.21 = (s32[2]{0:T(128)S(1)}, s32[2]{0:T(128)}, u32[]{:S(2)}) copy-start(s32[2]{0:T(128)} %param.26) | copy-start | bytes 28
  14.6 84.8 %all-gather.11.cloned.1.call-start = ((), (), s32[]{:S(2)}) async-start(), calls=%async_computation.17 | async-start | bytes 1310720 | tf_op jit(solution)/shard_map/all_gather | solution.py:37
  15.4 118.6 %all-gather.13.cloned.1.call-start = ((), (), s32[]{:S(2)}) async-start(), calls=%async_computation.18 | async-start | bytes 2949120 | tf_op jit(solution)/shard_map/all_gather | solution.py:37
  16.1 22.6 %all-to-all-start = ((bf16[32,2,512]{2,1,0:T(2,128)(2,1)}), bf16[32,2,512]{2,1,0:T(2,128)(2,1)S(1)}, u32[]{:S(2)}, u32[]{:S(2)}) async-start(bf16[32,2,512]{2,1,0:T(2,128)(2,1)} %reshape.244), calls=%async_computation | async-start | bytes 131072 | tf_op jit(solution)/shard_map/all_to_all | solution.py:65
  29.9 186.4 %all-gather.15.cloned.1.call-start = ((), (), s32[]{:S(2)}) async-start(), calls=%async_computation.19 | async-start | bytes 2621440 | tf_op jit(solution)/shard_map/all_gather | solution.py:37
  30.5 54.6 %copy-start.15 = (s32[512]{0:T(512)}, s32[512]{0:T(512)S(1)}, u32[]{:S(2)}) copy-start(s32[512]{0:T(512)S(1)} %iota_add_fusion.1) | copy-start | bytes 6148
  39.4 12.7 %all-to-all-start.1 = ((bf16[32,2,512]{2,1,0:T(2,128)(2,1)}), bf16[32,2,512]{2,1,0:T(2,128)(2,1)S(1)}, u32[]{:S(2)}, u32[]{:S(2)}) async-start(bf16[32,2,512]{2,1,0:T(2,128)(2,1)} %shard_map.166), calls=%async_computation.1 | async-start | bytes 131072 | tf_op jit(solution)/shard_map/all_to_all | solution.py:65
  53.2 0.6 copy-start.5
  53.8 22.1 %all-to-all-start.2 = ((bf16[16,4,16,128]{3,2,1,0:T(8,128)(2,1)}), bf16[16,4,16,128]{3,2,1,0:T(8,128)(2,1)S(1)}, u32[]{:S(2)}, u32[]{:S(2)}) async-start(bf16[16,4,16,128]{3,2,1,0:T(8,128)(2,1)} %get-tuple-element.20), calls=%async_computation.2 | async-start | bytes 524288 | tf_op jit(solution)/shard_map/all_to_all | solution.py:55
  77.7 14.5 %all-to-all-start.3 = ((bf16[32,4,4,128]{3,2,1,0:T(4,128)(2,1)}), bf16[32,4,4,128]{3,2,1,0:T(4,128)(2,1)S(1)}, u32[]{:S(2)}, u32[]{:S(2)}) async-start(bf16[32,4,4,128]{3,2,1,0:T(4,128)(2,1)} %shard_map.168), calls=%async_computation.3 | async-start | bytes 262144 | tf_op jit(solution)/shard_map/all_to_all | solution.py:65
  85.1 15.6 %copy-start = (bf16[4,1136,256]{2,1,0:T(8,128)(2,1)}, bf16[4,1136,256]{2,1,0:T(8,128)(2,1)S(1)}, u32[]{:S(2)}) copy-start(bf16[4,1136,256]{2,1,0:T(8,128)(2,1)S(1)} %broadcast_add_fusion.1.inverse) | copy-start | bytes 6979588
  94.2 17.7 %copy-start.10 = (s32[2,32]{1,0:T(2,128)S(1)}, s32[2,32]{1,0:T(2,128)}, u32[]{:S(2)}) copy-start(s32[2,32]{1,0:T(2,128)} %blocks.2) | copy-start | bytes 772
  95.4 10.4 %all-to-all-start.4 = ((bf16[8,2,4,512]{3,2,1,0:T(4,128)(2,1)}), bf16[8,2,4,512]{3,2,1,0:T(4,128)(2,1)S(1)}, u32[]{:S(2)}, u32[]{:S(2)}) async-start(bf16[8,2,4,512]{3,2,1,0:T(4,128)(2,1)} %shard_map.169), calls=%async_computation.4 | async-start | bytes 131072 | tf_op jit(solution)/shard_map/all_to_all | solution.py:51
  106.9 27.1 %copy-start.7 = (f32[2,4,512]{2,1,0:T(4,128)}, f32[2,4,512]{2,1,0:T(4,128)S(1)}, u32[]{:S(2)}) copy-start(f32[2,4,512]{2,1,0:T(4,128)S(1)} %get-tuple-element.28.scaled) | copy-start | bytes 49156
  106.9 14.1 %all-to-all-start.5 = ((bf16[16,2,4,512]{3,2,1,0:T(4,128)(2,1)}), bf16[16,2,4,512]{3,2,1,0:T(4,128)(2,1)S(1)}, u32[]{:S(2)}, u32[]{:S(2)}) async-start(bf16[16,2,4,512]{3,2,1,0:T(4,128)(2,1)} %get-tuple-element.25), calls=%async_computation.5 | async-start | bytes 262144 | tf_op jit(solution)/shard_map/all_to_all | solution.py:55
  121.7 11.1 %all-to-all-start.6 = ((bf16[8,2,4,512]{3,2,1,0:T(4,128)(2,1)}), bf16[8,2,4,512]{3,2,1,0:T(4,128)(2,1)S(1)}, u32[]{:S(2)}, u32[]{:S(2)}) async-start(bf16[8,2,4,512]{3,2,1,0:T(4,128)(2,1)} %shard_map.171), calls=%async_computation.6 | async-start | bytes 131072 | tf_op jit(solution)/shard_map/all_to_all | solution.py:51
  134.0 1.9 copy-start.12
  137.3 0.6 copy-start.4
  137.9 44.2 %copy-start.11 = (s32[2,32]{1,0:T(2,128)S(1)}, s32[2,32]{1,0:T(2,128)}, u32[]{:S(2)}) copy-start(s32[2,32]{1,0:T(2,128)} %blocks.2) | copy-start | bytes 772
  137.9 13.3 %all-to-all-start.7 = ((bf16[8,1,4,768]{3,2,1,0:T(4,128)(2,1)}), bf16[8,1,4,768]{3,2,1,0:T(4,128)(2,1)S(1)}, u32[]{:S(2)}, u32[]{:S(2)}) async-start(bf16[8,1,4,768]{3,2,1,0:T(4,128)(2,1)} %copy-done.4), calls=%async_computation.7 | async-start | bytes 98304 | tf_op jit(solution)/shard_map/all_to_all | solution.py:51
  144.8 47.6 %copy-start.8 = (f32[2,4,512]{2,1,0:T(4,128)S(1)}, f32[2,4,512]{2,1,0:T(4,128)}, u32[]{:S(2)}) copy-start(f32[2,4,512]{2,1,0:T(4,128)} %copy-done.7) | copy-start | bytes 49156
  151.2 41.2 %copy-start.1 = (bf16[4,1136,256]{2,1,0:T(8,128)(2,1)S(1)}, bf16[4,1136,256]{2,1,0:T(8,128)(2,1)}, u32[]{:S(2)}) copy-start(bf16[4,1136,256]{2,1,0:T(8,128)(2,1)} %copy-done) | copy-start | bytes 6979588
  170.8 27.7 %copy-start.16 = (s32[512]{0:T(512)S(1)}, s32[512]{0:T(512)}, u32[]{:S(2)}) copy-start(s32[512]{0:T(512)} %copy-done.15) | copy-start | bytes 6148
  170.8 27.7 %copy-start.19 = (s32[4]{0:T(128)S(1)}, s32[4]{0:T(128)}, u32[]{:S(2)}) copy-start(s32[4]{0:T(128)} %param.27) | copy-start | bytes 52
  193.5 16.8 %all-to-all-start.11 = ((bf16[16,2,4,1024]{3,2,1,0:T(4,128)(2,1)}), bf16[16,2,4,1024]{3,2,1,0:T(4,128)(2,1)S(1)}, u32[]{:S(2)}, u32[]{:S(2)}) async-start(bf16[16,2,4,1024]{3,2,1,0:T(4,128)(2,1)} %shard_map.176), calls=%async_computation.11 | async-start | bytes 524288 | tf_op jit(solution)/shard_map/all_to_all | solution.py:55
  212.2 12.7 %all-to-all-start.12 = ((bf16[8,2,4,1024]{3,2,1,0:T(4,128)(2,1)}), bf16[8,2,4,1024]{3,2,1,0:T(4,128)(2,1)S(1)}, u32[]{:S(2)}, u32[]{:S(2)}) async-start(bf16[8,2,4,1024]{3,2,1,0:T(4,128)(2,1)} %get-tuple-element.29), calls=%async_computation.12 | async-start | bytes 262144 | tf_op jit(solution)/shard_map/all_to_all | solution.py:51
  218.1 20.2 %copy-start.6 = (f32[4,4,512]{2,1,0:T(4,128)S(1)}, f32[4,4,512]{2,1,0:T(4,128)}, u32[]{:S(2)}) copy-start(f32[4,4,512]{2,1,0:T(4,128)} %copy-done.5) | copy-start | bytes 98308
  218.1 27.6 %copy-start.2 = (bf16[4,512,256]{2,1,0:T(8,128)(2,1)S(1)}, bf16[4,512,256]{2,1,0:T(8,128)(2,1)}, u32[]{:S(2)}) copy-start(bf16[4,512,256]{2,1,0:T(8,128)(2,1)} %inverse.1) | copy-start | bytes 3145732
  226.5 11.6 %all-to-all-start.13 = ((bf16[8,4,4,512]{3,2,1,0:T(4,128)(2,1)}), bf16[8,4,4,512]{3,2,1,0:T(4,128)(2,1)S(1)}, u32[]{:S(2)}, u32[]{:S(2)}) async-start(bf16[8,4,4,512]{3,2,1,0:T(4,128)(2,1)} %shard_map.178), calls=%async_computation.13 | async-start | bytes 262144 | tf_op jit(solution)/shard_map/all_to_all | solution.py:51
  238.2 32.4 %copy-start.14 = (f32[4,256]{1,0:T(4,128)S(1)}, f32[4,256]{1,0:T(4,128)}, u32[]{:S(2)}) copy-start(f32[4,256]{1,0:T(4,128)} %copy-done.13) | copy-start | bytes 12292
  246.8 23.8 %all-to-all-start.15 = ((bf16[16,4,16,256]{3,2,1,0:T(8,128)(2,1)}), bf16[16,4,16,256]{3,2,1,0:T(8,128)(2,1)S(1)}, u32[]{:S(2)}, u32[]{:S(2)}) async-start(bf16[16,4,16,256]{3,2,1,0:T(8,128)(2,1)} %shard_map.179), calls=%async_computation.15 | async-start | bytes 1048576 | tf_op jit(solution)/shard_map/all_to_all | solution.py:55
Sparse Core Ops, SparseCore 0:
  14.8 44.2 all-gather.8
  61.2 29.0 all-gather.10
  92.4 40.5 all-gather.12
  135.0 36.2 all-gather.14

commit v11 on v10

--- a/solution.py
+++ b/solution.py
@@ -40,6 +40,10 @@
 def settled(array, message):
     zero = lax.slice(message, (0,) * message.ndim, (1,) * message.ndim).reshape(()) * 0
     return array + zero.astype(array.dtype)
+
+
+def settled_by(array, zeros):
+    return array + zeros.reshape((1,) * (array.ndim - 1) + (-1,)).astype(array.dtype)
 
 
 def copies_of(value, size):
@@ -163,7 +167,8 @@
     return call(last_kernel, out, [], [got, inverse])
 
 
-def scatter_kernel(parts, out):
+def scatter_kernel(parts, out, zeros):
+    zeros[...] = jnp.zeros_like(zeros)
     width = out.shape[2]
     for f in range(parts.shape[1]):
         value = arrived(parts, f)
@@ -173,10 +178,10 @@
                 out[z * NEAR + x, f] = share
 
 
-def relay_scattered(parts):
+def relay_scattered(parts, zeros):
     _, fronts, rhs, count = parts.shape
     out = shape_of(lax.axis_size("col"), fronts, rhs // NEAR, count)
-    return call(scatter_kernel, out, [], [parts])
+    return call(scatter_kernel, (out, shape_of(1, zeros, dtype=F32)), [], [parts])
 
 
 def update_kernel(parts, mask, pivots, coupling, out, scaled):
@@ -207,20 +212,22 @@
     return call(relay_kernel, shape_of(far_size(), *parts.shape[1:]), [], [parts])
 
 
-def solved_kernel(parts, mask, out, solved):
+def solved_kernel(parts, mask, out, solved, zeros):
+    zeros[...] = jnp.zeros_like(zeros)
     for f in range(parts.shape[1]):
         value = arrived(parts, f) * mask[f]
         solved[f] = value
         write_copies(out, f, value)
 
 
-def relay_solved(parts, mask):
+def relay_solved(parts, mask, zeros):
     shape = parts.shape[1:]
-    out = (shape_of(far_size(), *shape), shape_of(*shape, dtype=F32))
+    out = (shape_of(far_size(), *shape), shape_of(*shape, dtype=F32), shape_of(1, zeros, dtype=F32))
     return call(solved_kernel, out, [], [parts, mask])
 
 
-def place_kernel(table, whole, source, mask, inverse, out, *, base):
+def place_kernel(table, whole, source, mask, inverse, out, zeros, *, base):
+    zeros[...] = jnp.zeros_like(zeros)
     n = inverse.shape[2]
     held = n // BLOCK
     count = out.shape[3]
@@ -250,8 +257,8 @@
         write_copies(out, p, total.T[: out.shape[2]])
 
 
-def place_and_solve(table, whole, source, mask, inverse, parents, count, base):
-    out = shape_of(far_size(), parents, whole.shape[2], count)
+def place_and_solve(table, whole, source, mask, inverse, parents, count, base, zeros):
+    out = (shape_of(far_size(), parents, whole.shape[2], count), shape_of(1, zeros, dtype=F32))
     return call(place_kernel, out, [table], [whole, source, mask, inverse], base=base)
 
 
@@ -364,35 +371,38 @@
 
     parts = send_col(relay_pieces(send_col(message)))
     message, scaled_low = first_update(near, parts, row_mask_low, pivots_low, coupling_low)
-    message = relay_scattered(send_row(message))
-    staged_mid = settled(packed_near, message)
+    message, zeros = relay_scattered(send_row(message), n1)
+    staged_mid = settled_by(packed_near, zeros)
     whole = send_col(message)
 
     halved = packed_near[:, 2 * k1 :].reshape(NEAR, rhs, -1)
     halved = lax.dynamic_slice_in_dim(halved, (col_at % NEAR) * width, width, 1).astype(F32)
     size = halved.shape[2] // 2
     others = halved[:, :, :size] + halved[:, :, size:]
-    message = place_and_solve(table_low, whole, others, wide_mask_mid, staged_mid, 2, k1, 0)
-    coupling_mid_near = settled(coupling_mid_near, message)
+    message, zeros = place_and_solve(
+        table_low, whole, others, wide_mask_mid, staged_mid, 2, k1, 0, k1
+    )
+    coupling_mid_near = settled_by(coupling_mid_near, zeros)
     parts = send_far(message)
 
     message, scaled_mid = update_of(parts, row_mask_mid, pivots_mid, coupling_mid_near)
     whole = send_far(relay(send_row(message)))
     inverse_top_near = settled(inverse_top_near, whole)
     k0 = inverse_top.shape[0]
-    parts = send_far(
-        place_and_solve(table_mid, whole, others, wide_mask_top, inverse_top_near, 1, k0, 2 * n1)
-    )
-
-    message, solution_top = relay_solved(
-        send_row(root_back(parts, pivots_top, inverse_top_near)), wide_mask_top
+    message, _ = place_and_solve(
+        table_mid, whole, others, wide_mask_top, inverse_top_near, 1, k0, 2 * n1, k1
+    )
+    parts = send_far(message)
+
+    message, solution_top, _ = relay_solved(
+        send_row(root_back(parts, pivots_top, inverse_top_near)), wide_mask_top, k2
     )
     message = pick_and_carry(far, blocks_mid, send_far(message), coupling_mid_near)
     parts = send_far(message)
-    message, solution_mid = relay_solved(
-        send_row(back(parts, scaled_mid, row_mask_mid, staged_mid)), wide_mask_mid
-    )
-    coupling_low_near = settled(coupling_low_near, message)
+    message, solution_mid, zeros = relay_solved(
+        send_row(back(parts, scaled_mid, row_mask_mid, staged_mid)), wide_mask_mid, k2
+    )
+    coupling_low_near = settled_by(coupling_low_near, zeros)
     parts = send_far(pick_and_carry(far, blocks_low, send_far(message), coupling_low_near))
     residual = (scaled_low - jnp.sum(parts.astype(F32), axis=0)) * row_mask_low
 

time: 280 us -> 279 us (level)
  local copies, waits for them, and re-layouts: 9.56 us -> 6.59 us
    add x4 -> x1, other arithmetic: 6.76 us -> 1.88 us  [settled(): return array + zero.astype(array.dtype)]
    add x0 -> x3, other arithmetic: none -> 4.86 us  [settled_by(): array + zeros.reshape((1,) * (array.ndim - 1) + (-1,)).astype(array.dtype)]
    slice x4 -> x1, local copies, waits for them, and re-layouts: 4.07 us -> 0.51 us  [settled(): lax.slice(message, (0,) * message.ndim, (1,) * message.ndim).reshape(()) * 0]
  transfers between devices with their start and end apart: 16 -> 16, of which waited for: 12 -> 12; matrix products, arithmetic and copies ran while one was open for 6% -> 5% of each run, Pallas kernels for 4% -> 4%
where the time goes in v11:
time: 279 us; the launch traced here: 277 us
  waiting for transfers between devices  109 us (39%)
  starting transfers between devices  68.9 us (25%)
  blocking collectives  47.4 us (17%)
  between operations  15 us (5%)
  other arithmetic  14.6 us (5%)
  Pallas kernels  14.4 us (5%)
  local copies, waits for them, and re-layouts  6.59 us (2%)
    all_to_all x4, waiting for transfers between devices, send_row(): return lax.all_to_all(copies, 'row', 0, 0, tiled=True)  47.5 us
    all_to_all x5, waiting for transfers between devices, send_far(): lax.all_to_all(copies, 'col', 0, 0, axis_index_groups=groups, tiled=True)  35 us
    all_to_all x4, starting transfers between devices, send_row(): return lax.all_to_all(copies, 'row', 0, 0, tiled=True)  26.8 us
    all_to_all x3, waiting for transfers between devices, send_col(): return lax.all_to_all(copies, 'col', 0, 0, tiled=True)  24.1 us
    all_to_all x3, starting transfers between devices, send_col(): return lax.all_to_all(copies, 'col', 0, 0, tiled=True)  21.4 us
    all_to_all x2, blocking collectives, send_far(): lax.all_to_all(copies, 'col', 0, 0, axis_index_groups=groups, tiled=True)  20.9 us
    all_to_all x5, starting transfers between devices, send_far(): lax.all_to_all(copies, 'col', 0, 0, axis_index_groups=groups, tiled=True)  20.5 us
    all_to_all x1, blocking collectives, send_row(): return lax.all_to_all(copies, 'row', 0, 0, tiled=True)  19.1 us
  transfers between devices with their start and end apart: 16, of which 12 were waited for; matrix products, arithmetic and copies ran while one was open for 5% of the time, Pallas kernels for 4%

profile of v11, /device:TPU:1, one launch (start us, length us, event | category | flops | bytes accessed | tf_op | source)
XLA Modules:
  0.0 277.1 jit_solution(6572896567346938199)
XLA Ops:
  7.2 0.7 compare_convert_fusion.5
  8.0 1.7 convolution_convert_fusion
  9.6 0.7 reshape.262
  10.3 0.7 slice_bitcast_fusion.4
  11.0 0.7 fusion
  11.8 0.7 subtract_convert_fusion.1
  12.7 1.9 pad_maximum_fusion
  14.7 0.7 all-gather.11.cloned.1.call-update
  15.4 0.7 all-gather.13.cloned.1.call-update
  16.1 13.7 %all-to-all-start = ((bf16[32,2,512]{2,1,0:T(2,128)(2,1)}), bf16[32,2,512]{2,1,0:T(2,128)(2,1)S(1)}, u32[]{:S(2)}, u32[]{:S(2)}) async-start(bf16[32,2,512]{2,1,0:T(2,128)(2,1)} %reshape.262), calls=%async_computation | async-start | bytes 131072 | tf_op jit(solution)/shard_map/all_to_all | solution.py:69
  30.8 7.9 %all-to-all-done.parts = bf16[32,2,512]{2,1,0:T(2,128)(2,1)S(1)} async-done(((bf16[32,2,512]{2,1,0:T(2,128)(2,1)}), bf16[32,2,512]{2,1,0:T(2,128)(2,1)S(1)}, u32[]{:S(2)}, u32[]{:S(2)}) %all-to-all-start) | async-done | bytes 65568 | tf_op jit(solution)/shard_map/all_to_all | solution.py:69
  38.7 0.7 shard_map.166
  39.3 3.9 %all-to-all-start.1 = ((bf16[32,2,512]{2,1,0:T(2,128)(2,1)}), bf16[32,2,512]{2,1,0:T(2,128)(2,1)S(1)}, u32[]{:S(2)}, u32[]{:S(2)}) async-start(bf16[32,2,512]{2,1,0:T(2,128)(2,1)} %shard_map.166), calls=%async_computation.1 | async-start | bytes 131072 | tf_op jit(solution)/shard_map/all_to_all | solution.py:69
  43.3 8.8 %all-to-all-done.1.parts = bf16[32,2,512]{2,1,0:T(2,128)(2,1)S(1)} async-done(((bf16[32,2,512]{2,1,0:T(2,128)(2,1)}), bf16[32,2,512]{2,1,0:T(2,128)(2,1)S(1)}, u32[]{:S(2)}, u32[]{:S(2)}) %all-to-all-start.1) | async-done | bytes 65568 | tf_op jit(solution)/shard_map/all_to_all | solution.py:69
  52.1 1.1 shard_map.167
  53.1 0.6 copy-done.5
  53.8 10.4 %all-to-all-start.2 = ((bf16[16,4,16,128]{3,2,1,0:T(8,128)(2,1)}), bf16[16,4,16,128]{3,2,1,0:T(8,128)(2,1)S(1)}, u32[]{:S(2)}, u32[]{:S(2)}) async-start(bf16[16,4,16,128]{3,2,1,0:T(8,128)(2,1)} %get-tuple-element.26), calls=%async_computation.2 | async-start | bytes 524288 | tf_op jit(solution)/shard_map/all_to_all | solution.py:59
  64.1 0.6 iota_add_fusion.5
  64.8 11.0 %all-to-all-done.2.parts = bf16[16,4,16,128]{3,2,1,0:T(8,128)(2,1)S(1)} async-done(((bf16[16,4,16,128]{3,2,1,0:T(8,128)(2,1)}), bf16[16,4,16,128]{3,2,1,0:T(8,128)(2,1)S(1)}, u32[]{:S(2)}, u32[]{:S(2)}) %all-to-all-start.2) | async-done | bytes 262176 | tf_op jit(solution)/shard_map/all_to_all | solution.py:59
  75.8 0.7 shard_map.168
  76.6 3.9 %all-to-all-start.3 = ((bf16[32,4,4,128]{3,2,1,0:T(4,128)(2,1)}), bf16[32,4,4,128]{3,2,1,0:T(4,128)(2,1)S(1)}, u32[]{:S(2)}, u32[]{:S(2)}) async-start(bf16[32,4,4,128]{3,2,1,0:T(4,128)(2,1)} %get-tuple-element.27), calls=%async_computation.3 | async-start | bytes 262144 | tf_op jit(solution)/shard_map/all_to_all | solution.py:69
  80.5 1.0 slice.56
  81.4 1.8 broadcast_add_fusion.1.inverse
  83.6 7.4 %all-to-all-done.3.whole = bf16[32,4,4,128]{3,2,1,0:T(4,128)(2,1)S(1)} async-done(((bf16[32,4,4,128]{3,2,1,0:T(4,128)(2,1)}), bf16[32,4,4,128]{3,2,1,0:T(4,128)(2,1)S(1)}, u32[]{:S(2)}, u32[]{:S(2)}) %all-to-all-start.3) | async-done | bytes 131104 | tf_op jit(solution)/shard_map/all_to_all | solution.py:69
  91.0 2.0 shard_map.169
  93.0 3.4 %all-to-all-start.4 = ((bf16[8,2,4,512]{3,2,1,0:T(4,128)(2,1)}), bf16[8,2,4,512]{3,2,1,0:T(4,128)(2,1)S(1)}, u32[]{:S(2)}, u32[]{:S(2)}) async-start(bf16[8,2,4,512]{3,2,1,0:T(4,128)(2,1)} %get-tuple-element.33), calls=%async_computation.4 | async-start | bytes 131072 | tf_op jit(solution)/shard_map/all_to_all | solution.py:55
  96.4 1.3 broadcast_add_fusion.3.coupling
  97.7 5.8 %all-to-all-done.4.parts = bf16[8,2,4,512]{3,2,1,0:T(4,128)(2,1)S(1)} async-done(((bf16[8,2,4,512]{3,2,1,0:T(4,128)(2,1)}), bf16[8,2,4,512]{3,2,1,0:T(4,128)(2,1)S(1)}, u32[]{:S(2)}, u32[]{:S(2)}) %all-to-all-start.4) | async-done | bytes 65568 | tf_op jit(solution)/shard_map/all_to_all | solution.py:55
  103.6 1.1 shard_map.170
  104.7 0.6 copy-done.7
  105.3 4.9 %all-to-all-start.5 = ((bf16[16,2,4,512]{3,2,1,0:T(4,128)(2,1)}), bf16[16,2,4,512]{3,2,1,0:T(4,128)(2,1)S(1)}, u32[]{:S(2)}, u32[]{:S(2)}) async-start(bf16[16,2,4,512]{3,2,1,0:T(4,128)(2,1)} %get-tuple-element.35), calls=%async_computation.5 | async-start | bytes 262144 | tf_op jit(solution)/shard_map/all_to_all | solution.py:59
  110.7 8.7 %all-to-all-done.5.parts = bf16[16,2,4,512]{3,2,1,0:T(4,128)(2,1)S(1)} async-done(((bf16[16,2,4,512]{3,2,1,0:T(4,128)(2,1)}), bf16[16,2,4,512]{3,2,1,0:T(4,128)(2,1)S(1)}, u32[]{:S(2)}, u32[]{:S(2)}) %all-to-all-start.5) | async-done | bytes 131104 | tf_op jit(solution)/shard_map/all_to_all | solution.py:59
  119.4 0.7 shard_map.171
  120.1 3.4 %all-to-all-start.6 = ((bf16[8,2,4,512]{3,2,1,0:T(4,128)(2,1)}), bf16[8,2,4,512]{3,2,1,0:T(4,128)(2,1)S(1)}, u32[]{:S(2)}, u32[]{:S(2)}) async-start(bf16[8,2,4,512]{3,2,1,0:T(4,128)(2,1)} %shard_map.171), calls=%async_computation.6 | async-start | bytes 131072 | tf_op jit(solution)/shard_map/all_to_all | solution.py:55
  123.5 0.6 broadcast_add_fusion.5.table
  124.0 7.1 %all-to-all-done.6.whole = bf16[8,2,4,512]{3,2,1,0:T(4,128)(2,1)S(1)} async-done(((bf16[8,2,4,512]{3,2,1,0:T(4,128)(2,1)}), bf16[8,2,4,512]{3,2,1,0:T(4,128)(2,1)S(1)}, u32[]{:S(2)}, u32[]{:S(2)}) %all-to-all-start.6) | async-done | bytes 65568 | tf_op jit(solution)/shard_map/all_to_all | solution.py:55
  132.4 1.9 broadcast_add_fusion
  134.3 1.9 shard_map.172
  136.2 0.6 copy-done.4
  136.8 7.1 %all-to-all-start.7 = ((bf16[8,1,4,768]{3,2,1,0:T(4,128)(2,1)}), bf16[8,1,4,768]{3,2,1,0:T(4,128)(2,1)S(1)}, u32[]{:S(2)}, u32[]{:S(2)}) async-start(bf16[8,1,4,768]{3,2,1,0:T(4,128)(2,1)} %copy-done.4), calls=%async_computation.7 | async-start | bytes 98304 | tf_op jit(solution)/shard_map/all_to_all | solution.py:55
  143.9 0.7 broadcast_in_dim.10.pivots
  144.6 6.4 %all-to-all-done.7.parts = bf16[8,1,4,768]{3,2,1,0:T(4,128)(2,1)S(1)} async-done(((bf16[8,1,4,768]{3,2,1,0:T(4,128)(2,1)}), bf16[8,1,4,768]{3,2,1,0:T(4,128)(2,1)S(1)}, u32[]{:S(2)}, u32[]{:S(2)}) %all-to-all-start.7) | async-done | bytes 49184 | tf_op jit(solution)/shard_map/all_to_all | solution.py:55
  151.4 19.1 %all_to_all.80.parts = bf16[16,1,4,1536]{3,2,1,0:T(4,128)(2,1)S(1)} all-to-all(bf16[16,1,4,1536]{3,2,1,0:T(4,128)(2,1)S(1)} %shard_map.173), channel_id=1, replica_groups=mesh['row'=16,'col'=32] {'row'}, dimensions={0} | all-to-all | bytes 393216 | tf_op jit(solution)/shard_map/all_to_all | solution.py:59
  170.5 0.6 shard_map.174
  171.1 11.4 %all_to_all.81.whole = bf16[8,1,4,1536]{3,2,1,0:T(4,128)(2,1)S(1)} all-to-all(bf16[8,1,4,1536]{3,2,1,0:T(4,128)(2,1)S(1)} %get-tuple-element.38), channel_id=1, replica_groups={{0,4,8,12,16,20,24,28},{1,5,9,13,17,21,25,29},{2,6,10,14,18,22,26,30},{..., dimensions={0} | all-to-all | bytes 196608 | tf_op jit(solution)/shard_map/all_to_all | solution.py:55
  182.5 0.8 shard_map.175
  183.3 9.5 %all_to_all.82.parts = bf16[8,2,4,512]{3,2,1,0:T(4,128)(2,1)S(1)} all-to-all(bf16[8,2,4,512]{3,2,1,0:T(4,128)(2,1)S(1)} %shard_map.175), channel_id=1, replica_groups={{0,4,8,12,16,20,24,28},{1,5,9,13,17,21,25,29},{2,6,10,14,18,22,26,30},{..., dimensions={0} | all-to-all | bytes 131072 | tf_op jit(solution)/shard_map/all_to_all | solution.py:55
  192.8 1.1 shard_map.176
  193.9 5.0 %all-to-all-start.11 = ((bf16[16,2,4,1024]{3,2,1,0:T(4,128)(2,1)}), bf16[16,2,4,1024]{3,2,1,0:T(4,128)(2,1)S(1)}, u32[]{:S(2)}, u32[]{:S(2)}) async-start(bf16[16,2,4,1024]{3,2,1,0:T(4,128)(2,1)} %shard_map.176), calls=%async_computation.11 | async-start | bytes 524288 | tf_op jit(solution)/shard_map/all_to_all | solution.py:59
  198.9 11.8 %all-to-all-done.11.parts = bf16[16,2,4,1024]{3,2,1,0:T(4,128)(2,1)S(1)} async-done(((bf16[16,2,4,1024]{3,2,1,0:T(4,128)(2,1)}), bf16[16,2,4,1024]{3,2,1,0:T(4,128)(2,1)S(1)}, u32[]{:S(2)}, u32[]{:S(2)}) %all-to-all-start.11) | async-done | bytes 262176 | tf_op jit(solution)/shard_map/all_to_all | solution.py:59
  210.7 0.7 shard_map.177
  211.4 3.4 %all-to-all-start.12 = ((bf16[8,2,4,1024]{3,2,1,0:T(4,128)(2,1)}), bf16[8,2,4,1024]{3,2,1,0:T(4,128)(2,1)S(1)}, u32[]{:S(2)}, u32[]{:S(2)}) async-start(bf16[8,2,4,1024]{3,2,1,0:T(4,128)(2,1)} %get-tuple-element.40), calls=%async_computation.12 | async-start | bytes 262144 | tf_op jit(solution)/shard_map/all_to_all | solution.py:55
  214.9 1.7 broadcast_add_fusion.2.coupling
  216.6 7.5 %all-to-all-done.12.whole = bf16[8,2,4,1024]{3,2,1,0:T(4,128)(2,1)S(1)} async-done(((bf16[8,2,4,1024]{3,2,1,0:T(4,128)(2,1)}), bf16[8,2,4,1024]{3,2,1,0:T(4,128)(2,1)S(1)}, u32[]{:S(2)}, u32[]{:S(2)}) %all-to-all-start.12) | async-done | bytes 131104 | tf_op jit(solution)/shard_map/all_to_all | solution.py:55
  224.1 1.6 shard_map.178
  225.7 3.4 %all-to-all-start.13 = ((bf16[8,4,4,512]{3,2,1,0:T(4,128)(2,1)}), bf16[8,4,4,512]{3,2,1,0:T(4,128)(2,1)S(1)}, u32[]{:S(2)}, u32[]{:S(2)}) async-start(bf16[8,4,4,512]{3,2,1,0:T(4,128)(2,1)} %shard_map.178), calls=%async_computation.13 | async-start | bytes 262144 | tf_op jit(solution)/shard_map/all_to_all | solution.py:55
  229.2 8.2 %all-to-all-done.13 = bf16[8,4,4,512]{3,2,1,0:T(4,128)(2,1)S(1)} async-done(((bf16[8,4,4,512]{3,2,1,0:T(4,128)(2,1)}), bf16[8,4,4,512]{3,2,1,0:T(4,128)(2,1)S(1)}, u32[]{:S(2)}, u32[]{:S(2)}) %all-to-all-start.13) | async-done | bytes 131104 | tf_op jit(solution)/shard_map/all_to_all | solution.py:55
  237.5 7.4 %all_to_all.83.got = bf16[4,4,3840]{2,1,0:T(4,128)(2,1)S(1)} all-to-all(bf16[4,4,3840]{2,1,0:T(4,128)(2,1)S(1)} %pad_maximum_fusion.1), channel_id=1, replica_groups={{0,1,2,3},{4,5,6,7},{8,9,10,11},{12,13,14,15},{16,17,18,19},{20,21,22,2..., dimensions={0} | all-to-all | bytes 245760 | tf_op jit(solution)/shard_map/all_to_all | solution.py:29
  244.9 1.1 shard_map.179
  246.0 6.5 %all-to-all-start.15 = ((bf16[16,4,16,256]{3,2,1,0:T(8,128)(2,1)}), bf16[16,4,16,256]{3,2,1,0:T(8,128)(2,1)S(1)}, u32[]{:S(2)}, u32[]{:S(2)}) async-start(bf16[16,4,16,256]{3,2,1,0:T(8,128)(2,1)} %shard_map.179), calls=%async_computation.15 | async-start | bytes 1048576 | tf_op jit(solution)/shard_map/all_to_all | solution.py:59
  252.6 0.6 pad_maximum_fusion.5
  253.2 0.6 slice_bitcast_fusion
  253.8 16.0 %all-to-all-done.15 = bf16[16,4,16,256]{3,2,1,0:T(8,128)(2,1)S(1)} async-done(((bf16[16,4,16,256]{3,2,1,0:T(8,128)(2,1)}), bf16[16,4,16,256]{3,2,1,0:T(8,128)(2,1)S(1)}, u32[]{:S(2)}, u32[]{:S(2)}) %all-to-all-start.15) | async-done | bytes 524320 | tf_op jit(solution)/shard_map/all_to_all | solution.py:59
  269.9 0.6 multiply_bitcast_fusion
  (96 shorter events, 3.6 us)
Async XLA Ops:
  7.2 73.3 %all-gather.9.cloned.1.call-start = ((), (), s32[]{:S(2)}) async-start(), calls=%async_computation.16 | async-start | bytes 2908160 | tf_op jit(solution)/shard_map/all_gather | solution.py:37
  8.0 3.1 %copy-start.13 = (f32[4,256]{1,0:T(4,128)}, f32[4,256]{1,0:T(4,128)S(1)}, u32[]{:S(2)}) copy-start(f32[4,256]{1,0:T(4,128)S(1)} %compare_convert_fusion.5) | copy-start | bytes 12292
  8.0 22.5 %copy-start.18 = (s32[4]{0:T(128)S(1)}, s32[4]{0:T(128)}, u32[]{:S(2)}) copy-start(s32[4]{0:T(128)} %param.27) | copy-start | bytes 52
  8.0 22.6 %copy-start.9 = (s32[4,32]{1,0:T(4,128)S(1)}, s32[4,32]{1,0:T(4,128)}, u32[]{:S(2)}) copy-start(s32[4,32]{1,0:T(4,128)} %blocks.3) | copy-start | bytes 1540
  9.6 33.6 %copy-start.17 = (f32[4,512]{1,0:T(4,128)S(1)}, f32[4,512]{1,0:T(4,128)}, u32[]{:S(2)}) copy-start(f32[4,512]{1,0:T(4,128)} %param.25) | copy-start | bytes 24580
  9.6 42.5 %copy-start.3 = (bf16[4,128,512]{2,1,0:T(8,128)(2,1)S(1)}, bf16[4,128,512]{2,1,0:T(8,128)(2,1)}, u32[]{:S(2)}) copy-start(bf16[4,128,512]{2,1,0:T(8,128)(2,1)} %coupling.1) | copy-start | bytes 1572868
  12.6 52.1 %copy-start.20 = (f32[2,512]{1,0:T(2,128)S(1)}, f32[2,512]{1,0:T(2,128)}, u32[]{:S(2)}) copy-start(f32[2,512]{1,0:T(2,128)} %param.24) | copy-start | bytes 12292
  12.6 52.1 %copy-start.23 = (s32[2]{0:T(128)S(1)}, s32[2]{0:T(128)}, u32[]{:S(2)}) copy-start(s32[2]{0:T(128)} %param.26) | copy-start | bytes 28
  14.6 81.8 %all-gather.11.cloned.1.call-start = ((), (), s32[]{:S(2)}) async-start(), calls=%async_computation.17 | async-start | bytes 1310720 | tf_op jit(solution)/shard_map/all_gather | solution.py:37
  15.4 117.0 %all-gather.13.cloned.1.call-start = ((), (), s32[]{:S(2)}) async-start(), calls=%async_computation.18 | async-start | bytes 2949120 | tf_op jit(solution)/shard_map/all_gather | solution.py:37
  16.1 22.6 %all-to-all-start = ((bf16[32,2,512]{2,1,0:T(2,128)(2,1)}), bf16[32,2,512]{2,1,0:T(2,128)(2,1)S(1)}, u32[]{:S(2)}, u32[]{:S(2)}) async-start(bf16[32,2,512]{2,1,0:T(2,128)(2,1)} %reshape.262), calls=%async_computation | async-start | bytes 131072 | tf_op jit(solution)/shard_map/all_to_all | solution.py:69
  29.8 185.0 %all-gather.15.cloned.1.call-start = ((), (), s32[]{:S(2)}) async-start(), calls=%async_computation.19 | async-start | bytes 2621440 | tf_op jit(solution)/shard_map/all_gather | solution.py:37
  30.4 12.8 %copy-start.21 = (s32[32]{0:T(128)}, s32[32]{0:T(128)S(1)}, u32[]{:S(2)}) copy-start(s32[32]{0:T(128)S(1)} %iota_add_fusion.4) | copy-start | bytes 388
  30.5 50.0 %copy-start.15 = (s32[512]{0:T(512)}, s32[512]{0:T(512)S(1)}, u32[]{:S(2)}) copy-start(s32[512]{0:T(512)S(1)} %iota_add_fusion.1) | copy-start | bytes 6148
  39.3 12.7 %all-to-all-start.1 = ((bf16[32,2,512]{2,1,0:T(2,128)(2,1)}), bf16[32,2,512]{2,1,0:T(2,128)(2,1)S(1)}, u32[]{:S(2)}, u32[]{:S(2)}) async-start(bf16[32,2,512]{2,1,0:T(2,128)(2,1)} %shard_map.166), calls=%async_computation.1 | async-start | bytes 131072 | tf_op jit(solution)/shard_map/all_to_all | solution.py:69
  53.1 0.6 copy-start.5
  53.8 22.1 %all-to-all-start.2 = ((bf16[16,4,16,128]{3,2,1,0:T(8,128)(2,1)}), bf16[16,4,16,128]{3,2,1,0:T(8,128)(2,1)S(1)}, u32[]{:S(2)}, u32[]{:S(2)}) async-start(bf16[16,4,16,128]{3,2,1,0:T(8,128)(2,1)} %get-tuple-element.26), calls=%async_computation.2 | async-start | bytes 524288 | tf_op jit(solution)/shard_map/all_to_all | solution.py:59
  76.6 14.5 %all-to-all-start.3 = ((bf16[32,4,4,128]{3,2,1,0:T(4,128)(2,1)}), bf16[32,4,4,128]{3,2,1,0:T(4,128)(2,1)S(1)}, u32[]{:S(2)}, u32[]{:S(2)}) async-start(bf16[32,4,4,128]{3,2,1,0:T(4,128)(2,1)} %get-tuple-element.27), calls=%async_computation.3 | async-start | bytes 262144 | tf_op jit(solution)/shard_map/all_to_all | solution.py:69
  83.3 14.5 %copy-start = (bf16[4,1136,256]{2,1,0:T(8,128)(2,1)}, bf16[4,1136,256]{2,1,0:T(8,128)(2,1)S(1)}, u32[]{:S(2)}) copy-start(bf16[4,1136,256]{2,1,0:T(8,128)(2,1)S(1)} %broadcast_add_fusion.1.inverse) | copy-start | bytes 6979588
  93.0 17.2 %copy-start.10 = (s32[2,32]{1,0:T(2,128)S(1)}, s32[2,32]{1,0:T(2,128)}, u32[]{:S(2)}) copy-start(s32[2,32]{1,0:T(2,128)} %blocks.2) | copy-start | bytes 772
  93.0 17.2 %copy-start.22 = (s32[32]{0:T(128)S(1)}, s32[32]{0:T(128)}, u32[]{:S(2)}) copy-start(s32[32]{0:T(128)} %copy-done.21) | copy-start | bytes 388
  93.0 17.2 %copy-start.24 = (s32[12]{0:T(128)S(1)}, s32[12]{0:T(128)}, u32[]{:S(2)}) copy-start(s32[12]{0:T(128)} %iota_add_fusion.5) | copy-start | bytes 148
  93.0 10.5 %all-to-all-start.4 = ((bf16[8,2,4,512]{3,2,1,0:T(4,128)(2,1)}), bf16[8,2,4,512]{3,2,1,0:T(4,128)(2,1)S(1)}, u32[]{:S(2)}, u32[]{:S(2)}) async-start(bf16[8,2,4,512]{3,2,1,0:T(4,128)(2,1)} %get-tuple-element.33), calls=%async_computation.4 | async-start | bytes 131072 | tf_op jit(solution)/shard_map/all_to_all | solution.py:55
  104.7 0.6 copy-start.7
  105.3 14.2 %all-to-all-start.5 = ((bf16[16,2,4,512]{3,2,1,0:T(4,128)(2,1)}), bf16[16,2,4,512]{3,2,1,0:T(4,128)(2,1)S(1)}, u32[]{:S(2)}, u32[]{:S(2)}) async-start(bf16[16,2,4,512]{3,2,1,0:T(4,128)(2,1)} %get-tuple-element.35), calls=%async_computation.5 | async-start | bytes 262144 | tf_op jit(solution)/shard_map/all_to_all | solution.py:59
  120.1 11.1 %all-to-all-start.6 = ((bf16[8,2,4,512]{3,2,1,0:T(4,128)(2,1)}), bf16[8,2,4,512]{3,2,1,0:T(4,128)(2,1)S(1)}, u32[]{:S(2)}, u32[]{:S(2)}) async-start(bf16[8,2,4,512]{3,2,1,0:T(4,128)(2,1)} %shard_map.171), calls=%async_computation.6 | async-start | bytes 131072 | tf_op jit(solution)/shard_map/all_to_all | solution.py:55
  132.4 1.9 copy-start.12
  136.2 0.6 copy-start.4
  136.8 45.7 %copy-start.11 = (s32[2,32]{1,0:T(2,128)S(1)}, s32[2,32]{1,0:T(2,128)}, u32[]{:S(2)}) copy-start(s32[2,32]{1,0:T(2,128)} %blocks.2) | copy-start | bytes 772
  136.8 14.1 %all-to-all-start.7 = ((bf16[8,1,4,768]{3,2,1,0:T(4,128)(2,1)}), bf16[8,1,4,768]{3,2,1,0:T(4,128)(2,1)S(1)}, u32[]{:S(2)}, u32[]{:S(2)}) async-start(bf16[8,1,4,768]{3,2,1,0:T(4,128)(2,1)} %copy-done.4), calls=%async_computation.7 | async-start | bytes 98304 | tf_op jit(solution)/shard_map/all_to_all | solution.py:55
  144.6 48.2 %copy-start.8 = (f32[2,4,512]{2,1,0:T(4,128)S(1)}, f32[2,4,512]{2,1,0:T(4,128)}, u32[]{:S(2)}) copy-start(f32[2,4,512]{2,1,0:T(4,128)} %copy-done.7) | copy-start | bytes 49156
  150.9 41.9 %copy-start.1 = (bf16[4,1136,256]{2,1,0:T(8,128)(2,1)S(1)}, bf16[4,1136,256]{2,1,0:T(8,128)(2,1)}, u32[]{:S(2)}) copy-start(bf16[4,1136,256]{2,1,0:T(8,128)(2,1)} %copy-done) | copy-start | bytes 6979588
  171.1 27.8 %copy-start.16 = (s32[512]{0:T(512)S(1)}, s32[512]{0:T(512)}, u32[]{:S(2)}) copy-start(s32[512]{0:T(512)} %copy-done.15) | copy-start | bytes 6148
  171.1 27.8 %copy-start.19 = (s32[4]{0:T(128)S(1)}, s32[4]{0:T(128)}, u32[]{:S(2)}) copy-start(s32[4]{0:T(128)} %param.27) | copy-start | bytes 52
  193.9 16.8 %all-to-all-start.11 = ((bf16[16,2,4,1024]{3,2,1,0:T(4,128)(2,1)}), bf16[16,2,4,1024]{3,2,1,0:T(4,128)(2,1)S(1)}, u32[]{:S(2)}, u32[]{:S(2)}) async-start(bf16[16,2,4,1024]{3,2,1,0:T(4,128)(2,1)} %shard_map.176), calls=%async_computation.11 | async-start | bytes 524288 | tf_op jit(solution)/shard_map/all_to_all | solution.py:59
  211.4 12.7 %all-to-all-start.12 = ((bf16[8,2,4,1024]{3,2,1,0:T(4,128)(2,1)}), bf16[8,2,4,1024]{3,2,1,0:T(4,128)(2,1)S(1)}, u32[]{:S(2)}, u32[]{:S(2)}) async-start(bf16[8,2,4,1024]{3,2,1,0:T(4,128)(2,1)} %get-tuple-element.40), calls=%async_computation.12 | async-start | bytes 262144 | tf_op jit(solution)/shard_map/all_to_all | solution.py:55
  216.6 20.8 %copy-start.6 = (f32[4,4,512]{2,1,0:T(4,128)S(1)}, f32[4,4,512]{2,1,0:T(4,128)}, u32[]{:S(2)}) copy-start(f32[4,4,512]{2,1,0:T(4,128)} %copy-done.5) | copy-start | bytes 98308
  216.6 28.3 %copy-start.2 = (bf16[4,512,256]{2,1,0:T(8,128)(2,1)S(1)}, bf16[4,512,256]{2,1,0:T(8,128)(2,1)}, u32[]{:S(2)}) copy-start(bf16[4,512,256]{2,1,0:T(8,128)(2,1)} %inverse.1) | copy-start | bytes 3145732
  225.7 11.6 %all-to-all-start.13 = ((bf16[8,4,4,512]{3,2,1,0:T(4,128)(2,1)}), bf16[8,4,4,512]{3,2,1,0:T(4,128)(2,1)S(1)}, u32[]{:S(2)}, u32[]{:S(2)}) async-start(bf16[8,4,4,512]{3,2,1,0:T(4,128)(2,1)} %shard_map.178), calls=%async_computation.13 | async-start | bytes 262144 | tf_op jit(solution)/shard_map/all_to_all | solution.py:55
  237.4 32.5 %copy-start.14 = (f32[4,256]{1,0:T(4,128)S(1)}, f32[4,256]{1,0:T(4,128)}, u32[]{:S(2)}) copy-start(f32[4,256]{1,0:T(4,128)} %copy-done.13) | copy-start | bytes 12292
  246.0 23.8 %all-to-all-start.15 = ((bf16[16,4,16,256]{3,2,1,0:T(8,128)(2,1)}), bf16[16,4,16,256]{3,2,1,0:T(8,128)(2,1)S(1)}, u32[]{:S(2)}, u32[]{:S(2)}) async-start(bf16[16,4,16,256]{3,2,1,0:T(8,128)(2,1)} %shard_map.179), calls=%async_computation.15 | async-start | bytes 1048576 | tf_op jit(solution)/shard_map/all_to_all | solution.py:59
Sparse Core Ops, SparseCore 0:
  14.7 44.2 all-gather.8
  61.2 28.7 all-gather.10
  92.0 40.1 all-gather.12
  134.2 36.2 all-gather.14
